TPU v7x, 128 devices: a whole 4x4x4 slice. The times are simulated.
128 devices in a mesh: dp: 2 (over core), context: 16 (over z, y), tensor: 4 (over x).
Axes of the slice: x: 4, y: 4, z: 4, core: 2. Of those that a mesh axis runs over, the one named last changes fastest.
Arguments:
- byte_grads: bfloat16 [2, 65536, 1024], P('dp', 'context'), may hold values from -6 to 6
- patch_starts: int32 [2, 8192], P('dp'), may hold values from 0 to 65535, as said below
- patch_owner: int32 [2, 8192], P('dp'), may hold values from 0 to 15, as said below
- attn_context: bfloat16 [2, 8192, 4096], P('dp', 'context', 'tensor'), may hold values from -0.0625 to 0.0625
- w_global: bfloat16 [4096, 4096], P(None, 'tensor'), may hold values from -0.09375 to 0.09375
- w_value: bfloat16 [4096, 1024], P('tensor'), may hold values from -0.09375 to 0.09375
- w_out: bfloat16 [1024, 1024], replicated, may hold values from -0.1875 to 0.1875
Outputs:
- context_grad: bfloat16 [2, 8192, 4096], P('dp', 'context', 'tensor')
- w_global_grad: float32 [4096, 4096], P(('dp', 'context'), 'tensor')
Inputs may be any that keep to these rules, and one draw needn't show every extreme that they name: `patch_starts`: every row rises strictly from 0. The patches that intersect the 4096 bytes of one index of context number at most 1024, and in every sequence the second index has exactly that many, the first of them at the last place of an aligned group of 16 patches. `patch_owner`: in every aligned group of 16 consecutive patches each index of context holds exactly one patch.
All inputs are finite; a program needn't handle non-finite values.
Results may differ from a plain program's by a relative error of at most 0.02.
Values may be sent and summed in bfloat16 or wider, within the bound.
No kernel may reach another device: no remote copies, remote signals or barrier semaphores. Data moves between devices by JAX's collectives and lax.ppermute only.
A program may use at most 128 MiB of HBM per device.

v0:
```python
import jax
import jax.numpy as jnp
from jax import lax
from jax.sharding import PartitionSpec as P


def segment_rows(columns, local_patch, most_rows, block_len):
    feat_width = columns.shape[1]
    slot_index = jnp.arange(block_len, dtype=jnp.int32)

    def one_block(block_index, running):
        labels = lax.dynamic_slice_in_dim(local_patch, block_index * block_len, block_len)
        first_slot = labels[0]
        byte_rows = lax.dynamic_slice_in_dim(columns, block_index * block_len, block_len, 0)
        onehot = (slot_index[:, None] == (labels - first_slot)[None, :]).astype(jnp.bfloat16)
        summed = jnp.dot(onehot, byte_rows, preferred_element_type=jnp.float32)
        current = lax.dynamic_slice_in_dim(running, first_slot, block_len, 0)
        return lax.dynamic_update_slice_in_dim(running, current + summed, first_slot, 0)

    start_sums = jnp.zeros((most_rows + block_len, feat_width), jnp.float32)
    running = lax.fori_loop(0, columns.shape[0] // block_len, one_block, start_sums)
    return running[:most_rows]


def project(patch_sums, w_out, w_value):
    highest = lax.Precision.HIGHEST
    value_grad = jnp.dot(patch_sums, w_out.astype(jnp.float32).T, precision=highest)
    return jnp.dot(value_grad, w_value.astype(jnp.float32).T, precision=highest)


def local(byte_grads, patch_starts, patch_owner, attn_context, w_global, w_value, w_out):
    groups_n = lax.axis_size("context")
    ctx_index = lax.axis_index("context")
    grad_bytes = byte_grads[0]
    bytes_n = grad_bytes.shape[0]
    starts_row = patch_starts[0]
    owner_row = patch_owner[0]
    patch_rows = attn_context.shape[1]
    most_rows = 2 * patch_rows
    group_slots = most_rows // groups_n + 1
    block_len = min(512, bytes_n)
    shard_edges = jnp.arange(groups_n, dtype=jnp.int32) * bytes_n
    first_all = jnp.sum((starts_row[None, :] <= shard_edges[:, None]).astype(jnp.int32), axis=1) - 1
    lowest = jnp.sum(jnp.where(jnp.arange(groups_n, dtype=jnp.int32) == ctx_index, first_all, 0))
    starts_pad = jnp.concatenate([starts_row, jnp.full((most_rows,), 2**30, jnp.int32)])
    window = lax.dynamic_slice_in_dim(starts_pad, lowest, most_rows)
    positions = (ctx_index * bytes_n + jnp.arange(bytes_n, dtype=jnp.int32)).reshape(
        bytes_n // block_len, block_len
    )
    counted = jnp.sum((window[None, None, :] <= positions[:, :, None]).astype(jnp.int32), axis=2)
    local_patch = counted.reshape(bytes_n) - 1
    patch_sums = segment_rows(grad_bytes, local_patch, most_rows, block_len)
    partial_rows = project(patch_sums, w_out, w_value)
    feat_width = partial_rows.shape[1]
    padded = jnp.zeros((group_slots * groups_n, feat_width), jnp.float32)
    padded = lax.dynamic_update_slice_in_dim(padded, partial_rows, lowest % groups_n, 0)
    grouped = padded.reshape(group_slots, groups_n, feat_width)
    owner_pad = jnp.concatenate(
        [owner_row, jnp.tile(jnp.arange(groups_n, dtype=jnp.int32), group_slots)]
    )
    owner_block = lax.dynamic_slice_in_dim(
        owner_pad, lowest // groups_n * groups_n, group_slots * groups_n
    )
    owner_block = owner_block.reshape(group_slots, groups_n)
    owner_ids = jnp.arange(groups_n, dtype=jnp.int32)
    placing = (owner_block[:, None, :] == owner_ids[None, :, None]).astype(jnp.float32)
    outgoing = jnp.einsum("gji,gif->gjf", placing, grouped, precision=lax.Precision.HIGHEST)
    incoming = lax.all_to_all(
        outgoing.astype(jnp.bfloat16), "context", split_axis=1, concat_axis=1, tiled=True
    ).astype(outgoing.dtype)
    group_first = first_all // groups_n

    def add_source(source, running):
        received_piece = lax.dynamic_index_in_dim(incoming, source, 1, keepdims=False)
        row_start = group_first[source]
        current = lax.dynamic_slice_in_dim(running, row_start, group_slots, 0)
        return lax.dynamic_update_slice_in_dim(running, current + received_piece, row_start, 0)

    start_rows = jnp.zeros((patch_rows + group_slots, feat_width), jnp.float32)
    collected = lax.fori_loop(0, groups_n, add_source, start_rows)[:patch_rows]
    rows_grad = collected.astype(jnp.bfloat16)
    context_full = lax.all_gather(attn_context[0], "tensor", axis=1, tiled=True)
    partial_term = lax.dot_general(
        rows_grad, w_global, (((1,), (1,)), ((), ())), preferred_element_type=jnp.float32
    )
    context_grad = lax.psum_scatter(
        partial_term.astype(jnp.bfloat16), "tensor", scatter_dimension=1, tiled=True
    )
    weight_grad = lax.psum_scatter(
        lax.dot_general(
            context_full, rows_grad, (((0,), (0,)), ((), ())), preferred_element_type=jnp.float32
        ).astype(jnp.bfloat16),
        ("dp", "context"),
        scatter_dimension=0,
        tiled=True,
    ).astype(jnp.float32)
    return (context_grad[None], weight_grad)


def solution(mesh):
    placed = (
        P("dp", "context", None),
        P("dp", None),
        P("dp", None),
        P("dp", "context", "tensor"),
        P(None, "tensor"),
        P("tensor", None),
        P(),
    )
    return jax.shard_map(
        local,
        mesh=mesh,
        in_specs=placed,
        out_specs=(P("dp", "context", "tensor"), P(("dp", "context"), "tensor")),
        check_vma=False,
    )
```

profile of v0, /device:TPU:1, one launch (start us, length us, event | category | flops | bytes accessed | tf_op | source)
XLA Modules:
  0.0 475.9 jit_solution(8112985141888153788)
XLA Ops:
  12.3 2.2 convert_reduce_fusion
  14.6 3.4 broadcast_in_dim.29
  18.0 110.1 %while.28 = (s32[]{:T(128)}, f32[1536,1024]{1,0:T(8,128)}, s32[4096]{0:T(1024)S(1)}, bf16[4096,1024]{1,0:T(8,128)(2,1)}, s32[]{:T(128)}, /*index=5*/s32[]{:T(128)}, s32[]{:T(128)}, s32[]{:T(128)}, s32[]{:T(128)}) while((s32[]{:T(128)}, f32[1536,1024]{1,0:T(8,128)}, s32[4096]{0:T(1024)S(1)}, bf16[4096,1024]{1,0:T(8,128)(2,1)}, ...), condition=%wide.region_4.5_spmd.clone, body=%wide.region_3.4_spmd.clone.sunk | while | flops 537657856 | bytes 9447629 | solution.py:21
  20.9 4.3 dynamic-slice_add_fusion.2
  25.2 6.8 %dynamic_update_slice.22 = f32[1536,1024]{1,0:T(8,128)} dynamic-update-slice(f32[1536,1024]{1,0:T(8,128)} %get-tuple-element.281, f32[512,1024]{1,0:T(8,128)} %dynamic-slice_add_fusion.2, s32[]{:T(128)S(6)} %select_n.78, s32[]{:T(128)} %constant.114.clone.1..sunk.1) | dynamic-update-slice | bytes 4194308 | tf_op jit(solution)/shard_map/while/body/eval_jaxpr/dynamic_update_slice | solution.py:18
  35.0 4.0 dynamic-slice_add_fusion.2
  39.0 6.8 %dynamic_update_slice.22 = f32[1536,1024]{1,0:T(8,128)} dynamic-update-slice(f32[1536,1024]{1,0:T(8,128)} %get-tuple-element.281, f32[512,1024]{1,0:T(8,128)} %dynamic-slice_add_fusion.2, s32[]{:T(128)S(6)} %select_n.78, s32[]{:T(128)} %constant.114.clone.1..sunk.1) | dynamic-update-slice | bytes 4194308 | tf_op jit(solution)/shard_map/while/body/eval_jaxpr/dynamic_update_slice | solution.py:18
  48.7 4.0 dynamic-slice_add_fusion.2
  52.7 6.8 %dynamic_update_slice.22 = f32[1536,1024]{1,0:T(8,128)} dynamic-update-slice(f32[1536,1024]{1,0:T(8,128)} %get-tuple-element.281, f32[512,1024]{1,0:T(8,128)} %dynamic-slice_add_fusion.2, s32[]{:T(128)S(6)} %select_n.78, s32[]{:T(128)} %constant.114.clone.1..sunk.1) | dynamic-update-slice | bytes 4194308 | tf_op jit(solution)/shard_map/while/body/eval_jaxpr/dynamic_update_slice | solution.py:18
  62.5 4.0 dynamic-slice_add_fusion.2
  66.5 6.8 %dynamic_update_slice.22 = f32[1536,1024]{1,0:T(8,128)} dynamic-update-slice(f32[1536,1024]{1,0:T(8,128)} %get-tuple-element.281, f32[512,1024]{1,0:T(8,128)} %dynamic-slice_add_fusion.2, s32[]{:T(128)S(6)} %select_n.78, s32[]{:T(128)} %constant.114.clone.1..sunk.1) | dynamic-update-slice | bytes 4194308 | tf_op jit(solution)/shard_map/while/body/eval_jaxpr/dynamic_update_slice | solution.py:18
  76.2 4.0 dynamic-slice_add_fusion.2
  80.2 6.8 %dynamic_update_slice.22 = f32[1536,1024]{1,0:T(8,128)} dynamic-update-slice(f32[1536,1024]{1,0:T(8,128)} %get-tuple-element.281, f32[512,1024]{1,0:T(8,128)} %dynamic-slice_add_fusion.2, s32[]{:T(128)S(6)} %select_n.78, s32[]{:T(128)} %constant.114.clone.1..sunk.1) | dynamic-update-slice | bytes 4194308 | tf_op jit(solution)/shard_map/while/body/eval_jaxpr/dynamic_update_slice | solution.py:18
  89.9 4.0 dynamic-slice_add_fusion.2
  93.9 6.8 %dynamic_update_slice.22 = f32[1536,1024]{1,0:T(8,128)} dynamic-update-slice(f32[1536,1024]{1,0:T(8,128)} %get-tuple-element.281, f32[512,1024]{1,0:T(8,128)} %dynamic-slice_add_fusion.2, s32[]{:T(128)S(6)} %select_n.78, s32[]{:T(128)} %constant.114.clone.1..sunk.1) | dynamic-update-slice | bytes 4194308 | tf_op jit(solution)/shard_map/while/body/eval_jaxpr/dynamic_update_slice | solution.py:18
  103.7 4.0 dynamic-slice_add_fusion.2
  107.7 6.8 %dynamic_update_slice.22 = f32[1536,1024]{1,0:T(8,128)} dynamic-update-slice(f32[1536,1024]{1,0:T(8,128)} %get-tuple-element.281, f32[512,1024]{1,0:T(8,128)} %dynamic-slice_add_fusion.2, s32[]{:T(128)S(6)} %select_n.78, s32[]{:T(128)} %constant.114.clone.1..sunk.1) | dynamic-update-slice | bytes 4194308 | tf_op jit(solution)/shard_map/while/body/eval_jaxpr/dynamic_update_slice | solution.py:18
  117.4 4.0 dynamic-slice_add_fusion.2
  121.4 6.8 %dynamic_update_slice.22 = f32[1536,1024]{1,0:T(8,128)} dynamic-update-slice(f32[1536,1024]{1,0:T(8,128)} %get-tuple-element.281, f32[512,1024]{1,0:T(8,128)} %dynamic-slice_add_fusion.2, s32[]{:T(128)S(6)} %select_n.78, s32[]{:T(128)} %constant.114.clone.1..sunk.1) | dynamic-update-slice | bytes 4194308 | tf_op jit(solution)/shard_map/while/body/eval_jaxpr/dynamic_update_slice | solution.py:18
  130.4 8.7 %fusion.6 = f32[1024,1024]{1,0:T(8,128)S(1)} fusion(bf16[1024,1024]{1,0:T(8,128)(2,1)S(1)} %copy-done, f32[1536,1024]{1,0:T(8,128)} %get-tuple-element.175), kind=kOutput, calls=%fused_computation.12 | convolution fusion | flops 12884901888 | bytes 10485760 | tf_op jit(solution)/shard_map/dot_general | solution.py:27
  139.1 8.3 %fusion.11 = f32[1024,1024]{1,0:T(8,128)} fusion(f32[1024,1024]{1,0:T(8,128)S(1)} %fusion.6, bf16[1024,1024]{1,0:T(8,128)(2,1)S(1)} %copy-done.3), kind=kOutput, calls=%fused_computation.32 | convolution fusion | flops 12884901888 | bytes 10485760 | tf_op jit(solution)/shard_map/dot_general | solution.py:28
  147.3 2.5 broadcast_in_dim.28
  149.8 11.6 %dynamic_update_slice.17 = f32[1040,1024]{1,0:T(8,128)} dynamic-update-slice(f32[1040,1024]{1,0:T(8,128)} %broadcast_in_dim.28, f32[1024,1024]{1,0:T(8,128)} %fusion.11, s32[]{:T(128)S(6)} %select_n.66, s32[]{:T(128)} %constant.114.clone.1) | dynamic-update-slice | bytes 8388612 | tf_op jit(solution)/shard_map/dynamic_update_slice | solution.py:56
  161.4 4.5 convolution_convert_fusion.1
  165.9 2.6 copy.15
  168.5 8.5 %all-to-all-start = ((bf16[65,16,1024]{2,0,1:T(8,128)(2,1)}), bf16[65,16,1024]{2,0,1:T(8,128)(2,1)}, u32[]{:S(2)}, u32[]{:S(2)}) async-start(bf16[65,16,1024]{2,0,1:T(8,128)(2,1)} %copy.15), calls=%async_computation | async-start | bytes 4718592 | tf_op jit(solution)/shard_map/all_to_all | solution.py:68
  177.1 34.4 %all-to-all-done = bf16[65,16,1024]{2,0,1:T(8,128)(2,1)} async-done(((bf16[65,16,1024]{2,0,1:T(8,128)(2,1)}), bf16[65,16,1024]{2,0,1:T(8,128)(2,1)}, u32[]{:S(2)}, u32[]{:S(2)}) %all-to-all-start) | async-done | bytes 2129952 | tf_op jit(solution)/shard_map/all_to_all | solution.py:68
  211.5 4.3 convert_element_type.34
  217.6 87.6 %while.27 = (s32[]{:T(128)}, f32[577,1024]{1,0:T(8,128)}, s32[16]{0:T(128)S(1)}, f32[65,16,1024]{2,0,1:T(8,128)}, s32[]{:T(128)}, /*index=5*/s32[]{:T(128)}, s32[]{:T(128)}) while((s32[]{:T(128)}, f32[577,1024]{1,0:T(8,128)}, s32[16]{0:T(128)S(1)}, f32[65,16,1024]{2,0,1:T(8,128)}, s32[]{:T(128)}, /*index=5*/s32[]{:T(128)}, s32[]{:T(128)}) %tuple.68), condition=%wide.region_6.7_spmd, body=%wide.region_5.6_spmd.sunk | while | flops 66565 | bytes 1331335 | solution.py:80
  221.2 1.8 dynamic_update_slice.21
  226.7 1.8 dynamic_update_slice.21
  232.1 1.8 dynamic_update_slice.21
  237.6 1.8 dynamic_update_slice.21
  243.1 1.8 dynamic_update_slice.21
  248.6 1.8 dynamic_update_slice.21
  254.0 1.8 dynamic_update_slice.21
  259.5 1.8 dynamic_update_slice.21
  265.0 1.8 dynamic_update_slice.21
  270.5 1.9 dynamic_update_slice.21
  276.0 1.9 dynamic_update_slice.21
  281.5 1.8 dynamic_update_slice.21
  286.9 1.8 dynamic_update_slice.21
  297.9 1.8 dynamic_update_slice.21
  305.1 10.6 %convert_bitcast_fusion = bf16[4096,1024]{0,1:T(8,128)(2,1)} fusion(bf16[1,512,4096]{2,1,0:T(8,128)(2,1)} %all-gather.3.cloned.1.call-done, f32[577,1024]{1,0:T(8,128)} %get-tuple-element.176), kind=kOutput, calls=%fused_computation.9 | convolution fusion | flops 4299161600 | bytes 13631488 | tf_op jit(solution)/shard_map/dot_general | solution.py:90
  315.8 12.0 %copy.17 = bf16[4096,1024]{1,0:T(8,128)(2,1)} copy(bf16[4096,1024]{0,1:T(8,128)(2,1)} %convert_bitcast_fusion) | data formatting | bytes 16777216
  328.1 10.6 %convolution_convert_fusion = bf16[512,4096]{1,0:T(8,128)(2,1)} fusion(bf16[4096,1024]{1,0:T(8,128)(2,1)} %param.15, f32[577,1024]{1,0:T(8,128)} %get-tuple-element.176), kind=kOutput, calls=%fused_computation.10 | convolution fusion | flops 4297064448 | bytes 13631488 | tf_op jit(solution)/shard_map/dot_general | solution.py:83
  338.7 79.7 %reduce-scatter.7.cloned.1.call-done = bf16[128,1024]{1,0:T(8,128)(2,1)} async-done(((bf16[4096,1024]{1,0:T(8,128)(2,1)}), bf16[128,1024]{1,0:T(8,128)(2,1)}) %reduce-scatter.7.cloned.1.call-update) | async-done | bytes 262160
  420.5 48.8 %reduce-scatter.5.cloned.1.call-done = bf16[512,1024]{1,0:T(8,128)(2,1)} async-done(((bf16[512,4096]{1,0:T(8,128)(2,1)}), bf16[512,1024]{1,0:T(8,128)(2,1)}) %reduce-scatter.5.cloned.1.call-update) | async-done | bytes 1048592 | tf_op jit(solution)/shard_map/reduce_scatter | solution.py:86
  (87 shorter events, 48.0 us)
Async XLA Ops:
  7.2 123.2 %copy-start = (bf16[1024,1024]{1,0:T(8,128)(2,1)S(1)}, bf16[1024,1024]{1,0:T(8,128)(2,1)}, u32[]{:S(2)}) copy-start(bf16[1024,1024]{1,0:T(8,128)(2,1)} %param.17) | copy-start | bytes 6291460
  7.2 298.0 %all-gather.3.cloned.1.call-start = ((), (), s32[]{:S(2)}) async-start(), calls=%async_computation.4 | async-start | bytes 5242880 | tf_op jit(solution)/shard_map/all_gather | solution.py:82
  18.0 112.2 %copy-start.2 = (s32[1,8192]{1,0:T(1,128)S(1)}, s32[1,8192]{1,0:T(1,128)}, u32[]{:S(2)}) copy-start(s32[1,8192]{1,0:T(1,128)} %param.13) | copy-start | bytes 98308
  130.4 8.7 %copy-start.3 = (bf16[1024,1024]{1,0:T(8,128)(2,1)S(1)}, bf16[1024,1024]{1,0:T(8,128)(2,1)}, u32[]{:S(2)}) copy-start(bf16[1024,1024]{1,0:T(8,128)(2,1)} %param.16) | copy-start | bytes 6291460
  168.5 43.0 %all-to-all-start = ((bf16[65,16,1024]{2,0,1:T(8,128)(2,1)}), bf16[65,16,1024]{2,0,1:T(8,128)(2,1)}, u32[]{:S(2)}, u32[]{:S(2)}) async-start(bf16[65,16,1024]{2,0,1:T(8,128)(2,1)} %copy.15), calls=%async_computation | async-start | bytes 4718592 | tf_op jit(solution)/shard_map/all_to_all | solution.py:68
  177.0 241.4 %reduce-scatter.7.cloned.1.call-start = ((), (), s32[]{:S(2)}) async-start(), calls=%async_computation.5 | async-start | bytes 8650752
  327.8 141.6 %reduce-scatter.5.cloned.1.call-start = ((), (), s32[]{:S(2)}) async-start(), calls=%async_computation.3 | async-start | bytes 5242880 | tf_op jit(solution)/shard_map/reduce_scatter | solution.py:86
  328.0 141.3 %copy-start.1 = (bf16[1024,1024]{1,0:T(8,128)(2,1)S(1)}, bf16[1024,1024]{1,0:T(8,128)(2,1)}, u32[]{:S(2)}) copy-start(bf16[1024,1024]{1,0:T(8,128)(2,1)} %param.17) | copy-start | bytes 6291460
Sparse Core Ops, SparseCore 0:
  9.7 51.3 all-gather.2
  327.9 90.5 reduce-scatter.6
  421.6 47.7 reduce-scatter.4
where the time goes:
time: 480 us; the launch traced here: 476 us
  waiting for transfers between devices  164 us (34%)
  local copies, waits for them, and re-layouts  135 us (28%)
  matrix products  74.9 us (16%)
  loops' own time  44.8 us (9%)
  other arithmetic  31.1 us (6%)
  between operations  17.8 us (4%)
  starting transfers between devices  8.88 us (2%)
    unnamed x4, waiting for transfers between devices  80.5 us
    dynamic_update_slice x8, local copies, waits for them, and re-layouts, one_block(): lax.dynamic_update_slice_in_dim(running, current + summed, first_slot, 0)  54.5 us
    reduce_scatter x1, waiting for transfers between devices, local(): lax.psum_scatter(partial_term.astype(jnp.bfloat16), 'tensor', scatter_dim...  48.8 us
    all_to_all x1, waiting for transfers between devices, local(): lax.all_to_all(outgoing.astype(jnp.bfloat16), 'context', split_axis=1, co...  34.4 us
    dot_general x8, matrix products, one_block(): summed = jnp.dot(onehot, byte_rows, preferred_element_type=jnp.float32)  32.2 us
    another operation x1, loops' own time, local(): collected = lax.fori_loop(0, groups_n, add_source, start_rows)[:patch_rows]  31.2 us
    dynamic_update_slice x16, local copies, waits for them, and re-layouts, add_source(): lax.dynamic_update_slice_in_dim(running, current + received_piece, row_st...  29.4 us
    add x16, other arithmetic, add_source(): current + received_piece  17.7 us
  transfers between devices with their start and end apart: 4, of which 3 were waited for; matrix products, arithmetic and copies ran while one was open for 46% of the time, Pallas kernels for 0%

commit v1 on v0

v1 whole, which is shorter than its diff:
```python
import functools

import jax
import jax.numpy as jnp
from jax import lax
from jax.experimental import pallas as pl
from jax.experimental.pallas import tpu as pltpu
from jax.sharding import PartitionSpec as P

LANES = 128
GROUP = 16
SUB = LANES // GROUP
WIN = 9
SLOT = WIN * SUB
VMEM = 48 * 1024 * 1024


def seg_kernel(idx_ref, starts_ref, owner_ref, bytes_ref, out_ref, next_ref, low_ref, high_ref, acc_ref):
    step = pl.program_id(0)
    block = bytes_ref.shape[0]
    shard = block * pl.num_programs(0)
    owners = out_ref.shape[0] // SLOT

    @pl.when(step == 0)
    def _():
        starts = starts_ref[...]
        rows = starts.shape[0]
        base = idx_ref[0] * shard
        count = jnp.sum((starts <= base).astype(jnp.float32)).astype(jnp.int32)
        first = jnp.minimum(lax.shift_right_logical(count - 1, 7), rows - WIN)
        lane = lax.broadcasted_iota(jnp.int32, starts.shape, 1)
        turned = pltpu.roll(starts, LANES - 1, 1)
        below = jnp.concatenate([turned[1:], jnp.full((1, LANES), 2**30, jnp.int32)], axis=0)
        next_ref[...] = jnp.where(lane == LANES - 1, below, turned)
        lane = lax.broadcasted_iota(jnp.int32, (SUB, LANES), 1)
        mine = lax.shift_right_logical(lane, 4) == lax.broadcasted_iota(jnp.int32, (SUB, LANES), 0)
        for t in range(WIN):
            low = jnp.clip(starts_ref[pl.ds(first + t, 1), :] - base, 0, shard).astype(jnp.float32)
            high = jnp.clip(next_ref[pl.ds(first + t, 1), :] - base, 0, shard).astype(jnp.float32)
            low = jnp.broadcast_to(low, (SUB, LANES))
            high = jnp.broadcast_to(high, (SUB, LANES))
            owner = jnp.broadcast_to(owner_ref[pl.ds(first + t, 1), :], (SUB, LANES))
            owner = jnp.where(mine, owner, -1)
            for j in range(owners):
                held = owner == j
                at = j * SLOT + t * SUB
                one = jnp.sum(jnp.where(held, low, 0.0), axis=1, keepdims=True)
                low_ref[at : at + SUB, :] = jnp.broadcast_to(one, (SUB, LANES))
                one = jnp.sum(jnp.where(held, high, 0.0), axis=1, keepdims=True)
                high_ref[at : at + SUB, :] = jnp.broadcast_to(one, (SUB, LANES))
        acc_ref[...] = jnp.zeros_like(acc_ref)

    low = low_ref[...]
    high = high_ref[...]
    parts = []
    for q in range(block // LANES):
        place = lax.broadcasted_iota(jnp.int32, (1, LANES), 1) + (step * block + q * LANES)
        place = place.astype(jnp.float32)
        parts.append(jnp.where((place >= low) & (place < high), 1.0, 0.0).astype(jnp.bfloat16))
    onehot = jnp.concatenate(parts, axis=1)
    acc_ref[...] += jnp.dot(onehot, bytes_ref[...], preferred_element_type=jnp.float32)

    @pl.when(step == pl.num_programs(0) - 1)
    def _():
        out_ref[...] = acc_ref[...].astype(jnp.bfloat16)


def segment_sums(idx, starts, owner, grads, owners, width, interpret=False):
    bytes_n = grads.shape[0]
    block = 512
    rows = owners * SLOT
    whole = pl.BlockSpec(starts.shape, lambda i, idx: (0, 0))
    return pl.pallas_call(
        seg_kernel,
        grid_spec=pltpu.PrefetchScalarGridSpec(
            num_scalar_prefetch=1,
            grid=(bytes_n // block,),
            in_specs=[whole, whole, pl.BlockSpec((block, width), lambda i, idx: (i, idx[1]))],
            out_specs=pl.BlockSpec((rows, width), lambda i, idx: (0, 0)),
            scratch_shapes=[
                pltpu.VMEM(starts.shape, jnp.int32),
                pltpu.VMEM((rows, LANES), jnp.float32),
                pltpu.VMEM((rows, LANES), jnp.float32),
                pltpu.VMEM((rows, width), jnp.float32),
            ],
        ),
        out_shape=jax.ShapeDtypeStruct((rows, width), jnp.bfloat16),
        compiler_params=pltpu.CompilerParams(vmem_limit_bytes=VMEM),
        interpret=interpret,
    )(idx, starts, owner, grads)


def collect_kernel(first_ref, in_ref, out_ref, wide_ref, acc_ref):
    wide_ref[...] = in_ref[...].astype(jnp.float32)
    acc_ref[...] = jnp.zeros_like(acc_ref)
    for s in range(in_ref.shape[0] // SLOT):
        at = pl.ds(pl.multiple_of(first_ref[s] * SUB, SUB), SLOT)
        acc_ref[at, :] += wide_ref[s * SLOT : (s + 1) * SLOT, :]
    total = acc_ref[...].astype(jnp.bfloat16)
    for x in range(out_ref.shape[0]):
        out_ref[x] = total


def collect(first, incoming, patch_rows, copies, interpret=False):
    rows, width = incoming.shape
    return pl.pallas_call(
        collect_kernel,
        in_specs=[pl.BlockSpec(memory_space=pltpu.SMEM), pl.BlockSpec(memory_space=pltpu.VMEM)],
        out_specs=pl.BlockSpec(memory_space=pltpu.VMEM),
        out_shape=jax.ShapeDtypeStruct((copies, patch_rows, width), jnp.bfloat16),
        scratch_shapes=[pltpu.VMEM((rows, width), jnp.float32), pltpu.VMEM((patch_rows, width), jnp.float32)],
        compiler_params=pltpu.CompilerParams(vmem_limit_bytes=VMEM),
        interpret=interpret,
    )(first, incoming)


def outer_kernel(half_ref, own_t_ref, far_t_ref, own_ref, far_ref, out_ref):
    total = jnp.dot(own_t_ref[...], own_ref[0], preferred_element_type=jnp.float32)
    total += jnp.dot(far_t_ref[...], far_ref[0], preferred_element_type=jnp.float32)
    out_ref[...] = total.astype(jnp.bfloat16)


def outer(half, own_t, far_t, own, far):
    cols, rows = own_t.shape
    parts, _, width = far.shape
    whole = pl.BlockSpec((cols, rows), lambda i, half: (0, 0))
    return pl.pallas_call(
        outer_kernel,
        grid_spec=pltpu.PrefetchScalarGridSpec(
            num_scalar_prefetch=1,
            grid=(parts,),
            in_specs=[
                whole,
                whole,
                pl.BlockSpec((1, rows, width), lambda i, half: (half[0] * parts + i, 0, 0)),
                pl.BlockSpec((1, rows, width), lambda i, half: (i, 0, 0)),
            ],
            out_specs=pl.BlockSpec((cols, width), lambda i, half: (0, i)),
        ),
        out_shape=jax.ShapeDtypeStruct((cols, parts * width), jnp.bfloat16),
        compiler_params=pltpu.CompilerParams(vmem_limit_bytes=VMEM),
    )(half, own_t, far_t, own, far)


def local(byte_grads, patch_starts, patch_owner, attn_context, w_global, w_value, w_out):
    dp_n, ctx_n, ten_n = (lax.axis_size(a) for a in ("dp", "context", "tensor"))
    dp = lax.axis_index("dp")
    ctx = lax.axis_index("context")
    ten = lax.axis_index("tensor")
    f32, bf16 = jnp.float32, jnp.bfloat16
    bytes_n, feats = byte_grads.shape[1:]
    width = feats // ten_n
    patch_rows, cols = attn_context.shape[1:]
    starts = patch_starts.reshape(-1, LANES)
    owner = patch_owner.reshape(-1, LANES)

    outgoing = segment_sums(jnp.stack([ctx, ten]), starts, owner, byte_grads[0], ctx_n, width)
    incoming = lax.all_to_all(outgoing, "context", split_axis=0, concat_axis=0, tiled=True)

    swap = [(i, dp_n - 1 - i) for i in range(dp_n)]
    far_context = lax.ppermute(attn_context[0], "dp", swap)
    own_t = attn_context[0].T
    far_t = far_context.T
    edges = jnp.arange(ctx_n, dtype=jnp.int32) * bytes_n
    counts = jnp.sum((patch_starts[0][None, :] <= edges[:, None]).astype(jnp.int32), axis=1)
    first = jnp.minimum((counts - 1) // LANES, starts.shape[0] - WIN)
    both = lax.dot_general(w_out, w_value, (((0,), (1,)), ((), ())), preferred_element_type=f32).astype(bf16)
    share = feats // (dp_n * ctx_n)
    some = lax.dynamic_slice_in_dim(both, (dp * ctx_n + ctx) * share, share, 0)
    term = lax.dot_general(some, w_global, (((1,), (1,)), ((), ())), preferred_element_type=f32).astype(bf16)
    term = lax.psum_scatter(term, "tensor", scatter_dimension=1, tiled=True)
    whole = lax.all_gather(term, ("dp", "context"), axis=0, tiled=True)

    sums = collect(first, incoming, patch_rows, ten_n)
    sums = lax.all_to_all(sums, "tensor", split_axis=0, concat_axis=0)
    half = ten_n // dp_n
    far_sums = lax.ppermute(lax.dynamic_slice_in_dim(sums, (dp_n - 1 - dp) * half, half, 0), "dp", swap)

    partial = outer(dp[None], own_t, far_t, sums, far_sums)
    pieces = lax.all_to_all(partial, "context", split_axis=0, concat_axis=0, tiled=True)
    rows_n = cols // ctx_n
    piece = jnp.sum(pieces.reshape(ctx_n, rows_n, -1).astype(f32), axis=0).astype(bf16)
    moves = []
    per = ctx_n * dp_n // ten_n
    cuts = ctx_n // per
    for d in range(dp_n):
        for c in range(ctx_n):
            for k in range(ten_n):
                to = (per * k + c // cuts) * ten_n + (c % cuts) * dp_n + d
                moves.append(((d * ctx_n + c) * ten_n + k, to))
    piece = lax.ppermute(piece, ("dp", "context", "tensor"), moves)
    block = lax.all_gather(piece, "tensor", axis=0)
    block = block.reshape(cuts, dp_n, rows_n, -1).transpose(0, 2, 1, 3).reshape(cuts * rows_n, feats)
    weight_grad = jnp.dot(block, both, preferred_element_type=f32)

    context_grad = lax.dot_general(
        sums, whole.reshape(ten_n, width, -1), (((0, 2), (0, 1)), ((), ())), preferred_element_type=f32
    ).astype(bf16)
    return (context_grad[None], weight_grad)


def solution(mesh):
    placed = (
        P("dp", "context", None),
        P("dp", None),
        P("dp", None),
        P("dp", "context", "tensor"),
        P(None, "tensor"),
        P("tensor", None),
        P(),
    )
    return jax.shard_map(
        local,
        mesh=mesh,
        in_specs=placed,
        out_specs=(P("dp", "context", "tensor"), P(("dp", "context"), "tensor")),
        check_vma=False,
    )
```

time: 480 us -> 148 us (0.31)
  the two profiles are of different devices: /device:TPU:1 before, /device:TPU:16 now
where the time goes in v1:
time: 148 us; the launch traced here: 147 us
  waiting for transfers between devices  48.9 us (33%)
  blocking collectives  33.7 us (23%)
  starting transfers between devices  14.9 us (10%)
  between operations  14.2 us (10%)
  matrix products  14 us (9%)
  Pallas kernels  12.4 us (8%)
  local copies, waits for them, and re-layouts  7.65 us (5%)
  other arithmetic  1.73 us (1%)
    reduce_scatter x1, waiting for transfers between devices, local(): term = lax.psum_scatter(term, 'tensor', scatter_dimension=1, tiled=True)  22.9 us
    all_to_all x1, blocking collectives, local(): lax.all_to_all(partial, 'context', split_axis=0, concat_axis=0, tiled=True)  21.3 us
    all_gather x1, blocking collectives, local(): block = lax.all_gather(piece, 'tensor', axis=0)  12.4 us
    all_to_all x1, waiting for transfers between devices, local(): sums = lax.all_to_all(sums, 'tensor', split_axis=0, concat_axis=0)  9.37 us
    pallas_call x1, Pallas kernels, segment_sums(): pl.pallas_call(seg_kernel, grid_spec=pltpu.PrefetchScalarGridSpec(num_sca...  8.86 us
    all_to_all x1, waiting for transfers between devices, local(): lax.all_to_all(outgoing, 'context', split_axis=0, concat_axis=0, tiled=True)  7.85 us
    all_to_all x1, starting transfers between devices, local(): lax.all_to_all(outgoing, 'context', split_axis=0, concat_axis=0, tiled=True)  7.4 us
    unnamed x16, local copies, waits for them, and re-layouts  7.34 us
  transfers between devices with their start and end apart: 7, of which 5 were waited for; matrix products, arithmetic and copies ran while one was open for 5% of the time, Pallas kernels for 8%

profile of v1, /device:TPU:16, one launch (start us, length us, event | category | flops | bytes accessed | tf_op | source)
XLA Modules:
  0.0 147.4 jit_solution(5808178327801393536)
XLA Ops:
  7.2 0.0 copy-start
  7.2 0.0 reduce-scatter.2.cloned.1.call-start
  7.2 1.5 %copy-done = bf16[1024,1024]{1,0:T(8,128)(2,1)S(1)} copy-done((bf16[1024,1024]{1,0:T(8,128)(2,1)S(1)}, bf16[1024,1024]{1,0:T(8,128)(2,1)}, u32[]{:S(2)}) %copy-start) | copy-done | bytes 2097176
  8.8 0.0 copy-start.5
  8.8 4.1 %convolution_convert_fusion.1 = bf16[1024,1024]{1,0:T(8,128)(2,1)S(1)} fusion(bf16[1024,1024]{1,0:T(8,128)(2,1)S(1)} %copy-done, bf16[1024,1024]{1,0:T(8,128)(2,1)} %param.12), kind=kOutput, calls=%fused_computation.2 | convolution fusion | flops 2148532224 | bytes 6291456 | tf_op jit(solution)/shard_map/dot_general | solution.py:167
  12.9 0.0 copy-start.6
  12.9 1.3 copy-done.6
  14.2 0.0 copy-done.5
  14.2 0.0 copy-start.3
  14.2 0.0 copy-start.4
  14.2 3.3 %convolution_convert_fusion = bf16[32,4096]{1,0:T(8,128)(2,1)} fusion(bf16[4096,1024]{1,0:T(8,128)(2,1)S(1)} %copy-done.5, bf16[1024,1024]{1,0:T(8,128)(2,1)S(1)} %convolution_convert_fusion.1, s32[]{:T(128)S(6)} %select_n.12), kind=kOutput, calls=%fused_computation | convolution fusion | flops 268566528 | bytes 8716292 | tf_op jit(solution)/shard_map/dot_general | solution.py:170
  17.5 0.0 reduce-scatter.2.cloned.1.call-update
  17.5 0.0 all-gather.3.cloned.1.call-start
  17.6 22.9 %reduce-scatter.2.cloned.1.call-done = bf16[32,1024]{1,0:T(8,128)(2,1)} async-done(((bf16[32,4096]{1,0:T(8,128)(2,1)}), bf16[32,1024]{1,0:T(8,128)(2,1)}) %reduce-scatter.2.cloned.1.call-update) | async-done | bytes 65552 | tf_op jit(solution)/shard_map/reduce_scatter | solution.py:171
  40.4 0.0 all-gather.3.cloned.1.call-update
  40.5 0.1 pad_add_fusion.idx_ref
  40.5 0.0 copy-done.3
  40.5 0.0 copy-done.4
  40.6 8.9 %shard_map.86 = bf16[1152,256]{1,0:T(8,128)(2,1)} custom-call(s32[2]{0:T(128)S(1)} %pad_add_fusion.idx_ref, s32[64,128]{1,0:T(8,128)S(1)} %bitcast.38, s32[64,128]{1,0:T(8,128)S(1)} %bitcast.40, bf16[4096,1024]{1,0:T(8,128)(2,1)} %bitcast.41), custom_call_target="tpu_custom_call" | custom-call | tf_op jit(solution)/shard_map/pallas_call | solution.py:73
  49.4 7.4 %all-to-all-start = ((bf16[16,72,256]{2,1,0:T(8,128)(2,1)}), bf16[16,72,256]{2,1,0:T(8,128)(2,1)S(1)}, u32[]{:S(2)}, u32[]{:S(2)}) async-start(bf16[16,72,256]{2,1,0:T(8,128)(2,1)} %bitcast.6), calls=%async_computation | async-start | bytes 1179648 | tf_op jit(solution)/shard_map/all_to_all | solution.py:158
  56.8 0.3 convert_reduce_fusion
  57.1 7.9 %all-to-all-done = bf16[16,72,256]{2,1,0:T(8,128)(2,1)S(1)} async-done(((bf16[16,72,256]{2,1,0:T(8,128)(2,1)}), bf16[16,72,256]{2,1,0:T(8,128)(2,1)S(1)}, u32[]{:S(2)}, u32[]{:S(2)}) %all-to-all-start) | async-done | bytes 589856 | tf_op jit(solution)/shard_map/all_to_all | solution.py:158
  65.0 0.8 shard_map.87
  65.8 0.0 copy-start.2
  65.8 1.0 copy-done.2
  66.7 3.5 %all-to-all-start.1 = ((bf16[4,512,256]{2,1,0:T(8,128)(2,1)}), bf16[4,512,256]{2,1,0:T(8,128)(2,1)S(1)}, u32[]{:S(2)}, u32[]{:S(2)}) async-start(bf16[4,512,256]{2,1,0:T(8,128)(2,1)} %copy-done.2), calls=%async_computation.1 | async-start | bytes 2097152 | tf_op jit(solution)/shard_map/all_to_all | solution.py:175
  70.3 2.3 %copy.13 = bf16[1,512,1024]{1,2,0:T(8,128)(2,1)} copy(bf16[1,512,1024]{2,1,0:T(8,128)(2,1)} %param.10) | data formatting | bytes 2097152 | tf_op args[3]
  72.5 0.0 collective-permute-start
  72.5 9.4 %all-to-all-done.1.own_ref = bf16[4,512,256]{2,1,0:T(8,128)(2,1)S(1)} async-done(((bf16[4,512,256]{2,1,0:T(8,128)(2,1)}), bf16[4,512,256]{2,1,0:T(8,128)(2,1)S(1)}, u32[]{:S(2)}, u32[]{:S(2)}) %all-to-all-start.1) | async-done | bytes 1048608 | tf_op jit(solution)/shard_map/all_to_all | solution.py:175
  81.9 0.1 collective-permute-start.1
  82.0 0.0 collective-permute-done
  82.0 1.9 %collective-permute-done.1.far_ref = bf16[2,512,256]{2,1,0:T(8,128)(2,1)S(1)} collective-permute-done((bf16[2,512,256]{2,1,0:T(8,128)(2,1)S(1)}, bf16[2,512,256]{2,1,0:T(8,128)(2,1)S(1)}, u32[]{:S(2)}, u32[]{:S(2)}) %collective-permute-start.1) | collective-permute-done | bytes 524320 | tf_op jit(solution)/shard_map/ppermute | solution.py:177
  83.9 0.0 copy-start.1
  83.9 1.2 copy-done.1
  85.2 2.7 %shard_map.88 = bf16[1024,512]{1,0:T(8,128)(2,1)S(1)} custom-call(s32[1]{0:T(128)} %bitcast.11.half_ref, bf16[1024,512]{1,0:T(8,128)(2,1)S(1)} %bitcast.35, bf16[1024,512]{1,0:T(8,128)(2,1)} %bitcast.14.far_t_ref, bf16[4,512,256]{2,1,0:T(8,128)(2,1)S(1)} %all-to-all-done.1.own_ref, bf16[2,512,256]{2,1,0:T(8,128)(2,1)S(1)} %collective-permute-done.1.far_ref), custom_call_target="tpu_custom_call" | custom-call | tf_op jit(solution)/shard_map/pallas_call | solution.py:127
  87.9 21.3 %all_to_all.25 = bf16[16,64,512]{2,1,0:T(8,128)(2,1)} all-to-all(bf16[16,64,512]{2,1,0:T(8,128)(2,1)S(1)} %bitcast.36), channel_id=1, replica_groups=mesh['dp'=2,'context'=16,'tensor'=4] {'context'}, dimensions={0} | all-to-all | bytes 2097152 | tf_op jit(solution)/shard_map/all_to_all | solution.py:180
  109.2 1.4 reduce_sum.22
  110.6 3.8 %collective-permute-start.2 = (bf16[64,512]{1,0:T(8,128)(2,1)S(1)}, bf16[64,512]{1,0:T(8,128)(2,1)S(1)}, u32[]{:S(2)}, u32[]{:S(2)}) collective-permute-start(bf16[64,512]{1,0:T(8,128)(2,1)S(1)} %reduce_sum.22), channel_id=1, source_target_pairs={{0,0},{1,32},{2,64},{3,96},{4,2},{5,34},{6,66},{7,98},{8,4},{9,36}... | collective-permute-start | bytes 196616 | tf_op jit(solution)/shard_map/ppermute | solution.py:191
  114.4 6.8 %collective-permute-done.2 = bf16[64,512]{1,0:T(8,128)(2,1)S(1)} collective-permute-done((bf16[64,512]{1,0:T(8,128)(2,1)S(1)}, bf16[64,512]{1,0:T(8,128)(2,1)S(1)}, u32[]{:S(2)}, u32[]{:S(2)}) %collective-permute-start.2) | collective-permute-done | bytes 65568 | tf_op jit(solution)/shard_map/ppermute | solution.py:191
  121.3 12.4 %all-gather = bf16[256,512]{1,0:T(8,128)(2,1)S(1)} all-gather(bf16[64,512]{1,0:T(8,128)(2,1)S(1)} %collective-permute-done.2), channel_id=2, replica_groups=mesh['dp'=2,'context'=16,'tensor'=4] {'tensor'}, dimensions={0}, use_global_device_ids=true | all-gather | bytes 327680 | tf_op jit(solution)/shard_map/all_gather | solution.py:192
  133.6 0.3 copy.14
  133.9 2.8 %fusion.4 = f32[128,1024]{1,0:T(8,128)} fusion(bf16[128,1024]{1,0:T(8,128)(2,1)S(1)} %bitcast.44, bf16[1024,1024]{1,0:T(8,128)(2,1)} %copy-done.6), kind=kOutput, calls=%fused_computation.15 | convolution fusion | flops 268435456 | bytes 2883584 | tf_op jit(solution)/shard_map/dot_general | solution.py:194
  136.8 0.0 all-gather.3.cloned.1.call-done
  136.8 3.8 %fusion = bf16[1,512,1024]{2,1,0:T(8,128)(2,1)} fusion(bf16[4,512,256]{2,1,0:T(8,128)(2,1)S(1)} %all-to-all-done.1.own_ref, bf16[4,256,1024]{2,1,0:T(8,128)(2,1)} %bitcast.45), kind=kOutput, calls=%fused_computation.3 | convolution fusion | flops 1074266112 | bytes 4194304 | tf_op jit(solution)/shard_map/dot_general | solution.py:196
  (4 shorter events, 0.1 us)
Async XLA Ops:
  7.2 1.6 %copy-start = (bf16[1024,1024]{1,0:T(8,128)(2,1)S(1)}, bf16[1024,1024]{1,0:T(8,128)(2,1)}, u32[]{:S(2)}) copy-start(bf16[1024,1024]{1,0:T(8,128)(2,1)} %param.13) | copy-start | bytes 6291460
  7.2 33.3 %reduce-scatter.2.cloned.1.call-start = ((), (), s32[]{:S(2)}) async-start(), calls=%async_computation.4 | async-start | bytes 327680 | tf_op jit(solution)/shard_map/reduce_scatter | solution.py:171
  8.8 5.5 %copy-start.5 = (bf16[4096,1024]{1,0:T(8,128)(2,1)S(1)}, bf16[4096,1024]{1,0:T(8,128)(2,1)}, u32[]{:S(2)}) copy-start(bf16[4096,1024]{1,0:T(8,128)(2,1)} %param.11) | copy-start | bytes 25165828
  12.9 1.3 copy-start.6
  14.2 26.3 %copy-start.3 = (s32[1,8192]{1,0:T(1,128)S(1)}, s32[1,8192]{1,0:T(1,128)}, u32[]{:S(2)}) copy-start(s32[1,8192]{1,0:T(1,128)} %param.8) | copy-start | bytes 98308
  14.2 26.3 %copy-start.4 = (s32[1,8192]{1,0:T(1,128)S(1)}, s32[1,8192]{1,0:T(1,128)}, u32[]{:S(2)}) copy-start(s32[1,8192]{1,0:T(1,128)} %param.9) | copy-start | bytes 98308
  17.5 119.3 %all-gather.3.cloned.1.call-start = ((), (), s32[]{:S(2)}) async-start(), calls=%async_computation.5 | async-start | bytes 2162688 | tf_op jit(solution)/shard_map/all_gather | solution.py:172
  49.4 15.5 %all-to-all-start = ((bf16[16,72,256]{2,1,0:T(8,128)(2,1)}), bf16[16,72,256]{2,1,0:T(8,128)(2,1)S(1)}, u32[]{:S(2)}, u32[]{:S(2)}) async-start(bf16[16,72,256]{2,1,0:T(8,128)(2,1)} %bitcast.6), calls=%async_computation | async-start | bytes 1179648 | tf_op jit(solution)/shard_map/all_to_all | solution.py:158
  65.8 1.0 copy-start.2
  66.7 15.2 %all-to-all-start.1 = ((bf16[4,512,256]{2,1,0:T(8,128)(2,1)}), bf16[4,512,256]{2,1,0:T(8,128)(2,1)S(1)}, u32[]{:S(2)}, u32[]{:S(2)}) async-start(bf16[4,512,256]{2,1,0:T(8,128)(2,1)} %copy-done.2), calls=%async_computation.1 | async-start | bytes 2097152 | tf_op jit(solution)/shard_map/all_to_all | solution.py:175
  72.5 9.5 %collective-permute-start = (bf16[512,1024]{0,1:T(8,128)(2,1)}, bf16[512,1024]{0,1:T(8,128)(2,1)}, u32[]{:S(2)}, u32[]{:S(2)}) collective-permute-start(bf16[512,1024]{0,1:T(8,128)(2,1)} %bitcast.34), channel_id=1, source_target_pairs={{0,64},{64,0},{1,65},{65,1},{2,66},{66,2},{3,67},{67,3},{4,68},{68... | collective-permute-start | bytes 3145736 | tf_op jit(solution)/shard_map/ppermute | solution.py:161
  81.9 2.0 %collective-permute-start.1 = (bf16[2,512,256]{2,1,0:T(8,128)(2,1)S(1)}, bf16[2,512,256]{2,1,0:T(8,128)(2,1)S(1)}, u32[]{:S(2)}, u32[]{:S(2)}) collective-permute-start(bf16[2,512,256]{2,1,0:T(8,128)(2,1)S(1)} %constant_dynamic-slice_fusion), channel_id=1, source_target_pairs={{0,64},{64,0},{1,65},{65,1},{2,66},{66,2},{3,67},{67,3},{4,68},{68... | collective-permute-start | bytes 1572872 | tf_op jit(solution)/shard_map/ppermute | solution.py:177
  83.9 1.2 copy-start.1
  110.6 10.7 %collective-permute-start.2 = (bf16[64,512]{1,0:T(8,128)(2,1)S(1)}, bf16[64,512]{1,0:T(8,128)(2,1)S(1)}, u32[]{:S(2)}, u32[]{:S(2)}) collective-permute-start(bf16[64,512]{1,0:T(8,128)(2,1)S(1)} %reduce_sum.22), channel_id=1, source_target_pairs={{0,0},{1,32},{2,64},{3,96},{4,2},{5,34},{6,66},{7,98},{8,4},{9,36}... | collective-permute-start | bytes 196616 | tf_op jit(solution)/shard_map/ppermute | solution.py:191
Sparse Core Ops, SparseCore 0:
  17.6 22.7 reduce-scatter.1
  43.0 45.0 all-gather.2

commit v2 on v1

--- a/solution.py
+++ b/solution.py
@@ -12,7 +12,8 @@
 SUB = LANES // GROUP
 WIN = 9
 SLOT = WIN * SUB
-VMEM = 48 * 1024 * 1024
+CUTS = (192, 320)
+VMEM = 24 * 1024 * 1024
 
 
 def seg_kernel(idx_ref, starts_ref, owner_ref, bytes_ref, out_ref, next_ref, low_ref, high_ref, acc_ref):
@@ -96,50 +97,147 @@
     for s in range(in_ref.shape[0] // SLOT):
         at = pl.ds(pl.multiple_of(first_ref[s] * SUB, SUB), SLOT)
         acc_ref[at, :] += wide_ref[s * SLOT : (s + 1) * SLOT, :]
-    total = acc_ref[...].astype(jnp.bfloat16)
-    for x in range(out_ref.shape[0]):
-        out_ref[x] = total
-
-
-def collect(first, incoming, patch_rows, copies, interpret=False):
+    out_ref[...] = acc_ref[...].astype(jnp.bfloat16)
+
+
+def collect(first, incoming, patch_rows, interpret=False):
     rows, width = incoming.shape
     return pl.pallas_call(
         collect_kernel,
         in_specs=[pl.BlockSpec(memory_space=pltpu.SMEM), pl.BlockSpec(memory_space=pltpu.VMEM)],
         out_specs=pl.BlockSpec(memory_space=pltpu.VMEM),
-        out_shape=jax.ShapeDtypeStruct((copies, patch_rows, width), jnp.bfloat16),
+        out_shape=jax.ShapeDtypeStruct((patch_rows, width), jnp.bfloat16),
         scratch_shapes=[pltpu.VMEM((rows, width), jnp.float32), pltpu.VMEM((patch_rows, width), jnp.float32)],
         compiler_params=pltpu.CompilerParams(vmem_limit_bytes=VMEM),
         interpret=interpret,
     )(first, incoming)
 
 
-def outer_kernel(half_ref, own_t_ref, far_t_ref, own_ref, far_ref, out_ref):
-    total = jnp.dot(own_t_ref[...], own_ref[0], preferred_element_type=jnp.float32)
-    total += jnp.dot(far_t_ref[...], far_ref[0], preferred_element_type=jnp.float32)
-    out_ref[...] = total.astype(jnp.bfloat16)
-
-
-def outer(half, own_t, far_t, own, far):
-    cols, rows = own_t.shape
-    parts, _, width = far.shape
-    whole = pl.BlockSpec((cols, rows), lambda i, half: (0, 0))
+def outer_kernel(idx_ref, mine_ref, third_ref, cross_ref, n0_ref, n1a_ref, n1b_ref, n1c_ref, f0_ref, f1a_ref, f1b_ref, f1c_ref, out_ref, near_t, far_t):
+    step = pl.program_id(0)
+
+    @pl.when(step == 0)
+    def _():
+        near = jnp.where(idx_ref[0] == 0, mine_ref[...], third_ref[...])
+        near_t[...] = near.T
+        far_t[...] = cross_ref[...].T
+
+    low = lax.rem(idx_ref[1], 2)
+    blocks = out_ref.shape[0] // 2
+    per = n0_ref.shape[1] // LANES
+    near1 = jnp.concatenate([n1a_ref[...], n1b_ref[...], n1c_ref[...]], axis=0)
+    far1 = jnp.concatenate([f1a_ref[...], f1b_ref[...], f1c_ref[...]], axis=0)
+    for near, far, which in ((n0_ref[...], f0_ref[...], low), (near1, far1, 1 - low)):
+        total = jnp.dot(near_t[...], near, preferred_element_type=jnp.float32)
+        total += jnp.dot(far_t[...], far, preferred_element_type=jnp.float32)
+        total = total.astype(jnp.bfloat16)
+        for i in range(per):
+            out_ref[which * blocks + step * per + i] = total[:, i * LANES : (i + 1) * LANES]
+
+
+def outer(idx, sums, columns):
+    rows, width = sums[0].shape
+    cols = columns[0].shape[1]
+    block = 256
+    whole = pl.BlockSpec((rows, width), lambda i, idx: (0, 0))
+    shape = (2 * cols // LANES, width, LANES)
     return pl.pallas_call(
         outer_kernel,
+        grid_spec=pltpu.PrefetchScalarGridSpec(
+            num_scalar_prefetch=1,
+            grid=(cols // block,),
+            in_specs=[whole] * len(sums)
+            + [pl.BlockSpec((c.shape[0], block), lambda i, idx: (0, i)) for c in columns],
+            out_specs=pl.BlockSpec(shape, lambda i, idx: (0, 0, 0)),
+            scratch_shapes=[pltpu.VMEM((width, rows), jnp.bfloat16)] * 2,
+        ),
+        out_shape=jax.ShapeDtypeStruct(shape, jnp.bfloat16),
+        compiler_params=pltpu.CompilerParams(vmem_limit_bytes=VMEM),
+    )(idx, *sums, *columns)
+
+
+def chain_kernel(idx_ref, value_ref, global_ref, a_ref, b_ref, c_ref, d_ref, turned_ref):
+    step = pl.program_id(0)
+    share = a_ref.shape[0]
+
+    @pl.when(step == 0)
+    def _():
+        turned_ref[...] = value_ref[...].T
+
+    at = pl.ds(pl.multiple_of(lax.rem(idx_ref[0], LANES // share) * share, share), share)
+    total = lax.dot_general(
+        turned_ref[at, :], global_ref[...], (((1,), (1,)), ((), ())), preferred_element_type=jnp.float32
+    ).astype(jnp.bfloat16)
+    for s, ref in enumerate((a_ref, b_ref, c_ref, d_ref)):
+
+        @pl.when(step == s)
+        def _(ref=ref):
+            ref[...] = total
+
+
+def chain_terms(idx, w_value, w_global, share, parts):
+    deep, feats = w_value.shape
+    rows = w_global.shape[0] // parts
+    per = LANES // share
+    return pl.pallas_call(
+        chain_kernel,
         grid_spec=pltpu.PrefetchScalarGridSpec(
             num_scalar_prefetch=1,
             grid=(parts,),
             in_specs=[
-                whole,
-                whole,
-                pl.BlockSpec((1, rows, width), lambda i, half: (half[0] * parts + i, 0, 0)),
-                pl.BlockSpec((1, rows, width), lambda i, half: (i, 0, 0)),
+                pl.BlockSpec((deep, LANES), lambda i, idx: (0, lax.div(idx[0], per))),
+                pl.BlockSpec((rows, deep), lambda i, idx: (lax.rem(idx[1] + i, parts), 0)),
             ],
-            out_specs=pl.BlockSpec((cols, width), lambda i, half: (0, i)),
+            out_specs=[pl.BlockSpec((share, rows), lambda i, idx: (0, 0))] * parts,
+            scratch_shapes=[pltpu.VMEM((LANES, deep), jnp.bfloat16)],
         ),
-        out_shape=jax.ShapeDtypeStruct((cols, parts * width), jnp.bfloat16),
-        compiler_params=pltpu.CompilerParams(vmem_limit_bytes=VMEM),
-    )(half, own_t, far_t, own, far)
+        out_shape=[jax.ShapeDtypeStruct((share, rows), jnp.bfloat16)] * parts,
+        compiler_params=pltpu.CompilerParams(vmem_limit_bytes=VMEM),
+    )(idx, w_value, w_global)
+
+
+def value_kernel(feat_ref, a_ref, b_ref, c_ref, d_ref, w_ref, out_ref):
+    width = a_ref.shape[1]
+    total = jnp.zeros(out_ref.shape, jnp.float32)
+    for s, ref in enumerate((a_ref, b_ref, c_ref, d_ref)):
+        at = pl.ds(pl.multiple_of(feat_ref[s] * width, width), width)
+        total += lax.dot_general(
+            ref[...], w_ref[:, at], (((1,), (1,)), ((), ())), preferred_element_type=jnp.float32
+        )
+    out_ref[...] = total.astype(jnp.bfloat16)
+
+
+def value(feats, pieces, weights):
+    vmem = pl.BlockSpec(memory_space=pltpu.VMEM)
+    return pl.pallas_call(
+        value_kernel,
+        in_specs=[pl.BlockSpec(memory_space=pltpu.SMEM)] + [vmem] * 5,
+        out_specs=vmem,
+        out_shape=jax.ShapeDtypeStruct((pieces[0].shape[0], weights.shape[0]), jnp.bfloat16),
+        compiler_params=pltpu.CompilerParams(vmem_limit_bytes=VMEM),
+    )(feats, *pieces, weights)
+
+
+def last_kernel(feat_ref, a_ref, b_ref, c_ref, d_ref, w_ref, out_ref):
+    total = jnp.zeros(out_ref.shape, jnp.float32)
+    for s, ref in enumerate((a_ref, b_ref, c_ref, d_ref)):
+        total += jnp.dot(ref[...].T, w_ref[feat_ref[s]], preferred_element_type=jnp.float32)
+    out_ref[...] = total
+
+
+def last(feats, pieces, weights):
+    vmem = pl.BlockSpec(memory_space=pltpu.VMEM)
+    return pl.pallas_call(
+        last_kernel,
+        in_specs=[pl.BlockSpec(memory_space=pltpu.SMEM)] + [vmem] * 5,
+        out_specs=vmem,
+        out_shape=jax.ShapeDtypeStruct((pieces[0].shape[1], weights.shape[2]), jnp.float32),
+        compiler_params=pltpu.CompilerParams(vmem_limit_bytes=VMEM),
+    )(feats, *pieces, weights)
+
+
+def after(value, *others):
+    return lax.optimization_barrier((value, *others))[0]
 
 
 def local(byte_grads, patch_starts, patch_owner, attn_context, w_global, w_value, w_out):
@@ -150,52 +248,75 @@
     f32, bf16 = jnp.float32, jnp.bfloat16
     bytes_n, feats = byte_grads.shape[1:]
     width = feats // ten_n
-    patch_rows, cols = attn_context.shape[1:]
+    patch_rows = attn_context.shape[1]
     starts = patch_starts.reshape(-1, LANES)
     owner = patch_owner.reshape(-1, LANES)
+    line = ("dp", "tensor")
+
+    def moves(target):
+        pairs = []
+        for d in range(dp_n):
+            for x in range(ten_n):
+                to = target(d, x)
+                if to is not None:
+                    pairs.append((d * ten_n + x, to[0] * ten_n + to[1]))
+        return pairs
+
+    swap = [(i, dp_n - 1 - i) for i in range(dp_n)]
+    pair = [(x, x ^ 1) for x in range(ten_n)]
+    near0 = attn_context[0]
+    far0 = lax.ppermute(near0, "dp", swap)
+    ends = (0,) + CUTS + (patch_rows,)
+    near1 = [lax.ppermute(near0[: ends[1]], "tensor", pair)]
 
     outgoing = segment_sums(jnp.stack([ctx, ten]), starts, owner, byte_grads[0], ctx_n, width)
+    outgoing = after(outgoing, near1[0])
     incoming = lax.all_to_all(outgoing, "context", split_axis=0, concat_axis=0, tiled=True)
 
-    swap = [(i, dp_n - 1 - i) for i in range(dp_n)]
-    far_context = lax.ppermute(attn_context[0], "dp", swap)
-    own_t = attn_context[0].T
-    far_t = far_context.T
+    near1.append(lax.ppermute(after(near0, outgoing)[ends[1] : ends[2]], "tensor", pair))
+    incoming = after(incoming, near1[1])
+    near1.append(lax.ppermute(after(near0, incoming)[ends[2] :], "tensor", pair))
+
+    share = feats // (dp_n * ctx_n)
+    where = after(jnp.stack([dp * ctx_n + ctx, ten]), outgoing)
+    terms = chain_terms(where, w_value, w_global, share, ten_n)
+    chain = terms[0].astype(f32)
+    for s in range(1, ten_n):
+        chain += lax.ppermute(terms[s], "tensor", [(x, (x + s) % ten_n) for x in range(ten_n)]).astype(f32)
+    chain = lax.all_gather(after(chain.astype(bf16), incoming), ("dp", "context"), axis=0, tiled=True)
+
     edges = jnp.arange(ctx_n, dtype=jnp.int32) * bytes_n
     counts = jnp.sum((patch_starts[0][None, :] <= edges[:, None]).astype(jnp.int32), axis=1)
     first = jnp.minimum((counts - 1) // LANES, starts.shape[0] - WIN)
-    both = lax.dot_general(w_out, w_value, (((0,), (1,)), ((), ())), preferred_element_type=f32).astype(bf16)
-    share = feats // (dp_n * ctx_n)
-    some = lax.dynamic_slice_in_dim(both, (dp * ctx_n + ctx) * share, share, 0)
-    term = lax.dot_general(some, w_global, (((1,), (1,)), ((), ())), preferred_element_type=f32).astype(bf16)
-    term = lax.psum_scatter(term, "tensor", scatter_dimension=1, tiled=True)
-    whole = lax.all_gather(term, ("dp", "context"), axis=0, tiled=True)
-
-    sums = collect(first, incoming, patch_rows, ten_n)
-    sums = lax.all_to_all(sums, "tensor", split_axis=0, concat_axis=0)
-    half = ten_n // dp_n
-    far_sums = lax.ppermute(lax.dynamic_slice_in_dim(sums, (dp_n - 1 - dp) * half, half, 0), "dp", swap)
-
-    partial = outer(dp[None], own_t, far_t, sums, far_sums)
+
+    sums = collect(first, incoming, patch_rows)
+    cross = lax.ppermute(sums, line, moves(lambda d, x: (0, x) if d == 1 else (1, ten_n - 1 - x)))
+    third = lax.ppermute(sums, line, moves(lambda d, x: (1, ten_n - 1 - x) if d == 1 else None))
+    far1 = [lax.ppermute(part, "dp", swap) for part in (near1[0], near1[1], after(near1[2], cross))]
+    columns = (near0, *near1, far0, *far1)
+    partial = outer(jnp.stack([dp, ten]), (sums, third, cross), columns)
     pieces = lax.all_to_all(partial, "context", split_axis=0, concat_axis=0, tiled=True)
-    rows_n = cols // ctx_n
-    piece = jnp.sum(pieces.reshape(ctx_n, rows_n, -1).astype(f32), axis=0).astype(bf16)
-    moves = []
-    per = ctx_n * dp_n // ten_n
-    cuts = ctx_n // per
-    for d in range(dp_n):
-        for c in range(ctx_n):
-            for k in range(ten_n):
-                to = (per * k + c // cuts) * ten_n + (c % cuts) * dp_n + d
-                moves.append(((d * ctx_n + c) * ten_n + k, to))
-    piece = lax.ppermute(piece, ("dp", "context", "tensor"), moves)
-    block = lax.all_gather(piece, "tensor", axis=0)
-    block = block.reshape(cuts, dp_n, rows_n, -1).transpose(0, 2, 1, 3).reshape(cuts * rows_n, feats)
-    weight_grad = jnp.dot(block, both, preferred_element_type=f32)
-
-    context_grad = lax.dot_general(
-        sums, whole.reshape(ten_n, width, -1), (((0, 2), (0, 1)), ((), ())), preferred_element_type=f32
+
+    late = after(sums, partial)
+    around = [late] + [
+        lax.ppermute(late, "tensor", [(x, (x + s) % ten_n) for x in range(ten_n)]) for s in (1, ten_n - 1, 2)
+    ]
+    order = jnp.stack([ten, (ten + ten_n - 1) % ten_n, (ten + 1) % ten_n, (ten + 2) % ten_n])
+    value_grad = value(order, around, w_out)
+    both = lax.dot_general(
+        after(w_out, partial), w_value, (((0,), (1,)), ((), ())), preferred_element_type=f32
     ).astype(bf16)
+
+    pieces = after(pieces, both)
+    piece = jnp.sum(pieces.astype(f32), axis=0).astype(bf16)
+    parts, blocks = [], []
+    for s in range(ten_n):
+        parts.append(lax.ppermute(piece, line, moves(lambda d, x, s=s: (x // 2, (2 * d + x % 2) ^ s))))
+        source = ten ^ s
+        near = 2 * dp + source % 2
+        blocks.append(jnp.where(source < 2, near, ten_n - 1 - near))
+    weight_grad = last(jnp.stack(blocks), parts, both.reshape(ten_n, width, -1))
+    context_grad = jnp.dot(value_grad, chain, preferred_element_type=f32).astype(bf16)
     return (context_grad[None], weight_grad)
 
 

time: 148 us -> 129 us (0.87)
  the two profiles are of different devices: /device:TPU:16 before, /device:TPU:1 now
where the time goes in v2:
time: 129 us; the launch traced here: 128 us
  starting transfers between devices  36.9 us (29%)
  waiting for transfers between devices  28.6 us (22%)
  Pallas kernels  19.6 us (15%)
  local copies, waits for them, and re-layouts  17.5 us (14%)
  between operations  14.3 us (11%)
  matrix products  8.44 us (7%)
  other arithmetic  2.69 us (2%)
    unnamed x28, local copies, waits for them, and re-layouts  16.4 us
    all_to_all x1, waiting for transfers between devices, local(): lax.all_to_all(partial, 'context', split_axis=0, concat_axis=0, tiled=True)  8.88 us
    all_to_all x1, starting transfers between devices, local(): lax.all_to_all(outgoing, 'context', split_axis=0, concat_axis=0, tiled=True)  7.77 us
    pallas_call x1, Pallas kernels, segment_sums(): pl.pallas_call(seg_kernel, grid_spec=pltpu.PrefetchScalarGridSpec(num_sca...  7.2 us
    all_to_all x1, starting transfers between devices, local(): lax.all_to_all(partial, 'context', split_axis=0, concat_axis=0, tiled=True)  6.83 us
    ppermute x4, starting transfers between devices, local(): lax.ppermute(piece, line, moves(lambda d, x, s=s: (x // 2, 2 * d + x % 2...  5.81 us
    ppermute x1, waiting for transfers between devices, local(): lax.ppermute(sums, line, moves(lambda d, x: (1, ten_n - 1 - x) if d == 1...  5.78 us
    ppermute x1, waiting for transfers between devices, local(): lax.ppermute(after(near0, outgoing)[ends[1]:ends[2]], 'tensor', pair)  4.75 us
  transfers between devices with their start and end apart: 22, of which 7 were waited for; matrix products, arithmetic and copies ran while one was open for 6% of the time, Pallas kernels for 15%

profile of v2, /device:TPU:1, one launch (start us, length us, event | category | flops | bytes accessed | tf_op | source)
XLA Modules:
  0.0 128.0 jit_solution(5800206512050800597)
XLA Ops:
  7.2 1.0 slice_bitcast_fusion
  8.2 2.1 %collective-permute-start = (bf16[192,1024]{1,0:T(8,128)(2,1)S(1)}, bf16[192,1024]{1,0:T(8,128)(2,1)S(1)}, u32[]{:S(2)}, u32[]{:S(2)}) collective-permute-start(bf16[192,1024]{1,0:T(8,128)(2,1)S(1)} %slice_bitcast_fusion), channel_id=1, source_target_pairs={{0,1},{1,0},{2,3},{3,2},{4,5},{5,4},{6,7},{7,6},{8,9},{9,8},{10,11... | collective-permute-start | bytes 1179656 | tf_op jit(solution)/shard_map/ppermute | solution.py:270
  10.4 3.4 %copy-done = bf16[1,4096,1024]{2,1,0:T(8,128)(2,1)S(1)} copy-done((bf16[1,4096,1024]{2,1,0:T(8,128)(2,1)S(1)}, bf16[1,4096,1024]{2,1,0:T(8,128)(2,1)}, u32[]{:S(2)}) %copy-start) | copy-done | bytes 8388632
  13.8 0.8 copy-done.11
  14.5 0.8 copy-done.13
  15.3 7.2 %shard_map.86 = bf16[1152,256]{1,0:T(8,128)(2,1)} custom-call(s32[2]{0:T(128)S(1)} %pad_add_fusion.1.idx_ref, s32[64,128]{1,0:T(8,128)S(1)} %bitcast.34, s32[64,128]{1,0:T(8,128)S(1)} %bitcast.36, bf16[4096,1024]{1,0:T(8,128)(2,1)S(1)} %bitcast.27), custom_call_target="tpu_custom_call" | custom-call | tf_op jit(solution)/shard_map/pallas_call | solution.py:74
  22.5 7.8 %all-to-all-start = ((bf16[16,72,256]{2,1,0:T(8,128)(2,1)}), bf16[16,72,256]{2,1,0:T(8,128)(2,1)S(1)}, u32[]{:S(2)}, u32[]{:S(2)}) async-start(bf16[16,72,256]{2,1,0:T(8,128)(2,1)} %bitcast.10), calls=%async_computation | async-start | bytes 1179648 | tf_op jit(solution)/shard_map/all_to_all | solution.py:274
  30.4 3.4 %copy-done.1 = bf16[4096,1024]{1,0:T(8,128)(2,1)S(1)} copy-done((bf16[4096,1024]{1,0:T(8,128)(2,1)S(1)}, bf16[4096,1024]{1,0:T(8,128)(2,1)}, u32[]{:S(2)}) %copy-start.1) | copy-done | bytes 8388632
  33.8 1.6 %copy-done.4 = bf16[1024,1024]{1,0:T(8,128)(2,1)S(1)} copy-done((bf16[1024,1024]{1,0:T(8,128)(2,1)S(1)}, bf16[1024,1024]{1,0:T(8,128)(2,1)}, u32[]{:S(2)}) %copy-start.4) | copy-done | bytes 2097176
  35.4 3.7 %shard_map.90 = (bf16[32,1024]{1,0:T(8,128)(2,1)S(1)}, bf16[32,1024]{1,0:T(8,128)(2,1)S(1)}, bf16[32,1024]{1,0:T(8,128)(2,1)S(1)}, bf16[32,1024]{1,0:T(8,128)(2,1)S(1)}) custom-call(s32[2]{0:T(128)S(1)} %pad_add_fusion.3.idx_ref, bf16[1024,1024]{1,0:T(8,128)(2,1)S(1)} %copy-done.4, bf16[4096,1024]{1,0:T(8,128)(2,1)S(1)} %copy-done.1), custom_call_target="tpu_custom_call" | custom-call | tf_op jit(solution)/shard_map/pallas_call | solution.py:182
  39.1 0.3 collective-permute-start.12
  39.4 2.7 %collective-permute-start.13 = (bf16[32,1024]{1,0:T(8,128)(2,1)S(1)}, bf16[32,1024]{1,0:T(8,128)(2,1)S(1)}, u32[]{:S(2)}, u32[]{:S(2)}) collective-permute-start(bf16[32,1024]{1,0:T(8,128)(2,1)S(1)} %get-tuple-element.25), channel_id=1, source_target_pairs={{0,2},{1,3},{2,0},{3,1},{4,6},{5,7},{6,4},{7,5},{8,10},{9,11},{10,... | collective-permute-start | bytes 196616 | tf_op jit(solution)/shard_map/ppermute | solution.py:285
  42.2 1.5 %collective-permute-start.14 = (bf16[32,1024]{1,0:T(8,128)(2,1)S(1)}, bf16[32,1024]{1,0:T(8,128)(2,1)S(1)}, u32[]{:S(2)}, u32[]{:S(2)}) collective-permute-start(bf16[32,1024]{1,0:T(8,128)(2,1)S(1)} %get-tuple-element.26), channel_id=1, source_target_pairs={{0,3},{1,0},{2,1},{3,2},{4,7},{5,4},{6,5},{7,6},{8,11},{9,8},{10,9... | collective-permute-start | bytes 196616 | tf_op jit(solution)/shard_map/ppermute | solution.py:285
  43.8 0.7 collective-permute-done.13
  44.5 1.0 collective-permute-done.14
  45.5 0.6 add_convert_fusion
  46.2 4.8 %collective-permute-done.1.n1b_ref = bf16[128,1024]{1,0:T(8,128)(2,1)S(1)} collective-permute-done((bf16[128,1024]{1,0:T(8,128)(2,1)S(1)}, bf16[128,1024]{1,0:T(8,128)(2,1)S(1)}, u32[]{:S(2)}, u32[]{:S(2)}) %collective-permute-start.1) | collective-permute-done | bytes 262176 | tf_op jit(solution)/shard_map/ppermute | solution.py:276
  51.0 2.4 %collective-permute-start.5 = (bf16[512,1024]{1,0:T(8,128)(2,1)S(1)}, bf16[512,1024]{1,0:T(8,128)(2,1)S(1)}, u32[]{:S(2)}, u32[]{:S(2)}) collective-permute-start(bf16[512,1024]{1,0:T(8,128)(2,1)S(1)} %bitcast.29), channel_id=1, source_target_pairs={{0,64},{64,0},{1,65},{65,1},{2,66},{66,2},{3,67},{67,3},{4,68},{68... | collective-permute-start | bytes 3145736 | tf_op jit(solution)/shard_map/ppermute | solution.py:268
  53.4 0.3 convert_reduce_fusion
  53.8 0.8 shard_map.87.mine_ref.a_ref
  54.5 0.4 collective-permute-start.3
  54.9 2.1 %collective-permute-start.6 = (bf16[192,1024]{1,0:T(8,128)(2,1)S(1)}, bf16[192,1024]{1,0:T(8,128)(2,1)S(1)}, u32[]{:S(2)}, u32[]{:S(2)}) collective-permute-start(bf16[192,1024]{1,0:T(8,128)(2,1)S(1)} %collective-permute-done.n1a_ref), channel_id=1, source_target_pairs={{0,64},{64,0},{1,65},{65,1},{2,66},{66,2},{3,67},{67,3},{4,68},{68... | collective-permute-start | bytes 1179656 | tf_op jit(solution)/shard_map/ppermute | solution.py:295
  57.0 4.6 %collective-permute-done.3.cross_ref = bf16[512,256]{1,0:T(8,128)(2,1)S(1)} collective-permute-done((bf16[512,256]{1,0:T(8,128)(2,1)S(1)}, bf16[512,256]{1,0:T(8,128)(2,1)S(1)}, u32[]{:S(2)}, u32[]{:S(2)}) %collective-permute-start.3) | collective-permute-done | bytes 262176 | tf_op jit(solution)/shard_map/ppermute | solution.py:293
  61.6 2.8 %collective-permute-done.4.n1c_ref = bf16[192,1024]{1,0:T(8,128)(2,1)S(1)} collective-permute-done((bf16[192,1024]{1,0:T(8,128)(2,1)S(1)}, bf16[192,1024]{1,0:T(8,128)(2,1)S(1)}, u32[]{:S(2)}, u32[]{:S(2)}) %collective-permute-start.4) | collective-permute-done | bytes 393248 | tf_op jit(solution)/shard_map/ppermute | solution.py:278
  64.4 0.8 collective-permute-start.8
  65.3 2.4 %collective-permute-start.2 = (bf16[512,256]{1,0:T(8,128)(2,1)S(1)}, bf16[512,256]{1,0:T(8,128)(2,1)S(1)}, u32[]{:S(2)}, u32[]{:S(2)}) collective-permute-start(bf16[512,256]{1,0:T(8,128)(2,1)S(1)} %shard_map.87.mine_ref.a_ref), channel_id=1, source_target_pairs={{64,67},{65,66},{66,65},{67,64},{68,71},{69,70},{70,69},{71,68},{7... | collective-permute-start | bytes 786440 | tf_op jit(solution)/shard_map/ppermute | solution.py:294
  67.8 5.8 %collective-permute-done.2.third_ref = bf16[512,256]{1,0:T(8,128)(2,1)S(1)} collective-permute-done((bf16[512,256]{1,0:T(8,128)(2,1)S(1)}, bf16[512,256]{1,0:T(8,128)(2,1)S(1)}, u32[]{:S(2)}, u32[]{:S(2)}) %collective-permute-start.2) | collective-permute-done | bytes 262176 | tf_op jit(solution)/shard_map/ppermute | solution.py:294
  73.6 4.2 %shard_map.88 = bf16[16,256,128]{2,1,0:T(8,128)(2,1)} custom-call(s32[2]{0:T(128)S(1)} %pad_add_fusion.2.idx_ref, bf16[512,256]{1,0:T(8,128)(2,1)S(1)} %shard_map.87.mine_ref.a_ref, bf16[512,256]{1,0:T(8,128)(2,1)S(1)} %collective-permute-done.2.third_ref, bf16[512,256]{1,0:T(8,128)(2,1)S(1)} %collective-permute-done.3.cross_ref, ...), custom_call_target="tpu_custom_call" | custom-call | tf_op jit(solution)/shard_map/pallas_call | solution.py:144
  77.8 6.8 %all-to-all-start.1 = ((bf16[16,256,128]{2,1,0:T(8,128)(2,1)}), bf16[16,256,128]{2,1,0:T(8,128)(2,1)}, u32[]{:S(2)}, u32[]{:S(2)}) async-start(bf16[16,256,128]{2,1,0:T(8,128)(2,1)} %shard_map.88), calls=%async_computation.1 | async-start | bytes 2097152 | tf_op jit(solution)/shard_map/all_to_all | solution.py:298
  84.8 0.4 collective-permute-start.10
  85.3 0.2 collective-permute-start.11
  85.4 0.9 collective-permute-start.9
  86.3 4.6 %convolution_convert_fusion = bf16[1024,1024]{1,0:T(8,128)(2,1)S(1)} fusion(bf16[1024,1024]{1,0:T(8,128)(2,1)} %w_ref.1, bf16[1024,1024]{1,0:T(8,128)(2,1)} %value_ref.1), kind=kOutput, calls=%fused_computation | convolution fusion | flops 2148532224 | bytes 6291456 | tf_op jit(solution)/shard_map/dot_general | solution.py:306
  90.9 8.9 %all-to-all-done.1 = bf16[16,256,128]{2,1,0:T(8,128)(2,1)} async-done(((bf16[16,256,128]{2,1,0:T(8,128)(2,1)}), bf16[16,256,128]{2,1,0:T(8,128)(2,1)}, u32[]{:S(2)}, u32[]{:S(2)}) %all-to-all-start.1) | async-done | bytes 1048608 | tf_op jit(solution)/shard_map/all_to_all | solution.py:298
  99.8 1.4 %reduce_sum.22 = bf16[256,128]{1,0:T(8,128)(2,1)S(1)} reduce(bf16[16,256,128]{2,1,0:T(8,128)(2,1)} %all-to-all-done.1, bf16[]{:T(256)} %constant.87.clone.1), dimensions={0}, to_apply=%region_1.2 | reduce | flops 491520 | bytes 1114114 | tf_op jit(solution)/shard_map/reduce_sum | solution.py:311
  101.2 1.9 %collective-permute-start.15 = (bf16[256,128]{1,0:T(8,128)(2,1)S(1)}, bf16[256,128]{1,0:T(8,128)(2,1)S(1)}, u32[]{:S(2)}, u32[]{:S(2)}) collective-permute-start(bf16[256,128]{1,0:T(8,128)(2,1)S(1)} %reduce_sum.22), channel_id=1, source_target_pairs={{0,0},{1,1},{2,64},{3,65},{64,2},{65,3},{66,66},{67,67},{4,4},{5,5... | collective-permute-start | bytes 196616 | tf_op jit(solution)/shard_map/ppermute | solution.py:314
  103.1 2.6 %collective-permute-start.16 = (bf16[256,128]{1,0:T(8,128)(2,1)S(1)}, bf16[256,128]{1,0:T(8,128)(2,1)S(1)}, u32[]{:S(2)}, u32[]{:S(2)}) collective-permute-start(bf16[256,128]{1,0:T(8,128)(2,1)S(1)} %reduce_sum.22), channel_id=1, source_target_pairs={{0,1},{1,0},{2,65},{3,64},{64,3},{65,2},{66,67},{67,66},{4,5},{5,4... | collective-permute-start | bytes 196616 | tf_op jit(solution)/shard_map/ppermute | solution.py:314
  105.8 0.7 copy-done.5
  106.5 0.7 copy-done.7
  107.2 1.3 collective-permute-start.18
  108.5 0.7 copy-done.9
  109.2 1.6 %copy-done.3 = bf16[1024,1024]{1,0:T(8,128)(2,1)S(1)} copy-done((bf16[1024,1024]{1,0:T(8,128)(2,1)S(1)}, bf16[1024,1024]{1,0:T(8,128)(2,1)}, u32[]{:S(2)}) %copy-start.3) | copy-done | bytes 2097176
  110.8 0.9 copy-done.6
  111.8 0.9 copy-done.8
  112.7 0.9 copy-done.10
  113.6 1.8 %shard_map.89 = bf16[512,1024]{1,0:T(8,128)(2,1)S(1)} custom-call(s32[4]{0:T(128)S(1)} %pad_add_fusion.feat_ref, bf16[512,256]{1,0:T(8,128)(2,1)S(1)} %shard_map.87.mine_ref.a_ref, bf16[512,256]{1,0:T(8,128)(2,1)S(1)} %copy-done.10, bf16[512,256]{1,0:T(8,128)(2,1)S(1)} %copy-done.6, bf16[512,256]{1,0:T(8,128)(2,1)S(1)} %copy-done.8, ...), custom_call_target="tpu_custom_call" | custom-call | tf_op jit(solution)/shard_map/pallas_call | solution.py:212
  115.5 1.8 %shard_map.91 = f32[128,1024]{1,0:T(8,128)} custom-call(s32[4]{0:T(128)S(1)} %pad_add_fusion.4.feat_ref, bf16[256,128]{1,0:T(8,128)(2,1)S(1)} %collective-permute-done.15.a_ref, bf16[256,128]{1,0:T(8,128)(2,1)S(1)} %collective-permute-done.16.b_ref, bf16[256,128]{1,0:T(8,128)(2,1)S(1)} %collective-permute-done.17.c_ref, ...), custom_call_target="tpu_custom_call" | custom-call | tf_op jit(solution)/shard_map/pallas_call | solution.py:230
  117.3 3.8 %fusion = bf16[1,512,1024]{2,1,0:T(8,128)(2,1)} fusion(bf16[512,1024]{1,0:T(8,128)(2,1)S(1)} %shard_map.89, bf16[1024,1024]{1,0:T(8,128)(2,1)} %all-gather.2.cloned.1.call-done), kind=kOutput, calls=%fused_computation.2 | convolution fusion | flops 1074266112 | bytes 4194304 | tf_op jit(solution)/shard_map/dot_general | solution.py:319
  (46 shorter events, 0.7 us)
Async XLA Ops:
  8.2 14.3 %collective-permute-start = (bf16[192,1024]{1,0:T(8,128)(2,1)S(1)}, bf16[192,1024]{1,0:T(8,128)(2,1)S(1)}, u32[]{:S(2)}, u32[]{:S(2)}) collective-permute-start(bf16[192,1024]{1,0:T(8,128)(2,1)S(1)} %slice_bitcast_fusion), channel_id=1, source_target_pairs={{0,1},{1,0},{2,3},{3,2},{4,5},{5,4},{6,7},{7,6},{8,9},{9,8},{10,11... | collective-permute-start | bytes 1179656 | tf_op jit(solution)/shard_map/ppermute | solution.py:270
  10.4 3.4 %copy-start = (bf16[1,4096,1024]{2,1,0:T(8,128)(2,1)S(1)}, bf16[1,4096,1024]{2,1,0:T(8,128)(2,1)}, u32[]{:S(2)}) copy-start(bf16[1,4096,1024]{2,1,0:T(8,128)(2,1)} %param.7) | copy-start | bytes 25165828
  13.8 0.8 copy-start.11
  14.5 0.8 copy-start.13
  22.5 28.5 %all-to-all-start = ((bf16[16,72,256]{2,1,0:T(8,128)(2,1)}), bf16[16,72,256]{2,1,0:T(8,128)(2,1)S(1)}, u32[]{:S(2)}, u32[]{:S(2)}) async-start(bf16[16,72,256]{2,1,0:T(8,128)(2,1)} %bitcast.10), calls=%async_computation | async-start | bytes 1179648 | tf_op jit(solution)/shard_map/all_to_all | solution.py:274
  30.3 87.1 %all-gather.2.cloned.1.call-start = ((), (), s32[]{:S(2)}) async-start(), calls=%async_computation.2 | async-start | bytes 2162688 | tf_op jit(solution)/shard_map/all_gather | solution.py:286
  30.4 3.4 %copy-start.1 = (bf16[4096,1024]{1,0:T(8,128)(2,1)S(1)}, bf16[4096,1024]{1,0:T(8,128)(2,1)}, u32[]{:S(2)}) copy-start(bf16[4096,1024]{1,0:T(8,128)(2,1)} %global_ref.1) | copy-start | bytes 25165828
  33.8 1.6 %copy-start.4 = (bf16[1024,1024]{1,0:T(8,128)(2,1)S(1)}, bf16[1024,1024]{1,0:T(8,128)(2,1)}, u32[]{:S(2)}) copy-start(bf16[1024,1024]{1,0:T(8,128)(2,1)} %value_ref.1) | copy-start | bytes 6291460
  35.4 8.3 %copy-start.2 = (bf16[1,512,1024]{2,1,0:T(8,128)(2,1)S(1)}, bf16[1,512,1024]{2,1,0:T(8,128)(2,1)}, u32[]{:S(2)}) copy-start(bf16[1,512,1024]{2,1,0:T(8,128)(2,1)} %param.10) | copy-start | bytes 3145732
  35.4 18.0 %copy-start.12 = (s32[1,8192]{1,0:T(1,128)S(1)}, s32[1,8192]{1,0:T(1,128)}, u32[]{:S(2)}) copy-start(s32[1,8192]{1,0:T(1,128)} %param.8) | copy-start | bytes 98308
  39.1 4.7 %collective-permute-start.12 = (bf16[32,1024]{1,0:T(8,128)(2,1)S(1)}, bf16[32,1024]{1,0:T(8,128)(2,1)S(1)}, u32[]{:S(2)}, u32[]{:S(2)}) collective-permute-start(bf16[32,1024]{1,0:T(8,128)(2,1)S(1)} %get-tuple-element.24), channel_id=1, source_target_pairs={{0,1},{1,2},{2,3},{3,0},{4,5},{5,6},{6,7},{7,4},{8,9},{9,10},{10,1... | collective-permute-start | bytes 196616 | tf_op jit(solution)/shard_map/ppermute | solution.py:285
  39.4 5.1 %collective-permute-start.13 = (bf16[32,1024]{1,0:T(8,128)(2,1)S(1)}, bf16[32,1024]{1,0:T(8,128)(2,1)S(1)}, u32[]{:S(2)}, u32[]{:S(2)}) collective-permute-start(bf16[32,1024]{1,0:T(8,128)(2,1)S(1)} %get-tuple-element.25), channel_id=1, source_target_pairs={{0,2},{1,3},{2,0},{3,1},{4,6},{5,7},{6,4},{7,5},{8,10},{9,11},{10,... | collective-permute-start | bytes 196616 | tf_op jit(solution)/shard_map/ppermute | solution.py:285
  42.2 3.3 %collective-permute-start.14 = (bf16[32,1024]{1,0:T(8,128)(2,1)S(1)}, bf16[32,1024]{1,0:T(8,128)(2,1)S(1)}, u32[]{:S(2)}, u32[]{:S(2)}) collective-permute-start(bf16[32,1024]{1,0:T(8,128)(2,1)S(1)} %get-tuple-element.26), channel_id=1, source_target_pairs={{0,3},{1,0},{2,1},{3,2},{4,7},{5,4},{6,5},{7,6},{8,11},{9,8},{10,9... | collective-permute-start | bytes 196616 | tf_op jit(solution)/shard_map/ppermute | solution.py:285
  43.7 7.2 %collective-permute-start.1 = (bf16[128,1024]{1,0:T(8,128)(2,1)S(1)}, bf16[128,1024]{1,0:T(8,128)(2,1)S(1)}, u32[]{:S(2)}, u32[]{:S(2)}) collective-permute-start(bf16[128,1024]{1,0:T(8,128)(2,1)S(1)} %slice.14), channel_id=1, source_target_pairs={{0,1},{1,0},{2,3},{3,2},{4,5},{5,4},{6,7},{7,6},{8,9},{9,8},{10,11... | collective-permute-start | bytes 786440 | tf_op jit(solution)/shard_map/ppermute | solution.py:276
  51.0 16.8 %collective-permute-start.5 = (bf16[512,1024]{1,0:T(8,128)(2,1)S(1)}, bf16[512,1024]{1,0:T(8,128)(2,1)S(1)}, u32[]{:S(2)}, u32[]{:S(2)}) collective-permute-start(bf16[512,1024]{1,0:T(8,128)(2,1)S(1)} %bitcast.29), channel_id=1, source_target_pairs={{0,64},{64,0},{1,65},{65,1},{2,66},{66,2},{3,67},{67,3},{4,68},{68... | collective-permute-start | bytes 3145736 | tf_op jit(solution)/shard_map/ppermute | solution.py:268
  53.7 10.8 %collective-permute-start.4 = (bf16[192,1024]{1,0:T(8,128)(2,1)S(1)}, bf16[192,1024]{1,0:T(8,128)(2,1)S(1)}, u32[]{:S(2)}, u32[]{:S(2)}) collective-permute-start(bf16[192,1024]{1,0:T(8,128)(2,1)S(1)} %slice.15), channel_id=1, source_target_pairs={{0,1},{1,0},{2,3},{3,2},{4,5},{5,4},{6,7},{7,6},{8,9},{9,8},{10,11... | collective-permute-start | bytes 1179656 | tf_op jit(solution)/shard_map/ppermute | solution.py:278
  54.5 7.1 %collective-permute-start.3 = (bf16[512,256]{1,0:T(8,128)(2,1)S(1)}, bf16[512,256]{1,0:T(8,128)(2,1)S(1)}, u32[]{:S(2)}, u32[]{:S(2)}) collective-permute-start(bf16[512,256]{1,0:T(8,128)(2,1)S(1)} %shard_map.87.mine_ref.a_ref), channel_id=1, source_target_pairs={{0,67},{1,66},{2,65},{3,64},{64,0},{65,1},{66,2},{67,3},{4,71},{5,... | collective-permute-start | bytes 786440 | tf_op jit(solution)/shard_map/ppermute | solution.py:293
  54.9 12.9 %collective-permute-start.6 = (bf16[192,1024]{1,0:T(8,128)(2,1)S(1)}, bf16[192,1024]{1,0:T(8,128)(2,1)S(1)}, u32[]{:S(2)}, u32[]{:S(2)}) collective-permute-start(bf16[192,1024]{1,0:T(8,128)(2,1)S(1)} %collective-permute-done.n1a_ref), channel_id=1, source_target_pairs={{0,64},{64,0},{1,65},{65,1},{2,66},{66,2},{3,67},{67,3},{4,68},{68... | collective-permute-start | bytes 1179656 | tf_op jit(solution)/shard_map/ppermute | solution.py:295
  64.4 9.1 %collective-permute-start.8 = (bf16[192,1024]{1,0:T(8,128)(2,1)S(1)}, bf16[192,1024]{1,0:T(8,128)(2,1)S(1)}, u32[]{:S(2)}, u32[]{:S(2)}) collective-permute-start(bf16[192,1024]{1,0:T(8,128)(2,1)S(1)} %collective-permute-done.4.n1c_ref), channel_id=1, source_target_pairs={{0,64},{64,0},{1,65},{65,1},{2,66},{66,2},{3,67},{67,3},{4,68},{68... | collective-permute-start | bytes 1179656 | tf_op jit(solution)/shard_map/ppermute | solution.py:295
  65.3 2.5 %collective-permute-start.7 = (bf16[128,1024]{1,0:T(8,128)(2,1)S(1)}, bf16[128,1024]{1,0:T(8,128)(2,1)S(1)}, u32[]{:S(2)}, u32[]{:S(2)}) collective-permute-start(bf16[128,1024]{1,0:T(8,128)(2,1)S(1)} %collective-permute-done.1.n1b_ref), channel_id=1, source_target_pairs={{0,64},{64,0},{1,65},{65,1},{2,66},{66,2},{3,67},{67,3},{4,68},{68... | collective-permute-start | bytes 786440 | tf_op jit(solution)/shard_map/ppermute | solution.py:295
  65.3 8.3 %collective-permute-start.2 = (bf16[512,256]{1,0:T(8,128)(2,1)S(1)}, bf16[512,256]{1,0:T(8,128)(2,1)S(1)}, u32[]{:S(2)}, u32[]{:S(2)}) collective-permute-start(bf16[512,256]{1,0:T(8,128)(2,1)S(1)} %shard_map.87.mine_ref.a_ref), channel_id=1, source_target_pairs={{64,67},{65,66},{66,65},{67,64},{68,71},{69,70},{70,69},{71,68},{7... | collective-permute-start | bytes 786440 | tf_op jit(solution)/shard_map/ppermute | solution.py:294
  77.8 22.0 %all-to-all-start.1 = ((bf16[16,256,128]{2,1,0:T(8,128)(2,1)}), bf16[16,256,128]{2,1,0:T(8,128)(2,1)}, u32[]{:S(2)}, u32[]{:S(2)}) async-start(bf16[16,256,128]{2,1,0:T(8,128)(2,1)} %shard_map.88), calls=%async_computation.1 | async-start | bytes 2097152 | tf_op jit(solution)/shard_map/all_to_all | solution.py:298
  84.8 20.9 %collective-permute-start.10 = (bf16[512,256]{1,0:T(8,128)(2,1)S(1)}, bf16[512,256]{1,0:T(8,128)(2,1)S(1)}, u32[]{:S(2)}, u32[]{:S(2)}) collective-permute-start(bf16[512,256]{1,0:T(8,128)(2,1)S(1)} %shard_map.87.mine_ref.a_ref), channel_id=1, source_target_pairs={{0,3},{1,0},{2,1},{3,2},{4,7},{5,4},{6,5},{7,6},{8,11},{9,8},{10,9... | collective-permute-start | bytes 786440 | tf_op jit(solution)/shard_map/ppermute | solution.py:302
  85.3 21.2 %collective-permute-start.11 = (bf16[512,256]{1,0:T(8,128)(2,1)S(1)}, bf16[512,256]{1,0:T(8,128)(2,1)S(1)}, u32[]{:S(2)}, u32[]{:S(2)}) collective-permute-start(bf16[512,256]{1,0:T(8,128)(2,1)S(1)} %shard_map.87.mine_ref.a_ref), channel_id=1, source_target_pairs={{0,2},{1,3},{2,0},{3,1},{4,6},{5,7},{6,4},{7,5},{8,10},{9,11},{10,... | collective-permute-start | bytes 786440 | tf_op jit(solution)/shard_map/ppermute | solution.py:302
  85.4 23.1 %collective-permute-start.9 = (bf16[512,256]{1,0:T(8,128)(2,1)S(1)}, bf16[512,256]{1,0:T(8,128)(2,1)S(1)}, u32[]{:S(2)}, u32[]{:S(2)}) collective-permute-start(bf16[512,256]{1,0:T(8,128)(2,1)S(1)} %shard_map.87.mine_ref.a_ref), channel_id=1, source_target_pairs={{0,1},{1,2},{2,3},{3,0},{4,5},{5,6},{6,7},{7,4},{8,9},{9,10},{10,1... | collective-permute-start | bytes 786440 | tf_op jit(solution)/shard_map/ppermute | solution.py:302
  101.2 14.3 %collective-permute-start.15 = (bf16[256,128]{1,0:T(8,128)(2,1)S(1)}, bf16[256,128]{1,0:T(8,128)(2,1)S(1)}, u32[]{:S(2)}, u32[]{:S(2)}) collective-permute-start(bf16[256,128]{1,0:T(8,128)(2,1)S(1)} %reduce_sum.22), channel_id=1, source_target_pairs={{0,0},{1,1},{2,64},{3,65},{64,2},{65,3},{66,66},{67,67},{4,4},{5,5... | collective-permute-start | bytes 196616 | tf_op jit(solution)/shard_map/ppermute | solution.py:314
  103.1 12.4 %collective-permute-start.16 = (bf16[256,128]{1,0:T(8,128)(2,1)S(1)}, bf16[256,128]{1,0:T(8,128)(2,1)S(1)}, u32[]{:S(2)}, u32[]{:S(2)}) collective-permute-start(bf16[256,128]{1,0:T(8,128)(2,1)S(1)} %reduce_sum.22), channel_id=1, source_target_pairs={{0,1},{1,0},{2,65},{3,64},{64,3},{65,2},{66,67},{67,66},{4,5},{5,4... | collective-permute-start | bytes 196616 | tf_op jit(solution)/shard_map/ppermute | solution.py:314
  105.8 0.7 copy-start.5
  106.5 9.1 %collective-permute-start.17 = (bf16[256,128]{1,0:T(8,128)(2,1)S(1)}, bf16[256,128]{1,0:T(8,128)(2,1)S(1)}, u32[]{:S(2)}, u32[]{:S(2)}) collective-permute-start(bf16[256,128]{1,0:T(8,128)(2,1)S(1)} %reduce_sum.22), channel_id=1, source_target_pairs={{0,2},{1,3},{2,66},{3,67},{64,0},{65,1},{66,64},{67,65},{4,6},{5,7... | collective-permute-start | bytes 196616 | tf_op jit(solution)/shard_map/ppermute | solution.py:314
  106.5 0.7 copy-start.7
  107.2 8.4 %collective-permute-start.18 = (bf16[256,128]{1,0:T(8,128)(2,1)S(1)}, bf16[256,128]{1,0:T(8,128)(2,1)S(1)}, u32[]{:S(2)}, u32[]{:S(2)}) collective-permute-start(bf16[256,128]{1,0:T(8,128)(2,1)S(1)} %reduce_sum.22), channel_id=1, source_target_pairs={{0,3},{1,2},{2,67},{3,66},{64,1},{65,0},{66,65},{67,64},{4,7},{5,6... | collective-permute-start | bytes 196616 | tf_op jit(solution)/shard_map/ppermute | solution.py:314
  108.5 0.7 copy-start.9
  109.2 1.6 %copy-start.3 = (bf16[1024,1024]{1,0:T(8,128)(2,1)S(1)}, bf16[1024,1024]{1,0:T(8,128)(2,1)}, u32[]{:S(2)}) copy-start(bf16[1024,1024]{1,0:T(8,128)(2,1)} %w_ref.1) | copy-start | bytes 6291460
  110.8 0.9 copy-start.6
  111.7 0.9 copy-start.8
  112.7 0.9 copy-start.10
Sparse Core Ops, SparseCore 0:
  51.1 52.8 all-gather.1

commit v3 on v2

--- a/solution.py
+++ b/solution.py
@@ -12,8 +12,10 @@
 SUB = LANES // GROUP
 WIN = 9
 SLOT = WIN * SUB
-CUTS = (192, 320)
+SIDE = 4
+CUT = 256
 VMEM = 24 * 1024 * 1024
+WIDE = 56 * 1024 * 1024
 
 
 def seg_kernel(idx_ref, starts_ref, owner_ref, bytes_ref, out_ref, next_ref, low_ref, high_ref, acc_ref):
@@ -86,7 +88,7 @@
             ],
         ),
         out_shape=jax.ShapeDtypeStruct((rows, width), jnp.bfloat16),
-        compiler_params=pltpu.CompilerParams(vmem_limit_bytes=VMEM),
+        compiler_params=pltpu.CompilerParams(vmem_limit_bytes=WIDE),
         interpret=interpret,
     )(idx, starts, owner, grads)
 
@@ -113,7 +115,7 @@
     )(first, incoming)
 
 
-def outer_kernel(idx_ref, mine_ref, third_ref, cross_ref, n0_ref, n1a_ref, n1b_ref, n1c_ref, f0_ref, f1a_ref, f1b_ref, f1c_ref, out_ref, near_t, far_t):
+def outer_kernel(idx_ref, mine_ref, third_ref, cross_ref, n0_ref, n1a_ref, n1b_ref, f0_ref, f1a_ref, f1b_ref, out_ref, both_ref, near_t, far_t):
     step = pl.program_id(0)
 
     @pl.when(step == 0)
@@ -121,12 +123,14 @@
         near = jnp.where(idx_ref[0] == 0, mine_ref[...], third_ref[...])
         near_t[...] = near.T
         far_t[...] = cross_ref[...].T
+        both_ref[0] = near
+        both_ref[1] = cross_ref[...]
 
     low = lax.rem(idx_ref[1], 2)
     blocks = out_ref.shape[0] // 2
     per = n0_ref.shape[1] // LANES
-    near1 = jnp.concatenate([n1a_ref[...], n1b_ref[...], n1c_ref[...]], axis=0)
-    far1 = jnp.concatenate([f1a_ref[...], f1b_ref[...], f1c_ref[...]], axis=0)
+    near1 = jnp.concatenate([n1a_ref[...], n1b_ref[...]], axis=0)
+    far1 = jnp.concatenate([f1a_ref[...], f1b_ref[...]], axis=0)
     for near, far, which in ((n0_ref[...], f0_ref[...], low), (near1, far1, 1 - low)):
         total = jnp.dot(near_t[...], near, preferred_element_type=jnp.float32)
         total += jnp.dot(far_t[...], far, preferred_element_type=jnp.float32)
@@ -148,23 +152,25 @@
             grid=(cols // block,),
             in_specs=[whole] * len(sums)
             + [pl.BlockSpec((c.shape[0], block), lambda i, idx: (0, i)) for c in columns],
-            out_specs=pl.BlockSpec(shape, lambda i, idx: (0, 0, 0)),
+            out_specs=[
+                pl.BlockSpec(shape, lambda i, idx: (0, 0, 0)),
+                pl.BlockSpec((2, rows, width), lambda i, idx: (0, 0, 0)),
+            ],
             scratch_shapes=[pltpu.VMEM((width, rows), jnp.bfloat16)] * 2,
         ),
-        out_shape=jax.ShapeDtypeStruct(shape, jnp.bfloat16),
-        compiler_params=pltpu.CompilerParams(vmem_limit_bytes=VMEM),
+        out_shape=[
+            jax.ShapeDtypeStruct(shape, jnp.bfloat16),
+            jax.ShapeDtypeStruct((2, rows, width), jnp.bfloat16),
+        ],
+        compiler_params=pltpu.CompilerParams(vmem_limit_bytes=WIDE),
     )(idx, *sums, *columns)
 
 
-def chain_kernel(idx_ref, value_ref, global_ref, a_ref, b_ref, c_ref, d_ref, turned_ref):
+def chain_kernel(idx_ref, both_ref, global_ref, a_ref, b_ref, c_ref, d_ref, turned_ref):
     step = pl.program_id(0)
     share = a_ref.shape[0]
-
-    @pl.when(step == 0)
-    def _():
-        turned_ref[...] = value_ref[...].T
-
-    at = pl.ds(pl.multiple_of(lax.rem(idx_ref[0], LANES // share) * share, share), share)
+    turned_ref[...] = both_ref[...].T
+    at = pl.ds(pl.multiple_of(lax.rem(idx_ref[1], LANES // share) * share, share), share)
     total = lax.dot_general(
         turned_ref[at, :], global_ref[...], (((1,), (1,)), ((), ())), preferred_element_type=jnp.float32
     ).astype(jnp.bfloat16)
@@ -175,53 +181,95 @@
             ref[...] = total
 
 
-def chain_terms(idx, w_value, w_global, share, parts):
-    deep, feats = w_value.shape
+def chain_terms(idx, both_t, w_global, share, parts):
+    deep, feats = both_t.shape
     rows = w_global.shape[0] // parts
-    per = LANES // share
+
+    def rows_of(i, idx):
+        half = lax.div(lax.rem(idx[2] + i, parts), 2)
+        block = (idx[0] + half - 2 * idx[0] * half) * 2 * SIDE + idx[1]
+        return (0, lax.div(block, LANES // share))
+
     return pl.pallas_call(
         chain_kernel,
         grid_spec=pltpu.PrefetchScalarGridSpec(
             num_scalar_prefetch=1,
             grid=(parts,),
             in_specs=[
-                pl.BlockSpec((deep, LANES), lambda i, idx: (0, lax.div(idx[0], per))),
-                pl.BlockSpec((rows, deep), lambda i, idx: (lax.rem(idx[1] + i, parts), 0)),
+                pl.BlockSpec((deep, LANES), rows_of),
+                pl.BlockSpec((rows, deep), lambda i, idx: (lax.rem(idx[2] + i, parts), 0)),
             ],
             out_specs=[pl.BlockSpec((share, rows), lambda i, idx: (0, 0))] * parts,
             scratch_shapes=[pltpu.VMEM((LANES, deep), jnp.bfloat16)],
         ),
         out_shape=[jax.ShapeDtypeStruct((share, rows), jnp.bfloat16)] * parts,
+        compiler_params=pltpu.CompilerParams(vmem_limit_bytes=WIDE),
+    )(idx, both_t, w_global)
+
+
+def theirs_kernel(idx_ref, near_ref, far_ref, low_ref, high_ref, out_ref, table_ref):
+    share = low_ref.shape[2]
+    deep = table_ref.shape[0] // 2
+    z, odd = lax.div(idx_ref[1], SIDE), lax.rem(idx_ref[1], 2)
+    for ref, base in ((low_ref, z), (high_ref, SIDE - 1 - z)):
+        for i in range(2):
+            for j in range(2):
+                other = base + i - 2 * i * lax.rem(base, 2)
+                to = 2 * other + odd + j - 2 * odd * j
+                table_ref[pl.ds(pl.multiple_of(to * share, share), share), :] = ref[i, j]
+    odd = lax.rem(idx_ref[2] + idx_ref[0], 2)
+    first = table_ref[pl.ds(pl.multiple_of(odd * deep, deep), deep), :]
+    second = table_ref[pl.ds(pl.multiple_of((1 - odd) * deep, deep), deep), :]
+    total = jnp.dot(near_ref[1], first, preferred_element_type=jnp.float32)
+    total += jnp.dot(far_ref[1], second, preferred_element_type=jnp.float32)
+    out_ref[...] = total.astype(jnp.bfloat16)
+
+
+def theirs(idx, near, far, low, high):
+    vmem = pl.BlockSpec(memory_space=pltpu.VMEM)
+    rows, cols = near.shape[1], low.shape[3]
+    deep = 8 * low.shape[2]
+    return pl.pallas_call(
+        theirs_kernel,
+        in_specs=[pl.BlockSpec(memory_space=pltpu.SMEM)] + [vmem] * 4,
+        out_specs=[vmem, vmem],
+        out_shape=[
+            jax.ShapeDtypeStruct((rows, cols), jnp.bfloat16),
+            jax.ShapeDtypeStruct((deep, cols), jnp.bfloat16),
+        ],
         compiler_params=pltpu.CompilerParams(vmem_limit_bytes=VMEM),
-    )(idx, w_value, w_global)
-
-
-def value_kernel(feat_ref, a_ref, b_ref, c_ref, d_ref, w_ref, out_ref):
-    width = a_ref.shape[1]
+    )(idx, near, far, low, high)
+
+
+def ours_kernel(idx_ref, near_ref, far_ref, table_ref, back_ref, out_ref):
+    deep = table_ref.shape[0] // 2
+    odd = lax.rem(idx_ref[2] + idx_ref[0], 2)
+    first = table_ref[pl.ds(pl.multiple_of(odd * deep, deep), deep), :]
+    second = table_ref[pl.ds(pl.multiple_of((1 - odd) * deep, deep), deep), :]
+    total = jnp.dot(near_ref[0], first, preferred_element_type=jnp.float32)
+    total += jnp.dot(far_ref[0], second, preferred_element_type=jnp.float32)
+    out_ref[...] = (total + back_ref[...].astype(jnp.float32)).astype(jnp.bfloat16)
+
+
+def ours(idx, near, far, table, back):
+    vmem = pl.BlockSpec(memory_space=pltpu.VMEM)
+    return pl.pallas_call(
+        ours_kernel,
+        in_specs=[pl.BlockSpec(memory_space=pltpu.SMEM)] + [vmem] * 4,
+        out_specs=vmem,
+        out_shape=jax.ShapeDtypeStruct(back.shape, jnp.bfloat16),
+        compiler_params=pltpu.CompilerParams(vmem_limit_bytes=VMEM),
+    )(idx, near, far, table, back)
+
+
+def last_kernel(feat_ref, a_ref, b_ref, c_ref, d_ref, w_ref, out_ref):
+    width = a_ref.shape[0]
     total = jnp.zeros(out_ref.shape, jnp.float32)
     for s, ref in enumerate((a_ref, b_ref, c_ref, d_ref)):
         at = pl.ds(pl.multiple_of(feat_ref[s] * width, width), width)
         total += lax.dot_general(
-            ref[...], w_ref[:, at], (((1,), (1,)), ((), ())), preferred_element_type=jnp.float32
+            ref[...].T, w_ref[:, at], (((1,), (1,)), ((), ())), preferred_element_type=jnp.float32
         )
-    out_ref[...] = total.astype(jnp.bfloat16)
-
-
-def value(feats, pieces, weights):
-    vmem = pl.BlockSpec(memory_space=pltpu.VMEM)
-    return pl.pallas_call(
-        value_kernel,
-        in_specs=[pl.BlockSpec(memory_space=pltpu.SMEM)] + [vmem] * 5,
-        out_specs=vmem,
-        out_shape=jax.ShapeDtypeStruct((pieces[0].shape[0], weights.shape[0]), jnp.bfloat16),
-        compiler_params=pltpu.CompilerParams(vmem_limit_bytes=VMEM),
-    )(feats, *pieces, weights)
-
-
-def last_kernel(feat_ref, a_ref, b_ref, c_ref, d_ref, w_ref, out_ref):
-    total = jnp.zeros(out_ref.shape, jnp.float32)
-    for s, ref in enumerate((a_ref, b_ref, c_ref, d_ref)):
-        total += jnp.dot(ref[...].T, w_ref[feat_ref[s]], preferred_element_type=jnp.float32)
     out_ref[...] = total
 
 
@@ -231,7 +279,7 @@
         last_kernel,
         in_specs=[pl.BlockSpec(memory_space=pltpu.SMEM)] + [vmem] * 5,
         out_specs=vmem,
-        out_shape=jax.ShapeDtypeStruct((pieces[0].shape[1], weights.shape[2]), jnp.float32),
+        out_shape=jax.ShapeDtypeStruct((pieces[0].shape[1], weights.shape[0]), jnp.float32),
         compiler_params=pltpu.CompilerParams(vmem_limit_bytes=VMEM),
     )(feats, *pieces, weights)
 
@@ -266,57 +314,59 @@
     pair = [(x, x ^ 1) for x in range(ten_n)]
     near0 = attn_context[0]
     far0 = lax.ppermute(near0, "dp", swap)
-    ends = (0,) + CUTS + (patch_rows,)
-    near1 = [lax.ppermute(near0[: ends[1]], "tensor", pair)]
-
-    outgoing = segment_sums(jnp.stack([ctx, ten]), starts, owner, byte_grads[0], ctx_n, width)
-    outgoing = after(outgoing, near1[0])
+    near1 = [lax.ppermute(near0[:CUT], "tensor", pair)]
+
+    here = jnp.stack([dp, ctx, ten])
+    outgoing = segment_sums(here[1:], starts, owner, byte_grads[0], ctx_n, width)
+    both_t = jnp.dot(after(w_value, outgoing), w_out, preferred_element_type=f32).astype(bf16)
+    outgoing = after(outgoing, near1[0], both_t)
     incoming = lax.all_to_all(outgoing, "context", split_axis=0, concat_axis=0, tiled=True)
 
-    near1.append(lax.ppermute(after(near0, outgoing)[ends[1] : ends[2]], "tensor", pair))
-    incoming = after(incoming, near1[1])
-    near1.append(lax.ppermute(after(near0, incoming)[ends[2] :], "tensor", pair))
-
-    share = feats // (dp_n * ctx_n)
-    where = after(jnp.stack([dp * ctx_n + ctx, ten]), outgoing)
-    terms = chain_terms(where, w_value, w_global, share, ten_n)
+    z, y = ctx // SIDE, ctx % SIDE
+    share = feats // (4 * SIDE)
+    where = after(jnp.stack([dp, 2 * z + y % 2, ten]), outgoing)
+    terms = chain_terms(where, both_t, w_global, share, ten_n)
     chain = terms[0].astype(f32)
     for s in range(1, ten_n):
         chain += lax.ppermute(terms[s], "tensor", [(x, (x + s) % ten_n) for x in range(ten_n)]).astype(f32)
-    chain = lax.all_gather(after(chain.astype(bf16), incoming), ("dp", "context"), axis=0, tiled=True)
-
+    chain = chain.astype(bf16)
     edges = jnp.arange(ctx_n, dtype=jnp.int32) * bytes_n
     counts = jnp.sum((patch_starts[0][None, :] <= edges[:, None]).astype(jnp.int32), axis=1)
     first = jnp.minimum((counts - 1) // LANES, starts.shape[0] - WIN)
-
+    incoming = after(incoming, first, chain)
+
+    near1.append(lax.ppermute(after(near0, incoming)[CUT:], "tensor", pair))
     sums = collect(first, incoming, patch_rows)
     cross = lax.ppermute(sums, line, moves(lambda d, x: (0, x) if d == 1 else (1, ten_n - 1 - x)))
     third = lax.ppermute(sums, line, moves(lambda d, x: (1, ten_n - 1 - x) if d == 1 else None))
-    far1 = [lax.ppermute(part, "dp", swap) for part in (near1[0], near1[1], after(near1[2], cross))]
+    far1 = [lax.ppermute(part, "dp", swap) for part in (near1[0], after(near1[1], cross, third))]
+
+    def along(target):
+        return [
+            (i * SIDE + j, target(i, j)[0] * SIDE + target(i, j)[1]) for i in range(SIDE) for j in range(SIDE)
+        ]
+
+    chain = after(chain, sums)
+    chain = jnp.stack([chain, lax.ppermute(chain, "context", along(lambda i, j: (i, j ^ 1)))])
+    chain = jnp.stack([chain, lax.ppermute(chain, "context", along(lambda i, j: (i ^ 1, j)))])
     columns = (near0, *near1, far0, *far1)
-    partial = outer(jnp.stack([dp, ten]), (sums, third, cross), columns)
+    partial, near = outer(after(jnp.stack([dp, ten]), chain), (sums, third, cross), columns)
     pieces = lax.all_to_all(partial, "context", split_axis=0, concat_axis=0, tiled=True)
-
-    late = after(sums, partial)
-    around = [late] + [
-        lax.ppermute(late, "tensor", [(x, (x + s) % ten_n) for x in range(ten_n)]) for s in (1, ten_n - 1, 2)
-    ]
-    order = jnp.stack([ten, (ten + ten_n - 1) % ten_n, (ten + 1) % ten_n, (ten + 2) % ten_n])
-    value_grad = value(order, around, w_out)
-    both = lax.dot_general(
-        after(w_out, partial), w_value, (((0,), (1,)), ((), ())), preferred_element_type=f32
-    ).astype(bf16)
-
-    pieces = after(pieces, both)
+    rest = lax.ppermute(after(chain, partial), "context", along(lambda i, j: (SIDE - 1 - i, j)))
+
+    far = lax.ppermute(near, "tensor", pair)
+    give, table = theirs(here, near, far, chain, rest)
+    pieces = after(pieces, give)
     piece = jnp.sum(pieces.astype(f32), axis=0).astype(bf16)
     parts, blocks = [], []
     for s in range(ten_n):
         parts.append(lax.ppermute(piece, line, moves(lambda d, x, s=s: (x // 2, (2 * d + x % 2) ^ s))))
         source = ten ^ s
-        near = 2 * dp + source % 2
-        blocks.append(jnp.where(source < 2, near, ten_n - 1 - near))
-    weight_grad = last(jnp.stack(blocks), parts, both.reshape(ten_n, width, -1))
-    context_grad = jnp.dot(value_grad, chain, preferred_element_type=f32).astype(bf16)
+        pick = 2 * dp + source % 2
+        blocks.append(jnp.where(source < 2, pick, ten_n - 1 - pick))
+    back = lax.ppermute(give, "dp", swap)
+    context_grad = ours(here, near, far, table, back)
+    weight_grad = last(jnp.stack(blocks), parts, both_t)
     return (context_grad[None], weight_grad)
 
 

time: 129 us -> 127 us (0.984)
  between operations: 14.3 us -> 0.83 us
  Pallas kernels: 19.6 us -> 31.5 us
  local copies, waits for them, and re-layouts: 17.5 us -> 6.83 us
  starting transfers between devices: 36.9 us -> 43.5 us
  waiting for transfers between devices: 28.6 us -> 32.6 us
  matrix products: 8.44 us -> 5.27 us
  other arithmetic: 2.69 us -> 5.48 us
    ppermute x6 -> x7, waiting for transfers between devices: 7.6 us -> 19.6 us  [the longest x1 14.2 us: local(): lax.ppermute(after(chain, partial), 'context', along(lambda i, j: (SIDE -...]
    unnamed x28, local copies, waits for them, and re-layouts: 16.4 us -> 4.53 us
    ppermute x6 -> x7, starting transfers between devices: 3.77 us -> 14.1 us  [the longest x1 3.23 us: local(): back = lax.ppermute(give, 'dp', swap)]
    all_to_all x1, waiting for transfers between devices: 8.88 us -> 0.01 us  [local(): lax.all_to_all(partial, 'context', split_axis=0, concat_axis=0, tiled=True)]
    ppermute x1, waiting for transfers between devices: 5.78 us -> 1.37 us  [local(): lax.ppermute(sums, line, moves(lambda d, x: (1, ten_n - 1 - x) if d == 1...]
    ppermute x4, waiting for transfers between devices: 0.01 us -> 4.11 us  [local(): lax.ppermute(piece, line, moves(lambda d, x, s=s: (x // 2, 2 * d + x % 2...]
    pallas_call x1 -> x2, Pallas kernels: 1.84 us -> 5.89 us  [the longest x1 2.97 us: theirs(): pl.pallas_call(theirs_kernel, in_specs=[pl.BlockSpec(memory_space=pltpu.S...]
    pallas_call x1, Pallas kernels: 3.74 us -> 7.38 us  [chain_terms(): pl.pallas_call(chain_kernel, grid_spec=pltpu.PrefetchScalarGridSpec(num_s...]
  transfers between devices with their start and end apart: 22 -> 21, of which waited for: 7 -> 10; matrix products, arithmetic and copies ran while one was open for 6% -> 9% of each run, Pallas kernels for 15% -> 18%
where the time goes in v3:
time: 127 us; the launch traced here: 126 us
  starting transfers between devices  43.5 us (34%)
  waiting for transfers between devices  32.6 us (26%)
  Pallas kernels  31.5 us (25%)
  local copies, waits for them, and re-layouts  6.83 us (5%)
  other arithmetic  5.48 us (4%)
  matrix products  5.27 us (4%)
    ppermute x1, waiting for transfers between devices, local(): lax.ppermute(after(chain, partial), 'context', along(lambda i, j: (SIDE -...  14.2 us
    pallas_call x1, Pallas kernels, segment_sums(): pl.pallas_call(seg_kernel, grid_spec=pltpu.PrefetchScalarGridSpec(num_sca...  9.12 us
    all_to_all x1, starting transfers between devices, local(): lax.all_to_all(outgoing, 'context', split_axis=0, concat_axis=0, tiled=True)  7.77 us
    pallas_call x1, Pallas kernels, chain_terms(): pl.pallas_call(chain_kernel, grid_spec=pltpu.PrefetchScalarGridSpec(num_s...  7.38 us
    ppermute x4, starting transfers between devices, local(): lax.ppermute(piece, line, moves(lambda d, x, s=s: (x // 2, 2 * d + x % 2...  7.1 us
    pallas_call x1, Pallas kernels, outer(): pl.pallas_call(outer_kernel, grid_spec=pltpu.PrefetchScalarGridSpec(num_s...  6.16 us
    ppermute x1, waiting for transfers between devices, local(): lax.ppermute(chain, 'context', along(lambda i, j: (i ^ 1, j)))  5.37 us
    dot_general x1, matrix products, local(): jnp.dot(after(w_value, outgoing), w_out, preferred_element_type=f32)  5.27 us
  transfers between devices with their start and end apart: 21, of which 10 were waited for; matrix products, arithmetic and copies ran while one was open for 9% of the time, Pallas kernels for 18%

profile of v3, /device:TPU:1, one launch (start us, length us, event | category | flops | bytes accessed | tf_op | source)
XLA Modules:
  0.0 126.0 jit_solution(16905862980217483843)
XLA Ops:
  0.6 1.2 slice_bitcast_fusion
  1.9 2.1 %collective-permute-start = (bf16[256,1024]{1,0:T(8,128)(2,1)S(1)}, bf16[256,1024]{1,0:T(8,128)(2,1)S(1)}, u32[]{:S(2)}, u32[]{:S(2)}) collective-permute-start(bf16[256,1024]{1,0:T(8,128)(2,1)S(1)} %slice_bitcast_fusion), channel_id=1, source_target_pairs={{0,1},{1,0},{2,3},{3,2},{4,5},{5,4},{6,7},{7,6},{8,9},{9,8},{10,11... | collective-permute-start | bytes 1572872 | tf_op jit(solution)/shard_map/ppermute | solution.py:317
  4.0 0.6 pad_add_fusion.1.idx_ref
  4.6 9.1 %shard_map.86 = bf16[1152,256]{1,0:T(8,128)(2,1)} custom-call(s32[2]{0:T(128)} %pad_add_fusion.1.idx_ref, s32[64,128]{1,0:T(8,128)} %bitcast.33, s32[64,128]{1,0:T(8,128)} %bitcast.36, bf16[4096,1024]{1,0:T(8,128)(2,1)} %bitcast.26), custom_call_target="tpu_custom_call" | custom-call | tf_op jit(solution)/shard_map/pallas_call | solution.py:76
  13.7 0.3 convert_reduce_fusion
  14.0 5.3 %convolution_convert_fusion.both_ref.w_ref = bf16[1024,1024]{1,0:T(8,128)(2,1)} fusion(bf16[1024,1024]{1,0:T(8,128)(2,1)S(1)} %copy-done, bf16[1024,1024]{1,0:T(8,128)(2,1)} %param.13), kind=kOutput, calls=%fused_computation | convolution fusion | flops 2148532224 | bytes 6291456 | tf_op jit(solution)/shard_map/dot_general | solution.py:321
  19.3 7.8 %all-to-all-start = ((bf16[16,72,256]{2,1,0:T(8,128)(2,1)}), bf16[16,72,256]{2,1,0:T(8,128)(2,1)S(1)}, u32[]{:S(2)}, u32[]{:S(2)}) async-start(bf16[16,72,256]{2,1,0:T(8,128)(2,1)} %bitcast.9), calls=%async_computation | async-start | bytes 1179648 | tf_op jit(solution)/shard_map/all_to_all | solution.py:323
  27.0 0.6 add_add_fusion.1.idx_ref
  27.6 7.4 %shard_map.87 = (bf16[64,1024]{1,0:T(8,128)(2,1)}, bf16[64,1024]{1,0:T(8,128)(2,1)}, bf16[64,1024]{1,0:T(8,128)(2,1)}, bf16[64,1024]{1,0:T(8,128)(2,1)}) custom-call(s32[3]{0:T(128)} %add_add_fusion.1.idx_ref, bf16[1024,1024]{1,0:T(8,128)(2,1)} %convolution_convert_fusion.both_ref.w_ref, bf16[4096,1024]{1,0:T(8,128)(2,1)} %global_ref.1), custom_call_target="tpu_custom_call" | custom-call | tf_op jit(solution)/shard_map/pallas_call | solution.py:193
  35.0 0.3 collective-permute-start.1
  35.3 2.7 %collective-permute-start.2 = (bf16[64,1024]{1,0:T(8,128)(2,1)}, bf16[64,1024]{1,0:T(8,128)(2,1)S(1)}, u32[]{:S(2)}, u32[]{:S(2)}) collective-permute-start(bf16[64,1024]{1,0:T(8,128)(2,1)} %get-tuple-element.25), channel_id=1, source_target_pairs={{0,2},{1,3},{2,0},{3,1},{4,6},{5,7},{6,4},{7,5},{8,10},{9,11},{10,... | collective-permute-start | bytes 393224 | tf_op jit(solution)/shard_map/ppermute | solution.py:331
  38.0 1.5 %collective-permute-start.3 = (bf16[64,1024]{1,0:T(8,128)(2,1)}, bf16[64,1024]{1,0:T(8,128)(2,1)S(1)}, u32[]{:S(2)}, u32[]{:S(2)}) collective-permute-start(bf16[64,1024]{1,0:T(8,128)(2,1)} %get-tuple-element.26), channel_id=1, source_target_pairs={{0,3},{1,0},{2,1},{3,2},{4,7},{5,4},{6,5},{7,6},{8,11},{9,8},{10,9... | collective-permute-start | bytes 393224 | tf_op jit(solution)/shard_map/ppermute | solution.py:331
  39.5 0.7 collective-permute-done.1
  40.2 2.8 %collective-permute-done.2 = bf16[64,1024]{1,0:T(8,128)(2,1)S(1)} collective-permute-done((bf16[64,1024]{1,0:T(8,128)(2,1)}, bf16[64,1024]{1,0:T(8,128)(2,1)S(1)}, u32[]{:S(2)}, u32[]{:S(2)}) %collective-permute-start.2) | collective-permute-done | bytes 131104 | tf_op jit(solution)/shard_map/ppermute | solution.py:331
  43.3 1.0 add_convert_fusion
  44.3 1.1 slice.13
  45.3 2.1 %collective-permute-start.8 = (bf16[256,1024]{1,0:T(8,128)(2,1)S(1)}, bf16[256,1024]{1,0:T(8,128)(2,1)S(1)}, u32[]{:S(2)}, u32[]{:S(2)}) collective-permute-start(bf16[256,1024]{1,0:T(8,128)(2,1)S(1)} %slice.13), channel_id=1, source_target_pairs={{0,1},{1,0},{2,3},{3,2},{4,5},{5,4},{6,7},{7,6},{8,9},{9,8},{10,11... | collective-permute-start | bytes 1572872 | tf_op jit(solution)/shard_map/ppermute | solution.py:338
  47.4 2.2 %collective-permute-start.9 = (bf16[512,1024]{1,0:T(8,128)(2,1)}, bf16[512,1024]{1,0:T(8,128)(2,1)S(1)}, u32[]{:S(2)}, u32[]{:S(2)}) collective-permute-start(bf16[512,1024]{1,0:T(8,128)(2,1)} %bitcast.28), channel_id=1, source_target_pairs={{0,64},{64,0},{1,65},{65,1},{2,66},{66,2},{3,67},{67,3},{4,68},{68... | collective-permute-start | bytes 3145736 | tf_op jit(solution)/shard_map/ppermute | solution.py:316
  49.6 0.8 shard_map.88.mine_ref
  50.5 3.2 %collective-permute-start.6 = (bf16[512,256]{1,0:T(8,128)(2,1)S(1)}, bf16[512,256]{1,0:T(8,128)(2,1)S(1)}, u32[]{:S(2)}, u32[]{:S(2)}) collective-permute-start(bf16[512,256]{1,0:T(8,128)(2,1)S(1)} %shard_map.88.mine_ref), channel_id=1, source_target_pairs={{64,67},{65,66},{66,65},{67,64},{68,71},{69,70},{70,69},{71,68},{7... | collective-permute-start | bytes 786440 | tf_op jit(solution)/shard_map/ppermute | solution.py:341
  53.7 1.4 %collective-permute-start.4 = (bf16[64,1024]{1,0:T(8,128)(2,1)S(1)}, bf16[64,1024]{1,0:T(8,128)(2,1)S(1)}, u32[]{:S(2)}, u32[]{:S(2)}) collective-permute-start(bf16[64,1024]{1,0:T(8,128)(2,1)S(1)} %add_convert_fusion), channel_id=1, source_target_pairs={{0,4},{4,0},{8,12},{12,8},{16,20},{20,16},{24,28},{28,24},{32,36},... | collective-permute-start | bytes 393224 | tf_op jit(solution)/shard_map/ppermute | solution.py:350
  55.1 3.7 %collective-permute-done.7.cross_ref = bf16[512,256]{1,0:T(8,128)(2,1)S(1)} collective-permute-done((bf16[512,256]{1,0:T(8,128)(2,1)S(1)}, bf16[512,256]{1,0:T(8,128)(2,1)S(1)}, u32[]{:S(2)}, u32[]{:S(2)}) %collective-permute-start.7) | collective-permute-done | bytes 262176 | tf_op jit(solution)/shard_map/ppermute | solution.py:340
  58.9 1.4 %collective-permute-done.6.third_ref = bf16[512,256]{1,0:T(8,128)(2,1)S(1)} collective-permute-done((bf16[512,256]{1,0:T(8,128)(2,1)S(1)}, bf16[512,256]{1,0:T(8,128)(2,1)S(1)}, u32[]{:S(2)}, u32[]{:S(2)}) %collective-permute-start.6) | collective-permute-done | bytes 262176 | tf_op jit(solution)/shard_map/ppermute | solution.py:341
  60.4 1.4 %collective-permute-start.5 = (bf16[2,64,1024]{2,1,0:T(8,128)(2,1)S(1)}, bf16[2,64,1024]{2,1,0:T(8,128)(2,1)S(1)}, u32[]{:S(2)}, u32[]{:S(2)}) collective-permute-start(bf16[2,64,1024]{2,1,0:T(8,128)(2,1)S(1)} %get-tuple-element.39), channel_id=1, source_target_pairs={{0,16},{4,20},{8,24},{12,28},{16,0},{20,4},{24,8},{28,12},{32,48},... | collective-permute-start | bytes 786440 | tf_op jit(solution)/shard_map/ppermute | solution.py:351
  61.9 0.7 pad_add_fusion.idx_ref
  62.5 5.4 %collective-permute-done.5 = bf16[2,64,1024]{2,1,0:T(8,128)(2,1)S(1)} collective-permute-done((bf16[2,64,1024]{2,1,0:T(8,128)(2,1)S(1)}, bf16[2,64,1024]{2,1,0:T(8,128)(2,1)S(1)}, u32[]{:S(2)}, u32[]{:S(2)}) %collective-permute-start.5) | collective-permute-done | bytes 262176 | tf_op jit(solution)/shard_map/ppermute | solution.py:351
  67.9 0.9 pad_maximum_fusion.low_ref
  68.8 0.7 copy-done.9
  69.6 0.3 copy-done.6
  69.9 0.8 copy-done.10
  70.7 6.2 %shard_map.89 = (bf16[16,256,128]{2,1,0:T(8,128)(2,1)}, bf16[2,512,256]{2,1,0:T(8,128)(2,1)}) custom-call(s32[2]{0:T(128)} %pad_add_fusion.idx_ref, bf16[512,256]{1,0:T(8,128)(2,1)} %copy-done.5, bf16[512,256]{1,0:T(8,128)(2,1)} %copy-done.12, bf16[512,256]{1,0:T(8,128)(2,1)} %copy-done.11, bf16[512,1024]{1,0:T(8,128)(2,1)} %bitcast.29, ...), custom_call_target="tpu_custom_call" | custom-call | tf_op jit(solution)/shard_map/pallas_call | solution.py:148
  76.8 2.7 %collective-permute-start.13 = (bf16[2,2,64,1024]{3,2,1,0:T(8,128)(2,1)}, bf16[2,2,64,1024]{3,2,1,0:T(8,128)(2,1)}, u32[]{:S(2)}, u32[]{:S(2)}) collective-permute-start(bf16[2,2,64,1024]{3,2,1,0:T(8,128)(2,1)} %pad_maximum_fusion.low_ref), channel_id=1, source_target_pairs={{0,48},{4,52},{8,56},{12,60},{16,32},{20,36},{24,40},{28,44},{32,1... | collective-permute-start | bytes 1572872 | tf_op jit(solution)/shard_map/ppermute | solution.py:355
  79.5 1.1 collective-permute-start.12
  80.6 4.4 %all-to-all-start.1 = ((bf16[16,256,128]{2,1,0:T(8,128)(2,1)}), bf16[16,256,128]{2,1,0:T(8,128)(2,1)}, u32[]{:S(2)}, u32[]{:S(2)}) async-start(bf16[16,256,128]{2,1,0:T(8,128)(2,1)} %get-tuple-element.33), calls=%async_computation.1 | async-start | bytes 2097152 | tf_op jit(solution)/shard_map/all_to_all | solution.py:354
  85.1 14.2 %collective-permute-done.13.high_ref = bf16[2,2,64,1024]{3,2,1,0:T(8,128)(2,1)} collective-permute-done((bf16[2,2,64,1024]{3,2,1,0:T(8,128)(2,1)}, bf16[2,2,64,1024]{3,2,1,0:T(8,128)(2,1)}, u32[]{:S(2)}, u32[]{:S(2)}) %collective-permute-start.13) | collective-permute-done | bytes 524320 | tf_op jit(solution)/shard_map/ppermute | solution.py:355
  99.4 3.0 %shard_map.90 = (bf16[512,1024]{1,0:T(8,128)(2,1)}, bf16[512,1024]{1,0:T(8,128)(2,1)S(1)}) custom-call(s32[3]{0:T(128)S(1)} %add_add_fusion.idx_ref, bf16[2,512,256]{2,1,0:T(8,128)(2,1)S(1)} %copy-done.2, bf16[2,512,256]{2,1,0:T(8,128)(2,1)S(1)} %collective-permute-done.12.far_ref, bf16[2,2,64,1024]{3,2,1,0:T(8,128)(2,1)} %pad_maximum_fusion.low_ref, ...), custom_call_target="tpu_custom_call" | custom-call | tf_op jit(solution)/shard_map/pallas_call | solution.py:232
  102.4 1.0 copy-done.3
  103.4 3.2 %collective-permute-start.14 = (bf16[512,1024]{1,0:T(8,128)(2,1)}, bf16[512,1024]{1,0:T(8,128)(2,1)}, u32[]{:S(2)}, u32[]{:S(2)}) collective-permute-start(bf16[512,1024]{1,0:T(8,128)(2,1)} %get-tuple-element.36), channel_id=1, source_target_pairs={{0,64},{64,0},{1,65},{65,1},{2,66},{66,2},{3,67},{67,3},{4,68},{68... | collective-permute-start | bytes 3145736 | tf_op jit(solution)/shard_map/ppermute | solution.py:367
  106.6 1.4 %reduce_sum.22 = bf16[256,128]{1,0:T(8,128)(2,1)S(1)} reduce(bf16[16,256,128]{2,1,0:T(8,128)(2,1)} %all-to-all-done.1, bf16[]{:T(256)} %constant.89.clone.1), dimensions={0}, to_apply=%region_1.2 | reduce | flops 491520 | bytes 1114114 | tf_op jit(solution)/shard_map/reduce_sum | solution.py:360
  108.0 2.6 %collective-permute-start.18 = (bf16[256,128]{1,0:T(8,128)(2,1)S(1)}, bf16[256,128]{1,0:T(8,128)(2,1)S(1)}, u32[]{:S(2)}, u32[]{:S(2)}) collective-permute-start(bf16[256,128]{1,0:T(8,128)(2,1)S(1)} %reduce_sum.22), channel_id=1, source_target_pairs={{0,3},{1,2},{2,67},{3,66},{64,1},{65,0},{66,65},{67,64},{4,7},{5,6... | collective-permute-start | bytes 196616 | tf_op jit(solution)/shard_map/ppermute | solution.py:363
  110.6 1.4 %collective-permute-start.17 = (bf16[256,128]{1,0:T(8,128)(2,1)S(1)}, bf16[256,128]{1,0:T(8,128)(2,1)S(1)}, u32[]{:S(2)}, u32[]{:S(2)}) collective-permute-start(bf16[256,128]{1,0:T(8,128)(2,1)S(1)} %reduce_sum.22), channel_id=1, source_target_pairs={{0,2},{1,3},{2,66},{3,67},{64,0},{65,1},{66,64},{67,65},{4,6},{5,7... | collective-permute-start | bytes 196616 | tf_op jit(solution)/shard_map/ppermute | solution.py:363
  112.2 2.9 %collective-permute-start.15 = (bf16[256,128]{1,0:T(8,128)(2,1)S(1)}, bf16[256,128]{1,0:T(8,128)(2,1)S(1)}, u32[]{:S(2)}, u32[]{:S(2)}) collective-permute-start(bf16[256,128]{1,0:T(8,128)(2,1)S(1)} %reduce_sum.22), channel_id=1, source_target_pairs={{0,0},{1,1},{2,64},{3,65},{64,2},{65,3},{66,66},{67,67},{4,4},{5,5... | collective-permute-start | bytes 196616 | tf_op jit(solution)/shard_map/ppermute | solution.py:363
  115.2 0.7 collective-permute-done.17.c_ref
  115.8 1.1 collective-permute-done.16.b_ref
  116.9 2.4 %collective-permute-done.15.a_ref = bf16[256,128]{1,0:T(8,128)(2,1)S(1)} collective-permute-done((bf16[256,128]{1,0:T(8,128)(2,1)S(1)}, bf16[256,128]{1,0:T(8,128)(2,1)S(1)}, u32[]{:S(2)}, u32[]{:S(2)}) %collective-permute-start.15) | collective-permute-done | bytes 65568 | tf_op jit(solution)/shard_map/ppermute | solution.py:363
  119.3 1.6 %copy-done.1 = bf16[1024,1024]{1,0:T(8,128)(2,1)S(1)} copy-done((bf16[1024,1024]{1,0:T(8,128)(2,1)S(1)}, bf16[1024,1024]{1,0:T(8,128)(2,1)}, u32[]{:S(2)}) %copy-start.1) | copy-done | bytes 2097176
  120.9 2.2 %shard_map.92 = f32[128,1024]{1,0:T(8,128)} custom-call(s32[4]{0:T(128)S(1)} %pad_add_fusion.2.feat_ref, bf16[256,128]{1,0:T(8,128)(2,1)S(1)} %collective-permute-done.15.a_ref, bf16[256,128]{1,0:T(8,128)(2,1)S(1)} %collective-permute-done.16.b_ref, bf16[256,128]{1,0:T(8,128)(2,1)S(1)} %collective-permute-done.17.c_ref, ...), custom_call_target="tpu_custom_call" | custom-call | tf_op jit(solution)/shard_map/pallas_call | solution.py:278
  123.1 2.9 %shard_map.91 = bf16[512,1024]{1,0:T(8,128)(2,1)} custom-call(s32[3]{0:T(128)S(1)} %add_add_fusion.idx_ref, bf16[2,512,256]{2,1,0:T(8,128)(2,1)S(1)} %copy-done.2, bf16[2,512,256]{2,1,0:T(8,128)(2,1)S(1)} %collective-permute-done.12.far_ref, bf16[512,1024]{1,0:T(8,128)(2,1)S(1)} %copy-done.4, bf16[512,1024]{1,0:T(8,128)(2,1)} %collective-permute-done.14.back_ref), custom_call_target="tpu_custom_call" | custom-call | tf_op jit(solution)/shard_map/pallas_call | solution.py:256
  (44 shorter events, 0.9 us)
Async XLA Ops:
  0.6 13.3 %copy-start = (bf16[1024,1024]{1,0:T(8,128)(2,1)S(1)}, bf16[1024,1024]{1,0:T(8,128)(2,1)}, u32[]{:S(2)}) copy-start(bf16[1024,1024]{1,0:T(8,128)(2,1)} %param.12) | copy-start | bytes 6291460
  1.9 17.4 %collective-permute-start = (bf16[256,1024]{1,0:T(8,128)(2,1)S(1)}, bf16[256,1024]{1,0:T(8,128)(2,1)S(1)}, u32[]{:S(2)}, u32[]{:S(2)}) collective-permute-start(bf16[256,1024]{1,0:T(8,128)(2,1)S(1)} %slice_bitcast_fusion), channel_id=1, source_target_pairs={{0,1},{1,0},{2,3},{3,2},{4,5},{5,4},{6,7},{7,6},{8,9},{9,8},{10,11... | collective-permute-start | bytes 1572872 | tf_op jit(solution)/shard_map/ppermute | solution.py:317
  4.6 9.1 %copy-start.13 = (s32[1,8192]{1,0:T(1,128)S(1)}, s32[1,8192]{1,0:T(1,128)}, u32[]{:S(2)}) copy-start(s32[1,8192]{1,0:T(1,128)} %param.8) | copy-start | bytes 98308
  19.3 39.6 %copy-start.7 = (bf16[256,1024]{1,0:T(8,128)(2,1)}, bf16[256,1024]{1,0:T(8,128)(2,1)S(1)}, u32[]{:S(2)}) copy-start(bf16[256,1024]{1,0:T(8,128)(2,1)S(1)} %collective-permute-done.n1a_ref) | copy-start | bytes 1572868
  19.3 25.0 %all-to-all-start = ((bf16[16,72,256]{2,1,0:T(8,128)(2,1)}), bf16[16,72,256]{2,1,0:T(8,128)(2,1)S(1)}, u32[]{:S(2)}, u32[]{:S(2)}) async-start(bf16[16,72,256]{2,1,0:T(8,128)(2,1)} %bitcast.9), calls=%async_computation | async-start | bytes 1179648 | tf_op jit(solution)/shard_map/all_to_all | solution.py:323
  35.0 5.2 %collective-permute-start.1 = (bf16[64,1024]{1,0:T(8,128)(2,1)}, bf16[64,1024]{1,0:T(8,128)(2,1)S(1)}, u32[]{:S(2)}, u32[]{:S(2)}) collective-permute-start(bf16[64,1024]{1,0:T(8,128)(2,1)} %get-tuple-element.24), channel_id=1, source_target_pairs={{0,1},{1,2},{2,3},{3,0},{4,5},{5,6},{6,7},{7,4},{8,9},{9,10},{10,1... | collective-permute-start | bytes 393224 | tf_op jit(solution)/shard_map/ppermute | solution.py:331
  35.3 7.7 %collective-permute-start.2 = (bf16[64,1024]{1,0:T(8,128)(2,1)}, bf16[64,1024]{1,0:T(8,128)(2,1)S(1)}, u32[]{:S(2)}, u32[]{:S(2)}) collective-permute-start(bf16[64,1024]{1,0:T(8,128)(2,1)} %get-tuple-element.25), channel_id=1, source_target_pairs={{0,2},{1,3},{2,0},{3,1},{4,6},{5,7},{6,4},{7,5},{8,10},{9,11},{10,... | collective-permute-start | bytes 393224 | tf_op jit(solution)/shard_map/ppermute | solution.py:331
  38.0 5.2 %collective-permute-start.3 = (bf16[64,1024]{1,0:T(8,128)(2,1)}, bf16[64,1024]{1,0:T(8,128)(2,1)S(1)}, u32[]{:S(2)}, u32[]{:S(2)}) collective-permute-start(bf16[64,1024]{1,0:T(8,128)(2,1)} %get-tuple-element.26), channel_id=1, source_target_pairs={{0,3},{1,0},{2,1},{3,2},{4,7},{5,4},{6,5},{7,6},{8,11},{9,8},{10,9... | collective-permute-start | bytes 393224 | tf_op jit(solution)/shard_map/ppermute | solution.py:331
  45.3 14.9 %collective-permute-start.8 = (bf16[256,1024]{1,0:T(8,128)(2,1)S(1)}, bf16[256,1024]{1,0:T(8,128)(2,1)S(1)}, u32[]{:S(2)}, u32[]{:S(2)}) collective-permute-start(bf16[256,1024]{1,0:T(8,128)(2,1)S(1)} %slice.13), channel_id=1, source_target_pairs={{0,1},{1,0},{2,3},{3,2},{4,5},{5,4},{6,7},{7,6},{8,9},{9,8},{10,11... | collective-permute-start | bytes 1572872 | tf_op jit(solution)/shard_map/ppermute | solution.py:338
  47.4 21.3 %collective-permute-start.9 = (bf16[512,1024]{1,0:T(8,128)(2,1)}, bf16[512,1024]{1,0:T(8,128)(2,1)S(1)}, u32[]{:S(2)}, u32[]{:S(2)}) collective-permute-start(bf16[512,1024]{1,0:T(8,128)(2,1)} %bitcast.28), channel_id=1, source_target_pairs={{0,64},{64,0},{1,65},{65,1},{2,66},{66,2},{3,67},{67,3},{4,68},{68... | collective-permute-start | bytes 3145736 | tf_op jit(solution)/shard_map/ppermute | solution.py:316
  50.4 18.4 %copy-start.5 = (bf16[512,256]{1,0:T(8,128)(2,1)}, bf16[512,256]{1,0:T(8,128)(2,1)S(1)}, u32[]{:S(2)}) copy-start(bf16[512,256]{1,0:T(8,128)(2,1)S(1)} %shard_map.88.mine_ref) | copy-start | bytes 786436
  50.4 8.5 %collective-permute-start.7 = (bf16[512,256]{1,0:T(8,128)(2,1)S(1)}, bf16[512,256]{1,0:T(8,128)(2,1)S(1)}, u32[]{:S(2)}, u32[]{:S(2)}) collective-permute-start(bf16[512,256]{1,0:T(8,128)(2,1)S(1)} %shard_map.88.mine_ref), channel_id=1, source_target_pairs={{0,67},{1,66},{2,65},{3,64},{64,0},{65,1},{66,2},{67,3},{4,71},{5,... | collective-permute-start | bytes 786440 | tf_op jit(solution)/shard_map/ppermute | solution.py:340
  50.5 9.8 %collective-permute-start.6 = (bf16[512,256]{1,0:T(8,128)(2,1)S(1)}, bf16[512,256]{1,0:T(8,128)(2,1)S(1)}, u32[]{:S(2)}, u32[]{:S(2)}) collective-permute-start(bf16[512,256]{1,0:T(8,128)(2,1)S(1)} %shard_map.88.mine_ref), channel_id=1, source_target_pairs={{64,67},{65,66},{66,65},{67,64},{68,71},{69,70},{70,69},{71,68},{7... | collective-permute-start | bytes 786440 | tf_op jit(solution)/shard_map/ppermute | solution.py:341
  53.7 6.7 %collective-permute-start.4 = (bf16[64,1024]{1,0:T(8,128)(2,1)S(1)}, bf16[64,1024]{1,0:T(8,128)(2,1)S(1)}, u32[]{:S(2)}, u32[]{:S(2)}) collective-permute-start(bf16[64,1024]{1,0:T(8,128)(2,1)S(1)} %add_convert_fusion), channel_id=1, source_target_pairs={{0,4},{4,0},{8,12},{12,8},{16,20},{20,16},{24,28},{28,24},{32,36},... | collective-permute-start | bytes 393224 | tf_op jit(solution)/shard_map/ppermute | solution.py:350
  58.9 9.9 %copy-start.11 = (bf16[512,256]{1,0:T(8,128)(2,1)}, bf16[512,256]{1,0:T(8,128)(2,1)S(1)}, u32[]{:S(2)}) copy-start(bf16[512,256]{1,0:T(8,128)(2,1)S(1)} %collective-permute-done.7.cross_ref) | copy-start | bytes 786436
  58.9 9.9 %collective-permute-start.10 = (bf16[256,1024]{1,0:T(8,128)(2,1)S(1)}, bf16[256,1024]{1,0:T(8,128)(2,1)S(1)}, u32[]{:S(2)}, u32[]{:S(2)}) collective-permute-start(bf16[256,1024]{1,0:T(8,128)(2,1)S(1)} %collective-permute-done.n1a_ref), channel_id=1, source_target_pairs={{0,64},{64,0},{1,65},{65,1},{2,66},{66,2},{3,67},{67,3},{4,68},{68... | collective-permute-start | bytes 1572872 | tf_op jit(solution)/shard_map/ppermute | solution.py:342
  60.3 8.5 %copy-start.12 = (bf16[512,256]{1,0:T(8,128)(2,1)}, bf16[512,256]{1,0:T(8,128)(2,1)S(1)}, u32[]{:S(2)}) copy-start(bf16[512,256]{1,0:T(8,128)(2,1)S(1)} %collective-permute-done.6.third_ref) | copy-start | bytes 786436
  60.3 8.5 %copy-start.8 = (bf16[256,1024]{1,0:T(8,128)(2,1)}, bf16[256,1024]{1,0:T(8,128)(2,1)S(1)}, u32[]{:S(2)}) copy-start(bf16[256,1024]{1,0:T(8,128)(2,1)S(1)} %collective-permute-done.8.n1b_ref) | copy-start | bytes 1572868
  60.3 8.5 %collective-permute-start.11 = (bf16[256,1024]{1,0:T(8,128)(2,1)S(1)}, bf16[256,1024]{1,0:T(8,128)(2,1)S(1)}, u32[]{:S(2)}, u32[]{:S(2)}) collective-permute-start(bf16[256,1024]{1,0:T(8,128)(2,1)S(1)} %collective-permute-done.8.n1b_ref), channel_id=1, source_target_pairs={{0,64},{64,0},{1,65},{65,1},{2,66},{66,2},{3,67},{67,3},{4,68},{68... | collective-permute-start | bytes 1572872 | tf_op jit(solution)/shard_map/ppermute | solution.py:342
  60.4 7.5 %collective-permute-start.5 = (bf16[2,64,1024]{2,1,0:T(8,128)(2,1)S(1)}, bf16[2,64,1024]{2,1,0:T(8,128)(2,1)S(1)}, u32[]{:S(2)}, u32[]{:S(2)}) collective-permute-start(bf16[2,64,1024]{2,1,0:T(8,128)(2,1)S(1)} %get-tuple-element.39), channel_id=1, source_target_pairs={{0,16},{4,20},{8,24},{12,28},{16,0},{20,4},{24,8},{28,12},{32,48},... | collective-permute-start | bytes 786440 | tf_op jit(solution)/shard_map/ppermute | solution.py:351
  68.7 0.8 copy-start.9
  68.8 1.1 copy-start.6
  69.9 0.8 copy-start.10
  76.8 22.6 %copy-start.2 = (bf16[2,512,256]{2,1,0:T(8,128)(2,1)S(1)}, bf16[2,512,256]{2,1,0:T(8,128)(2,1)}, u32[]{:S(2)}) copy-start(bf16[2,512,256]{2,1,0:T(8,128)(2,1)} %get-tuple-element.32.near_ref) | copy-start | bytes 1572868
  76.8 22.5 %collective-permute-start.13 = (bf16[2,2,64,1024]{3,2,1,0:T(8,128)(2,1)}, bf16[2,2,64,1024]{3,2,1,0:T(8,128)(2,1)}, u32[]{:S(2)}, u32[]{:S(2)}) collective-permute-start(bf16[2,2,64,1024]{3,2,1,0:T(8,128)(2,1)} %pad_maximum_fusion.low_ref), channel_id=1, source_target_pairs={{0,48},{4,52},{8,56},{12,60},{16,32},{20,36},{24,40},{28,44},{32,1... | collective-permute-start | bytes 1572872 | tf_op jit(solution)/shard_map/ppermute | solution.py:355
  79.5 19.9 %collective-permute-start.12 = (bf16[2,512,256]{2,1,0:T(8,128)(2,1)}, bf16[2,512,256]{2,1,0:T(8,128)(2,1)S(1)}, u32[]{:S(2)}, u32[]{:S(2)}) collective-permute-start(bf16[2,512,256]{2,1,0:T(8,128)(2,1)} %get-tuple-element.32.near_ref), channel_id=1, source_target_pairs={{0,1},{1,0},{2,3},{3,2},{4,5},{5,4},{6,7},{7,6},{8,9},{9,8},{10,11... | collective-permute-start | bytes 1572872 | tf_op jit(solution)/shard_map/ppermute | solution.py:357
  80.6 26.0 %all-to-all-start.1 = ((bf16[16,256,128]{2,1,0:T(8,128)(2,1)}), bf16[16,256,128]{2,1,0:T(8,128)(2,1)}, u32[]{:S(2)}, u32[]{:S(2)}) async-start(bf16[16,256,128]{2,1,0:T(8,128)(2,1)} %get-tuple-element.33), calls=%async_computation.1 | async-start | bytes 2097152 | tf_op jit(solution)/shard_map/all_to_all | solution.py:354
  102.4 1.0 copy-start.3
  103.4 19.7 %collective-permute-start.14 = (bf16[512,1024]{1,0:T(8,128)(2,1)}, bf16[512,1024]{1,0:T(8,128)(2,1)}, u32[]{:S(2)}, u32[]{:S(2)}) collective-permute-start(bf16[512,1024]{1,0:T(8,128)(2,1)} %get-tuple-element.36), channel_id=1, source_target_pairs={{0,64},{64,0},{1,65},{65,1},{2,66},{66,2},{3,67},{67,3},{4,68},{68... | collective-permute-start | bytes 3145736 | tf_op jit(solution)/shard_map/ppermute | solution.py:367
  108.0 7.2 %collective-permute-start.18 = (bf16[256,128]{1,0:T(8,128)(2,1)S(1)}, bf16[256,128]{1,0:T(8,128)(2,1)S(1)}, u32[]{:S(2)}, u32[]{:S(2)}) collective-permute-start(bf16[256,128]{1,0:T(8,128)(2,1)S(1)} %reduce_sum.22), channel_id=1, source_target_pairs={{0,3},{1,2},{2,67},{3,66},{64,1},{65,0},{66,65},{67,64},{4,7},{5,6... | collective-permute-start | bytes 196616 | tf_op jit(solution)/shard_map/ppermute | solution.py:363
  110.6 5.2 %collective-permute-start.17 = (bf16[256,128]{1,0:T(8,128)(2,1)S(1)}, bf16[256,128]{1,0:T(8,128)(2,1)S(1)}, u32[]{:S(2)}, u32[]{:S(2)}) collective-permute-start(bf16[256,128]{1,0:T(8,128)(2,1)S(1)} %reduce_sum.22), channel_id=1, source_target_pairs={{0,2},{1,3},{2,66},{3,67},{64,0},{65,1},{66,64},{67,65},{4,6},{5,7... | collective-permute-start | bytes 196616 | tf_op jit(solution)/shard_map/ppermute | solution.py:363
  112.0 4.9 %collective-permute-start.16 = (bf16[256,128]{1,0:T(8,128)(2,1)S(1)}, bf16[256,128]{1,0:T(8,128)(2,1)S(1)}, u32[]{:S(2)}, u32[]{:S(2)}) collective-permute-start(bf16[256,128]{1,0:T(8,128)(2,1)S(1)} %reduce_sum.22), channel_id=1, source_target_pairs={{0,1},{1,0},{2,65},{3,64},{64,3},{65,2},{66,67},{67,66},{4,5},{5,4... | collective-permute-start | bytes 196616 | tf_op jit(solution)/shard_map/ppermute | solution.py:363
  112.2 7.1 %collective-permute-start.15 = (bf16[256,128]{1,0:T(8,128)(2,1)S(1)}, bf16[256,128]{1,0:T(8,128)(2,1)S(1)}, u32[]{:S(2)}, u32[]{:S(2)}) collective-permute-start(bf16[256,128]{1,0:T(8,128)(2,1)S(1)} %reduce_sum.22), channel_id=1, source_target_pairs={{0,0},{1,1},{2,64},{3,65},{64,2},{65,3},{66,66},{67,67},{4,4},{5,5... | collective-permute-start | bytes 196616 | tf_op jit(solution)/shard_map/ppermute | solution.py:363
  119.3 1.6 %copy-start.1 = (bf16[1024,1024]{1,0:T(8,128)(2,1)S(1)}, bf16[1024,1024]{1,0:T(8,128)(2,1)}, u32[]{:S(2)}) copy-start(bf16[1024,1024]{1,0:T(8,128)(2,1)} %convolution_convert_fusion.both_ref.w_ref) | copy-start | bytes 6291460
  120.9 2.2 %copy-start.4 = (bf16[512,1024]{1,0:T(8,128)(2,1)S(1)}, bf16[512,1024]{1,0:T(8,128)(2,1)}, u32[]{:S(2)}) copy-start(bf16[512,1024]{1,0:T(8,128)(2,1)} %copy-done.3) | copy-start | bytes 3145732

commit v4 on v3

v4 whole, which is shorter than its diff:
```python
import functools

import jax
import jax.numpy as jnp
from jax import lax
from jax.experimental import pallas as pl
from jax.experimental.pallas import tpu as pltpu
from jax.sharding import PartitionSpec as P

LANES = 128
GROUP = 16
SUB = LANES // GROUP
WIN = 9
SLOT = WIN * SUB
SIDE = 4
CUT = 256
VMEM = 24 * 1024 * 1024
WIDE = 56 * 1024 * 1024


def seg_kernel(idx_ref, starts_ref, owner_ref, bytes_ref, out_ref, next_ref, low_ref, high_ref, acc_ref, turn_ref, row_ref):
    step = pl.program_id(0)
    steps = pl.num_programs(0)
    block = bytes_ref.shape[0]
    shard = block * steps
    owners = LANES // SUB

    @pl.when(step == 0)
    def _():
        starts = starts_ref[...]
        rows = starts.shape[0]
        base = idx_ref[0] * shard
        for k in range(row_ref.shape[0]):
            count = jnp.sum((starts <= base + k * block).astype(jnp.float32)).astype(jnp.int32)
            row_ref[k] = lax.shift_right_logical(count - 1, 7)
        first = jnp.minimum(row_ref[0], rows - WIN)
        for k in range(row_ref.shape[0]):
            row_ref[k] = row_ref[k] - first
        lane = lax.broadcasted_iota(jnp.int32, starts.shape, 1)
        turned = pltpu.roll(starts, LANES - 1, 1)
        below = jnp.concatenate([turned[1:], jnp.full((1, LANES), 2**30, jnp.int32)], axis=0)
        next_ref[...] = jnp.where(lane == LANES - 1, below, turned)
        lane = lax.broadcasted_iota(jnp.int32, (SUB, LANES), 1)
        mine = lax.shift_right_logical(lane, 4) == lax.broadcasted_iota(jnp.int32, (SUB, LANES), 0)
        for t in range(WIN):
            low = jnp.clip(starts_ref[pl.ds(first + t, 1), :] - base, 0, shard).astype(jnp.float32)
            high = jnp.clip(next_ref[pl.ds(first + t, 1), :] - base, 0, shard).astype(jnp.float32)
            low = jnp.broadcast_to(low, (SUB, LANES))
            high = jnp.broadcast_to(high, (SUB, LANES))
            owner = jnp.broadcast_to(owner_ref[pl.ds(first + t, 1), :], (SUB, LANES))
            owner = jnp.where(mine, owner, -1)
            for j in range(owners):
                held = owner == j
                at = t * LANES + j * SUB
                one = jnp.sum(jnp.where(held, low, 0.0), axis=1, keepdims=True)
                low_ref[at : at + SUB, :] = jnp.broadcast_to(one, (SUB, LANES))
                one = jnp.sum(jnp.where(held, high, 0.0), axis=1, keepdims=True)
                high_ref[at : at + SUB, :] = jnp.broadcast_to(one, (SUB, LANES))
        acc_ref[...] = jnp.zeros_like(acc_ref)

    values = bytes_ref[...]

    def one_row(t, carry):
        at = pl.ds(pl.multiple_of(t * LANES, LANES), LANES)
        low = low_ref[at, :]
        high = high_ref[at, :]
        parts = []
        for q in range(block // LANES):
            place = lax.broadcasted_iota(jnp.int32, (1, LANES), 1) + (step * block + q * LANES)
            place = place.astype(jnp.float32)
            parts.append(jnp.where((place >= low) & (place < high), 1.0, 0.0).astype(jnp.bfloat16))
        onehot = jnp.concatenate(parts, axis=1)
        acc_ref[at, :] += jnp.dot(onehot, values, preferred_element_type=jnp.float32)
        return carry

    lax.fori_loop(row_ref[step], jnp.minimum(row_ref[step + 1], WIN - 1) + 1, one_row, 0)

    @pl.when(step == steps - 1)
    def _():
        for t in range(WIN):
            for j in range(owners):
                turn_ref[j * SLOT + t * SUB : j * SLOT + (t + 1) * SUB, :] = acc_ref[
                    t * LANES + j * SUB : t * LANES + (j + 1) * SUB, :
                ]
        out_ref[...] = turn_ref[...].astype(jnp.bfloat16)


def segment_sums(idx, starts, owner, grads, owners, width, interpret=False):
    bytes_n = grads.shape[0]
    block = 512
    rows = owners * SLOT
    whole = pl.BlockSpec(starts.shape, lambda i, idx: (0, 0))
    return pl.pallas_call(
        seg_kernel,
        grid_spec=pltpu.PrefetchScalarGridSpec(
            num_scalar_prefetch=1,
            grid=(bytes_n // block,),
            in_specs=[whole, whole, pl.BlockSpec((block, width), lambda i, idx: (i, idx[1]))],
            out_specs=pl.BlockSpec((rows, width), lambda i, idx: (0, 0)),
            scratch_shapes=[
                pltpu.VMEM(starts.shape, jnp.int32),
                pltpu.VMEM((rows, LANES), jnp.float32),
                pltpu.VMEM((rows, LANES), jnp.float32),
                pltpu.VMEM((rows, width), jnp.float32),
                pltpu.VMEM((rows, width), jnp.float32),
                pltpu.SMEM((bytes_n // block + 1,), jnp.int32),
            ],
        ),
        out_shape=jax.ShapeDtypeStruct((rows, width), jnp.bfloat16),
        compiler_params=pltpu.CompilerParams(vmem_limit_bytes=WIDE),
        interpret=interpret,
    )(idx, starts, owner, grads)


def collect_kernel(first_ref, in_ref, out_ref, wide_ref, acc_ref):
    wide_ref[...] = in_ref[...].astype(jnp.float32)
    acc_ref[...] = jnp.zeros_like(acc_ref)
    for s in range(in_ref.shape[0] // SLOT):
        at = pl.ds(pl.multiple_of(first_ref[s] * SUB, SUB), SLOT)
        acc_ref[at, :] += wide_ref[s * SLOT : (s + 1) * SLOT, :]
    out_ref[...] = acc_ref[...].T.astype(jnp.bfloat16)


def collect(first, incoming, patch_rows, interpret=False):
    rows, width = incoming.shape
    return pl.pallas_call(
        collect_kernel,
        in_specs=[pl.BlockSpec(memory_space=pltpu.SMEM), pl.BlockSpec(memory_space=pltpu.VMEM)],
        out_specs=pl.BlockSpec(memory_space=pltpu.VMEM),
        out_shape=jax.ShapeDtypeStruct((width, patch_rows), jnp.bfloat16),
        scratch_shapes=[pltpu.VMEM((rows, width), jnp.float32), pltpu.VMEM((patch_rows, width), jnp.float32)],
        compiler_params=pltpu.CompilerParams(vmem_limit_bytes=VMEM),
        interpret=interpret,
    )(first, incoming)


def outer_kernel(idx_ref, mine_ref, third_ref, cross_ref, n0_ref, n1a_ref, n1b_ref, f0_ref, f1a_ref, f1b_ref, out_ref, both_ref):
    step = pl.program_id(0)

    @pl.when(step == 0)
    def _():
        both_ref[0] = jnp.where(idx_ref[0] == 0, mine_ref[...], third_ref[...])
        both_ref[1] = cross_ref[...]

    low = lax.rem(idx_ref[1], 2)
    blocks = out_ref.shape[0] // 2
    per = n0_ref.shape[1] // LANES
    near1 = jnp.concatenate([n1a_ref[...], n1b_ref[...]], axis=0)
    far1 = jnp.concatenate([f1a_ref[...], f1b_ref[...]], axis=0)
    for near, far, which in ((n0_ref[...], f0_ref[...], low), (near1, far1, 1 - low)):
        total = jnp.dot(both_ref[0], near, preferred_element_type=jnp.float32)
        total += jnp.dot(both_ref[1], far, preferred_element_type=jnp.float32)
        total = total.astype(jnp.bfloat16)
        for i in range(per):
            out_ref[which * blocks + step * per + i] = total[:, i * LANES : (i + 1) * LANES]


def outer(idx, sums, columns):
    width, rows = sums[0].shape
    cols = columns[0].shape[1]
    block = 256
    whole = pl.BlockSpec((width, rows), lambda i, idx: (0, 0))
    shape = (2 * cols // LANES, width, LANES)
    return pl.pallas_call(
        outer_kernel,
        grid_spec=pltpu.PrefetchScalarGridSpec(
            num_scalar_prefetch=1,
            grid=(cols // block,),
            in_specs=[whole] * len(sums)
            + [pl.BlockSpec((c.shape[0], block), lambda i, idx: (0, i)) for c in columns],
            out_specs=[
                pl.BlockSpec(shape, lambda i, idx: (0, 0, 0)),
                pl.BlockSpec((2, width, rows), lambda i, idx: (0, 0, 0)),
            ],
        ),
        out_shape=[
            jax.ShapeDtypeStruct(shape, jnp.bfloat16),
            jax.ShapeDtypeStruct((2, width, rows), jnp.bfloat16),
        ],
        compiler_params=pltpu.CompilerParams(vmem_limit_bytes=VMEM),
    )(idx, *sums, *columns)


def chain_kernel(idx_ref, value_ref, out_w_ref, g0_ref, g1_ref, g2_ref, g3_ref, both_ref, p0_ref, p1_ref, p2_ref, p3_ref):
    step = pl.program_id(0)
    rows = value_ref.shape[0]
    at = pl.ds(pl.multiple_of(step * rows, rows), rows)
    both_ref[at, :] = jnp.dot(
        value_ref[...], out_w_ref[...], preferred_element_type=jnp.float32
    ).astype(jnp.bfloat16)

    @pl.when(step == pl.num_programs(0) - 1)
    def _():
        wide = p0_ref.shape[1]
        for s, (g, p) in enumerate(((g0_ref, p0_ref), (g1_ref, p1_ref), (g2_ref, p2_ref), (g3_ref, p3_ref))):
            half = lax.div(lax.rem(idx_ref[2] + s, 4), 2)
            half = idx_ref[0] + half - 2 * idx_ref[0] * half
            cols = pl.ds(pl.multiple_of(half * wide, wide), wide)
            p[...] = jnp.dot(g[...], both_ref[:, cols], preferred_element_type=jnp.float32).astype(jnp.bfloat16)


def chain_terms(idx, w_value, w_out, w_global, parts):
    deep, feats = w_value.shape
    rows = w_global.shape[0] // parts // 4
    block = deep // 4

    def rows_of(s):
        return lambda i, idx: (lax.rem(idx[2] + s, parts) * 4 + idx[1], 0)

    return pl.pallas_call(
        chain_kernel,
        grid_spec=pltpu.PrefetchScalarGridSpec(
            num_scalar_prefetch=1,
            grid=(deep // block,),
            in_specs=[
                pl.BlockSpec((block, w_value.shape[1]), lambda i, idx: (i, 0)),
                pl.BlockSpec(w_out.shape, lambda i, idx: (0, 0)),
            ]
            + [pl.BlockSpec((rows, deep), rows_of(s)) for s in range(parts)],
            out_specs=[pl.BlockSpec((deep, feats), lambda i, idx: (0, 0))]
            + [pl.BlockSpec((rows, feats // 2), lambda i, idx: (0, 0))] * parts,
        ),
        out_shape=[jax.ShapeDtypeStruct((deep, feats), jnp.bfloat16)]
        + [jax.ShapeDtypeStruct((rows, feats // 2), jnp.bfloat16)] * parts,
        compiler_params=pltpu.CompilerParams(vmem_limit_bytes=WIDE),
    )(idx, w_value, w_out, w_global, w_global, w_global, w_global)


def rows_kernel(which, idx_ref, near_ref, far_ref, low_ref, high_ref, *rest):
    out_ref = rest[-1]
    deep = near_ref.shape[1]
    odd = lax.rem(idx_ref[2] + idx_ref[0], 2)
    near = near_ref[which].T
    far = far_ref[which].T
    rows = low_ref.shape[1]
    for i, ref in enumerate((low_ref, high_ref)):
        for j in range(2):
            z, y = lax.div(idx_ref[1], 2), lax.rem(idx_ref[1], 2)
            at = 2 * (z + i - 2 * i * z) + y + j - 2 * j * y
            at = pl.ds(pl.multiple_of(at * rows, rows), rows)
            first = ref[j, :, pl.ds(pl.multiple_of(odd * deep, deep), deep)]
            second = ref[j, :, pl.ds(pl.multiple_of((1 - odd) * deep, deep), deep)]
            dims = (((1,), (1,)), ((), ()))
            total = lax.dot_general(near, first, dims, preferred_element_type=jnp.float32)
            total += lax.dot_general(far, second, dims, preferred_element_type=jnp.float32)
            if len(rest) > 1:
                total += rest[0][:, at].astype(jnp.float32)
            out_ref[:, at] = total.astype(jnp.bfloat16)


def context_rows(which, idx, near, far, low, high, *back):
    vmem = pl.BlockSpec(memory_space=pltpu.VMEM)
    return pl.pallas_call(
        functools.partial(rows_kernel, which),
        in_specs=[pl.BlockSpec(memory_space=pltpu.SMEM)] + [vmem] * (4 + len(back)),
        out_specs=vmem,
        out_shape=jax.ShapeDtypeStruct((near.shape[2], 4 * low.shape[1]), jnp.bfloat16),
        compiler_params=pltpu.CompilerParams(vmem_limit_bytes=VMEM),
    )(idx, near, far, low, high, *back)


def last_kernel(feat_ref, a_ref, b_ref, c_ref, d_ref, w_ref, out_ref):
    width = a_ref.shape[0]
    total = jnp.zeros(out_ref.shape, jnp.float32)
    for s, ref in enumerate((a_ref, b_ref, c_ref, d_ref)):
        at = pl.ds(pl.multiple_of(feat_ref[s] * width, width), width)
        total += lax.dot_general(
            ref[...].T, w_ref[:, at], (((1,), (1,)), ((), ())), preferred_element_type=jnp.float32
        )
    out_ref[...] = total


def last(feats, pieces, weights):
    cols, deep = weights.shape
    block = 256
    whole = pl.BlockSpec(pieces[0].shape, lambda i, feats: (0, 0))
    return pl.pallas_call(
        last_kernel,
        grid_spec=pltpu.PrefetchScalarGridSpec(
            num_scalar_prefetch=1,
            grid=(cols // block,),
            in_specs=[whole] * len(pieces) + [pl.BlockSpec((block, deep), lambda i, feats: (i, 0))],
            out_specs=pl.BlockSpec((pieces[0].shape[1], block), lambda i, feats: (0, i)),
        ),
        out_shape=jax.ShapeDtypeStruct((pieces[0].shape[1], cols), jnp.float32),
        compiler_params=pltpu.CompilerParams(vmem_limit_bytes=VMEM),
    )(feats, *pieces, weights)


def after(value, *others):
    return lax.optimization_barrier((value, *others))[0]


def local(byte_grads, patch_starts, patch_owner, attn_context, w_global, w_value, w_out):
    dp_n, ctx_n, ten_n = (lax.axis_size(a) for a in ("dp", "context", "tensor"))
    dp = lax.axis_index("dp")
    ctx = lax.axis_index("context")
    ten = lax.axis_index("tensor")
    f32, bf16 = jnp.float32, jnp.bfloat16
    bytes_n, feats = byte_grads.shape[1:]
    width = feats // ten_n
    patch_rows = attn_context.shape[1]
    starts = patch_starts.reshape(-1, LANES)
    owner = patch_owner.reshape(-1, LANES)
    line = ("dp", "tensor")

    def moves(target):
        pairs = []
        for d in range(dp_n):
            for x in range(ten_n):
                to = target(d, x)
                if to is not None:
                    pairs.append((d * ten_n + x, to[0] * ten_n + to[1]))
        return pairs

    swap = [(i, dp_n - 1 - i) for i in range(dp_n)]
    pair = [(x, x ^ 1) for x in range(ten_n)]
    near0 = attn_context[0]
    far0 = lax.ppermute(near0, "dp", swap)
    near1 = [lax.ppermute(near0[:CUT], "tensor", pair)]

    outgoing = segment_sums(jnp.stack([ctx, ten]), starts, owner, byte_grads[0], ctx_n, width)

    here = jnp.stack([dp, 2 * (ctx // SIDE % 2) + ctx % 2, ten])
    both_t, *terms = chain_terms(after(here, outgoing), w_value, w_out, w_global, ten_n)
    outgoing = after(outgoing, near1[0], both_t)
    incoming = lax.all_to_all(outgoing, "context", split_axis=0, concat_axis=0, tiled=True)

    chain = terms[0].astype(f32)
    for s in range(1, ten_n):
        term = after(terms[s], outgoing)
        chain += lax.ppermute(term, "tensor", [(x, (x + s) % ten_n) for x in range(ten_n)]).astype(f32)
    chain = chain.astype(bf16)
    edges = jnp.arange(ctx_n, dtype=jnp.int32) * bytes_n
    counts = jnp.sum((patch_starts[0][None, :] <= edges[:, None]).astype(jnp.int32), axis=1)
    first = jnp.minimum((counts - 1) // LANES, starts.shape[0] - WIN)
    incoming = after(incoming, first, chain)

    near1.append(lax.ppermute(after(near0, incoming)[CUT:], "tensor", pair))
    sums = collect(first, incoming, patch_rows)
    cross = lax.ppermute(sums, line, moves(lambda d, x: (0, x) if d == 1 else (1, ten_n - 1 - x)))
    third = lax.ppermute(sums, line, moves(lambda d, x: (1, ten_n - 1 - x) if d == 1 else None))

    def along(target):
        return [
            (i * SIDE + j, target(i, j)[0] * SIDE + target(i, j)[1]) for i in range(SIDE) for j in range(SIDE)
        ]

    chain = after(chain, sums)
    chain = jnp.stack([chain, lax.ppermute(chain, "context", along(lambda i, j: (i, j ^ 1)))])
    far1 = [lax.ppermute(part, "dp", swap) for part in (near1[0], after(near1[1], cross, third, chain))]
    columns = (near0, *near1, far0, *far1)
    partial, near = outer(jnp.stack([dp, ten]), (sums, third, cross), columns)
    pieces = lax.all_to_all(partial, "context", split_axis=0, concat_axis=0, tiled=True)
    rest = lax.ppermute(after(chain, partial), "context", along(lambda i, j: (i ^ 1, j)))

    far = lax.ppermute(near, "tensor", pair)
    give = context_rows(1, here, near, far, chain, rest)
    pieces = after(pieces, give)
    piece = jnp.sum(pieces.astype(f32), axis=0).astype(bf16)
    parts, blocks = [], []
    for s in range(ten_n):
        parts.append(lax.ppermute(piece, line, moves(lambda d, x, s=s: (x // 2, (2 * d + x % 2) ^ s))))
        source = ten ^ s
        pick = 2 * dp + source % 2
        blocks.append(jnp.where(source < 2, pick, ten_n - 1 - pick))
    back = lax.ppermute(give, "dp", swap)
    context_grad = context_rows(0, here, near, far, chain, rest, back)
    weight_grad = last(jnp.stack(blocks), parts, both_t)
    return (context_grad[None], weight_grad)


def solution(mesh):
    placed = (
        P("dp", "context", None),
        P("dp", None),
        P("dp", None),
        P("dp", "context", "tensor"),
        P(None, "tensor"),
        P("tensor", None),
        P(),
    )
    return jax.shard_map(
        local,
        mesh=mesh,
        in_specs=placed,
        out_specs=(P("dp", "context", "tensor"), P(("dp", "context"), "tensor")),
        check_vma=False,
    )
```

time: 127 us -> 113 us (0.89)
  local copies, waits for them, and re-layouts: 6.83 us -> 1.13 us
  matrix products: 5.27 us -> 0 us
  other arithmetic: 5.48 us -> 4.18 us
    dot_general x1 -> x0, matrix products: 5.27 us -> none  [local(): jnp.dot(after(w_value, outgoing), w_out, preferred_element_type=f32)]
    unnamed x28 -> x8, local copies, waits for them, and re-layouts: 4.53 us -> 0.02 us
    ppermute x1, waiting for transfers between devices: 0.01 us -> 3.13 us  [local(): lax.ppermute(chain, 'context', along(lambda i, j: (i, j ^ 1)))]
    ppermute x1, waiting for transfers between devices: 3.74 us -> 0.68 us  [local(): lax.ppermute(sums, line, moves(lambda d, x: (0, x) if d == 1 else (1, ten...]
    ppermute x5 -> x4, starting transfers between devices: 8.63 us -> 5.78 us  [the longest x3 4.6 us: local(): lax.ppermute(term, 'tensor', [(x, (x + s) % ten_n) for x in range(ten_n)])]
    ppermute x5 -> x4, waiting for transfers between devices: 23.4 us -> 21.1 us  [the longest x1 11 us: local(): lax.ppermute(after(chain, partial), 'context', along(lambda i, j: (i ^ 1,...]
    pallas_call x1, Pallas kernels: 6.16 us -> 4.04 us  [outer(): pl.pallas_call(outer_kernel, grid_spec=pltpu.PrefetchScalarGridSpec(num_s...]
    pallas_call x1, Pallas kernels: 7.38 us -> 9.39 us  [chain_terms(): pl.pallas_call(chain_kernel, grid_spec=pltpu.PrefetchScalarGridSpec(num_s...]
  transfers between devices with their start and end apart: 21 -> 20, of which waited for: 10 -> 11; matrix products, arithmetic and copies ran while one was open for 9% -> 4% of each run, Pallas kernels for 18% -> 21%
where the time goes in v4:
time: 113 us; the launch traced here: 112 us
  starting transfers between devices  42.4 us (38%)
  waiting for transfers between devices  32.4 us (29%)
  Pallas kernels  31.5 us (28%)
  other arithmetic  4.18 us (4%)
    ppermute x1, waiting for transfers between devices, local(): lax.ppermute(after(chain, partial), 'context', along(lambda i, j: (i ^ 1,...  11 us
    ppermute x3, waiting for transfers between devices, local(): lax.ppermute(term, 'tensor', [(x, (x + s) % ten_n) for x in range(ten_n)])  10.1 us
    pallas_call x1, Pallas kernels, chain_terms(): pl.pallas_call(chain_kernel, grid_spec=pltpu.PrefetchScalarGridSpec(num_s...  9.39 us
    pallas_call x1, Pallas kernels, segment_sums(): pl.pallas_call(seg_kernel, grid_spec=pltpu.PrefetchScalarGridSpec(num_sca...  8 us
    all_to_all x1, starting transfers between devices, local(): lax.all_to_all(outgoing, 'context', split_axis=0, concat_axis=0, tiled=True)  7.85 us
    ppermute x4, starting transfers between devices, local(): lax.ppermute(piece, line, moves(lambda d, x, s=s: (x // 2, 2 * d + x % 2...  6.54 us
    pallas_call x2, Pallas kernels, context_rows(): pl.pallas_call(functools.partial(rows_kernel, which), in_specs=[pl.BlockS...  6.38 us
    all_to_all x1, starting transfers between devices, local(): lax.all_to_all(partial, 'context', split_axis=0, concat_axis=0, tiled=True)  6.24 us
  transfers between devices with their start and end apart: 20, of which 11 were waited for; matrix products, arithmetic and copies ran while one was open for 4% of the time, Pallas kernels for 21%

profile of v4, /device:TPU:1, one launch (start us, length us, event | category | flops | bytes accessed | tf_op | source)
XLA Modules:
  0.0 112.4 jit_solution(1575890479934688434)
XLA Ops:
  0.6 1.1 slice_bitcast_fusion
  1.7 2.1 %collective-permute-start = (bf16[256,1024]{1,0:T(8,128)(2,1)S(1)}, bf16[256,1024]{1,0:T(8,128)(2,1)S(1)}, u32[]{:S(2)}, u32[]{:S(2)}) collective-permute-start(bf16[256,1024]{1,0:T(8,128)(2,1)S(1)} %slice_bitcast_fusion), channel_id=1, source_target_pairs={{0,1},{1,0},{2,3},{3,2},{4,5},{5,4},{6,7},{7,6},{8,9},{9,8},{10,11... | collective-permute-start | bytes 1572872 | tf_op jit(solution)/shard_map/ppermute | solution.py:320
  3.8 0.6 pad_add_fusion.2.idx_ref
  4.5 8.0 %shard_map.86 = bf16[1152,256]{1,0:T(8,128)(2,1)} custom-call(s32[2]{0:T(128)} %pad_add_fusion.2.idx_ref, s32[64,128]{1,0:T(8,128)} %bitcast.28, s32[64,128]{1,0:T(8,128)} %bitcast.30, bf16[4096,1024]{1,0:T(8,128)(2,1)} %bitcast.24), custom_call_target="tpu_custom_call" | custom-call | tf_op jit(solution)/shard_map/pallas_call | solution.py:93
  12.5 0.6 pad_add_fusion.idx_ref
  13.1 9.4 %shard_map.87 = (bf16[1024,1024]{1,0:T(8,128)(2,1)}, bf16[256,512]{1,0:T(8,128)(2,1)}, bf16[256,512]{1,0:T(8,128)(2,1)}, bf16[256,512]{1,0:T(8,128)(2,1)}, bf16[256,512]{1,0:T(8,128)(2,1)}) custom-call(s32[3]{0:T(128)} %pad_add_fusion.idx_ref, bf16[1024,1024]{1,0:T(8,128)(2,1)} %value_ref.1, bf16[1024,1024]{1,0:T(8,128)(2,1)} %out_w_ref.1, ...), custom_call_target="tpu_custom_call" | custom-call | tf_op jit(solution)/shard_map/pallas_call | solution.py:210
  22.5 7.9 %all-to-all-start = ((bf16[16,72,256]{2,1,0:T(8,128)(2,1)}), bf16[16,72,256]{2,1,0:T(8,128)(2,1)S(1)}, u32[]{:S(2)}, u32[]{:S(2)}) async-start(bf16[16,72,256]{2,1,0:T(8,128)(2,1)} %bitcast.9), calls=%async_computation | async-start | bytes 1179648 | tf_op jit(solution)/shard_map/all_to_all | solution.py:327
  30.3 0.3 collective-permute-start.1
  30.7 2.7 %collective-permute-start.2 = (bf16[256,512]{1,0:T(8,128)(2,1)}, bf16[256,512]{1,0:T(8,128)(2,1)S(1)}, u32[]{:S(2)}, u32[]{:S(2)}) collective-permute-start(bf16[256,512]{1,0:T(8,128)(2,1)} %get-tuple-element.27), channel_id=1, source_target_pairs={{0,2},{1,3},{2,0},{3,1},{4,6},{5,7},{6,4},{7,5},{8,10},{9,11},{10,... | collective-permute-start | bytes 786440 | tf_op jit(solution)/shard_map/ppermute | solution.py:332
  33.4 1.5 %collective-permute-start.3 = (bf16[256,512]{1,0:T(8,128)(2,1)}, bf16[256,512]{1,0:T(8,128)(2,1)S(1)}, u32[]{:S(2)}, u32[]{:S(2)}) collective-permute-start(bf16[256,512]{1,0:T(8,128)(2,1)} %get-tuple-element.29), channel_id=1, source_target_pairs={{0,3},{1,0},{2,1},{3,2},{4,7},{5,4},{6,5},{7,6},{8,11},{9,8},{10,9... | collective-permute-start | bytes 786440 | tf_op jit(solution)/shard_map/ppermute | solution.py:332
  34.9 0.3 convert_reduce_fusion
  35.2 3.2 %collective-permute-done.1 = bf16[256,512]{1,0:T(8,128)(2,1)S(1)} collective-permute-done((bf16[256,512]{1,0:T(8,128)(2,1)}, bf16[256,512]{1,0:T(8,128)(2,1)S(1)}, u32[]{:S(2)}, u32[]{:S(2)}) %collective-permute-start.1) | collective-permute-done | bytes 262176 | tf_op jit(solution)/shard_map/ppermute | solution.py:332
  38.4 6.0 %collective-permute-done.2 = bf16[256,512]{1,0:T(8,128)(2,1)S(1)} collective-permute-done((bf16[256,512]{1,0:T(8,128)(2,1)}, bf16[256,512]{1,0:T(8,128)(2,1)S(1)}, u32[]{:S(2)}, u32[]{:S(2)}) %collective-permute-start.2) | collective-permute-done | bytes 262176 | tf_op jit(solution)/shard_map/ppermute | solution.py:332
  44.3 1.0 collective-permute-done.3
  45.3 1.1 add_convert_fusion
  46.4 2.0 %collective-permute-start.6 = (bf16[256,1024]{1,0:T(8,128)(2,1)S(1)}, bf16[256,1024]{1,0:T(8,128)(2,1)S(1)}, u32[]{:S(2)}, u32[]{:S(2)}) collective-permute-start(bf16[256,1024]{1,0:T(8,128)(2,1)S(1)} %slice.11), channel_id=1, source_target_pairs={{0,1},{1,0},{2,3},{3,2},{4,5},{5,4},{6,7},{7,6},{8,9},{9,8},{10,11... | collective-permute-start | bytes 1572872 | tf_op jit(solution)/shard_map/ppermute | solution.py:339
  48.5 1.2 %collective-permute-start.7 = (bf16[512,1024]{1,0:T(8,128)(2,1)S(1)}, bf16[512,1024]{1,0:T(8,128)(2,1)S(1)}, u32[]{:S(2)}, u32[]{:S(2)}) collective-permute-start(bf16[512,1024]{1,0:T(8,128)(2,1)S(1)} %bitcast.21), channel_id=1, source_target_pairs={{0,64},{64,0},{1,65},{65,1},{2,66},{66,2},{3,67},{67,3},{4,68},{68... | collective-permute-start | bytes 3145736 | tf_op jit(solution)/shard_map/ppermute | solution.py:319
  49.7 0.9 shard_map.88.mine_ref
  50.6 1.4 %collective-permute-start.9 = (bf16[256,512]{1,0:T(8,128)(2,1)S(1)}, bf16[256,512]{1,0:T(8,128)(2,1)S(1)}, u32[]{:S(2)}, u32[]{:S(2)}) collective-permute-start(bf16[256,512]{1,0:T(8,128)(2,1)S(1)} %add_convert_fusion), channel_id=1, source_target_pairs={{0,4},{4,0},{8,12},{12,8},{16,20},{20,16},{24,28},{28,24},{32,36},... | collective-permute-start | bytes 786440 | tf_op jit(solution)/shard_map/ppermute | solution.py:350
  52.0 0.3 collective-permute-start.5
  52.3 3.2 %collective-permute-start.4 = (bf16[256,512]{1,0:T(8,128)(2,1)S(1)}, bf16[256,512]{1,0:T(8,128)(2,1)S(1)}, u32[]{:S(2)}, u32[]{:S(2)}) collective-permute-start(bf16[256,512]{1,0:T(8,128)(2,1)S(1)} %shard_map.88.mine_ref), channel_id=1, source_target_pairs={{64,67},{65,66},{66,65},{67,64},{68,71},{69,70},{70,69},{71,68},{7... | collective-permute-start | bytes 786440 | tf_op jit(solution)/shard_map/ppermute | solution.py:342
  55.5 3.1 %collective-permute-done.9 = bf16[256,512]{1,0:T(8,128)(2,1)S(1)} collective-permute-done((bf16[256,512]{1,0:T(8,128)(2,1)S(1)}, bf16[256,512]{1,0:T(8,128)(2,1)S(1)}, u32[]{:S(2)}, u32[]{:S(2)}) %collective-permute-start.9) | collective-permute-done | bytes 262176 | tf_op jit(solution)/shard_map/ppermute | solution.py:350
  58.6 0.8 collective-permute-start.8
  59.4 0.1 pad_maximum_fusion.low_ref
  59.5 0.7 collective-permute-done.5.cross_ref
  60.1 1.7 %collective-permute-done.4.third_ref = bf16[256,512]{1,0:T(8,128)(2,1)S(1)} collective-permute-done((bf16[256,512]{1,0:T(8,128)(2,1)S(1)}, bf16[256,512]{1,0:T(8,128)(2,1)S(1)}, u32[]{:S(2)}, u32[]{:S(2)}) %collective-permute-start.4) | collective-permute-done | bytes 262176 | tf_op jit(solution)/shard_map/ppermute | solution.py:342
  61.8 0.0 collective-permute-done.6.n1b_ref
  61.8 0.1 pad_add_fusion.1.idx_ref
  61.9 0.0 collective-permute-done.8.f1a_ref
  61.9 1.8 %collective-permute-done.10.f1b_ref = bf16[256,1024]{1,0:T(8,128)(2,1)S(1)} collective-permute-done((bf16[256,1024]{1,0:T(8,128)(2,1)S(1)}, bf16[256,1024]{1,0:T(8,128)(2,1)S(1)}, u32[]{:S(2)}, u32[]{:S(2)}) %collective-permute-start.10) | collective-permute-done | bytes 524320 | tf_op jit(solution)/shard_map/ppermute | solution.py:351
  63.7 4.0 %shard_map.89 = (bf16[16,256,128]{2,1,0:T(8,128)(2,1)}, bf16[2,256,512]{2,1,0:T(8,128)(2,1)S(1)}) custom-call(s32[2]{0:T(128)S(1)} %pad_add_fusion.1.idx_ref, bf16[256,512]{1,0:T(8,128)(2,1)S(1)} %shard_map.88.mine_ref, bf16[256,512]{1,0:T(8,128)(2,1)S(1)} %collective-permute-done.4.third_ref, bf16[256,512]{1,0:T(8,128)(2,1)S(1)} %collective-permute-done.5.cross_ref, ...), custom_call_target="tpu_custom_call" | custom-call | tf_op jit(solution)/shard_map/pallas_call | solution.py:164
  67.7 1.2 %collective-permute-start.12 = (bf16[2,256,512]{2,1,0:T(8,128)(2,1)S(1)}, bf16[2,256,512]{2,1,0:T(8,128)(2,1)}, u32[]{:S(2)}, u32[]{:S(2)}) collective-permute-start(bf16[2,256,512]{2,1,0:T(8,128)(2,1)S(1)} %pad_maximum_fusion.low_ref), channel_id=1, source_target_pairs={{0,16},{4,20},{8,24},{12,28},{16,0},{20,4},{24,8},{28,12},{32,48},... | collective-permute-start | bytes 1572872 | tf_op jit(solution)/shard_map/ppermute | solution.py:355
  68.9 0.8 collective-permute-start.11
  69.7 6.2 %all-to-all-start.1 = ((bf16[16,256,128]{2,1,0:T(8,128)(2,1)}), bf16[16,256,128]{2,1,0:T(8,128)(2,1)}, u32[]{:S(2)}, u32[]{:S(2)}) async-start(bf16[16,256,128]{2,1,0:T(8,128)(2,1)} %get-tuple-element.35), calls=%async_computation.1 | async-start | bytes 2097152 | tf_op jit(solution)/shard_map/all_to_all | solution.py:354
  76.0 11.0 %collective-permute-done.12.high_ref = bf16[2,256,512]{2,1,0:T(8,128)(2,1)} collective-permute-done((bf16[2,256,512]{2,1,0:T(8,128)(2,1)S(1)}, bf16[2,256,512]{2,1,0:T(8,128)(2,1)}, u32[]{:S(2)}, u32[]{:S(2)}) %collective-permute-start.12) | collective-permute-done | bytes 524320 | tf_op jit(solution)/shard_map/ppermute | solution.py:355
  87.0 3.0 %shard_map.90 = bf16[512,1024]{1,0:T(8,128)(2,1)} custom-call(s32[3]{0:T(128)S(1)} %copy-done.2, bf16[2,256,512]{2,1,0:T(8,128)(2,1)S(1)} %get-tuple-element.34.near_ref, bf16[2,256,512]{2,1,0:T(8,128)(2,1)} %collective-permute-done.11.far_ref, bf16[2,256,512]{2,1,0:T(8,128)(2,1)S(1)} %pad_maximum_fusion.low_ref, ...), custom_call_target="tpu_custom_call" | custom-call | tf_op jit(solution)/shard_map/pallas_call | solution.py:253
  90.0 4.2 %collective-permute-start.13 = (bf16[512,1024]{1,0:T(8,128)(2,1)}, bf16[512,1024]{1,0:T(8,128)(2,1)}, u32[]{:S(2)}, u32[]{:S(2)}) collective-permute-start(bf16[512,1024]{1,0:T(8,128)(2,1)} %shard_map.90), channel_id=1, source_target_pairs={{0,64},{64,0},{1,65},{65,1},{2,66},{66,2},{3,67},{67,3},{4,68},{68... | collective-permute-start | bytes 3145736 | tf_op jit(solution)/shard_map/ppermute | solution.py:367
  94.2 0.4 all-to-all-done.1
  94.6 1.4 %reduce_sum.22 = bf16[256,128]{1,0:T(8,128)(2,1)S(1)} reduce(bf16[16,256,128]{2,1,0:T(8,128)(2,1)} %all-to-all-done.1, bf16[]{:T(256)} %constant.85.clone.1), dimensions={0}, to_apply=%region_1.2 | reduce | flops 491520 | bytes 1114114 | tf_op jit(solution)/shard_map/reduce_sum | solution.py:360
  96.0 1.7 %collective-permute-start.17 = (bf16[256,128]{1,0:T(8,128)(2,1)S(1)}, bf16[256,128]{1,0:T(8,128)(2,1)S(1)}, u32[]{:S(2)}, u32[]{:S(2)}) collective-permute-start(bf16[256,128]{1,0:T(8,128)(2,1)S(1)} %reduce_sum.22), channel_id=1, source_target_pairs={{0,3},{1,2},{2,67},{3,66},{64,1},{65,0},{66,65},{67,64},{4,7},{5,6... | collective-permute-start | bytes 196616 | tf_op jit(solution)/shard_map/ppermute | solution.py:363
  97.7 1.4 %collective-permute-start.16 = (bf16[256,128]{1,0:T(8,128)(2,1)S(1)}, bf16[256,128]{1,0:T(8,128)(2,1)S(1)}, u32[]{:S(2)}, u32[]{:S(2)}) collective-permute-start(bf16[256,128]{1,0:T(8,128)(2,1)S(1)} %reduce_sum.22), channel_id=1, source_target_pairs={{0,2},{1,3},{2,66},{3,67},{64,0},{65,1},{66,64},{67,65},{4,6},{5,7... | collective-permute-start | bytes 196616 | tf_op jit(solution)/shard_map/ppermute | solution.py:363
  99.0 0.1 collective-permute-start.15
  99.1 3.4 %collective-permute-start.14 = (bf16[256,128]{1,0:T(8,128)(2,1)S(1)}, bf16[256,128]{1,0:T(8,128)(2,1)S(1)}, u32[]{:S(2)}, u32[]{:S(2)}) collective-permute-start(bf16[256,128]{1,0:T(8,128)(2,1)S(1)} %reduce_sum.22), channel_id=1, source_target_pairs={{0,0},{1,1},{2,64},{3,65},{64,2},{65,3},{66,66},{67,67},{4,4},{5,5... | collective-permute-start | bytes 196616 | tf_op jit(solution)/shard_map/ppermute | solution.py:363
  102.5 0.1 pad_add_fusion.3.feat_ref
  102.6 1.4 %collective-permute-done.15.b_ref = bf16[256,128]{1,0:T(8,128)(2,1)S(1)} collective-permute-done((bf16[256,128]{1,0:T(8,128)(2,1)S(1)}, bf16[256,128]{1,0:T(8,128)(2,1)S(1)}, u32[]{:S(2)}, u32[]{:S(2)}) %collective-permute-start.15) | collective-permute-done | bytes 65568 | tf_op jit(solution)/shard_map/ppermute | solution.py:363
  104.0 2.2 %collective-permute-done.14.a_ref = bf16[256,128]{1,0:T(8,128)(2,1)S(1)} collective-permute-done((bf16[256,128]{1,0:T(8,128)(2,1)S(1)}, bf16[256,128]{1,0:T(8,128)(2,1)S(1)}, u32[]{:S(2)}, u32[]{:S(2)}) %collective-permute-start.14) | collective-permute-done | bytes 65568 | tf_op jit(solution)/shard_map/ppermute | solution.py:363
  106.2 2.8 %shard_map.92 = f32[128,1024]{1,0:T(8,128)} custom-call(s32[4]{0:T(128)S(1)} %pad_add_fusion.3.feat_ref, bf16[256,128]{1,0:T(8,128)(2,1)S(1)} %collective-permute-done.14.a_ref, bf16[256,128]{1,0:T(8,128)(2,1)S(1)} %collective-permute-done.15.b_ref, bf16[256,128]{1,0:T(8,128)(2,1)S(1)} %collective-permute-done.16.c_ref, ...), custom_call_target="tpu_custom_call" | custom-call | tf_op jit(solution)/shard_map/pallas_call | solution.py:277
  109.0 3.4 %shard_map.91 = bf16[512,1024]{1,0:T(8,128)(2,1)} custom-call(s32[3]{0:T(128)S(1)} %copy-done.2, bf16[2,256,512]{2,1,0:T(8,128)(2,1)S(1)} %get-tuple-element.34.near_ref, bf16[2,256,512]{2,1,0:T(8,128)(2,1)} %collective-permute-done.11.far_ref, bf16[2,256,512]{2,1,0:T(8,128)(2,1)S(1)} %pad_maximum_fusion.low_ref, ...), custom_call_target="tpu_custom_call" | custom-call | tf_op jit(solution)/shard_map/pallas_call | solution.py:253
  (19 shorter events, 0.1 us)
Async XLA Ops:
  1.7 20.8 %collective-permute-start = (bf16[256,1024]{1,0:T(8,128)(2,1)S(1)}, bf16[256,1024]{1,0:T(8,128)(2,1)S(1)}, u32[]{:S(2)}, u32[]{:S(2)}) collective-permute-start(bf16[256,1024]{1,0:T(8,128)(2,1)S(1)} %slice_bitcast_fusion), channel_id=1, source_target_pairs={{0,1},{1,0},{2,3},{3,2},{4,5},{5,4},{6,7},{7,6},{8,9},{9,8},{10,11... | collective-permute-start | bytes 1572872 | tf_op jit(solution)/shard_map/ppermute | solution.py:320
  13.1 21.9 %copy-start.3 = (s32[1,8192]{1,0:T(1,128)S(1)}, s32[1,8192]{1,0:T(1,128)}, u32[]{:S(2)}) copy-start(s32[1,8192]{1,0:T(1,128)} %param.8) | copy-start | bytes 98308
  22.5 23.9 %copy-start = (bf16[1,512,1024]{2,1,0:T(8,128)(2,1)S(1)}, bf16[1,512,1024]{2,1,0:T(8,128)(2,1)}, u32[]{:S(2)}) copy-start(bf16[1,512,1024]{2,1,0:T(8,128)(2,1)} %param.10) | copy-start | bytes 3145732
  22.5 23.9 %all-to-all-start = ((bf16[16,72,256]{2,1,0:T(8,128)(2,1)}), bf16[16,72,256]{2,1,0:T(8,128)(2,1)S(1)}, u32[]{:S(2)}, u32[]{:S(2)}) async-start(bf16[16,72,256]{2,1,0:T(8,128)(2,1)} %bitcast.9), calls=%async_computation | async-start | bytes 1179648 | tf_op jit(solution)/shard_map/all_to_all | solution.py:327
  30.3 8.0 %collective-permute-start.1 = (bf16[256,512]{1,0:T(8,128)(2,1)}, bf16[256,512]{1,0:T(8,128)(2,1)S(1)}, u32[]{:S(2)}, u32[]{:S(2)}) collective-permute-start(bf16[256,512]{1,0:T(8,128)(2,1)} %get-tuple-element.25), channel_id=1, source_target_pairs={{0,1},{1,2},{2,3},{3,0},{4,5},{5,6},{6,7},{7,4},{8,9},{9,10},{10,1... | collective-permute-start | bytes 786440 | tf_op jit(solution)/shard_map/ppermute | solution.py:332
  30.7 13.7 %collective-permute-start.2 = (bf16[256,512]{1,0:T(8,128)(2,1)}, bf16[256,512]{1,0:T(8,128)(2,1)S(1)}, u32[]{:S(2)}, u32[]{:S(2)}) collective-permute-start(bf16[256,512]{1,0:T(8,128)(2,1)} %get-tuple-element.27), channel_id=1, source_target_pairs={{0,2},{1,3},{2,0},{3,1},{4,6},{5,7},{6,4},{7,5},{8,10},{9,11},{10,... | collective-permute-start | bytes 786440 | tf_op jit(solution)/shard_map/ppermute | solution.py:332
  33.4 11.9 %collective-permute-start.3 = (bf16[256,512]{1,0:T(8,128)(2,1)}, bf16[256,512]{1,0:T(8,128)(2,1)S(1)}, u32[]{:S(2)}, u32[]{:S(2)}) collective-permute-start(bf16[256,512]{1,0:T(8,128)(2,1)} %get-tuple-element.29), channel_id=1, source_target_pairs={{0,3},{1,0},{2,1},{3,2},{4,7},{5,4},{6,5},{7,6},{8,11},{9,8},{10,9... | collective-permute-start | bytes 786440 | tf_op jit(solution)/shard_map/ppermute | solution.py:332
  46.4 15.4 %collective-permute-start.6 = (bf16[256,1024]{1,0:T(8,128)(2,1)S(1)}, bf16[256,1024]{1,0:T(8,128)(2,1)S(1)}, u32[]{:S(2)}, u32[]{:S(2)}) collective-permute-start(bf16[256,1024]{1,0:T(8,128)(2,1)S(1)} %slice.11), channel_id=1, source_target_pairs={{0,1},{1,0},{2,3},{3,2},{4,5},{5,4},{6,7},{7,6},{8,9},{9,8},{10,11... | collective-permute-start | bytes 1572872 | tf_op jit(solution)/shard_map/ppermute | solution.py:339
  48.5 13.4 %collective-permute-start.7 = (bf16[512,1024]{1,0:T(8,128)(2,1)S(1)}, bf16[512,1024]{1,0:T(8,128)(2,1)S(1)}, u32[]{:S(2)}, u32[]{:S(2)}) collective-permute-start(bf16[512,1024]{1,0:T(8,128)(2,1)S(1)} %bitcast.21), channel_id=1, source_target_pairs={{0,64},{64,0},{1,65},{65,1},{2,66},{66,2},{3,67},{67,3},{4,68},{68... | collective-permute-start | bytes 3145736 | tf_op jit(solution)/shard_map/ppermute | solution.py:319
  50.6 8.0 %collective-permute-start.9 = (bf16[256,512]{1,0:T(8,128)(2,1)S(1)}, bf16[256,512]{1,0:T(8,128)(2,1)S(1)}, u32[]{:S(2)}, u32[]{:S(2)}) collective-permute-start(bf16[256,512]{1,0:T(8,128)(2,1)S(1)} %add_convert_fusion), channel_id=1, source_target_pairs={{0,4},{4,0},{8,12},{12,8},{16,20},{20,16},{24,28},{28,24},{32,36},... | collective-permute-start | bytes 786440 | tf_op jit(solution)/shard_map/ppermute | solution.py:350
  52.0 8.2 %collective-permute-start.5 = (bf16[256,512]{1,0:T(8,128)(2,1)S(1)}, bf16[256,512]{1,0:T(8,128)(2,1)S(1)}, u32[]{:S(2)}, u32[]{:S(2)}) collective-permute-start(bf16[256,512]{1,0:T(8,128)(2,1)S(1)} %shard_map.88.mine_ref), channel_id=1, source_target_pairs={{0,67},{1,66},{2,65},{3,64},{64,0},{65,1},{66,2},{67,3},{4,71},{5,... | collective-permute-start | bytes 786440 | tf_op jit(solution)/shard_map/ppermute | solution.py:341
  52.3 9.5 %collective-permute-start.4 = (bf16[256,512]{1,0:T(8,128)(2,1)S(1)}, bf16[256,512]{1,0:T(8,128)(2,1)S(1)}, u32[]{:S(2)}, u32[]{:S(2)}) collective-permute-start(bf16[256,512]{1,0:T(8,128)(2,1)S(1)} %shard_map.88.mine_ref), channel_id=1, source_target_pairs={{64,67},{65,66},{66,65},{67,64},{68,71},{69,70},{70,69},{71,68},{7... | collective-permute-start | bytes 786440 | tf_op jit(solution)/shard_map/ppermute | solution.py:342
  58.6 3.3 %collective-permute-start.8 = (bf16[256,1024]{1,0:T(8,128)(2,1)S(1)}, bf16[256,1024]{1,0:T(8,128)(2,1)S(1)}, u32[]{:S(2)}, u32[]{:S(2)}) collective-permute-start(bf16[256,1024]{1,0:T(8,128)(2,1)S(1)} %collective-permute-done.n1a_ref), channel_id=1, source_target_pairs={{0,64},{64,0},{1,65},{65,1},{2,66},{66,2},{3,67},{67,3},{4,68},{68... | collective-permute-start | bytes 1572872 | tf_op jit(solution)/shard_map/ppermute | solution.py:351
  61.8 1.9 %collective-permute-start.10 = (bf16[256,1024]{1,0:T(8,128)(2,1)S(1)}, bf16[256,1024]{1,0:T(8,128)(2,1)S(1)}, u32[]{:S(2)}, u32[]{:S(2)}) collective-permute-start(bf16[256,1024]{1,0:T(8,128)(2,1)S(1)} %collective-permute-done.6.n1b_ref), channel_id=1, source_target_pairs={{0,64},{64,0},{1,65},{65,1},{2,66},{66,2},{3,67},{67,3},{4,68},{68... | collective-permute-start | bytes 1572872 | tf_op jit(solution)/shard_map/ppermute | solution.py:351
  67.7 19.3 %copy-start.2 = (s32[3]{0:T(128)S(1)}, s32[3]{0:T(128)}, u32[]{:S(2)}) copy-start(s32[3]{0:T(128)} %pad_add_fusion.idx_ref) | copy-start | bytes 40
  67.7 19.2 %collective-permute-start.12 = (bf16[2,256,512]{2,1,0:T(8,128)(2,1)S(1)}, bf16[2,256,512]{2,1,0:T(8,128)(2,1)}, u32[]{:S(2)}, u32[]{:S(2)}) collective-permute-start(bf16[2,256,512]{2,1,0:T(8,128)(2,1)S(1)} %pad_maximum_fusion.low_ref), channel_id=1, source_target_pairs={{0,16},{4,20},{8,24},{12,28},{16,0},{20,4},{24,8},{28,12},{32,48},... | collective-permute-start | bytes 1572872 | tf_op jit(solution)/shard_map/ppermute | solution.py:355
  68.9 18.1 %collective-permute-start.11 = (bf16[2,256,512]{2,1,0:T(8,128)(2,1)S(1)}, bf16[2,256,512]{2,1,0:T(8,128)(2,1)}, u32[]{:S(2)}, u32[]{:S(2)}) collective-permute-start(bf16[2,256,512]{2,1,0:T(8,128)(2,1)S(1)} %get-tuple-element.34.near_ref), channel_id=1, source_target_pairs={{0,1},{1,0},{2,3},{3,2},{4,5},{5,4},{6,7},{7,6},{8,9},{9,8},{10,11... | collective-permute-start | bytes 1572872 | tf_op jit(solution)/shard_map/ppermute | solution.py:357
  69.7 24.9 %all-to-all-start.1 = ((bf16[16,256,128]{2,1,0:T(8,128)(2,1)}), bf16[16,256,128]{2,1,0:T(8,128)(2,1)}, u32[]{:S(2)}, u32[]{:S(2)}) async-start(bf16[16,256,128]{2,1,0:T(8,128)(2,1)} %get-tuple-element.35), calls=%async_computation.1 | async-start | bytes 2097152 | tf_op jit(solution)/shard_map/all_to_all | solution.py:354
  76.0 30.2 %copy-start.1 = (bf16[1024,1024]{1,0:T(8,128)(2,1)S(1)}, bf16[1024,1024]{1,0:T(8,128)(2,1)}, u32[]{:S(2)}) copy-start(bf16[1024,1024]{1,0:T(8,128)(2,1)} %get-tuple-element.21.w_ref) | copy-start | bytes 6291460
  90.0 19.0 %collective-permute-start.13 = (bf16[512,1024]{1,0:T(8,128)(2,1)}, bf16[512,1024]{1,0:T(8,128)(2,1)}, u32[]{:S(2)}, u32[]{:S(2)}) collective-permute-start(bf16[512,1024]{1,0:T(8,128)(2,1)} %shard_map.90), channel_id=1, source_target_pairs={{0,64},{64,0},{1,65},{65,1},{2,66},{66,2},{3,67},{67,3},{4,68},{68... | collective-permute-start | bytes 3145736 | tf_op jit(solution)/shard_map/ppermute | solution.py:367
  96.0 6.6 %collective-permute-start.17 = (bf16[256,128]{1,0:T(8,128)(2,1)S(1)}, bf16[256,128]{1,0:T(8,128)(2,1)S(1)}, u32[]{:S(2)}, u32[]{:S(2)}) collective-permute-start(bf16[256,128]{1,0:T(8,128)(2,1)S(1)} %reduce_sum.22), channel_id=1, source_target_pairs={{0,3},{1,2},{2,67},{3,66},{64,1},{65,0},{66,65},{67,64},{4,7},{5,6... | collective-permute-start | bytes 196616 | tf_op jit(solution)/shard_map/ppermute | solution.py:363
  97.7 4.9 %collective-permute-start.16 = (bf16[256,128]{1,0:T(8,128)(2,1)S(1)}, bf16[256,128]{1,0:T(8,128)(2,1)S(1)}, u32[]{:S(2)}, u32[]{:S(2)}) collective-permute-start(bf16[256,128]{1,0:T(8,128)(2,1)S(1)} %reduce_sum.22), channel_id=1, source_target_pairs={{0,2},{1,3},{2,66},{3,67},{64,0},{65,1},{66,64},{67,65},{4,6},{5,7... | collective-permute-start | bytes 196616 | tf_op jit(solution)/shard_map/ppermute | solution.py:363
  99.0 4.9 %collective-permute-start.15 = (bf16[256,128]{1,0:T(8,128)(2,1)S(1)}, bf16[256,128]{1,0:T(8,128)(2,1)S(1)}, u32[]{:S(2)}, u32[]{:S(2)}) collective-permute-start(bf16[256,128]{1,0:T(8,128)(2,1)S(1)} %reduce_sum.22), channel_id=1, source_target_pairs={{0,1},{1,0},{2,65},{3,64},{64,3},{65,2},{66,67},{67,66},{4,5},{5,4... | collective-permute-start | bytes 196616 | tf_op jit(solution)/shard_map/ppermute | solution.py:363
  99.1 7.1 %collective-permute-start.14 = (bf16[256,128]{1,0:T(8,128)(2,1)S(1)}, bf16[256,128]{1,0:T(8,128)(2,1)S(1)}, u32[]{:S(2)}, u32[]{:S(2)}) collective-permute-start(bf16[256,128]{1,0:T(8,128)(2,1)S(1)} %reduce_sum.22), channel_id=1, source_target_pairs={{0,0},{1,1},{2,64},{3,65},{64,2},{65,3},{66,66},{67,67},{4,4},{5,5... | collective-permute-start | bytes 196616 | tf_op jit(solution)/shard_map/ppermute | solution.py:363

commit v5 on v4

v5 whole, which is shorter than its diff:
```python
import functools

import jax
import jax.numpy as jnp
from jax import lax
from jax.experimental import pallas as pl
from jax.experimental.pallas import tpu as pltpu
from jax.sharding import PartitionSpec as P

LANES = 128
GROUP = 16
SUB = LANES // GROUP
WIN = 9
SLOT = WIN * SUB
SIDE = 4
CUT = 256
VMEM = 24 * 1024 * 1024
WIDE = 56 * 1024 * 1024


def seg_kernel(starts_ref, owner_ref, bytes_ref, out_ref, next_ref, low_ref, high_ref, acc_ref, turn_ref, held_ref, row_ref, sems):
    steps = sems.shape[0]
    shard, width = held_ref.shape
    block = shard // steps
    owners = LANES // SUB
    from_col = pl.ds(pl.multiple_of(lax.axis_index("tensor") * width, width), width)
    copies = []
    for k in range(steps):
        at = pl.ds(k * block, block)
        copies.append(pltpu.make_async_copy(bytes_ref.at[at, from_col], held_ref.at[at, :], sems.at[k]))
        copies[k].start()

    starts = starts_ref[...]
    rows = starts.shape[0]
    base = lax.axis_index("context") * shard
    for k in range(steps + 1):
        count = jnp.sum((starts <= base + k * block).astype(jnp.float32)).astype(jnp.int32)
        row_ref[k] = lax.shift_right_logical(count - 1, 7)
    first = jnp.minimum(row_ref[0], rows - WIN)
    lane = lax.broadcasted_iota(jnp.int32, starts.shape, 1)
    turned = pltpu.roll(starts, LANES - 1, 1)
    below = jnp.concatenate([turned[1:], jnp.full((1, LANES), 2**30, jnp.int32)], axis=0)
    next_ref[...] = jnp.where(lane == LANES - 1, below, turned)
    lane = lax.broadcasted_iota(jnp.int32, (SUB, LANES), 1)
    mine = lax.shift_right_logical(lane, 4) == lax.broadcasted_iota(jnp.int32, (SUB, LANES), 0)
    for t in range(WIN):
        low = jnp.clip(starts_ref[pl.ds(first + t, 1), :] - base, 0, shard).astype(jnp.float32)
        high = jnp.clip(next_ref[pl.ds(first + t, 1), :] - base, 0, shard).astype(jnp.float32)
        low = jnp.broadcast_to(low, (SUB, LANES))
        high = jnp.broadcast_to(high, (SUB, LANES))
        owner = jnp.broadcast_to(owner_ref[pl.ds(first + t, 1), :], (SUB, LANES))
        owner = jnp.where(mine, owner, -1)
        for j in range(owners):
            held = owner == j
            at = t * LANES + j * SUB
            one = jnp.sum(jnp.where(held, low, 0.0), axis=1, keepdims=True)
            low_ref[at : at + SUB, :] = jnp.broadcast_to(one, (SUB, LANES))
            one = jnp.sum(jnp.where(held, high, 0.0), axis=1, keepdims=True)
            high_ref[at : at + SUB, :] = jnp.broadcast_to(one, (SUB, LANES))
    acc_ref[...] = jnp.zeros_like(acc_ref)

    for k in range(steps):
        copies[k].wait()

        def one_row(t, carry, k=k):
            at = pl.ds(pl.multiple_of(t * LANES, LANES), LANES)
            low = low_ref[at, :]
            high = high_ref[at, :]
            parts = []
            for q in range(block // LANES):
                place = lax.broadcasted_iota(jnp.int32, (1, LANES), 1) + (k * block + q * LANES)
                place = place.astype(jnp.float32)
                parts.append(jnp.where((place >= low) & (place < high), 1.0, 0.0).astype(jnp.bfloat16))
            onehot = jnp.concatenate(parts, axis=1)
            acc_ref[at, :] += jnp.dot(
                onehot, held_ref[k * block : (k + 1) * block, :], preferred_element_type=jnp.float32
            )
            return carry

        lax.fori_loop(row_ref[k] - first, jnp.minimum(row_ref[k + 1] - first, WIN - 1) + 1, one_row, 0)

    for t in range(WIN):
        for j in range(owners):
            turn_ref[j * SLOT + t * SUB : j * SLOT + (t + 1) * SUB, :] = acc_ref[
                t * LANES + j * SUB : t * LANES + (j + 1) * SUB, :
            ]
    out_ref[...] = turn_ref[...].astype(jnp.bfloat16)


def segment_sums(starts, owner, grads, owners, width):
    steps = 8
    rows = owners * SLOT
    vmem = pl.BlockSpec(memory_space=pltpu.VMEM)
    return pl.pallas_call(
        seg_kernel,
        in_specs=[vmem, vmem, pl.BlockSpec(memory_space=pl.ANY)],
        out_shape=jax.ShapeDtypeStruct((rows, width), jnp.bfloat16),
        scratch_shapes=[
            pltpu.VMEM(starts.shape, jnp.int32),
            pltpu.VMEM((rows, LANES), jnp.float32),
            pltpu.VMEM((rows, LANES), jnp.float32),
            pltpu.VMEM((rows, width), jnp.float32),
            pltpu.VMEM((rows, width), jnp.float32),
            pltpu.VMEM((grads.shape[0], width), jnp.bfloat16),
            pltpu.SMEM((steps + 1,), jnp.int32),
            pltpu.SemaphoreType.DMA((steps,)),
        ],
        compiler_params=pltpu.CompilerParams(vmem_limit_bytes=WIDE),
    )(starts, owner, grads)


def collect_kernel(first_ref, in_ref, out_ref, wide_ref, acc_ref):
    wide_ref[...] = in_ref[...].astype(jnp.float32)
    acc_ref[...] = jnp.zeros_like(acc_ref)
    for s in range(in_ref.shape[0] // SLOT):
        at = pl.ds(pl.multiple_of(first_ref[s] * SUB, SUB), SLOT)
        acc_ref[at, :] += wide_ref[s * SLOT : (s + 1) * SLOT, :]
    out_ref[...] = acc_ref[...].T.astype(jnp.bfloat16)


def collect(first, incoming, patch_rows, interpret=False):
    rows, width = incoming.shape
    return pl.pallas_call(
        collect_kernel,
        in_specs=[pl.BlockSpec(memory_space=pltpu.SMEM), pl.BlockSpec(memory_space=pltpu.VMEM)],
        out_specs=pl.BlockSpec(memory_space=pltpu.VMEM),
        out_shape=jax.ShapeDtypeStruct((width, patch_rows), jnp.bfloat16),
        scratch_shapes=[pltpu.VMEM((rows, width), jnp.float32), pltpu.VMEM((patch_rows, width), jnp.float32)],
        compiler_params=pltpu.CompilerParams(vmem_limit_bytes=VMEM),
        interpret=interpret,
    )(first, incoming)


def outer_kernel(mine_ref, third_ref, cross_ref, n0_ref, n1a_ref, n1b_ref, f0_ref, f1a_ref, f1b_ref, out_ref, both_ref, held_ref, sems):
    near_t = jnp.where(lax.axis_index("dp") == 0, mine_ref[...], third_ref[...])
    far_t = cross_ref[...]
    both_ref[0] = near_t
    both_ref[1] = far_t
    low = lax.rem(lax.axis_index("tensor"), 2)
    blocks = out_ref.shape[0] // 2
    cols = n0_ref.shape[1]
    wide = 256
    per = wide // LANES
    copies = []
    for i in range(cols // wide):
        at = slice(i * wide, (i + 1) * wide)
        near1 = jnp.concatenate([n1a_ref[:, at], n1b_ref[:, at]], axis=0)
        far1 = jnp.concatenate([f1a_ref[:, at], f1b_ref[:, at]], axis=0)
        for k, (near, far, which) in enumerate(((n0_ref[:, at], f0_ref[:, at], low), (near1, far1, 1 - low))):
            total = jnp.dot(near_t, near, preferred_element_type=jnp.float32)
            total += jnp.dot(far_t, far, preferred_element_type=jnp.float32)
            total = total.astype(jnp.bfloat16)
            here = k * blocks + i * per
            for j in range(per):
                held_ref[here + j] = total[:, j * LANES : (j + 1) * LANES]
            copy = pltpu.make_async_copy(
                held_ref.at[pl.ds(here, per)],
                out_ref.at[pl.ds(which * blocks + i * per, per)],
                sems.at[2 * i + k],
            )
            copy.start()
            copies.append(copy)
    for copy in copies:
        copy.wait()


def outer(sums, columns):
    width, rows = sums[0].shape
    cols = columns[0].shape[1]
    vmem = pl.BlockSpec(memory_space=pltpu.VMEM)
    shape = (2 * cols // LANES, width, LANES)
    return pl.pallas_call(
        outer_kernel,
        in_specs=[vmem] * (len(sums) + len(columns)),
        out_specs=[pl.BlockSpec(memory_space=pltpu.HBM), vmem],
        out_shape=[
            jax.ShapeDtypeStruct(shape, jnp.bfloat16),
            jax.ShapeDtypeStruct((2, width, rows), jnp.bfloat16),
        ],
        scratch_shapes=[pltpu.VMEM(shape, jnp.bfloat16), pltpu.SemaphoreType.DMA((2 * cols // 256,))],
        compiler_params=pltpu.CompilerParams(vmem_limit_bytes=VMEM),
    )(*sums, *columns)


def quarter():
    ctx = lax.axis_index("context")
    return 2 * lax.rem(lax.div(ctx, SIDE), 2) + lax.rem(ctx, 2)


def chain_kernel(value_ref, out_w_ref, global_ref, both_ref, p0_ref, p1_ref, p2_ref, p3_ref, held_ref, sems):
    rows, wide = p0_ref.shape
    parts = held_ref.shape[0]
    dp, ten = lax.axis_index("dp"), lax.axis_index("tensor")
    copies = []
    for s in range(parts):
        at = (lax.rem(ten + s, parts) * 4 + quarter()) * rows
        copy = pltpu.make_async_copy(global_ref.at[pl.ds(pl.multiple_of(at, rows), rows)], held_ref.at[s], sems.at[s])
        copy.start()
        copies.append(copy)
    both_ref[...] = jnp.dot(
        value_ref[...], out_w_ref[...], preferred_element_type=jnp.float32
    ).astype(jnp.bfloat16)
    for s, p in enumerate((p0_ref, p1_ref, p2_ref, p3_ref)):
        copies[s].wait()
        half = lax.div(lax.rem(ten + s, parts), 2)
        half = dp + half - 2 * dp * half
        cols = pl.ds(pl.multiple_of(half * wide, wide), wide)
        p[...] = jnp.dot(held_ref[s], both_ref[:, cols], preferred_element_type=jnp.float32).astype(jnp.bfloat16)


def chain_terms(w_value, w_out, w_global, parts):
    deep, feats = w_value.shape
    rows = w_global.shape[0] // parts // 4
    vmem = pl.BlockSpec(memory_space=pltpu.VMEM)
    return pl.pallas_call(
        chain_kernel,
        in_specs=[vmem, vmem, pl.BlockSpec(memory_space=pl.ANY)],
        out_specs=[vmem] * (1 + parts),
        out_shape=[jax.ShapeDtypeStruct((deep, feats), jnp.bfloat16)]
        + [jax.ShapeDtypeStruct((rows, feats // 2), jnp.bfloat16)] * parts,
        scratch_shapes=[pltpu.VMEM((parts, rows, deep), jnp.bfloat16), pltpu.SemaphoreType.DMA((parts,))],
        compiler_params=pltpu.CompilerParams(vmem_limit_bytes=WIDE),
    )(w_value, w_out, w_global)


def rows_kernel(which, near_ref, far_ref, low_ref, high_ref, *rest):
    out_ref = rest[-1]
    deep = near_ref.shape[1]
    odd = lax.rem(lax.axis_index("tensor") + lax.axis_index("dp"), 2)
    near = near_ref[which].T
    far = far_ref[which].T
    rows = low_ref.shape[1]
    for i, ref in enumerate((low_ref, high_ref)):
        for j in range(2):
            z, y = lax.div(quarter(), 2), lax.rem(quarter(), 2)
            at = 2 * (z + i - 2 * i * z) + y + j - 2 * j * y
            at = pl.ds(pl.multiple_of(at * rows, rows), rows)
            first = ref[j, :, pl.ds(pl.multiple_of(odd * deep, deep), deep)]
            second = ref[j, :, pl.ds(pl.multiple_of((1 - odd) * deep, deep), deep)]
            dims = (((1,), (1,)), ((), ()))
            total = lax.dot_general(near, first, dims, preferred_element_type=jnp.float32)
            total += lax.dot_general(far, second, dims, preferred_element_type=jnp.float32)
            if len(rest) > 1:
                total += rest[0][:, at].astype(jnp.float32)
            out_ref[:, at] = total.astype(jnp.bfloat16)


def context_rows(which, near, far, low, high, *back):
    vmem = pl.BlockSpec(memory_space=pltpu.VMEM)
    return pl.pallas_call(
        functools.partial(rows_kernel, which),
        in_specs=[vmem] * (4 + len(back)),
        out_specs=vmem,
        out_shape=jax.ShapeDtypeStruct((near.shape[2], 4 * low.shape[1]), jnp.bfloat16),
        compiler_params=pltpu.CompilerParams(vmem_limit_bytes=VMEM),
    )(near, far, low, high, *back)


def last_kernel(a_ref, b_ref, c_ref, d_ref, w_ref, out_ref):
    width = a_ref.shape[0]
    dp, ten = lax.axis_index("dp"), lax.axis_index("tensor")
    total = jnp.zeros(out_ref.shape, jnp.float32)
    for s, ref in enumerate((a_ref, b_ref, c_ref, d_ref)):
        source = lax.bitwise_xor(ten, s)
        near = 2 * dp + lax.rem(source, 2)
        at = jnp.where(source < 2, near, 3 - near)
        total += lax.dot_general(
            ref[...].T,
            w_ref[:, pl.ds(pl.multiple_of(at * width, width), width)],
            (((1,), (1,)), ((), ())),
            preferred_element_type=jnp.float32,
        )
    out_ref[...] = total


def last(pieces, weights):
    vmem = pl.BlockSpec(memory_space=pltpu.VMEM)
    return pl.pallas_call(
        last_kernel,
        in_specs=[vmem] * (len(pieces) + 1),
        out_shape=jax.ShapeDtypeStruct((pieces[0].shape[1], weights.shape[0]), jnp.float32),
        compiler_params=pltpu.CompilerParams(vmem_limit_bytes=VMEM),
    )(*pieces, weights)


def after(value, *others):
    return lax.optimization_barrier((value, *others))[0]


def local(byte_grads, patch_starts, patch_owner, attn_context, w_global, w_value, w_out):
    dp_n, ctx_n, ten_n = (lax.axis_size(a) for a in ("dp", "context", "tensor"))
    f32, bf16 = jnp.float32, jnp.bfloat16
    bytes_n, feats = byte_grads.shape[1:]
    width = feats // ten_n
    patch_rows = attn_context.shape[1]
    starts = patch_starts.reshape(-1, LANES)
    owner = patch_owner.reshape(-1, LANES)
    line = ("dp", "tensor")

    def moves(target):
        pairs = []
        for d in range(dp_n):
            for x in range(ten_n):
                to = target(d, x)
                if to is not None:
                    pairs.append((d * ten_n + x, to[0] * ten_n + to[1]))
        return pairs

    swap = [(i, dp_n - 1 - i) for i in range(dp_n)]
    pair = [(x, x ^ 1) for x in range(ten_n)]
    near0 = attn_context[0]
    far0 = lax.ppermute(near0, "dp", swap)
    near1 = [lax.ppermute(near0[:CUT], "tensor", pair)]

    outgoing = segment_sums(starts, owner, byte_grads[0], ctx_n, width)

    both_t, *terms = chain_terms(after(w_value, outgoing), w_out, w_global, ten_n)
    outgoing = after(outgoing, near1[0], both_t, far0)
    incoming = lax.all_to_all(outgoing, "context", split_axis=0, concat_axis=0, tiled=True)

    chain = terms[0].astype(f32)
    for s in range(1, ten_n):
        term = after(terms[s], outgoing)
        chain += lax.ppermute(term, "tensor", [(x, (x + s) % ten_n) for x in range(ten_n)]).astype(f32)
    chain = chain.astype(bf16)
    edges = jnp.arange(ctx_n, dtype=jnp.int32) * bytes_n
    counts = jnp.sum((patch_starts[0][None, :] <= edges[:, None]).astype(jnp.int32), axis=1)
    first = jnp.minimum((counts - 1) // LANES, starts.shape[0] - WIN)
    far1 = [lax.ppermute(near1[0], "dp", swap)]
    incoming = after(incoming, first, far1[0])

    near1.append(lax.ppermute(after(near0, incoming)[CUT:], "tensor", pair))
    sums = collect(first, incoming, patch_rows)
    cross = lax.ppermute(sums, line, moves(lambda d, x: (0, x) if d == 1 else (1, ten_n - 1 - x)))
    third = lax.ppermute(sums, line, moves(lambda d, x: (1, ten_n - 1 - x) if d == 1 else None))

    def along(target):
        return [
            (i * SIDE + j, target(i, j)[0] * SIDE + target(i, j)[1]) for i in range(SIDE) for j in range(SIDE)
        ]

    chain = after(chain, sums)
    far1.append(lax.ppermute(after(near1[1], cross, third, chain), "dp", swap))
    other = lax.ppermute(chain, "context", along(lambda i, j: (i, j ^ 1)))
    columns = (near0, *near1, far0, *far1)
    partial, near = outer((sums, third, cross), columns)
    pieces = lax.all_to_all(partial, "context", split_axis=0, concat_axis=0, tiled=True)
    chain = jnp.stack([after(chain, partial), after(other, partial)])
    rest = lax.ppermute(chain, "context", along(lambda i, j: (i ^ 1, j)))

    far = lax.ppermute(near, "tensor", pair)
    give = context_rows(1, near, far, chain, rest)
    pieces = after(pieces, give)
    piece = jnp.sum(pieces.astype(f32), axis=0).astype(bf16)
    parts = []
    for s in range(ten_n):
        parts.append(lax.ppermute(piece, line, moves(lambda d, x, s=s: (x // 2, (2 * d + x % 2) ^ s))))
    back = lax.ppermute(give, "dp", swap)
    context_grad = context_rows(0, near, far, chain, rest, back)
    weight_grad = last(parts, both_t)
    return (context_grad[None], weight_grad)


def solution(mesh):
    placed = (
        P("dp", "context", None),
        P("dp", None),
        P("dp", None),
        P("dp", "context", "tensor"),
        P(None, "tensor"),
        P("tensor", None),
        P(),
    )
    return jax.shard_map(
        local,
        mesh=mesh,
        in_specs=placed,
        out_specs=(P("dp", "context", "tensor"), P(("dp", "context"), "tensor")),
        check_vma=False,
    )
```

time: 113 us -> 117 us (1.035)
  waiting for transfers between devices: 32.4 us -> 43.3 us
  Pallas kernels: 31.5 us -> 26.7 us
  starting transfers between devices: 42.4 us -> 38.3 us
  local copies, waits for them, and re-layouts: 1.13 us -> 4.86 us
  other arithmetic: 4.18 us -> 1.84 us
    all_to_all x1, waiting for transfers between devices: 0.01 us -> 8.52 us  [local(): lax.all_to_all(outgoing, 'context', split_axis=0, concat_axis=0, tiled=True)]
    ppermute x3, waiting for transfers between devices: 10.1 us -> 15 us  [local(): lax.ppermute(term, 'tensor', [(x, (x + s) % ten_n) for x in range(ten_n)])]
    pallas_call x6, Pallas kernels: 30.6 us -> 25.8 us  [the longest x1 7.7 us: chain_terms(): pl.pallas_call(chain_kernel, in_specs=[vmem, vmem, pl.BlockSpec(memory_sp...]
    unnamed x8 -> x22, local copies, waits for them, and re-layouts: 0.02 us -> 3.75 us
    ppermute x1, starting transfers between devices: 2.05 us -> 0.09 us  [local(): near1.append(lax.ppermute(after(near0, incoming)[CUT:], 'tensor', pair))]
    all_to_all x1, starting transfers between devices: 6.24 us -> 4.34 us  [local(): lax.all_to_all(partial, 'context', split_axis=0, concat_axis=0, tiled=True)]
    ppermute x1, waiting for transfers between devices: 1.66 us -> 0.01 us  [local(): lax.ppermute(sums, line, moves(lambda d, x: (1, ten_n - 1 - x) if d == 1...]
    ppermute x4, starting transfers between devices: 6.54 us -> 8.04 us  [local(): lax.ppermute(piece, line, moves(lambda d, x, s=s: (x // 2, 2 * d + x % 2...]
  transfers between devices with their start and end apart: 20 -> 20, of which waited for: 11 -> 8; matrix products, arithmetic and copies ran while one was open for 4% -> 3% of each run, Pallas kernels for 21% -> 20%
where the time goes in v5:
time: 117 us; the launch traced here: 116 us
  waiting for transfers between devices  43.3 us (37%)
  starting transfers between devices  38.3 us (33%)
  Pallas kernels  26.7 us (23%)
  local copies, waits for them, and re-layouts  4.86 us (4%)
  other arithmetic  1.84 us (2%)
    ppermute x1, waiting for transfers between devices, local(): rest = lax.ppermute(chain, 'context', along(lambda i, j: (i ^ 1, j)))  16 us
    ppermute x3, waiting for transfers between devices, local(): lax.ppermute(term, 'tensor', [(x, (x + s) % ten_n) for x in range(ten_n)])  15 us
    all_to_all x1, waiting for transfers between devices, local(): lax.all_to_all(outgoing, 'context', split_axis=0, concat_axis=0, tiled=True)  8.52 us
    ppermute x4, starting transfers between devices, local(): lax.ppermute(piece, line, moves(lambda d, x, s=s: (x // 2, 2 * d + x % 2...  8.04 us
    all_to_all x1, starting transfers between devices, local(): lax.all_to_all(outgoing, 'context', split_axis=0, concat_axis=0, tiled=True)  7.96 us
    pallas_call x1, Pallas kernels, chain_terms(): pl.pallas_call(chain_kernel, in_specs=[vmem, vmem, pl.BlockSpec(memory_sp...  7.7 us
    pallas_call x2, Pallas kernels, context_rows(): pl.pallas_call(functools.partial(rows_kernel, which), in_specs=[vmem] * (...  6.38 us
    pallas_call x1, Pallas kernels, segment_sums(): pl.pallas_call(seg_kernel, in_specs=[vmem, vmem, pl.BlockSpec(memory_spac...  5.08 us
  transfers between devices with their start and end apart: 20, of which 8 were waited for; matrix products, arithmetic and copies ran while one was open for 3% of the time, Pallas kernels for 20%

profile of v5, /device:TPU:1, one launch (start us, length us, event | category | flops | bytes accessed | tf_op | source)
XLA Modules:
  0.0 115.9 jit_solution(7403305024502840729)
XLA Ops:
  0.6 1.5 %collective-permute-start.1 = (bf16[512,1024]{1,0:T(8,128)(2,1)}, bf16[512,1024]{1,0:T(8,128)(2,1)S(1)}, u32[]{:S(2)}, u32[]{:S(2)}) collective-permute-start(bf16[512,1024]{1,0:T(8,128)(2,1)} %bitcast.12), channel_id=1, source_target_pairs={{0,64},{64,0},{1,65},{65,1},{2,66},{66,2},{3,67},{67,3},{4,68},{68... | collective-permute-start | bytes 3145736 | tf_op jit(solution)/shard_map/ppermute | solution.py:312
  2.1 1.1 slice_bitcast_fusion
  3.2 1.4 %collective-permute-start = (bf16[256,1024]{1,0:T(8,128)(2,1)S(1)}, bf16[256,1024]{1,0:T(8,128)(2,1)S(1)}, u32[]{:S(2)}, u32[]{:S(2)}) collective-permute-start(bf16[256,1024]{1,0:T(8,128)(2,1)S(1)} %slice_bitcast_fusion), channel_id=1, source_target_pairs={{0,1},{1,0},{2,3},{3,2},{4,5},{5,4},{6,7},{7,6},{8,9},{9,8},{10,11... | collective-permute-start | bytes 1572872 | tf_op jit(solution)/shard_map/ppermute | solution.py:313
  4.6 5.1 %shard_map.86 = bf16[1152,256]{1,0:T(8,128)(2,1)} custom-call(s32[64,128]{1,0:T(8,128)} %bitcast.20, s32[64,128]{1,0:T(8,128)} %bitcast.22, bf16[4096,1024]{1,0:T(8,128)(2,1)} %bitcast.16), custom_call_target="tpu_custom_call" | custom-call | tf_op jit(solution)/shard_map/pallas_call | solution.py:94
  9.7 0.0 copy-start.8
  9.7 0.0 copy-start
  9.7 7.7 %shard_map.87 = (bf16[1024,1024]{1,0:T(8,128)(2,1)}, bf16[256,512]{1,0:T(8,128)(2,1)}, bf16[256,512]{1,0:T(8,128)(2,1)}, bf16[256,512]{1,0:T(8,128)(2,1)}, bf16[256,512]{1,0:T(8,128)(2,1)}) custom-call(bf16[1024,1024]{1,0:T(8,128)(2,1)} %value_ref, bf16[1024,1024]{1,0:T(8,128)(2,1)} %out_w_ref.1, bf16[4096,1024]{1,0:T(8,128)(2,1)} %global_ref.1), custom_call_target="tpu_custom_call" | custom-call | tf_op jit(solution)/shard_map/pallas_call | solution.py:215
  17.4 0.0 collective-permute-done.n1a_ref
  17.5 0.0 copy-start.2
  17.5 1.0 copy-done.2
  18.4 8.0 %all-to-all-start = ((bf16[16,72,256]{2,1,0:T(8,128)(2,1)}), bf16[16,72,256]{2,1,0:T(8,128)(2,1)S(1)}, u32[]{:S(2)}, u32[]{:S(2)}) async-start(bf16[16,72,256]{2,1,0:T(8,128)(2,1)} %bitcast.6), calls=%async_computation | async-start | bytes 1179648 | tf_op jit(solution)/shard_map/all_to_all | solution.py:319
  26.4 0.7 collective-permute-start.2
  27.1 0.3 convert_reduce_fusion
  27.3 1.0 collective-permute-start.6
  28.4 0.2 collective-permute-done.2.f1a_ref
  28.6 0.8 copy-done.5
  29.4 8.5 %all-to-all-done = bf16[16,72,256]{2,1,0:T(8,128)(2,1)S(1)} async-done(((bf16[16,72,256]{2,1,0:T(8,128)(2,1)}), bf16[16,72,256]{2,1,0:T(8,128)(2,1)S(1)}, u32[]{:S(2)}, u32[]{:S(2)}) %all-to-all-start) | async-done | bytes 589856 | tf_op jit(solution)/shard_map/all_to_all | solution.py:319
  38.0 0.1 collective-permute-start.5
  38.1 2.5 %collective-permute-start.7 = (bf16[256,512]{1,0:T(8,128)(2,1)S(1)}, bf16[256,512]{1,0:T(8,128)(2,1)S(1)}, u32[]{:S(2)}, u32[]{:S(2)}) collective-permute-start(bf16[256,512]{1,0:T(8,128)(2,1)S(1)} %copy-done.10), channel_id=1, source_target_pairs={{0,2},{1,3},{2,0},{3,1},{4,6},{5,7},{6,4},{7,5},{8,10},{9,11},{10,... | collective-permute-start | bytes 786440 | tf_op jit(solution)/shard_map/ppermute | solution.py:324
  40.6 1.3 %collective-permute-start.8 = (bf16[256,512]{1,0:T(8,128)(2,1)S(1)}, bf16[256,512]{1,0:T(8,128)(2,1)S(1)}, u32[]{:S(2)}, u32[]{:S(2)}) collective-permute-start(bf16[256,512]{1,0:T(8,128)(2,1)S(1)} %copy-done.9), channel_id=1, source_target_pairs={{0,3},{1,0},{2,1},{3,2},{4,7},{5,4},{6,5},{7,6},{8,11},{9,8},{10,9... | collective-permute-start | bytes 786440 | tf_op jit(solution)/shard_map/ppermute | solution.py:324
  41.9 0.9 shard_map.88.mine_ref
  42.8 1.9 %collective-permute-start.3 = (bf16[256,512]{1,0:T(8,128)(2,1)S(1)}, bf16[256,512]{1,0:T(8,128)(2,1)S(1)}, u32[]{:S(2)}, u32[]{:S(2)}) collective-permute-start(bf16[256,512]{1,0:T(8,128)(2,1)S(1)} %shard_map.88.mine_ref), channel_id=1, source_target_pairs={{64,67},{65,66},{66,65},{67,64},{68,71},{69,70},{70,69},{71,68},{7... | collective-permute-start | bytes 786440 | tf_op jit(solution)/shard_map/ppermute | solution.py:335
  44.7 1.3 %collective-permute-start.4 = (bf16[256,512]{1,0:T(8,128)(2,1)S(1)}, bf16[256,512]{1,0:T(8,128)(2,1)S(1)}, u32[]{:S(2)}, u32[]{:S(2)}) collective-permute-start(bf16[256,512]{1,0:T(8,128)(2,1)S(1)} %shard_map.88.mine_ref), channel_id=1, source_target_pairs={{0,67},{1,66},{2,65},{3,64},{64,0},{65,1},{66,2},{67,3},{4,71},{5,... | collective-permute-start | bytes 786440 | tf_op jit(solution)/shard_map/ppermute | solution.py:334
  46.1 9.9 %collective-permute-done.7 = bf16[256,512]{1,0:T(8,128)(2,1)S(1)} collective-permute-done((bf16[256,512]{1,0:T(8,128)(2,1)S(1)}, bf16[256,512]{1,0:T(8,128)(2,1)S(1)}, u32[]{:S(2)}, u32[]{:S(2)}) %collective-permute-start.7) | collective-permute-done | bytes 262176 | tf_op jit(solution)/shard_map/ppermute | solution.py:324
  55.9 5.1 %collective-permute-done.8 = bf16[256,512]{1,0:T(8,128)(2,1)S(1)} collective-permute-done((bf16[256,512]{1,0:T(8,128)(2,1)S(1)}, bf16[256,512]{1,0:T(8,128)(2,1)S(1)}, u32[]{:S(2)}, u32[]{:S(2)}) %collective-permute-start.8) | collective-permute-done | bytes 262176 | tf_op jit(solution)/shard_map/ppermute | solution.py:324
  61.1 0.1 add_convert_fusion
  61.2 0.0 collective-permute-done.3.third_ref
  61.2 2.7 %collective-permute-start.9 = (bf16[256,1024]{1,0:T(8,128)(2,1)S(1)}, bf16[256,1024]{1,0:T(8,128)(2,1)S(1)}, u32[]{:S(2)}, u32[]{:S(2)}) collective-permute-start(bf16[256,1024]{1,0:T(8,128)(2,1)S(1)} %collective-permute-done.5.n1b_ref), channel_id=1, source_target_pairs={{0,64},{64,0},{1,65},{65,1},{2,66},{66,2},{3,67},{67,3},{4,68},{68... | collective-permute-start | bytes 1572872 | tf_op jit(solution)/shard_map/ppermute | solution.py:343
  63.9 0.3 collective-permute-start.11
  64.2 1.2 %collective-permute-done.9.f1b_ref = bf16[256,1024]{1,0:T(8,128)(2,1)S(1)} collective-permute-done((bf16[256,1024]{1,0:T(8,128)(2,1)S(1)}, bf16[256,1024]{1,0:T(8,128)(2,1)S(1)}, u32[]{:S(2)}, u32[]{:S(2)}) %collective-permute-start.9) | collective-permute-done | bytes 524320 | tf_op jit(solution)/shard_map/ppermute | solution.py:343
  65.5 1.2 %copy-done.3 = bf16[512,1024]{1,0:T(8,128)(2,1)S(1)} copy-done((bf16[512,1024]{1,0:T(8,128)(2,1)S(1)}, bf16[512,1024]{1,0:T(8,128)(2,1)}, u32[]{:S(2)}) %copy-start.3) | copy-done | bytes 1048600
  66.7 5.0 %shard_map.89 = (bf16[16,256,128]{2,1,0:T(8,128)(2,1)S(1)}, bf16[2,256,512]{2,1,0:T(8,128)(2,1)S(1)}) custom-call(bf16[256,512]{1,0:T(8,128)(2,1)S(1)} %shard_map.88.mine_ref, bf16[256,512]{1,0:T(8,128)(2,1)S(1)} %collective-permute-done.3.third_ref, bf16[256,512]{1,0:T(8,128)(2,1)S(1)} %collective-permute-done.4.cross_ref, bf16[512,1024]{1,0:T(8,128)(2,1)S(1)} %bitcast.14, ...), custom_call_target="tpu_custom_call" | custom-call | tf_op jit(solution)/shard_map/pallas_call | solution.py:172
  71.7 0.1 collective-permute-done.11
  71.8 0.1 pad_maximum_fusion.low_ref
  71.8 0.1 collective-permute-start.12
  71.9 0.7 copy-done.4
  72.7 4.3 %all-to-all-start.1 = ((bf16[16,256,128]{2,1,0:T(8,128)(2,1)}), bf16[16,256,128]{2,1,0:T(8,128)(2,1)}, u32[]{:S(2)}, u32[]{:S(2)}) async-start(bf16[16,256,128]{2,1,0:T(8,128)(2,1)} %copy-done.4), calls=%async_computation.1 | async-start | bytes 2097152 | tf_op jit(solution)/shard_map/all_to_all | solution.py:347
  77.0 16.0 %collective-permute-done.12.high_ref = bf16[2,256,512]{2,1,0:T(8,128)(2,1)} collective-permute-done((bf16[2,256,512]{2,1,0:T(8,128)(2,1)S(1)}, bf16[2,256,512]{2,1,0:T(8,128)(2,1)}, u32[]{:S(2)}, u32[]{:S(2)}) %collective-permute-start.12) | collective-permute-done | bytes 524320 | tf_op jit(solution)/shard_map/ppermute | solution.py:349
  93.0 3.0 %shard_map.90 = bf16[512,1024]{1,0:T(8,128)(2,1)} custom-call(bf16[2,256,512]{2,1,0:T(8,128)(2,1)S(1)} %get-tuple-element.35.near_ref, bf16[2,256,512]{2,1,0:T(8,128)(2,1)} %collective-permute-done.10.far_ref, bf16[2,256,512]{2,1,0:T(8,128)(2,1)S(1)} %pad_maximum_fusion.low_ref, bf16[2,256,512]{2,1,0:T(8,128)(2,1)} %collective-permute-done.12.high_ref), custom_call_target="tpu_custom_call" | custom-call | tf_op jit(solution)/shard_map/pallas_call | solution.py:250
  96.0 3.1 %collective-permute-start.13 = (bf16[512,1024]{1,0:T(8,128)(2,1)}, bf16[512,1024]{1,0:T(8,128)(2,1)}, u32[]{:S(2)}, u32[]{:S(2)}) collective-permute-start(bf16[512,1024]{1,0:T(8,128)(2,1)} %shard_map.90), channel_id=1, source_target_pairs={{0,64},{64,0},{1,65},{65,1},{2,66},{66,2},{3,67},{67,3},{4,68},{68... | collective-permute-start | bytes 3145736 | tf_op jit(solution)/shard_map/ppermute | solution.py:358
  99.2 1.4 %reduce_sum.22 = bf16[256,128]{1,0:T(8,128)(2,1)S(1)} reduce(bf16[16,256,128]{2,1,0:T(8,128)(2,1)} %all-to-all-done.1, bf16[]{:T(256)} %constant.25.clone.1), dimensions={0}, to_apply=%region_1.2 | reduce | flops 491520 | bytes 1114114 | tf_op jit(solution)/shard_map/reduce_sum | solution.py:354
  100.5 4.2 %collective-permute-start.14 = (bf16[256,128]{1,0:T(8,128)(2,1)S(1)}, bf16[256,128]{1,0:T(8,128)(2,1)S(1)}, u32[]{:S(2)}, u32[]{:S(2)}) collective-permute-start(bf16[256,128]{1,0:T(8,128)(2,1)S(1)} %reduce_sum.22), channel_id=1, source_target_pairs={{0,0},{1,1},{2,64},{3,65},{64,2},{65,3},{66,66},{67,67},{4,4},{5,5... | collective-permute-start | bytes 196616 | tf_op jit(solution)/shard_map/ppermute | solution.py:357
  104.7 0.1 collective-permute-start.15
  104.8 0.1 collective-permute-start.16
  104.9 3.7 %collective-permute-start.17 = (bf16[256,128]{1,0:T(8,128)(2,1)S(1)}, bf16[256,128]{1,0:T(8,128)(2,1)S(1)}, u32[]{:S(2)}, u32[]{:S(2)}) collective-permute-start(bf16[256,128]{1,0:T(8,128)(2,1)S(1)} %reduce_sum.22), channel_id=1, source_target_pairs={{0,3},{1,2},{2,67},{3,66},{64,1},{65,0},{66,65},{67,64},{4,7},{5,6... | collective-permute-start | bytes 196616 | tf_op jit(solution)/shard_map/ppermute | solution.py:357
  108.6 2.3 %collective-permute-done.15.b_ref = bf16[256,128]{1,0:T(8,128)(2,1)S(1)} collective-permute-done((bf16[256,128]{1,0:T(8,128)(2,1)S(1)}, bf16[256,128]{1,0:T(8,128)(2,1)S(1)}, u32[]{:S(2)}, u32[]{:S(2)}) %collective-permute-start.15) | collective-permute-done | bytes 65568 | tf_op jit(solution)/shard_map/ppermute | solution.py:357
  110.9 1.6 %shard_map.92 = f32[128,1024]{1,0:T(8,128)} custom-call(bf16[256,128]{1,0:T(8,128)(2,1)S(1)} %collective-permute-done.14.a_ref, bf16[256,128]{1,0:T(8,128)(2,1)S(1)} %collective-permute-done.15.b_ref, bf16[256,128]{1,0:T(8,128)(2,1)S(1)} %collective-permute-done.16.c_ref, bf16[256,128]{1,0:T(8,128)(2,1)S(1)} %collective-permute-done.17.d_ref, ...), custom_call_target="tpu_custom_call" | custom-call | tf_op jit(solution)/shard_map/pallas_call | solution.py:278
  112.6 3.4 %shard_map.91 = bf16[512,1024]{1,0:T(8,128)(2,1)} custom-call(bf16[2,256,512]{2,1,0:T(8,128)(2,1)S(1)} %get-tuple-element.35.near_ref, bf16[2,256,512]{2,1,0:T(8,128)(2,1)} %collective-permute-done.10.far_ref, bf16[2,256,512]{2,1,0:T(8,128)(2,1)S(1)} %pad_maximum_fusion.low_ref, bf16[2,256,512]{2,1,0:T(8,128)(2,1)} %collective-permute-done.12.high_ref, ...), custom_call_target="tpu_custom_call" | custom-call | tf_op jit(solution)/shard_map/pallas_call | solution.py:250
  (29 shorter events, 0.1 us)
Async XLA Ops:
  0.6 16.8 %collective-permute-start.1 = (bf16[512,1024]{1,0:T(8,128)(2,1)}, bf16[512,1024]{1,0:T(8,128)(2,1)S(1)}, u32[]{:S(2)}, u32[]{:S(2)}) collective-permute-start(bf16[512,1024]{1,0:T(8,128)(2,1)} %bitcast.12), channel_id=1, source_target_pairs={{0,64},{64,0},{1,65},{65,1},{2,66},{66,2},{3,67},{67,3},{4,68},{68... | collective-permute-start | bytes 3145736 | tf_op jit(solution)/shard_map/ppermute | solution.py:312
  3.2 14.2 %collective-permute-start = (bf16[256,1024]{1,0:T(8,128)(2,1)S(1)}, bf16[256,1024]{1,0:T(8,128)(2,1)S(1)}, u32[]{:S(2)}, u32[]{:S(2)}) collective-permute-start(bf16[256,1024]{1,0:T(8,128)(2,1)S(1)} %slice_bitcast_fusion), channel_id=1, source_target_pairs={{0,1},{1,0},{2,3},{3,2},{4,5},{5,4},{6,7},{7,6},{8,9},{9,8},{10,11... | collective-permute-start | bytes 1572872 | tf_op jit(solution)/shard_map/ppermute | solution.py:313
  9.7 17.4 %copy-start.8 = (s32[1,8192]{1,0:T(1,128)S(1)}, s32[1,8192]{1,0:T(1,128)}, u32[]{:S(2)}) copy-start(s32[1,8192]{1,0:T(1,128)} %param.8) | copy-start | bytes 98308
  9.7 28.2 %copy-start = (bf16[1,512,1024]{2,1,0:T(8,128)(2,1)S(1)}, bf16[1,512,1024]{2,1,0:T(8,128)(2,1)}, u32[]{:S(2)}) copy-start(bf16[1,512,1024]{2,1,0:T(8,128)(2,1)} %param.10) | copy-start | bytes 3145732
  17.4 20.6 %copy-start.10 = (bf16[256,512]{1,0:T(8,128)(2,1)S(1)}, bf16[256,512]{1,0:T(8,128)(2,1)}, u32[]{:S(2)}) copy-start(bf16[256,512]{1,0:T(8,128)(2,1)} %get-tuple-element.30) | copy-start | bytes 786436
  17.4 23.1 %copy-start.9 = (bf16[256,512]{1,0:T(8,128)(2,1)S(1)}, bf16[256,512]{1,0:T(8,128)(2,1)}, u32[]{:S(2)}) copy-start(bf16[256,512]{1,0:T(8,128)(2,1)} %get-tuple-element.32) | copy-start | bytes 786436
  17.4 43.6 %copy-start.7 = (bf16[256,512]{1,0:T(8,128)(2,1)S(1)}, bf16[256,512]{1,0:T(8,128)(2,1)}, u32[]{:S(2)}) copy-start(bf16[256,512]{1,0:T(8,128)(2,1)} %get-tuple-element.26) | copy-start | bytes 786436
  17.5 1.0 copy-start.2
  18.4 19.5 %all-to-all-start = ((bf16[16,72,256]{2,1,0:T(8,128)(2,1)}), bf16[16,72,256]{2,1,0:T(8,128)(2,1)S(1)}, u32[]{:S(2)}, u32[]{:S(2)}) async-start(bf16[16,72,256]{2,1,0:T(8,128)(2,1)} %bitcast.6), calls=%async_computation | async-start | bytes 1179648 | tf_op jit(solution)/shard_map/all_to_all | solution.py:319
  26.4 2.2 %collective-permute-start.2 = (bf16[256,1024]{1,0:T(8,128)(2,1)S(1)}, bf16[256,1024]{1,0:T(8,128)(2,1)S(1)}, u32[]{:S(2)}, u32[]{:S(2)}) collective-permute-start(bf16[256,1024]{1,0:T(8,128)(2,1)S(1)} %collective-permute-done.n1a_ref), channel_id=1, source_target_pairs={{0,64},{64,0},{1,65},{65,1},{2,66},{66,2},{3,67},{67,3},{4,68},{68... | collective-permute-start | bytes 1572872 | tf_op jit(solution)/shard_map/ppermute | solution.py:329
  27.3 17.4 %collective-permute-start.6 = (bf16[256,512]{1,0:T(8,128)(2,1)}, bf16[256,512]{1,0:T(8,128)(2,1)S(1)}, u32[]{:S(2)}, u32[]{:S(2)}) collective-permute-start(bf16[256,512]{1,0:T(8,128)(2,1)} %get-tuple-element.28), channel_id=1, source_target_pairs={{0,1},{1,2},{2,3},{3,0},{4,5},{5,6},{6,7},{7,4},{8,9},{9,10},{10,1... | collective-permute-start | bytes 786440 | tf_op jit(solution)/shard_map/ppermute | solution.py:324
  28.6 0.8 copy-start.5
  37.9 27.5 %copy-start.6 = (bf16[256,1024]{1,0:T(8,128)(2,1)S(1)}, bf16[256,1024]{1,0:T(8,128)(2,1)}, u32[]{:S(2)}) copy-start(bf16[256,1024]{1,0:T(8,128)(2,1)} %copy-done.5) | copy-start | bytes 1572868
  38.0 23.3 %collective-permute-start.5 = (bf16[256,1024]{1,0:T(8,128)(2,1)S(1)}, bf16[256,1024]{1,0:T(8,128)(2,1)S(1)}, u32[]{:S(2)}, u32[]{:S(2)}) collective-permute-start(bf16[256,1024]{1,0:T(8,128)(2,1)S(1)} %slice.11), channel_id=1, source_target_pairs={{0,1},{1,0},{2,3},{3,2},{4,5},{5,4},{6,7},{7,6},{8,9},{9,8},{10,11... | collective-permute-start | bytes 1572872 | tf_op jit(solution)/shard_map/ppermute | solution.py:332
  38.1 17.9 %collective-permute-start.7 = (bf16[256,512]{1,0:T(8,128)(2,1)S(1)}, bf16[256,512]{1,0:T(8,128)(2,1)S(1)}, u32[]{:S(2)}, u32[]{:S(2)}) collective-permute-start(bf16[256,512]{1,0:T(8,128)(2,1)S(1)} %copy-done.10), channel_id=1, source_target_pairs={{0,2},{1,3},{2,0},{3,1},{4,6},{5,7},{6,4},{7,5},{8,10},{9,11},{10,... | collective-permute-start | bytes 786440 | tf_op jit(solution)/shard_map/ppermute | solution.py:324
  40.6 20.5 %collective-permute-start.8 = (bf16[256,512]{1,0:T(8,128)(2,1)S(1)}, bf16[256,512]{1,0:T(8,128)(2,1)S(1)}, u32[]{:S(2)}, u32[]{:S(2)}) collective-permute-start(bf16[256,512]{1,0:T(8,128)(2,1)S(1)} %copy-done.9), channel_id=1, source_target_pairs={{0,3},{1,0},{2,1},{3,2},{4,7},{5,4},{6,5},{7,6},{8,11},{9,8},{10,9... | collective-permute-start | bytes 786440 | tf_op jit(solution)/shard_map/ppermute | solution.py:324
  42.8 18.4 %collective-permute-start.3 = (bf16[256,512]{1,0:T(8,128)(2,1)S(1)}, bf16[256,512]{1,0:T(8,128)(2,1)S(1)}, u32[]{:S(2)}, u32[]{:S(2)}) collective-permute-start(bf16[256,512]{1,0:T(8,128)(2,1)S(1)} %shard_map.88.mine_ref), channel_id=1, source_target_pairs={{64,67},{65,66},{66,65},{67,64},{68,71},{69,70},{70,69},{71,68},{7... | collective-permute-start | bytes 786440 | tf_op jit(solution)/shard_map/ppermute | solution.py:335
  44.7 16.5 %collective-permute-start.4 = (bf16[256,512]{1,0:T(8,128)(2,1)S(1)}, bf16[256,512]{1,0:T(8,128)(2,1)S(1)}, u32[]{:S(2)}, u32[]{:S(2)}) collective-permute-start(bf16[256,512]{1,0:T(8,128)(2,1)S(1)} %shard_map.88.mine_ref), channel_id=1, source_target_pairs={{0,67},{1,66},{2,65},{3,64},{64,0},{65,1},{66,2},{67,3},{4,71},{5,... | collective-permute-start | bytes 786440 | tf_op jit(solution)/shard_map/ppermute | solution.py:334
  61.2 4.2 %collective-permute-start.9 = (bf16[256,1024]{1,0:T(8,128)(2,1)S(1)}, bf16[256,1024]{1,0:T(8,128)(2,1)S(1)}, u32[]{:S(2)}, u32[]{:S(2)}) collective-permute-start(bf16[256,1024]{1,0:T(8,128)(2,1)S(1)} %collective-permute-done.5.n1b_ref), channel_id=1, source_target_pairs={{0,64},{64,0},{1,65},{65,1},{2,66},{66,2},{3,67},{67,3},{4,68},{68... | collective-permute-start | bytes 1572872 | tf_op jit(solution)/shard_map/ppermute | solution.py:343
  63.9 7.9 %collective-permute-start.11 = (bf16[256,512]{1,0:T(8,128)(2,1)S(1)}, bf16[256,512]{1,0:T(8,128)(2,1)S(1)}, u32[]{:S(2)}, u32[]{:S(2)}) collective-permute-start(bf16[256,512]{1,0:T(8,128)(2,1)S(1)} %add_convert_fusion), channel_id=1, source_target_pairs={{0,4},{4,0},{8,12},{12,8},{16,20},{20,16},{24,28},{28,24},{32,36},... | collective-permute-start | bytes 786440 | tf_op jit(solution)/shard_map/ppermute | solution.py:344
  65.4 1.2 %copy-start.3 = (bf16[512,1024]{1,0:T(8,128)(2,1)S(1)}, bf16[512,1024]{1,0:T(8,128)(2,1)}, u32[]{:S(2)}) copy-start(bf16[512,1024]{1,0:T(8,128)(2,1)} %copy-done.2) | copy-start | bytes 3145732
  71.7 1.0 copy-start.4
  71.8 21.2 %collective-permute-start.12 = (bf16[2,256,512]{2,1,0:T(8,128)(2,1)S(1)}, bf16[2,256,512]{2,1,0:T(8,128)(2,1)}, u32[]{:S(2)}, u32[]{:S(2)}) collective-permute-start(bf16[2,256,512]{2,1,0:T(8,128)(2,1)S(1)} %pad_maximum_fusion.low_ref), channel_id=1, source_target_pairs={{0,16},{4,20},{8,24},{12,28},{16,0},{20,4},{24,8},{28,12},{32,48},... | collective-permute-start | bytes 1572872 | tf_op jit(solution)/shard_map/ppermute | solution.py:349
  72.7 20.4 %collective-permute-start.10 = (bf16[2,256,512]{2,1,0:T(8,128)(2,1)S(1)}, bf16[2,256,512]{2,1,0:T(8,128)(2,1)}, u32[]{:S(2)}, u32[]{:S(2)}) collective-permute-start(bf16[2,256,512]{2,1,0:T(8,128)(2,1)S(1)} %get-tuple-element.35.near_ref), channel_id=1, source_target_pairs={{0,1},{1,0},{2,3},{3,2},{4,5},{5,4},{6,7},{7,6},{8,9},{9,8},{10,11... | collective-permute-start | bytes 1572872 | tf_op jit(solution)/shard_map/ppermute | solution.py:351
  72.7 26.5 %all-to-all-start.1 = ((bf16[16,256,128]{2,1,0:T(8,128)(2,1)}), bf16[16,256,128]{2,1,0:T(8,128)(2,1)}, u32[]{:S(2)}, u32[]{:S(2)}) async-start(bf16[16,256,128]{2,1,0:T(8,128)(2,1)} %copy-done.4), calls=%async_computation.1 | async-start | bytes 2097152 | tf_op jit(solution)/shard_map/all_to_all | solution.py:347
  77.0 33.9 %copy-start.1 = (bf16[1024,1024]{1,0:T(8,128)(2,1)S(1)}, bf16[1024,1024]{1,0:T(8,128)(2,1)}, u32[]{:S(2)}) copy-start(bf16[1024,1024]{1,0:T(8,128)(2,1)} %get-tuple-element.22.w_ref) | copy-start | bytes 6291460
  96.0 16.5 %collective-permute-start.13 = (bf16[512,1024]{1,0:T(8,128)(2,1)}, bf16[512,1024]{1,0:T(8,128)(2,1)}, u32[]{:S(2)}, u32[]{:S(2)}) collective-permute-start(bf16[512,1024]{1,0:T(8,128)(2,1)} %shard_map.90), channel_id=1, source_target_pairs={{0,64},{64,0},{1,65},{65,1},{2,66},{66,2},{3,67},{67,3},{4,68},{68... | collective-permute-start | bytes 3145736 | tf_op jit(solution)/shard_map/ppermute | solution.py:358
  100.5 8.1 %collective-permute-start.14 = (bf16[256,128]{1,0:T(8,128)(2,1)S(1)}, bf16[256,128]{1,0:T(8,128)(2,1)S(1)}, u32[]{:S(2)}, u32[]{:S(2)}) collective-permute-start(bf16[256,128]{1,0:T(8,128)(2,1)S(1)} %reduce_sum.22), channel_id=1, source_target_pairs={{0,0},{1,1},{2,64},{3,65},{64,2},{65,3},{66,66},{67,67},{4,4},{5,5... | collective-permute-start | bytes 196616 | tf_op jit(solution)/shard_map/ppermute | solution.py:357
  104.7 6.2 %collective-permute-start.15 = (bf16[256,128]{1,0:T(8,128)(2,1)S(1)}, bf16[256,128]{1,0:T(8,128)(2,1)S(1)}, u32[]{:S(2)}, u32[]{:S(2)}) collective-permute-start(bf16[256,128]{1,0:T(8,128)(2,1)S(1)} %reduce_sum.22), channel_id=1, source_target_pairs={{0,1},{1,0},{2,65},{3,64},{64,3},{65,2},{66,67},{67,66},{4,5},{5,4... | collective-permute-start | bytes 196616 | tf_op jit(solution)/shard_map/ppermute | solution.py:357
  104.8 6.1 %collective-permute-start.16 = (bf16[256,128]{1,0:T(8,128)(2,1)S(1)}, bf16[256,128]{1,0:T(8,128)(2,1)S(1)}, u32[]{:S(2)}, u32[]{:S(2)}) collective-permute-start(bf16[256,128]{1,0:T(8,128)(2,1)S(1)} %reduce_sum.22), channel_id=1, source_target_pairs={{0,2},{1,3},{2,66},{3,67},{64,0},{65,1},{66,64},{67,65},{4,6},{5,7... | collective-permute-start | bytes 196616 | tf_op jit(solution)/shard_map/ppermute | solution.py:357
  104.9 6.0 %collective-permute-start.17 = (bf16[256,128]{1,0:T(8,128)(2,1)S(1)}, bf16[256,128]{1,0:T(8,128)(2,1)S(1)}, u32[]{:S(2)}, u32[]{:S(2)}) collective-permute-start(bf16[256,128]{1,0:T(8,128)(2,1)S(1)} %reduce_sum.22), channel_id=1, source_target_pairs={{0,3},{1,2},{2,67},{3,66},{64,1},{65,0},{66,65},{67,64},{4,7},{5,6... | collective-permute-start | bytes 196616 | tf_op jit(solution)/shard_map/ppermute | solution.py:357

commit v6 on v5

--- a/solution.py
+++ b/solution.py
@@ -13,7 +13,7 @@
 WIN = 9
 SLOT = WIN * SUB
 SIDE = 4
-CUT = 256
+CUT = 320
 VMEM = 24 * 1024 * 1024
 WIDE = 56 * 1024 * 1024
 
@@ -182,76 +182,93 @@
     )(*sums, *columns)
 
 
-def quarter():
+def eighth():
     ctx = lax.axis_index("context")
-    return 2 * lax.rem(lax.div(ctx, SIDE), 2) + lax.rem(ctx, 2)
-
-
-def chain_kernel(value_ref, out_w_ref, global_ref, both_ref, p0_ref, p1_ref, p2_ref, p3_ref, held_ref, sems):
-    rows, wide = p0_ref.shape
-    parts = held_ref.shape[0]
+    return 2 * lax.div(ctx, SIDE) + lax.rem(ctx, 2)
+
+
+def flip(a, b):
+    return a + b - 2 * b * lax.rem(a, 2)
+
+
+def chain_kernel(value_ref, out_w_ref, global_ref, both_ref, own_ref, pair_ref, away_ref, held_ref, sems):
+    rows, wide = own_ref.shape
     dp, ten = lax.axis_index("dp"), lax.axis_index("tensor")
+    targets = (ten, flip(ten, 1), 3 - ten, flip(3 - ten, 1))
     copies = []
-    for s in range(parts):
-        at = (lax.rem(ten + s, parts) * 4 + quarter()) * rows
+    for s, target in enumerate(targets):
+        at = (target * 8 + eighth()) * rows
         copy = pltpu.make_async_copy(global_ref.at[pl.ds(pl.multiple_of(at, rows), rows)], held_ref.at[s], sems.at[s])
         copy.start()
         copies.append(copy)
     both_ref[...] = jnp.dot(
         value_ref[...], out_w_ref[...], preferred_element_type=jnp.float32
     ).astype(jnp.bfloat16)
-    for s, p in enumerate((p0_ref, p1_ref, p2_ref, p3_ref)):
+    for s in range(0, 4, 2):
         copies[s].wait()
-        half = lax.div(lax.rem(ten + s, parts), 2)
-        half = dp + half - 2 * dp * half
+        copies[s + 1].wait()
+        half = flip(dp, lax.div(targets[s], 2))
         cols = pl.ds(pl.multiple_of(half * wide, wide), wide)
-        p[...] = jnp.dot(held_ref[s], both_ref[:, cols], preferred_element_type=jnp.float32).astype(jnp.bfloat16)
-
-
-def chain_terms(w_value, w_out, w_global, parts):
+        left = jnp.concatenate([held_ref[s], held_ref[s + 1]], axis=0)
+        total = jnp.dot(left, both_ref[:, cols], preferred_element_type=jnp.float32).astype(jnp.bfloat16)
+        if s == 0:
+            own_ref[...] = total[:rows]
+            pair_ref[...] = total[rows:]
+        else:
+            away_ref[0] = total[:rows]
+            away_ref[1] = total[rows:]
+
+
+def chain_terms(w_value, w_out, w_global):
     deep, feats = w_value.shape
-    rows = w_global.shape[0] // parts // 4
-    vmem = pl.BlockSpec(memory_space=pltpu.VMEM)
+    rows = w_global.shape[0] // 32
+    vmem = pl.BlockSpec(memory_space=pltpu.VMEM)
+    part = jax.ShapeDtypeStruct((rows, feats // 2), jnp.bfloat16)
     return pl.pallas_call(
         chain_kernel,
         in_specs=[vmem, vmem, pl.BlockSpec(memory_space=pl.ANY)],
-        out_specs=[vmem] * (1 + parts),
-        out_shape=[jax.ShapeDtypeStruct((deep, feats), jnp.bfloat16)]
-        + [jax.ShapeDtypeStruct((rows, feats // 2), jnp.bfloat16)] * parts,
-        scratch_shapes=[pltpu.VMEM((parts, rows, deep), jnp.bfloat16), pltpu.SemaphoreType.DMA((parts,))],
+        out_specs=[vmem] * 4,
+        out_shape=[
+            jax.ShapeDtypeStruct((deep, feats), jnp.bfloat16),
+            part,
+            part,
+            jax.ShapeDtypeStruct((2, rows, feats // 2), jnp.bfloat16),
+        ],
+        scratch_shapes=[pltpu.VMEM((4, rows, deep), jnp.bfloat16), pltpu.SemaphoreType.DMA((4,))],
         compiler_params=pltpu.CompilerParams(vmem_limit_bytes=WIDE),
     )(w_value, w_out, w_global)
 
 
 def rows_kernel(which, near_ref, far_ref, low_ref, high_ref, *rest):
-    out_ref = rest[-1]
+    out_ref, table_ref = rest[-2:]
     deep = near_ref.shape[1]
+    rows = low_ref.shape[2]
+    z, y = lax.div(eighth(), 2), lax.rem(eighth(), 2)
+    for ref, base in ((low_ref, z), (high_ref, SIDE - 1 - z)):
+        for i in range(2):
+            for j in range(2):
+                to = 2 * flip(base, i) + flip(y, j)
+                table_ref[pl.ds(pl.multiple_of(to * rows, rows), rows), :] = ref[i, j]
     odd = lax.rem(lax.axis_index("tensor") + lax.axis_index("dp"), 2)
-    near = near_ref[which].T
-    far = far_ref[which].T
-    rows = low_ref.shape[1]
-    for i, ref in enumerate((low_ref, high_ref)):
-        for j in range(2):
-            z, y = lax.div(quarter(), 2), lax.rem(quarter(), 2)
-            at = 2 * (z + i - 2 * i * z) + y + j - 2 * j * y
-            at = pl.ds(pl.multiple_of(at * rows, rows), rows)
-            first = ref[j, :, pl.ds(pl.multiple_of(odd * deep, deep), deep)]
-            second = ref[j, :, pl.ds(pl.multiple_of((1 - odd) * deep, deep), deep)]
-            dims = (((1,), (1,)), ((), ()))
-            total = lax.dot_general(near, first, dims, preferred_element_type=jnp.float32)
-            total += lax.dot_general(far, second, dims, preferred_element_type=jnp.float32)
-            if len(rest) > 1:
-                total += rest[0][:, at].astype(jnp.float32)
-            out_ref[:, at] = total.astype(jnp.bfloat16)
+    dims = (((1,), (1,)), ((), ()))
+    first = table_ref[:, pl.ds(pl.multiple_of(odd * deep, deep), deep)]
+    second = table_ref[:, pl.ds(pl.multiple_of((1 - odd) * deep, deep), deep)]
+    total = lax.dot_general(near_ref[which].T, first, dims, preferred_element_type=jnp.float32)
+    total += lax.dot_general(far_ref[which].T, second, dims, preferred_element_type=jnp.float32)
+    if len(rest) > 2:
+        total += rest[0][...].astype(jnp.float32)
+    out_ref[...] = total.astype(jnp.bfloat16)
 
 
 def context_rows(which, near, far, low, high, *back):
     vmem = pl.BlockSpec(memory_space=pltpu.VMEM)
+    cols, half = 8 * low.shape[2], low.shape[3]
     return pl.pallas_call(
         functools.partial(rows_kernel, which),
         in_specs=[vmem] * (4 + len(back)),
         out_specs=vmem,
-        out_shape=jax.ShapeDtypeStruct((near.shape[2], 4 * low.shape[1]), jnp.bfloat16),
+        out_shape=jax.ShapeDtypeStruct((near.shape[2], cols), jnp.bfloat16),
+        scratch_shapes=[pltpu.VMEM((cols, half), jnp.bfloat16)],
         compiler_params=pltpu.CompilerParams(vmem_limit_bytes=VMEM),
     )(near, far, low, high, *back)
 
@@ -312,41 +329,41 @@
     far0 = lax.ppermute(near0, "dp", swap)
     near1 = [lax.ppermute(near0[:CUT], "tensor", pair)]
 
-    outgoing = segment_sums(starts, owner, byte_grads[0], ctx_n, width)
-
-    both_t, *terms = chain_terms(after(w_value, outgoing), w_out, w_global, ten_n)
-    outgoing = after(outgoing, near1[0], both_t, far0)
+    def along(target):
+        return [
+            (i * SIDE + j, target(i, j)[0] * SIDE + target(i, j)[1]) for i in range(SIDE) for j in range(SIDE)
+        ]
+
+    both_t, own, paired, away = chain_terms(w_value, w_out, w_global)
+    away = lax.ppermute(away, "tensor", [(x, ten_n - 1 - x) for x in range(ten_n)])
+
+    outgoing = segment_sums(after(starts, both_t), owner, byte_grads[0], ctx_n, width)
+    outgoing = after(outgoing, near1[0], far0, away)
     incoming = lax.all_to_all(outgoing, "context", split_axis=0, concat_axis=0, tiled=True)
 
-    chain = terms[0].astype(f32)
-    for s in range(1, ten_n):
-        term = after(terms[s], outgoing)
-        chain += lax.ppermute(term, "tensor", [(x, (x + s) % ten_n) for x in range(ten_n)]).astype(f32)
-    chain = chain.astype(bf16)
+    away = after(away, outgoing)
+    paired = (paired.astype(f32) + away[1].astype(f32)).astype(bf16)
+    paired = lax.ppermute(paired, "tensor", pair)
+    chain = (own.astype(f32) + away[0].astype(f32) + paired.astype(f32)).astype(bf16)
+    chain = jnp.stack([chain, lax.ppermute(chain, "context", along(lambda i, j: (i, j ^ 1)))])
     edges = jnp.arange(ctx_n, dtype=jnp.int32) * bytes_n
     counts = jnp.sum((patch_starts[0][None, :] <= edges[:, None]).astype(jnp.int32), axis=1)
     first = jnp.minimum((counts - 1) // LANES, starts.shape[0] - WIN)
     far1 = [lax.ppermute(near1[0], "dp", swap)]
-    incoming = after(incoming, first, far1[0])
+    incoming = after(incoming, first, far1[0], chain)
 
     near1.append(lax.ppermute(after(near0, incoming)[CUT:], "tensor", pair))
     sums = collect(first, incoming, patch_rows)
     cross = lax.ppermute(sums, line, moves(lambda d, x: (0, x) if d == 1 else (1, ten_n - 1 - x)))
     third = lax.ppermute(sums, line, moves(lambda d, x: (1, ten_n - 1 - x) if d == 1 else None))
-
-    def along(target):
-        return [
-            (i * SIDE + j, target(i, j)[0] * SIDE + target(i, j)[1]) for i in range(SIDE) for j in range(SIDE)
-        ]
-
     chain = after(chain, sums)
-    far1.append(lax.ppermute(after(near1[1], cross, third, chain), "dp", swap))
-    other = lax.ppermute(chain, "context", along(lambda i, j: (i, j ^ 1)))
+    other = lax.ppermute(chain, "context", along(lambda i, j: (i ^ 1, j)))
+    far1.append(lax.ppermute(after(near1[1], cross, third), "dp", swap))
     columns = (near0, *near1, far0, *far1)
     partial, near = outer((sums, third, cross), columns)
     pieces = lax.all_to_all(partial, "context", split_axis=0, concat_axis=0, tiled=True)
     chain = jnp.stack([after(chain, partial), after(other, partial)])
-    rest = lax.ppermute(chain, "context", along(lambda i, j: (i ^ 1, j)))
+    rest = lax.ppermute(chain, "context", along(lambda i, j: (SIDE - 1 - i, j)))
 
     far = lax.ppermute(near, "tensor", pair)
     give = context_rows(1, near, far, chain, rest)

time: 117 us -> 110 us (0.940)
  waiting for transfers between devices: 43.3 us -> 39.3 us
  local copies, waits for them, and re-layouts: 4.86 us -> 3.24 us
  other arithmetic: 1.84 us -> 3.37 us
  Pallas kernels: 26.7 us -> 25.5 us
    all_to_all x1, waiting for transfers between devices: 8.52 us -> 0.46 us  [local(): lax.all_to_all(outgoing, 'context', split_axis=0, concat_axis=0, tiled=True)]
    ppermute x1, waiting for transfers between devices: 0.01 us -> 4.78 us  [local(): lax.ppermute(sums, line, moves(lambda d, x: (1, ten_n - 1 - x) if d == 1...]
    ppermute x6, waiting for transfers between devices: 32.3 us -> 28.3 us  [the longest x1 16.4 us: local(): rest = lax.ppermute(chain, 'context', along(lambda i, j: (SIDE - 1 - i, j)))]
    ppermute x1, waiting for transfers between devices: 0.01 us -> 2.54 us  [local(): lax.ppermute(sums, line, moves(lambda d, x: (0, x) if d == 1 else (1, ten...]
    ppermute x4, starting transfers between devices: 8.04 us -> 5.92 us  [local(): lax.ppermute(piece, line, moves(lambda d, x, s=s: (x // 2, 2 * d + x % 2...]
    ppermute x1, starting transfers between devices: 1.93 us -> 3.72 us  [local(): lax.ppermute(sums, line, moves(lambda d, x: (1, ten_n - 1 - x) if d == 1...]
    unnamed x22 -> x18, local copies, waits for them, and re-layouts: 3.75 us -> 2.09 us
    convert_element_type x1 -> x2, other arithmetic: 0.14 us -> 1.65 us  [the longest x1 0.96 us: local(): (own.astype(f32) + away[0].astype(f32) + paired.astype(f32)).astype(bf16)]
  transfers between devices with their start and end apart: 20 -> 20, of which waited for: 8 -> 10; matrix products, arithmetic and copies ran while one was open for 3% -> 3% of each run, Pallas kernels for 20% -> 20%
where the time goes in v6:
time: 110 us
  waiting for transfers between devices  39.3 us (36%)
  starting transfers between devices  37.2 us (34%)
  Pallas kernels  25.5 us (23%)
  other arithmetic  3.37 us (3%)
  local copies, waits for them, and re-layouts  3.24 us (3%)
    ppermute x1, waiting for transfers between devices, local(): rest = lax.ppermute(chain, 'context', along(lambda i, j: (SIDE - 1 - i, j)))  16.4 us
    ppermute x1, waiting for transfers between devices, local(): lax.ppermute(chain, 'context', along(lambda i, j: (i, j ^ 1)))  8.86 us
    all_to_all x1, starting transfers between devices, local(): lax.all_to_all(outgoing, 'context', split_axis=0, concat_axis=0, tiled=True)  7.77 us
    pallas_call x1, Pallas kernels, chain_terms(): pl.pallas_call(chain_kernel, in_specs=[vmem, vmem, pl.BlockSpec(memory_sp...  6.54 us
    pallas_call x2, Pallas kernels, context_rows(): pl.pallas_call(functools.partial(rows_kernel, which), in_specs=[vmem] * (...  6.37 us
    ppermute x4, starting transfers between devices, local(): lax.ppermute(piece, line, moves(lambda d, x, s=s: (x // 2, 2 * d + x % 2...  5.92 us
    pallas_call x1, Pallas kernels, segment_sums(): pl.pallas_call(seg_kernel, in_specs=[vmem, vmem, pl.BlockSpec(memory_spac...  5.12 us
    pallas_call x1, Pallas kernels, outer(): pl.pallas_call(outer_kernel, in_specs=[vmem] * (len(sums) + len(columns))...  5.02 us
  transfers between devices with their start and end apart: 20, of which 10 were waited for; matrix products, arithmetic and copies ran while one was open for 3% of the time, Pallas kernels for 20%

profile of v6, /device:TPU:1, one launch (start us, length us, event | category | flops | bytes accessed | tf_op | source)
XLA Modules:
  0.0 109.5 jit_solution(14100113207527948753)
XLA Ops:
  0.6 1.5 %collective-permute-start.1 = (bf16[512,1024]{1,0:T(8,128)(2,1)}, bf16[512,1024]{1,0:T(8,128)(2,1)S(1)}, u32[]{:S(2)}, u32[]{:S(2)}) collective-permute-start(bf16[512,1024]{1,0:T(8,128)(2,1)} %bitcast.20), channel_id=1, source_target_pairs={{0,64},{64,0},{1,65},{65,1},{2,66},{66,2},{3,67},{67,3},{4,68},{68... | collective-permute-start | bytes 3145736 | tf_op jit(solution)/shard_map/ppermute | solution.py:329
  2.1 1.1 %slice_bitcast_fusion = bf16[320,1024]{1,0:T(8,128)(2,1)S(1)} fusion(bf16[1,512,1024]{2,1,0:T(8,128)(2,1)} %param.10), kind=kLoop, calls=%fused_computation | loop fusion | bytes 1310720 | tf_op jit(solution)/shard_map/slice | solution.py:330
  3.3 1.4 %collective-permute-start = (bf16[320,1024]{1,0:T(8,128)(2,1)S(1)}, bf16[320,1024]{1,0:T(8,128)(2,1)S(1)}, u32[]{:S(2)}, u32[]{:S(2)}) collective-permute-start(bf16[320,1024]{1,0:T(8,128)(2,1)S(1)} %slice_bitcast_fusion), channel_id=1, source_target_pairs={{0,1},{1,0},{2,3},{3,2},{4,5},{5,4},{6,7},{7,6},{8,9},{9,8},{10,11... | collective-permute-start | bytes 1966088 | tf_op jit(solution)/shard_map/ppermute | solution.py:330
  4.6 6.5 %shard_map.86 = (bf16[1024,1024]{1,0:T(8,128)(2,1)}, bf16[128,512]{1,0:T(8,128)(2,1)}, bf16[128,512]{1,0:T(8,128)(2,1)}, bf16[2,128,512]{2,1,0:T(8,128)(2,1)}) custom-call(bf16[1024,1024]{1,0:T(8,128)(2,1)} %value_ref.1, bf16[1024,1024]{1,0:T(8,128)(2,1)} %out_w_ref.1, bf16[4096,1024]{1,0:T(8,128)(2,1)} %global_ref.1), custom_call_target="tpu_custom_call" | custom-call | tf_op jit(solution)/shard_map/pallas_call | solution.py:227
  11.2 1.9 %collective-permute-start.2 = (bf16[2,128,512]{2,1,0:T(8,128)(2,1)}, bf16[2,128,512]{2,1,0:T(8,128)(2,1)S(1)}, u32[]{:S(2)}, u32[]{:S(2)}) collective-permute-start(bf16[2,128,512]{2,1,0:T(8,128)(2,1)} %get-tuple-element.20), channel_id=1, source_target_pairs={{0,3},{1,2},{2,1},{3,0},{4,7},{5,6},{6,5},{7,4},{8,11},{9,10},{10,... | collective-permute-start | bytes 786440 | tf_op jit(solution)/shard_map/ppermute | solution.py:338
  13.1 5.1 %shard_map.87 = bf16[1152,256]{1,0:T(8,128)(2,1)} custom-call(s32[64,128]{1,0:T(8,128)} %bitcast.30, s32[64,128]{1,0:T(8,128)} %bitcast.33, bf16[4096,1024]{1,0:T(8,128)(2,1)} %bitcast.24), custom_call_target="tpu_custom_call" | custom-call | tf_op jit(solution)/shard_map/pallas_call | solution.py:94
  18.2 0.0 copy-start
  18.2 2.1 %collective-permute-done.2 = bf16[2,128,512]{2,1,0:T(8,128)(2,1)S(1)} collective-permute-done((bf16[2,128,512]{2,1,0:T(8,128)(2,1)}, bf16[2,128,512]{2,1,0:T(8,128)(2,1)S(1)}, u32[]{:S(2)}, u32[]{:S(2)}) %collective-permute-start.2) | collective-permute-done | bytes 262176 | tf_op jit(solution)/shard_map/ppermute | solution.py:338
  20.3 0.0 collective-permute-done.n1a_ref
  20.3 0.0 collective-permute-done.1.f0_ref
  20.3 1.0 copy-done.2
  21.3 0.7 fusion
  22.0 0.7 collective-permute-start.4
  22.7 1.1 collective-permute-start.3
  23.7 0.3 convert_reduce_fusion
  24.0 7.8 %all-to-all-start = ((bf16[16,72,256]{2,1,0:T(8,128)(2,1)}), bf16[16,72,256]{2,1,0:T(8,128)(2,1)S(1)}, u32[]{:S(2)}, u32[]{:S(2)}) async-start(bf16[16,72,256]{2,1,0:T(8,128)(2,1)} %bitcast.25), calls=%async_computation | async-start | bytes 1179648 | tf_op jit(solution)/shard_map/all_to_all | solution.py:342
  31.8 0.0 collective-permute-done.4
  31.8 1.0 fusion.2
  32.8 1.4 %collective-permute-start.5 = (bf16[128,512]{1,0:T(8,128)(2,1)S(1)}, bf16[128,512]{1,0:T(8,128)(2,1)S(1)}, u32[]{:S(2)}, u32[]{:S(2)}) collective-permute-start(bf16[128,512]{1,0:T(8,128)(2,1)S(1)} %fusion.2), channel_id=1, source_target_pairs={{0,4},{4,0},{8,12},{12,8},{16,20},{20,16},{24,28},{28,24},{32,36},... | collective-permute-start | bytes 393224 | tf_op jit(solution)/shard_map/ppermute | solution.py:348
  34.2 8.9 %collective-permute-done.5 = bf16[128,512]{1,0:T(8,128)(2,1)S(1)} collective-permute-done((bf16[128,512]{1,0:T(8,128)(2,1)S(1)}, bf16[128,512]{1,0:T(8,128)(2,1)S(1)}, u32[]{:S(2)}, u32[]{:S(2)}) %collective-permute-start.5) | collective-permute-done | bytes 131104 | tf_op jit(solution)/shard_map/ppermute | solution.py:348
  43.1 0.0 collective-permute-done.3.f1a_ref
  43.1 0.5 all-to-all-done
  43.6 1.2 %collective-permute-start.8 = (bf16[192,1024]{1,0:T(8,128)(2,1)S(1)}, bf16[192,1024]{1,0:T(8,128)(2,1)S(1)}, u32[]{:S(2)}, u32[]{:S(2)}) collective-permute-start(bf16[192,1024]{1,0:T(8,128)(2,1)S(1)} %slice.19), channel_id=1, source_target_pairs={{0,1},{1,0},{2,3},{3,2},{4,5},{5,4},{6,7},{7,6},{8,9},{9,8},{10,11... | collective-permute-start | bytes 1179656 | tf_op jit(solution)/shard_map/ppermute | solution.py:355
  44.8 0.9 shard_map.88.mine_ref
  45.7 3.7 %collective-permute-start.6 = (bf16[256,512]{1,0:T(8,128)(2,1)S(1)}, bf16[256,512]{1,0:T(8,128)(2,1)S(1)}, u32[]{:S(2)}, u32[]{:S(2)}) collective-permute-start(bf16[256,512]{1,0:T(8,128)(2,1)S(1)} %shard_map.88.mine_ref), channel_id=1, source_target_pairs={{64,67},{65,66},{66,65},{67,64},{68,71},{69,70},{70,69},{71,68},{7... | collective-permute-start | bytes 786440 | tf_op jit(solution)/shard_map/ppermute | solution.py:358
  49.4 0.1 collective-permute-start.7
  49.5 4.8 %collective-permute-done.6.third_ref = bf16[256,512]{1,0:T(8,128)(2,1)S(1)} collective-permute-done((bf16[256,512]{1,0:T(8,128)(2,1)S(1)}, bf16[256,512]{1,0:T(8,128)(2,1)S(1)}, u32[]{:S(2)}, u32[]{:S(2)}) %collective-permute-start.6) | collective-permute-done | bytes 262176 | tf_op jit(solution)/shard_map/ppermute | solution.py:358
  54.2 2.5 %collective-permute-done.7.cross_ref = bf16[256,512]{1,0:T(8,128)(2,1)S(1)} collective-permute-done((bf16[256,512]{1,0:T(8,128)(2,1)S(1)}, bf16[256,512]{1,0:T(8,128)(2,1)S(1)}, u32[]{:S(2)}, u32[]{:S(2)}) %collective-permute-start.7) | collective-permute-done | bytes 262176 | tf_op jit(solution)/shard_map/ppermute | solution.py:357
  56.8 0.8 collective-permute-start.11
  57.6 1.0 collective-permute-done.9.f1b_ref
  58.5 1.1 copy-done.6
  59.6 5.0 %shard_map.89 = (bf16[16,256,128]{2,1,0:T(8,128)(2,1)S(1)}, bf16[2,256,512]{2,1,0:T(8,128)(2,1)S(1)}) custom-call(bf16[256,512]{1,0:T(8,128)(2,1)S(1)} %shard_map.88.mine_ref, bf16[256,512]{1,0:T(8,128)(2,1)S(1)} %collective-permute-done.6.third_ref, bf16[256,512]{1,0:T(8,128)(2,1)S(1)} %collective-permute-done.7.cross_ref, bf16[512,1024]{1,0:T(8,128)(2,1)S(1)} %bitcast.22, ...), custom_call_target="tpu_custom_call" | custom-call | tf_op jit(solution)/shard_map/pallas_call | solution.py:172
  64.7 0.1 pad_maximum_fusion.low_ref
  64.7 2.0 %collective-permute-start.12 = (bf16[2,2,128,512]{3,2,1,0:T(8,128)(2,1)S(1)}, bf16[2,2,128,512]{3,2,1,0:T(8,128)(2,1)}, u32[]{:S(2)}, u32[]{:S(2)}) collective-permute-start(bf16[2,2,128,512]{3,2,1,0:T(8,128)(2,1)S(1)} %pad_maximum_fusion.low_ref), channel_id=1, source_target_pairs={{0,48},{4,52},{8,56},{12,60},{16,32},{20,36},{24,40},{28,44},{32,1... | collective-permute-start | bytes 1572872 | tf_op jit(solution)/shard_map/ppermute | solution.py:366
  66.8 4.6 %all-to-all-start.1 = ((bf16[16,256,128]{2,1,0:T(8,128)(2,1)}), bf16[16,256,128]{2,1,0:T(8,128)(2,1)}, u32[]{:S(2)}, u32[]{:S(2)}) async-start(bf16[16,256,128]{2,1,0:T(8,128)(2,1)} %copy-done.4), calls=%async_computation.1 | async-start | bytes 2097152 | tf_op jit(solution)/shard_map/all_to_all | solution.py:364
  71.4 16.4 %collective-permute-done.12.high_ref = bf16[2,2,128,512]{3,2,1,0:T(8,128)(2,1)} collective-permute-done((bf16[2,2,128,512]{3,2,1,0:T(8,128)(2,1)S(1)}, bf16[2,2,128,512]{3,2,1,0:T(8,128)(2,1)}, u32[]{:S(2)}, u32[]{:S(2)}) %collective-permute-start.12) | collective-permute-done | bytes 524320 | tf_op jit(solution)/shard_map/ppermute | solution.py:366
  87.8 0.0 collective-permute-done.10.far_ref
  87.8 3.0 %shard_map.90 = bf16[512,1024]{1,0:T(8,128)(2,1)} custom-call(bf16[2,256,512]{2,1,0:T(8,128)(2,1)S(1)} %get-tuple-element.28.near_ref, bf16[2,256,512]{2,1,0:T(8,128)(2,1)} %collective-permute-done.10.far_ref, bf16[2,2,128,512]{3,2,1,0:T(8,128)(2,1)S(1)} %pad_maximum_fusion.low_ref, bf16[2,2,128,512]{3,2,1,0:T(8,128)(2,1)} %collective-permute-done.12.high_ref), custom_call_target="tpu_custom_call" | custom-call | tf_op jit(solution)/shard_map/pallas_call | solution.py:266
  90.8 3.2 %collective-permute-start.13 = (bf16[512,1024]{1,0:T(8,128)(2,1)}, bf16[512,1024]{1,0:T(8,128)(2,1)}, u32[]{:S(2)}, u32[]{:S(2)}) collective-permute-start(bf16[512,1024]{1,0:T(8,128)(2,1)} %shard_map.90), channel_id=1, source_target_pairs={{0,64},{64,0},{1,65},{65,1},{2,66},{66,2},{3,67},{67,3},{4,68},{68... | collective-permute-start | bytes 3145736 | tf_op jit(solution)/shard_map/ppermute | solution.py:375
  94.0 1.4 %reduce_sum.22 = bf16[256,128]{1,0:T(8,128)(2,1)S(1)} reduce(bf16[16,256,128]{2,1,0:T(8,128)(2,1)} %all-to-all-done.1, bf16[]{:T(256)} %constant.25.clone.1), dimensions={0}, to_apply=%region_1.2 | reduce | flops 491520 | bytes 1114114 | tf_op jit(solution)/shard_map/reduce_sum | solution.py:371
  95.4 2.0 %collective-permute-start.14 = (bf16[256,128]{1,0:T(8,128)(2,1)S(1)}, bf16[256,128]{1,0:T(8,128)(2,1)S(1)}, u32[]{:S(2)}, u32[]{:S(2)}) collective-permute-start(bf16[256,128]{1,0:T(8,128)(2,1)S(1)} %reduce_sum.22), channel_id=1, source_target_pairs={{0,0},{1,1},{2,64},{3,65},{64,2},{65,3},{66,66},{67,67},{4,4},{5,5... | collective-permute-start | bytes 196616 | tf_op jit(solution)/shard_map/ppermute | solution.py:374
  97.4 1.7 %collective-permute-start.15 = (bf16[256,128]{1,0:T(8,128)(2,1)S(1)}, bf16[256,128]{1,0:T(8,128)(2,1)S(1)}, u32[]{:S(2)}, u32[]{:S(2)}) collective-permute-start(bf16[256,128]{1,0:T(8,128)(2,1)S(1)} %reduce_sum.22), channel_id=1, source_target_pairs={{0,1},{1,0},{2,65},{3,64},{64,3},{65,2},{66,67},{67,66},{4,5},{5,4... | collective-permute-start | bytes 196616 | tf_op jit(solution)/shard_map/ppermute | solution.py:374
  99.1 2.2 %collective-permute-start.17 = (bf16[256,128]{1,0:T(8,128)(2,1)S(1)}, bf16[256,128]{1,0:T(8,128)(2,1)S(1)}, u32[]{:S(2)}, u32[]{:S(2)}) collective-permute-start(bf16[256,128]{1,0:T(8,128)(2,1)S(1)} %reduce_sum.22), channel_id=1, source_target_pairs={{0,3},{1,2},{2,67},{3,66},{64,1},{65,0},{66,65},{67,64},{4,7},{5,6... | collective-permute-start | bytes 196616 | tf_op jit(solution)/shard_map/ppermute | solution.py:374
  101.3 1.3 %collective-permute-done.14.a_ref = bf16[256,128]{1,0:T(8,128)(2,1)S(1)} collective-permute-done((bf16[256,128]{1,0:T(8,128)(2,1)S(1)}, bf16[256,128]{1,0:T(8,128)(2,1)S(1)}, u32[]{:S(2)}, u32[]{:S(2)}) %collective-permute-start.14) | collective-permute-done | bytes 65568 | tf_op jit(solution)/shard_map/ppermute | solution.py:374
  102.6 1.2 %collective-permute-done.15.b_ref = bf16[256,128]{1,0:T(8,128)(2,1)S(1)} collective-permute-done((bf16[256,128]{1,0:T(8,128)(2,1)S(1)}, bf16[256,128]{1,0:T(8,128)(2,1)S(1)}, u32[]{:S(2)}, u32[]{:S(2)}) %collective-permute-start.15) | collective-permute-done | bytes 65568 | tf_op jit(solution)/shard_map/ppermute | solution.py:374
  103.8 0.7 collective-permute-done.17.d_ref
  104.5 1.6 %shard_map.92 = f32[128,1024]{1,0:T(8,128)} custom-call(bf16[256,128]{1,0:T(8,128)(2,1)S(1)} %collective-permute-done.14.a_ref, bf16[256,128]{1,0:T(8,128)(2,1)S(1)} %collective-permute-done.15.b_ref, bf16[256,128]{1,0:T(8,128)(2,1)S(1)} %collective-permute-done.16.c_ref, bf16[256,128]{1,0:T(8,128)(2,1)S(1)} %collective-permute-done.17.d_ref, ...), custom_call_target="tpu_custom_call" | custom-call | tf_op jit(solution)/shard_map/pallas_call | solution.py:295
  106.1 3.4 %shard_map.91 = bf16[512,1024]{1,0:T(8,128)(2,1)} custom-call(bf16[2,256,512]{2,1,0:T(8,128)(2,1)S(1)} %get-tuple-element.28.near_ref, bf16[2,256,512]{2,1,0:T(8,128)(2,1)} %collective-permute-done.10.far_ref, bf16[2,2,128,512]{3,2,1,0:T(8,128)(2,1)S(1)} %pad_maximum_fusion.low_ref, bf16[2,2,128,512]{3,2,1,0:T(8,128)(2,1)} %collective-permute-done.12.high_ref, ...), custom_call_target="tpu_custom_call" | custom-call | tf_op jit(solution)/shard_map/pallas_call | solution.py:266
  (27 shorter events, 0.1 us)
Async XLA Ops:
  0.6 19.7 %collective-permute-start.1 = (bf16[512,1024]{1,0:T(8,128)(2,1)}, bf16[512,1024]{1,0:T(8,128)(2,1)S(1)}, u32[]{:S(2)}, u32[]{:S(2)}) collective-permute-start(bf16[512,1024]{1,0:T(8,128)(2,1)} %bitcast.20), channel_id=1, source_target_pairs={{0,64},{64,0},{1,65},{65,1},{2,66},{66,2},{3,67},{67,3},{4,68},{68... | collective-permute-start | bytes 3145736 | tf_op jit(solution)/shard_map/ppermute | solution.py:329
  3.3 17.0 %collective-permute-start = (bf16[320,1024]{1,0:T(8,128)(2,1)S(1)}, bf16[320,1024]{1,0:T(8,128)(2,1)S(1)}, u32[]{:S(2)}, u32[]{:S(2)}) collective-permute-start(bf16[320,1024]{1,0:T(8,128)(2,1)S(1)} %slice_bitcast_fusion), channel_id=1, source_target_pairs={{0,1},{1,0},{2,3},{3,2},{4,5},{5,4},{6,7},{7,6},{8,9},{9,8},{10,11... | collective-permute-start | bytes 1966088 | tf_op jit(solution)/shard_map/ppermute | solution.py:330
  11.2 9.1 %collective-permute-start.2 = (bf16[2,128,512]{2,1,0:T(8,128)(2,1)}, bf16[2,128,512]{2,1,0:T(8,128)(2,1)S(1)}, u32[]{:S(2)}, u32[]{:S(2)}) collective-permute-start(bf16[2,128,512]{2,1,0:T(8,128)(2,1)} %get-tuple-element.20), channel_id=1, source_target_pairs={{0,3},{1,2},{2,1},{3,0},{4,7},{5,6},{6,5},{7,4},{8,11},{9,10},{10,... | collective-permute-start | bytes 786440 | tf_op jit(solution)/shard_map/ppermute | solution.py:338
  13.1 8.2 %copy-start.8 = (bf16[128,512]{1,0:T(8,128)(2,1)S(1)}, bf16[128,512]{1,0:T(8,128)(2,1)}, u32[]{:S(2)}) copy-start(bf16[128,512]{1,0:T(8,128)(2,1)} %get-tuple-element.24) | copy-start | bytes 393220
  13.1 10.7 %copy-start.7 = (s32[1,8192]{1,0:T(1,128)S(1)}, s32[1,8192]{1,0:T(1,128)}, u32[]{:S(2)}) copy-start(s32[1,8192]{1,0:T(1,128)} %param.8) | copy-start | bytes 98308
  18.2 25.4 %copy-start = (bf16[1,512,1024]{2,1,0:T(8,128)(2,1)S(1)}, bf16[1,512,1024]{2,1,0:T(8,128)(2,1)}, u32[]{:S(2)}) copy-start(bf16[1,512,1024]{2,1,0:T(8,128)(2,1)} %param.10) | copy-start | bytes 3145732
  20.3 1.0 copy-start.2
  22.0 9.8 %collective-permute-start.4 = (bf16[128,512]{1,0:T(8,128)(2,1)}, bf16[128,512]{1,0:T(8,128)(2,1)S(1)}, u32[]{:S(2)}, u32[]{:S(2)}) collective-permute-start(bf16[128,512]{1,0:T(8,128)(2,1)} %fusion), channel_id=1, source_target_pairs={{0,1},{1,0},{2,3},{3,2},{4,5},{5,4},{6,7},{7,6},{8,9},{9,8},{10,11... | collective-permute-start | bytes 393224 | tf_op jit(solution)/shard_map/ppermute | solution.py:346
  22.7 20.4 %collective-permute-start.3 = (bf16[320,1024]{1,0:T(8,128)(2,1)S(1)}, bf16[320,1024]{1,0:T(8,128)(2,1)S(1)}, u32[]{:S(2)}, u32[]{:S(2)}) collective-permute-start(bf16[320,1024]{1,0:T(8,128)(2,1)S(1)} %collective-permute-done.n1a_ref), channel_id=1, source_target_pairs={{0,64},{64,0},{1,65},{65,1},{2,66},{66,2},{3,67},{67,3},{4,68},{68... | collective-permute-start | bytes 1966088 | tf_op jit(solution)/shard_map/ppermute | solution.py:352
  24.0 19.6 %all-to-all-start = ((bf16[16,72,256]{2,1,0:T(8,128)(2,1)}), bf16[16,72,256]{2,1,0:T(8,128)(2,1)S(1)}, u32[]{:S(2)}, u32[]{:S(2)}) async-start(bf16[16,72,256]{2,1,0:T(8,128)(2,1)} %bitcast.25), calls=%async_computation | async-start | bytes 1179648 | tf_op jit(solution)/shard_map/all_to_all | solution.py:342
  32.8 10.3 %collective-permute-start.5 = (bf16[128,512]{1,0:T(8,128)(2,1)S(1)}, bf16[128,512]{1,0:T(8,128)(2,1)S(1)}, u32[]{:S(2)}, u32[]{:S(2)}) collective-permute-start(bf16[128,512]{1,0:T(8,128)(2,1)S(1)} %fusion.2), channel_id=1, source_target_pairs={{0,4},{4,0},{8,12},{12,8},{16,20},{20,16},{24,28},{28,24},{32,36},... | collective-permute-start | bytes 393224 | tf_op jit(solution)/shard_map/ppermute | solution.py:348
  43.1 14.5 %copy-start.5 = (bf16[320,1024]{1,0:T(8,128)(2,1)}, bf16[320,1024]{1,0:T(8,128)(2,1)S(1)}, u32[]{:S(2)}) copy-start(bf16[320,1024]{1,0:T(8,128)(2,1)S(1)} %collective-permute-done.3.f1a_ref) | copy-start | bytes 1966084
  43.6 14.9 %copy-start.3 = (bf16[512,1024]{1,0:T(8,128)(2,1)S(1)}, bf16[512,1024]{1,0:T(8,128)(2,1)}, u32[]{:S(2)}) copy-start(bf16[512,1024]{1,0:T(8,128)(2,1)} %copy-done.2) | copy-start | bytes 3145732
  43.6 13.2 %collective-permute-start.8 = (bf16[192,1024]{1,0:T(8,128)(2,1)S(1)}, bf16[192,1024]{1,0:T(8,128)(2,1)S(1)}, u32[]{:S(2)}, u32[]{:S(2)}) collective-permute-start(bf16[192,1024]{1,0:T(8,128)(2,1)S(1)} %slice.19), channel_id=1, source_target_pairs={{0,1},{1,0},{2,3},{3,2},{4,5},{5,4},{6,7},{7,6},{8,9},{9,8},{10,11... | collective-permute-start | bytes 1179656 | tf_op jit(solution)/shard_map/ppermute | solution.py:355
  45.7 8.6 %collective-permute-start.6 = (bf16[256,512]{1,0:T(8,128)(2,1)S(1)}, bf16[256,512]{1,0:T(8,128)(2,1)S(1)}, u32[]{:S(2)}, u32[]{:S(2)}) collective-permute-start(bf16[256,512]{1,0:T(8,128)(2,1)S(1)} %shard_map.88.mine_ref), channel_id=1, source_target_pairs={{64,67},{65,66},{66,65},{67,64},{68,71},{69,70},{70,69},{71,68},{7... | collective-permute-start | bytes 786440 | tf_op jit(solution)/shard_map/ppermute | solution.py:358
  49.4 7.4 %collective-permute-start.7 = (bf16[256,512]{1,0:T(8,128)(2,1)S(1)}, bf16[256,512]{1,0:T(8,128)(2,1)S(1)}, u32[]{:S(2)}, u32[]{:S(2)}) collective-permute-start(bf16[256,512]{1,0:T(8,128)(2,1)S(1)} %shard_map.88.mine_ref), channel_id=1, source_target_pairs={{0,67},{1,66},{2,65},{3,64},{64,0},{65,1},{66,2},{67,3},{4,71},{5,... | collective-permute-start | bytes 786440 | tf_op jit(solution)/shard_map/ppermute | solution.py:357
  56.8 1.7 %collective-permute-start.9 = (bf16[192,1024]{1,0:T(8,128)(2,1)S(1)}, bf16[192,1024]{1,0:T(8,128)(2,1)S(1)}, u32[]{:S(2)}, u32[]{:S(2)}) collective-permute-start(bf16[192,1024]{1,0:T(8,128)(2,1)S(1)} %collective-permute-done.8.n1b_ref), channel_id=1, source_target_pairs={{0,64},{64,0},{1,65},{65,1},{2,66},{66,2},{3,67},{67,3},{4,68},{68... | collective-permute-start | bytes 1179656 | tf_op jit(solution)/shard_map/ppermute | solution.py:361
  56.8 7.9 %collective-permute-start.11 = (bf16[2,128,512]{2,1,0:T(8,128)(2,1)S(1)}, bf16[2,128,512]{2,1,0:T(8,128)(2,1)S(1)}, u32[]{:S(2)}, u32[]{:S(2)}) collective-permute-start(bf16[2,128,512]{2,1,0:T(8,128)(2,1)S(1)} %pad_maximum_fusion.1), channel_id=1, source_target_pairs={{0,16},{4,20},{8,24},{12,28},{16,0},{20,4},{24,8},{28,12},{32,48},... | collective-permute-start | bytes 786440 | tf_op jit(solution)/shard_map/ppermute | solution.py:360
  58.5 1.1 copy-start.6
  64.6 2.1 %copy-start.4 = (bf16[16,256,128]{2,1,0:T(8,128)(2,1)}, bf16[16,256,128]{2,1,0:T(8,128)(2,1)S(1)}, u32[]{:S(2)}) copy-start(bf16[16,256,128]{2,1,0:T(8,128)(2,1)S(1)} %get-tuple-element.30) | copy-start | bytes 3145732
  64.7 23.1 %collective-permute-start.12 = (bf16[2,2,128,512]{3,2,1,0:T(8,128)(2,1)S(1)}, bf16[2,2,128,512]{3,2,1,0:T(8,128)(2,1)}, u32[]{:S(2)}, u32[]{:S(2)}) collective-permute-start(bf16[2,2,128,512]{3,2,1,0:T(8,128)(2,1)S(1)} %pad_maximum_fusion.low_ref), channel_id=1, source_target_pairs={{0,48},{4,52},{8,56},{12,60},{16,32},{20,36},{24,40},{28,44},{32,1... | collective-permute-start | bytes 1572872 | tf_op jit(solution)/shard_map/ppermute | solution.py:366
  66.8 21.1 %collective-permute-start.10 = (bf16[2,256,512]{2,1,0:T(8,128)(2,1)S(1)}, bf16[2,256,512]{2,1,0:T(8,128)(2,1)}, u32[]{:S(2)}, u32[]{:S(2)}) collective-permute-start(bf16[2,256,512]{2,1,0:T(8,128)(2,1)S(1)} %get-tuple-element.28.near_ref), channel_id=1, source_target_pairs={{0,1},{1,0},{2,3},{3,2},{4,5},{5,4},{6,7},{7,6},{8,9},{9,8},{10,11... | collective-permute-start | bytes 1572872 | tf_op jit(solution)/shard_map/ppermute | solution.py:368
  66.8 27.2 %all-to-all-start.1 = ((bf16[16,256,128]{2,1,0:T(8,128)(2,1)}), bf16[16,256,128]{2,1,0:T(8,128)(2,1)}, u32[]{:S(2)}, u32[]{:S(2)}) async-start(bf16[16,256,128]{2,1,0:T(8,128)(2,1)} %copy-done.4), calls=%async_computation.1 | async-start | bytes 2097152 | tf_op jit(solution)/shard_map/all_to_all | solution.py:364
  71.4 33.1 %copy-start.1 = (bf16[1024,1024]{1,0:T(8,128)(2,1)S(1)}, bf16[1024,1024]{1,0:T(8,128)(2,1)}, u32[]{:S(2)}) copy-start(bf16[1024,1024]{1,0:T(8,128)(2,1)} %get-tuple-element.18.w_ref) | copy-start | bytes 6291460
  90.8 15.3 %collective-permute-start.13 = (bf16[512,1024]{1,0:T(8,128)(2,1)}, bf16[512,1024]{1,0:T(8,128)(2,1)}, u32[]{:S(2)}, u32[]{:S(2)}) collective-permute-start(bf16[512,1024]{1,0:T(8,128)(2,1)} %shard_map.90), channel_id=1, source_target_pairs={{0,64},{64,0},{1,65},{65,1},{2,66},{66,2},{3,67},{67,3},{4,68},{68... | collective-permute-start | bytes 3145736 | tf_op jit(solution)/shard_map/ppermute | solution.py:375
  95.4 7.2 %collective-permute-start.14 = (bf16[256,128]{1,0:T(8,128)(2,1)S(1)}, bf16[256,128]{1,0:T(8,128)(2,1)S(1)}, u32[]{:S(2)}, u32[]{:S(2)}) collective-permute-start(bf16[256,128]{1,0:T(8,128)(2,1)S(1)} %reduce_sum.22), channel_id=1, source_target_pairs={{0,0},{1,1},{2,64},{3,65},{64,2},{65,3},{66,66},{67,67},{4,4},{5,5... | collective-permute-start | bytes 196616 | tf_op jit(solution)/shard_map/ppermute | solution.py:374
  97.4 6.4 %collective-permute-start.15 = (bf16[256,128]{1,0:T(8,128)(2,1)S(1)}, bf16[256,128]{1,0:T(8,128)(2,1)S(1)}, u32[]{:S(2)}, u32[]{:S(2)}) collective-permute-start(bf16[256,128]{1,0:T(8,128)(2,1)S(1)} %reduce_sum.22), channel_id=1, source_target_pairs={{0,1},{1,0},{2,65},{3,64},{64,3},{65,2},{66,67},{67,66},{4,5},{5,4... | collective-permute-start | bytes 196616 | tf_op jit(solution)/shard_map/ppermute | solution.py:374
  99.1 4.7 %collective-permute-start.16 = (bf16[256,128]{1,0:T(8,128)(2,1)S(1)}, bf16[256,128]{1,0:T(8,128)(2,1)S(1)}, u32[]{:S(2)}, u32[]{:S(2)}) collective-permute-start(bf16[256,128]{1,0:T(8,128)(2,1)S(1)} %reduce_sum.22), channel_id=1, source_target_pairs={{0,2},{1,3},{2,66},{3,67},{64,0},{65,1},{66,64},{67,65},{4,6},{5,7... | collective-permute-start | bytes 196616 | tf_op jit(solution)/shard_map/ppermute | solution.py:374
  99.1 5.4 %collective-permute-start.17 = (bf16[256,128]{1,0:T(8,128)(2,1)S(1)}, bf16[256,128]{1,0:T(8,128)(2,1)S(1)}, u32[]{:S(2)}, u32[]{:S(2)}) collective-permute-start(bf16[256,128]{1,0:T(8,128)(2,1)S(1)} %reduce_sum.22), channel_id=1, source_target_pairs={{0,3},{1,2},{2,67},{3,66},{64,1},{65,0},{66,65},{67,64},{4,7},{5,6... | collective-permute-start | bytes 196616 | tf_op jit(solution)/shard_map/ppermute | solution.py:374

commit v7 on v6

--- a/solution.py
+++ b/solution.py
@@ -338,27 +338,27 @@
     away = lax.ppermute(away, "tensor", [(x, ten_n - 1 - x) for x in range(ten_n)])
 
     outgoing = segment_sums(after(starts, both_t), owner, byte_grads[0], ctx_n, width)
-    outgoing = after(outgoing, near1[0], far0, away)
+    outgoing = after(outgoing, near1[0], away)
     incoming = lax.all_to_all(outgoing, "context", split_axis=0, concat_axis=0, tiled=True)
 
     away = after(away, outgoing)
     paired = (paired.astype(f32) + away[1].astype(f32)).astype(bf16)
     paired = lax.ppermute(paired, "tensor", pair)
     chain = (own.astype(f32) + away[0].astype(f32) + paired.astype(f32)).astype(bf16)
-    chain = jnp.stack([chain, lax.ppermute(chain, "context", along(lambda i, j: (i, j ^ 1)))])
     edges = jnp.arange(ctx_n, dtype=jnp.int32) * bytes_n
     counts = jnp.sum((patch_starts[0][None, :] <= edges[:, None]).astype(jnp.int32), axis=1)
     first = jnp.minimum((counts - 1) // LANES, starts.shape[0] - WIN)
     far1 = [lax.ppermute(near1[0], "dp", swap)]
-    incoming = after(incoming, first, far1[0], chain)
+    incoming = after(incoming, first, far0, far1[0], chain)
 
     near1.append(lax.ppermute(after(near0, incoming)[CUT:], "tensor", pair))
     sums = collect(first, incoming, patch_rows)
     cross = lax.ppermute(sums, line, moves(lambda d, x: (0, x) if d == 1 else (1, ten_n - 1 - x)))
     third = lax.ppermute(sums, line, moves(lambda d, x: (1, ten_n - 1 - x) if d == 1 else None))
-    chain = after(chain, sums)
+    other = lax.ppermute(after(chain, sums), "context", along(lambda i, j: (i, j ^ 1)))
+    far1.append(lax.ppermute(after(near1[1], cross, third, other), "dp", swap))
+    chain = jnp.stack([chain, other])
     other = lax.ppermute(chain, "context", along(lambda i, j: (i ^ 1, j)))
-    far1.append(lax.ppermute(after(near1[1], cross, third), "dp", swap))
     columns = (near0, *near1, far0, *far1)
     partial, near = outer((sums, third, cross), columns)
     pieces = lax.all_to_all(partial, "context", split_axis=0, concat_axis=0, tiled=True)
@@ -366,12 +366,11 @@
     rest = lax.ppermute(chain, "context", along(lambda i, j: (SIDE - 1 - i, j)))
 
     far = lax.ppermute(near, "tensor", pair)
-    give = context_rows(1, near, far, chain, rest)
-    pieces = after(pieces, give)
     piece = jnp.sum(pieces.astype(f32), axis=0).astype(bf16)
     parts = []
     for s in range(ten_n):
         parts.append(lax.ppermute(piece, line, moves(lambda d, x, s=s: (x // 2, (2 * d + x % 2) ^ s))))
+    give = context_rows(1, after(near, parts[0]), far, chain, rest)
     back = lax.ppermute(give, "dp", swap)
     context_grad = context_rows(0, near, far, chain, rest, back)
     weight_grad = last(parts, both_t)

time: 110 us -> 114 us (1.036)
  waiting for transfers between devices: 39.3 us -> 46 us
  Pallas kernels: 25.5 us -> 22.3 us
    ppermute x1, waiting for transfers between devices: 0.01 us -> 17.3 us  [local(): other = lax.ppermute(chain, 'context', along(lambda i, j: (i ^ 1, j)))]
    ppermute x1, waiting for transfers between devices: 16.4 us -> 0.01 us  [local(): rest = lax.ppermute(chain, 'context', along(lambda i, j: (SIDE - 1 - i, j)))]
    ppermute x4, waiting for transfers between devices: 3.19 us -> 10.2 us  [local(): lax.ppermute(piece, line, moves(lambda d, x, s=s: (x // 2, 2 * d + x % 2...]
    ppermute x1, waiting for transfers between devices: 0.01 us -> 5.08 us  [local(): paired = lax.ppermute(paired, 'tensor', pair)]
    ppermute x2, waiting for transfers between devices: 9.82 us -> 5.38 us  [the longest x1 3.68 us: local(): lax.ppermute(after(chain, sums), 'context', along(lambda i, j: (i, j ^ 1)))]
    ppermute x4, starting transfers between devices: 5.92 us -> 10.3 us  [local(): lax.ppermute(piece, line, moves(lambda d, x, s=s: (x // 2, 2 * d + x % 2...]
    ppermute x1, waiting for transfers between devices: 4.78 us -> 0.63 us  [local(): lax.ppermute(sums, line, moves(lambda d, x: (1, ten_n - 1 - x) if d == 1...]
    ppermute x1, starting transfers between devices: 3.18 us -> 0.09 us  [local(): back = lax.ppermute(give, 'dp', swap)]
  transfers between devices with their start and end apart: 20 -> 20, of which waited for: 10 -> 10; matrix products, arithmetic and copies ran while one was open for 3% -> 3% of each run, Pallas kernels for 20% -> 12%
where the time goes in v7:
time: 114 us
  waiting for transfers between devices  46 us (40%)
  starting transfers between devices  36.5 us (32%)
  Pallas kernels  22.3 us (20%)
  local copies, waits for them, and re-layouts  4.2 us (4%)
  other arithmetic  3.83 us (3%)
    ppermute x1, waiting for transfers between devices, local(): other = lax.ppermute(chain, 'context', along(lambda i, j: (i ^ 1, j)))  17.3 us
    ppermute x4, starting transfers between devices, local(): lax.ppermute(piece, line, moves(lambda d, x, s=s: (x // 2, 2 * d + x % 2...  10.3 us
    ppermute x4, waiting for transfers between devices, local(): lax.ppermute(piece, line, moves(lambda d, x, s=s: (x // 2, 2 * d + x % 2...  10.2 us
    all_to_all x1, starting transfers between devices, local(): lax.all_to_all(outgoing, 'context', split_axis=0, concat_axis=0, tiled=True)  7.77 us
    pallas_call x1, Pallas kernels, chain_terms(): pl.pallas_call(chain_kernel, in_specs=[vmem, vmem, pl.BlockSpec(memory_sp...  6.54 us
    pallas_call x1, Pallas kernels, segment_sums(): pl.pallas_call(seg_kernel, in_specs=[vmem, vmem, pl.BlockSpec(memory_spac...  5.13 us
    ppermute x1, waiting for transfers between devices, local(): paired = lax.ppermute(paired, 'tensor', pair)  5.08 us
    pallas_call x2, Pallas kernels, context_rows(): pl.pallas_call(functools.partial(rows_kernel, which), in_specs=[vmem] * (...  5.04 us
  transfers between devices with their start and end apart: 20, of which 10 were waited for; matrix products, arithmetic and copies ran while one was open for 3% of the time, Pallas kernels for 12%

profile of v7, /device:TPU:1, one launch (start us, length us, event | category | flops | bytes accessed | tf_op | source)
XLA Modules:
  0.0 113.7 jit_solution(9622329733785967308)
XLA Ops:
  0.6 1.1 slice_bitcast_fusion
  1.8 2.1 %collective-permute-start = (bf16[320,1024]{1,0:T(8,128)(2,1)S(1)}, bf16[320,1024]{1,0:T(8,128)(2,1)S(1)}, u32[]{:S(2)}, u32[]{:S(2)}) collective-permute-start(bf16[320,1024]{1,0:T(8,128)(2,1)S(1)} %slice_bitcast_fusion), channel_id=1, source_target_pairs={{0,1},{1,0},{2,3},{3,2},{4,5},{5,4},{6,7},{7,6},{8,9},{9,8},{10,11... | collective-permute-start | bytes 1966088 | tf_op jit(solution)/shard_map/ppermute | solution.py:330
  3.9 1.0 collective-permute-start.2
  4.8 6.5 %shard_map.86 = (bf16[1024,1024]{1,0:T(8,128)(2,1)}, bf16[128,512]{1,0:T(8,128)(2,1)}, bf16[128,512]{1,0:T(8,128)(2,1)}, bf16[2,128,512]{2,1,0:T(8,128)(2,1)}) custom-call(bf16[1024,1024]{1,0:T(8,128)(2,1)} %value_ref.1, bf16[1024,1024]{1,0:T(8,128)(2,1)} %out_w_ref.1, bf16[4096,1024]{1,0:T(8,128)(2,1)} %global_ref.1), custom_call_target="tpu_custom_call" | custom-call | tf_op jit(solution)/shard_map/pallas_call | solution.py:227
  11.4 1.9 %collective-permute-start.1 = (bf16[2,128,512]{2,1,0:T(8,128)(2,1)}, bf16[2,128,512]{2,1,0:T(8,128)(2,1)S(1)}, u32[]{:S(2)}, u32[]{:S(2)}) collective-permute-start(bf16[2,128,512]{2,1,0:T(8,128)(2,1)} %get-tuple-element.20), channel_id=1, source_target_pairs={{0,3},{1,2},{2,1},{3,0},{4,7},{5,6},{6,5},{7,4},{8,11},{9,10},{10,... | collective-permute-start | bytes 786440 | tf_op jit(solution)/shard_map/ppermute | solution.py:338
  13.3 5.1 %shard_map.87 = bf16[1152,256]{1,0:T(8,128)(2,1)} custom-call(s32[64,128]{1,0:T(8,128)} %bitcast.30, s32[64,128]{1,0:T(8,128)} %bitcast.33, bf16[4096,1024]{1,0:T(8,128)(2,1)} %bitcast.24), custom_call_target="tpu_custom_call" | custom-call | tf_op jit(solution)/shard_map/pallas_call | solution.py:94
  18.4 0.0 copy-start
  18.5 0.3 convert_reduce_fusion
  18.7 2.1 %collective-permute-done.1 = bf16[2,128,512]{2,1,0:T(8,128)(2,1)S(1)} collective-permute-done((bf16[2,128,512]{2,1,0:T(8,128)(2,1)}, bf16[2,128,512]{2,1,0:T(8,128)(2,1)S(1)}, u32[]{:S(2)}, u32[]{:S(2)}) %collective-permute-start.1) | collective-permute-done | bytes 262176 | tf_op jit(solution)/shard_map/ppermute | solution.py:338
  20.8 0.0 collective-permute-done.n1a_ref
  20.8 0.7 copy-done.6
  21.5 7.8 %all-to-all-start = ((bf16[16,72,256]{2,1,0:T(8,128)(2,1)}), bf16[16,72,256]{2,1,0:T(8,128)(2,1)S(1)}, u32[]{:S(2)}, u32[]{:S(2)}) async-start(bf16[16,72,256]{2,1,0:T(8,128)(2,1)} %bitcast.25), calls=%async_computation | async-start | bytes 1179648 | tf_op jit(solution)/shard_map/all_to_all | solution.py:342
  29.3 1.1 collective-permute-start.3
  30.5 0.9 fusion
  31.4 0.1 collective-permute-start.4
  31.5 5.1 %collective-permute-done.4 = bf16[128,512]{1,0:T(8,128)(2,1)S(1)} collective-permute-done((bf16[128,512]{1,0:T(8,128)(2,1)S(1)}, bf16[128,512]{1,0:T(8,128)(2,1)S(1)}, u32[]{:S(2)}, u32[]{:S(2)}) %collective-permute-start.4) | collective-permute-done | bytes 131104 | tf_op jit(solution)/shard_map/ppermute | solution.py:346
  36.6 1.0 fusion.2
  37.6 0.0 copy-start.2
  37.6 2.7 %all-to-all-done = bf16[16,72,256]{2,1,0:T(8,128)(2,1)S(1)} async-done(((bf16[16,72,256]{2,1,0:T(8,128)(2,1)}), bf16[16,72,256]{2,1,0:T(8,128)(2,1)S(1)}, u32[]{:S(2)}, u32[]{:S(2)}) %all-to-all-start) | async-done | bytes 589856 | tf_op jit(solution)/shard_map/all_to_all | solution.py:342
  40.3 0.1 collective-permute-start.7
  40.4 0.9 shard_map.88.mine_ref
  41.3 3.7 %collective-permute-start.5 = (bf16[256,512]{1,0:T(8,128)(2,1)S(1)}, bf16[256,512]{1,0:T(8,128)(2,1)S(1)}, u32[]{:S(2)}, u32[]{:S(2)}) collective-permute-start(bf16[256,512]{1,0:T(8,128)(2,1)S(1)} %shard_map.88.mine_ref), channel_id=1, source_target_pairs={{64,67},{65,66},{66,65},{67,64},{68,71},{69,70},{70,69},{71,68},{7... | collective-permute-start | bytes 786440 | tf_op jit(solution)/shard_map/ppermute | solution.py:357
  45.0 0.1 collective-permute-start.6
  45.1 0.5 collective-permute-start.8
  45.6 3.7 %collective-permute-done.8 = bf16[128,512]{1,0:T(8,128)(2,1)S(1)} collective-permute-done((bf16[128,512]{1,0:T(8,128)(2,1)S(1)}, bf16[128,512]{1,0:T(8,128)(2,1)S(1)}, u32[]{:S(2)}, u32[]{:S(2)}) %collective-permute-start.8) | collective-permute-done | bytes 131104 | tf_op jit(solution)/shard_map/ppermute | solution.py:358
  49.3 0.6 collective-permute-done.5.third_ref
  49.9 2.5 %collective-permute-done.6.cross_ref = bf16[256,512]{1,0:T(8,128)(2,1)S(1)} collective-permute-done((bf16[256,512]{1,0:T(8,128)(2,1)S(1)}, bf16[256,512]{1,0:T(8,128)(2,1)S(1)}, u32[]{:S(2)}, u32[]{:S(2)}) %collective-permute-start.6) | collective-permute-done | bytes 262176 | tf_op jit(solution)/shard_map/ppermute | solution.py:356
  52.5 1.7 %collective-permute-done.9.f1b_ref = bf16[192,1024]{1,0:T(8,128)(2,1)S(1)} collective-permute-done((bf16[192,1024]{1,0:T(8,128)(2,1)S(1)}, bf16[192,1024]{1,0:T(8,128)(2,1)S(1)}, u32[]{:S(2)}, u32[]{:S(2)}) %collective-permute-start.9) | collective-permute-done | bytes 393248 | tf_op jit(solution)/shard_map/ppermute | solution.py:359
  54.2 1.2 %copy-done.3 = bf16[512,1024]{1,0:T(8,128)(2,1)S(1)} copy-done((bf16[512,1024]{1,0:T(8,128)(2,1)S(1)}, bf16[512,1024]{1,0:T(8,128)(2,1)}, u32[]{:S(2)}) %copy-start.3) | copy-done | bytes 1048600
  55.4 1.1 copy-done.5
  56.5 3.1 %shard_map.89 = (bf16[16,256,128]{2,1,0:T(8,128)(2,1)}, bf16[2,256,512]{2,1,0:T(8,128)(2,1)S(1)}) custom-call(bf16[256,512]{1,0:T(8,128)(2,1)S(1)} %shard_map.88.mine_ref, bf16[256,512]{1,0:T(8,128)(2,1)S(1)} %collective-permute-done.5.third_ref, bf16[256,512]{1,0:T(8,128)(2,1)S(1)} %collective-permute-done.6.cross_ref, bf16[512,1024]{1,0:T(8,128)(2,1)S(1)} %bitcast.22, ...), custom_call_target="tpu_custom_call" | custom-call | tf_op jit(solution)/shard_map/pallas_call | solution.py:172
  59.6 4.5 %all-to-all-start.1 = ((bf16[16,256,128]{2,1,0:T(8,128)(2,1)}), bf16[16,256,128]{2,1,0:T(8,128)(2,1)}, u32[]{:S(2)}, u32[]{:S(2)}) async-start(bf16[16,256,128]{2,1,0:T(8,128)(2,1)} %get-tuple-element.30), calls=%async_computation.1 | async-start | bytes 2097152 | tf_op jit(solution)/shard_map/all_to_all | solution.py:364
  64.1 1.4 %collective-permute-start.11 = (bf16[2,128,512]{2,1,0:T(8,128)(2,1)S(1)}, bf16[2,128,512]{2,1,0:T(8,128)(2,1)S(1)}, u32[]{:S(2)}, u32[]{:S(2)}) collective-permute-start(bf16[2,128,512]{2,1,0:T(8,128)(2,1)S(1)} %pad_maximum_fusion.1), channel_id=1, source_target_pairs={{0,16},{4,20},{8,24},{12,28},{16,0},{20,4},{24,8},{28,12},{32,48},... | collective-permute-start | bytes 786440 | tf_op jit(solution)/shard_map/ppermute | solution.py:361
  65.5 17.3 %collective-permute-done.11 = bf16[2,128,512]{2,1,0:T(8,128)(2,1)S(1)} collective-permute-done((bf16[2,128,512]{2,1,0:T(8,128)(2,1)S(1)}, bf16[2,128,512]{2,1,0:T(8,128)(2,1)S(1)}, u32[]{:S(2)}, u32[]{:S(2)}) %collective-permute-start.11) | collective-permute-done | bytes 262176 | tf_op jit(solution)/shard_map/ppermute | solution.py:361
  82.8 0.1 pad_maximum_fusion.low_ref
  82.9 1.9 %collective-permute-start.12 = (bf16[2,2,128,512]{3,2,1,0:T(8,128)(2,1)S(1)}, bf16[2,2,128,512]{3,2,1,0:T(8,128)(2,1)}, u32[]{:S(2)}, u32[]{:S(2)}) collective-permute-start(bf16[2,2,128,512]{3,2,1,0:T(8,128)(2,1)S(1)} %pad_maximum_fusion.low_ref), channel_id=1, source_target_pairs={{0,48},{4,52},{8,56},{12,60},{16,32},{20,36},{24,40},{28,44},{32,1... | collective-permute-start | bytes 1572872 | tf_op jit(solution)/shard_map/ppermute | solution.py:366
  84.8 0.0 collective-permute-start.10
  84.8 1.5 %reduce_sum.22 = bf16[256,128]{1,0:T(8,128)(2,1)S(1)} reduce(bf16[16,256,128]{2,1,0:T(8,128)(2,1)} %all-to-all-done.1, bf16[]{:T(256)} %constant.25.clone.1), dimensions={0}, to_apply=%region_1.2 | reduce | flops 491520 | bytes 1114114 | tf_op jit(solution)/shard_map/reduce_sum | solution.py:369
  86.3 6.4 %collective-permute-start.13 = (bf16[256,128]{1,0:T(8,128)(2,1)S(1)}, bf16[256,128]{1,0:T(8,128)(2,1)S(1)}, u32[]{:S(2)}, u32[]{:S(2)}) collective-permute-start(bf16[256,128]{1,0:T(8,128)(2,1)S(1)} %reduce_sum.22), channel_id=1, source_target_pairs={{0,0},{1,1},{2,64},{3,65},{64,2},{65,3},{66,66},{67,67},{4,4},{5,5... | collective-permute-start | bytes 196616 | tf_op jit(solution)/shard_map/ppermute | solution.py:372
  92.8 7.9 %collective-permute-done.13.a_ref = bf16[256,128]{1,0:T(8,128)(2,1)S(1)} collective-permute-done((bf16[256,128]{1,0:T(8,128)(2,1)S(1)}, bf16[256,128]{1,0:T(8,128)(2,1)S(1)}, u32[]{:S(2)}, u32[]{:S(2)}) %collective-permute-start.13) | collective-permute-done | bytes 65568 | tf_op jit(solution)/shard_map/ppermute | solution.py:372
  100.7 2.0 %shard_map.90 = bf16[512,1024]{1,0:T(8,128)(2,1)S(1)} custom-call(bf16[2,256,512]{2,1,0:T(8,128)(2,1)S(1)} %get-tuple-element.33.near_ref, bf16[2,256,512]{2,1,0:T(8,128)(2,1)} %collective-permute-done.10.far_ref, bf16[2,2,128,512]{3,2,1,0:T(8,128)(2,1)S(1)} %pad_maximum_fusion.low_ref, bf16[2,2,128,512]{3,2,1,0:T(8,128)(2,1)} %collective-permute-done.12.high_ref), custom_call_target="tpu_custom_call" | custom-call | tf_op jit(solution)/shard_map/pallas_call | solution.py:266
  102.7 0.1 collective-permute-start.14
  102.8 0.3 collective-permute-start.15
  103.1 0.2 collective-permute-start.16
  103.3 3.4 %collective-permute-start.17 = (bf16[256,128]{1,0:T(8,128)(2,1)S(1)}, bf16[256,128]{1,0:T(8,128)(2,1)S(1)}, u32[]{:S(2)}, u32[]{:S(2)}) collective-permute-start(bf16[256,128]{1,0:T(8,128)(2,1)S(1)} %reduce_sum.22), channel_id=1, source_target_pairs={{0,3},{1,2},{2,67},{3,66},{64,1},{65,0},{66,65},{67,64},{4,7},{5,6... | collective-permute-start | bytes 196616 | tf_op jit(solution)/shard_map/ppermute | solution.py:372
  106.7 2.3 %collective-permute-done.15.b_ref = bf16[256,128]{1,0:T(8,128)(2,1)S(1)} collective-permute-done((bf16[256,128]{1,0:T(8,128)(2,1)S(1)}, bf16[256,128]{1,0:T(8,128)(2,1)S(1)}, u32[]{:S(2)}, u32[]{:S(2)}) %collective-permute-start.15) | collective-permute-done | bytes 65568 | tf_op jit(solution)/shard_map/ppermute | solution.py:372
  109.0 1.6 %shard_map.92 = f32[128,1024]{1,0:T(8,128)} custom-call(bf16[256,128]{1,0:T(8,128)(2,1)S(1)} %collective-permute-done.13.a_ref, bf16[256,128]{1,0:T(8,128)(2,1)S(1)} %collective-permute-done.15.b_ref, bf16[256,128]{1,0:T(8,128)(2,1)S(1)} %collective-permute-done.16.c_ref, bf16[256,128]{1,0:T(8,128)(2,1)S(1)} %collective-permute-done.17.d_ref, ...), custom_call_target="tpu_custom_call" | custom-call | tf_op jit(solution)/shard_map/pallas_call | solution.py:295
  110.7 3.0 %shard_map.91 = bf16[512,1024]{1,0:T(8,128)(2,1)} custom-call(bf16[2,256,512]{2,1,0:T(8,128)(2,1)S(1)} %get-tuple-element.33.near_ref, bf16[2,256,512]{2,1,0:T(8,128)(2,1)} %collective-permute-done.10.far_ref, bf16[2,2,128,512]{3,2,1,0:T(8,128)(2,1)S(1)} %pad_maximum_fusion.low_ref, bf16[2,2,128,512]{3,2,1,0:T(8,128)(2,1)} %collective-permute-done.12.high_ref, ...), custom_call_target="tpu_custom_call" | custom-call | tf_op jit(solution)/shard_map/pallas_call | solution.py:266
  (27 shorter events, 0.1 us)
Async XLA Ops:
  1.8 19.1 %collective-permute-start = (bf16[320,1024]{1,0:T(8,128)(2,1)S(1)}, bf16[320,1024]{1,0:T(8,128)(2,1)S(1)}, u32[]{:S(2)}, u32[]{:S(2)}) collective-permute-start(bf16[320,1024]{1,0:T(8,128)(2,1)S(1)} %slice_bitcast_fusion), channel_id=1, source_target_pairs={{0,1},{1,0},{2,3},{3,2},{4,5},{5,4},{6,7},{7,6},{8,9},{9,8},{10,11... | collective-permute-start | bytes 1966088 | tf_op jit(solution)/shard_map/ppermute | solution.py:330
  3.9 33.7 %collective-permute-start.2 = (bf16[512,1024]{1,0:T(8,128)(2,1)}, bf16[512,1024]{1,0:T(8,128)(2,1)S(1)}, u32[]{:S(2)}, u32[]{:S(2)}) collective-permute-start(bf16[512,1024]{1,0:T(8,128)(2,1)} %bitcast.20), channel_id=1, source_target_pairs={{0,64},{64,0},{1,65},{65,1},{2,66},{66,2},{3,67},{67,3},{4,68},{68... | collective-permute-start | bytes 3145736 | tf_op jit(solution)/shard_map/ppermute | solution.py:329
  11.4 9.4 %collective-permute-start.1 = (bf16[2,128,512]{2,1,0:T(8,128)(2,1)}, bf16[2,128,512]{2,1,0:T(8,128)(2,1)S(1)}, u32[]{:S(2)}, u32[]{:S(2)}) collective-permute-start(bf16[2,128,512]{2,1,0:T(8,128)(2,1)} %get-tuple-element.20), channel_id=1, source_target_pairs={{0,3},{1,2},{2,1},{3,0},{4,7},{5,6},{6,5},{7,4},{8,11},{9,10},{10,... | collective-permute-start | bytes 786440 | tf_op jit(solution)/shard_map/ppermute | solution.py:338
  13.3 5.2 %copy-start.7 = (s32[1,8192]{1,0:T(1,128)S(1)}, s32[1,8192]{1,0:T(1,128)}, u32[]{:S(2)}) copy-start(s32[1,8192]{1,0:T(1,128)} %param.8) | copy-start | bytes 98308
  13.3 17.2 %copy-start.8 = (bf16[128,512]{1,0:T(8,128)(2,1)S(1)}, bf16[128,512]{1,0:T(8,128)(2,1)}, u32[]{:S(2)}) copy-start(bf16[128,512]{1,0:T(8,128)(2,1)} %get-tuple-element.24) | copy-start | bytes 393220
  18.4 21.9 %copy-start = (bf16[1,512,1024]{2,1,0:T(8,128)(2,1)S(1)}, bf16[1,512,1024]{2,1,0:T(8,128)(2,1)}, u32[]{:S(2)}) copy-start(bf16[1,512,1024]{2,1,0:T(8,128)(2,1)} %param.10) | copy-start | bytes 3145732
  20.8 0.7 copy-start.6
  21.5 30.9 %copy-start.4 = (bf16[320,1024]{1,0:T(8,128)(2,1)}, bf16[320,1024]{1,0:T(8,128)(2,1)S(1)}, u32[]{:S(2)}) copy-start(bf16[320,1024]{1,0:T(8,128)(2,1)S(1)} %collective-permute-done.n1a_ref) | copy-start | bytes 1966084
  21.5 18.7 %all-to-all-start = ((bf16[16,72,256]{2,1,0:T(8,128)(2,1)}), bf16[16,72,256]{2,1,0:T(8,128)(2,1)S(1)}, u32[]{:S(2)}, u32[]{:S(2)}) async-start(bf16[16,72,256]{2,1,0:T(8,128)(2,1)} %bitcast.25), calls=%async_computation | async-start | bytes 1179648 | tf_op jit(solution)/shard_map/all_to_all | solution.py:342
  29.3 11.0 %collective-permute-start.3 = (bf16[320,1024]{1,0:T(8,128)(2,1)S(1)}, bf16[320,1024]{1,0:T(8,128)(2,1)}, u32[]{:S(2)}, u32[]{:S(2)}) collective-permute-start(bf16[320,1024]{1,0:T(8,128)(2,1)S(1)} %collective-permute-done.n1a_ref), channel_id=1, source_target_pairs={{0,64},{64,0},{1,65},{65,1},{2,66},{66,2},{3,67},{67,3},{4,68},{68... | collective-permute-start | bytes 1966088 | tf_op jit(solution)/shard_map/ppermute | solution.py:351
  31.4 5.2 %collective-permute-start.4 = (bf16[128,512]{1,0:T(8,128)(2,1)S(1)}, bf16[128,512]{1,0:T(8,128)(2,1)S(1)}, u32[]{:S(2)}, u32[]{:S(2)}) collective-permute-start(bf16[128,512]{1,0:T(8,128)(2,1)S(1)} %fusion), channel_id=1, source_target_pairs={{0,1},{1,0},{2,3},{3,2},{4,5},{5,4},{6,7},{7,6},{8,9},{9,8},{10,11... | collective-permute-start | bytes 393224 | tf_op jit(solution)/shard_map/ppermute | solution.py:346
  37.6 14.8 %copy-start.2 = (bf16[512,1024]{1,0:T(8,128)(2,1)}, bf16[512,1024]{1,0:T(8,128)(2,1)S(1)}, u32[]{:S(2)}) copy-start(bf16[512,1024]{1,0:T(8,128)(2,1)S(1)} %collective-permute-done.2.f0_ref) | copy-start | bytes 3145732
  40.3 12.1 %collective-permute-start.7 = (bf16[192,1024]{1,0:T(8,128)(2,1)S(1)}, bf16[192,1024]{1,0:T(8,128)(2,1)S(1)}, u32[]{:S(2)}, u32[]{:S(2)}) collective-permute-start(bf16[192,1024]{1,0:T(8,128)(2,1)S(1)} %slice.19), channel_id=1, source_target_pairs={{0,1},{1,0},{2,3},{3,2},{4,5},{5,4},{6,7},{7,6},{8,9},{9,8},{10,11... | collective-permute-start | bytes 1179656 | tf_op jit(solution)/shard_map/ppermute | solution.py:354
  41.3 8.6 %collective-permute-start.5 = (bf16[256,512]{1,0:T(8,128)(2,1)S(1)}, bf16[256,512]{1,0:T(8,128)(2,1)S(1)}, u32[]{:S(2)}, u32[]{:S(2)}) collective-permute-start(bf16[256,512]{1,0:T(8,128)(2,1)S(1)} %shard_map.88.mine_ref), channel_id=1, source_target_pairs={{64,67},{65,66},{66,65},{67,64},{68,71},{69,70},{70,69},{71,68},{7... | collective-permute-start | bytes 786440 | tf_op jit(solution)/shard_map/ppermute | solution.py:357
  45.0 7.4 %collective-permute-start.6 = (bf16[256,512]{1,0:T(8,128)(2,1)S(1)}, bf16[256,512]{1,0:T(8,128)(2,1)S(1)}, u32[]{:S(2)}, u32[]{:S(2)}) collective-permute-start(bf16[256,512]{1,0:T(8,128)(2,1)S(1)} %shard_map.88.mine_ref), channel_id=1, source_target_pairs={{0,67},{1,66},{2,65},{3,64},{64,0},{65,1},{66,2},{67,3},{4,71},{5,... | collective-permute-start | bytes 786440 | tf_op jit(solution)/shard_map/ppermute | solution.py:356
  45.1 4.2 %collective-permute-start.8 = (bf16[128,512]{1,0:T(8,128)(2,1)S(1)}, bf16[128,512]{1,0:T(8,128)(2,1)S(1)}, u32[]{:S(2)}, u32[]{:S(2)}) collective-permute-start(bf16[128,512]{1,0:T(8,128)(2,1)S(1)} %fusion.2), channel_id=1, source_target_pairs={{0,4},{4,0},{8,12},{12,8},{16,20},{20,16},{24,28},{28,24},{32,36},... | collective-permute-start | bytes 393224 | tf_op jit(solution)/shard_map/ppermute | solution.py:358
  52.4 1.7 %collective-permute-start.9 = (bf16[192,1024]{1,0:T(8,128)(2,1)S(1)}, bf16[192,1024]{1,0:T(8,128)(2,1)S(1)}, u32[]{:S(2)}, u32[]{:S(2)}) collective-permute-start(bf16[192,1024]{1,0:T(8,128)(2,1)S(1)} %collective-permute-done.7.n1b_ref), channel_id=1, source_target_pairs={{0,64},{64,0},{1,65},{65,1},{2,66},{66,2},{3,67},{67,3},{4,68},{68... | collective-permute-start | bytes 1179656 | tf_op jit(solution)/shard_map/ppermute | solution.py:359
  54.2 1.2 %copy-start.3 = (bf16[512,1024]{1,0:T(8,128)(2,1)S(1)}, bf16[512,1024]{1,0:T(8,128)(2,1)}, u32[]{:S(2)}) copy-start(bf16[512,1024]{1,0:T(8,128)(2,1)} %copy-done.2) | copy-start | bytes 3145732
  55.4 1.1 copy-start.5
  59.6 25.2 %all-to-all-start.1 = ((bf16[16,256,128]{2,1,0:T(8,128)(2,1)}), bf16[16,256,128]{2,1,0:T(8,128)(2,1)}, u32[]{:S(2)}, u32[]{:S(2)}) async-start(bf16[16,256,128]{2,1,0:T(8,128)(2,1)} %get-tuple-element.30), calls=%async_computation.1 | async-start | bytes 2097152 | tf_op jit(solution)/shard_map/all_to_all | solution.py:364
  64.1 18.7 %collective-permute-start.11 = (bf16[2,128,512]{2,1,0:T(8,128)(2,1)S(1)}, bf16[2,128,512]{2,1,0:T(8,128)(2,1)S(1)}, u32[]{:S(2)}, u32[]{:S(2)}) collective-permute-start(bf16[2,128,512]{2,1,0:T(8,128)(2,1)S(1)} %pad_maximum_fusion.1), channel_id=1, source_target_pairs={{0,16},{4,20},{8,24},{12,28},{16,0},{20,4},{24,8},{28,12},{32,48},... | collective-permute-start | bytes 786440 | tf_op jit(solution)/shard_map/ppermute | solution.py:361
  82.9 17.7 %collective-permute-start.12 = (bf16[2,2,128,512]{3,2,1,0:T(8,128)(2,1)S(1)}, bf16[2,2,128,512]{3,2,1,0:T(8,128)(2,1)}, u32[]{:S(2)}, u32[]{:S(2)}) collective-permute-start(bf16[2,2,128,512]{3,2,1,0:T(8,128)(2,1)S(1)} %pad_maximum_fusion.low_ref), channel_id=1, source_target_pairs={{0,48},{4,52},{8,56},{12,60},{16,32},{20,36},{24,40},{28,44},{32,1... | collective-permute-start | bytes 1572872 | tf_op jit(solution)/shard_map/ppermute | solution.py:366
  84.8 24.3 %copy-start.1 = (bf16[1024,1024]{1,0:T(8,128)(2,1)S(1)}, bf16[1024,1024]{1,0:T(8,128)(2,1)}, u32[]{:S(2)}) copy-start(bf16[1024,1024]{1,0:T(8,128)(2,1)} %get-tuple-element.18.w_ref) | copy-start | bytes 6291460
  84.8 15.9 %collective-permute-start.10 = (bf16[2,256,512]{2,1,0:T(8,128)(2,1)S(1)}, bf16[2,256,512]{2,1,0:T(8,128)(2,1)}, u32[]{:S(2)}, u32[]{:S(2)}) collective-permute-start(bf16[2,256,512]{2,1,0:T(8,128)(2,1)S(1)} %get-tuple-element.33.near_ref), channel_id=1, source_target_pairs={{0,1},{1,0},{2,3},{3,2},{4,5},{5,4},{6,7},{7,6},{8,9},{9,8},{10,11... | collective-permute-start | bytes 1572872 | tf_op jit(solution)/shard_map/ppermute | solution.py:368
  86.3 14.3 %collective-permute-start.13 = (bf16[256,128]{1,0:T(8,128)(2,1)S(1)}, bf16[256,128]{1,0:T(8,128)(2,1)S(1)}, u32[]{:S(2)}, u32[]{:S(2)}) collective-permute-start(bf16[256,128]{1,0:T(8,128)(2,1)S(1)} %reduce_sum.22), channel_id=1, source_target_pairs={{0,0},{1,1},{2,64},{3,65},{64,2},{65,3},{66,66},{67,67},{4,4},{5,5... | collective-permute-start | bytes 196616 | tf_op jit(solution)/shard_map/ppermute | solution.py:372
  102.7 8.0 %collective-permute-start.14 = (bf16[512,1024]{1,0:T(8,128)(2,1)S(1)}, bf16[512,1024]{1,0:T(8,128)(2,1)S(1)}, u32[]{:S(2)}, u32[]{:S(2)}) collective-permute-start(bf16[512,1024]{1,0:T(8,128)(2,1)S(1)} %shard_map.90), channel_id=1, source_target_pairs={{0,64},{64,0},{1,65},{65,1},{2,66},{66,2},{3,67},{67,3},{4,68},{68... | collective-permute-start | bytes 3145736 | tf_op jit(solution)/shard_map/ppermute | solution.py:374
  102.8 6.2 %collective-permute-start.15 = (bf16[256,128]{1,0:T(8,128)(2,1)S(1)}, bf16[256,128]{1,0:T(8,128)(2,1)S(1)}, u32[]{:S(2)}, u32[]{:S(2)}) collective-permute-start(bf16[256,128]{1,0:T(8,128)(2,1)S(1)} %reduce_sum.22), channel_id=1, source_target_pairs={{0,1},{1,0},{2,65},{3,64},{64,3},{65,2},{66,67},{67,66},{4,5},{5,4... | collective-permute-start | bytes 196616 | tf_op jit(solution)/shard_map/ppermute | solution.py:372
  103.1 5.9 %collective-permute-start.16 = (bf16[256,128]{1,0:T(8,128)(2,1)S(1)}, bf16[256,128]{1,0:T(8,128)(2,1)S(1)}, u32[]{:S(2)}, u32[]{:S(2)}) collective-permute-start(bf16[256,128]{1,0:T(8,128)(2,1)S(1)} %reduce_sum.22), channel_id=1, source_target_pairs={{0,2},{1,3},{2,66},{3,67},{64,0},{65,1},{66,64},{67,65},{4,6},{5,7... | collective-permute-start | bytes 196616 | tf_op jit(solution)/shard_map/ppermute | solution.py:372
  103.3 5.7 %collective-permute-start.17 = (bf16[256,128]{1,0:T(8,128)(2,1)S(1)}, bf16[256,128]{1,0:T(8,128)(2,1)S(1)}, u32[]{:S(2)}, u32[]{:S(2)}) collective-permute-start(bf16[256,128]{1,0:T(8,128)(2,1)S(1)} %reduce_sum.22), channel_id=1, source_target_pairs={{0,3},{1,2},{2,67},{3,66},{64,1},{65,0},{66,65},{67,64},{4,7},{5,6... | collective-permute-start | bytes 196616 | tf_op jit(solution)/shard_map/ppermute | solution.py:372

commit v8 on v7

--- a/solution.py
+++ b/solution.py
@@ -131,24 +131,36 @@
     )(first, incoming)
 
 
-def outer_kernel(mine_ref, third_ref, cross_ref, n0_ref, n1a_ref, n1b_ref, f0_ref, f1a_ref, f1b_ref, out_ref, both_ref, held_ref, sems):
+def outer_kernel(mine_ref, third_ref, cross_ref, n0_ref, n1a_ref, n1b_ref, f0_ref, f1a_ref, f1b_ref, out_ref, both_ref, cols_ref, held_ref, in_sems, sems):
+    cut, cols = n1a_ref.shape
+    rows = n0_ref.shape[0]
+    arrivals = []
+    for k, (ref, to, low, high) in enumerate((
+        (n0_ref, 0, 0, rows),
+        (f0_ref, 1, 0, rows),
+        (n1a_ref, 2, 0, cut),
+        (n1b_ref, 2, cut, rows),
+        (f1a_ref, 3, 0, cut),
+        (f1b_ref, 3, cut, rows),
+    )):
+        arrivals.append(pltpu.make_async_copy(ref, cols_ref.at[to, pl.ds(low, high - low)], in_sems.at[k]))
+        arrivals[k].start()
     near_t = jnp.where(lax.axis_index("dp") == 0, mine_ref[...], third_ref[...])
     far_t = cross_ref[...]
     both_ref[0] = near_t
     both_ref[1] = far_t
     low = lax.rem(lax.axis_index("tensor"), 2)
     blocks = out_ref.shape[0] // 2
-    cols = n0_ref.shape[1]
     wide = 256
     per = wide // LANES
     copies = []
-    for i in range(cols // wide):
-        at = slice(i * wide, (i + 1) * wide)
-        near1 = jnp.concatenate([n1a_ref[:, at], n1b_ref[:, at]], axis=0)
-        far1 = jnp.concatenate([f1a_ref[:, at], f1b_ref[:, at]], axis=0)
-        for k, (near, far, which) in enumerate(((n0_ref[:, at], f0_ref[:, at], low), (near1, far1, 1 - low))):
-            total = jnp.dot(near_t, near, preferred_element_type=jnp.float32)
-            total += jnp.dot(far_t, far, preferred_element_type=jnp.float32)
+    for k, which in ((0, low), (1, 1 - low)):
+        for arrival in arrivals[:2] if k == 0 else arrivals[2:]:
+            arrival.wait()
+        for i in range(cols // wide):
+            at = slice(i * wide, (i + 1) * wide)
+            total = jnp.dot(near_t, cols_ref[2 * k, :, at], preferred_element_type=jnp.float32)
+            total += jnp.dot(far_t, cols_ref[2 * k + 1, :, at], preferred_element_type=jnp.float32)
             total = total.astype(jnp.bfloat16)
             here = k * blocks + i * per
             for j in range(per):
@@ -171,14 +183,19 @@
     shape = (2 * cols // LANES, width, LANES)
     return pl.pallas_call(
         outer_kernel,
-        in_specs=[vmem] * (len(sums) + len(columns)),
+        in_specs=[vmem] * len(sums) + [pl.BlockSpec(memory_space=pl.ANY)] * len(columns),
         out_specs=[pl.BlockSpec(memory_space=pltpu.HBM), vmem],
         out_shape=[
             jax.ShapeDtypeStruct(shape, jnp.bfloat16),
             jax.ShapeDtypeStruct((2, width, rows), jnp.bfloat16),
         ],
-        scratch_shapes=[pltpu.VMEM(shape, jnp.bfloat16), pltpu.SemaphoreType.DMA((2 * cols // 256,))],
-        compiler_params=pltpu.CompilerParams(vmem_limit_bytes=VMEM),
+        scratch_shapes=[
+            pltpu.VMEM((4, rows, cols), jnp.bfloat16),
+            pltpu.VMEM(shape, jnp.bfloat16),
+            pltpu.SemaphoreType.DMA((len(columns),)),
+            pltpu.SemaphoreType.DMA((2 * cols // 256,)),
+        ],
+        compiler_params=pltpu.CompilerParams(vmem_limit_bytes=62 * 1024 * 1024),
     )(*sums, *columns)
 
 
@@ -360,7 +377,7 @@
     chain = jnp.stack([chain, other])
     other = lax.ppermute(chain, "context", along(lambda i, j: (i ^ 1, j)))
     columns = (near0, *near1, far0, *far1)
-    partial, near = outer((sums, third, cross), columns)
+    partial, near = outer((after(sums, other), third, cross), columns)
     pieces = lax.all_to_all(partial, "context", split_axis=0, concat_axis=0, tiled=True)
     chain = jnp.stack([after(chain, partial), after(other, partial)])
     rest = lax.ppermute(chain, "context", along(lambda i, j: (SIDE - 1 - i, j)))
@@ -370,7 +387,7 @@
     parts = []
     for s in range(ten_n):
         parts.append(lax.ppermute(piece, line, moves(lambda d, x, s=s: (x // 2, (2 * d + x % 2) ^ s))))
-    give = context_rows(1, after(near, parts[0]), far, chain, rest)
+    give = context_rows(1, after(near, *parts), far, chain, rest)
     back = lax.ppermute(give, "dp", swap)
     context_grad = context_rows(0, near, far, chain, rest, back)
     weight_grad = last(parts, both_t)

time: 114 us -> 113 us (level); the launches traced: 114 us -> 111 us
  waiting for transfers between devices: 46 us -> 39.4 us
  Pallas kernels: 22.3 us -> 25.1 us
  starting transfers between devices: 36.5 us -> 38.7 us
    all_to_all x1, waiting for transfers between devices: 0.01 us -> 12.6 us  [local(): lax.all_to_all(partial, 'context', split_axis=0, concat_axis=0, tiled=True)]
    ppermute x1, waiting for transfers between devices: 17.3 us -> 8.05 us  [local(): other = lax.ppermute(chain, 'context', along(lambda i, j: (i ^ 1, j)))]
    ppermute x4, waiting for transfers between devices: 10.2 us -> 2.63 us  [local(): lax.ppermute(piece, line, moves(lambda d, x, s=s: (x // 2, 2 * d + x % 2...]
    pallas_call x1, Pallas kernels: 3.12 us -> 5.71 us  [outer(): pl.pallas_call(outer_kernel, in_specs=[vmem] * len(sums) + [pl.BlockSpec(...]
    ppermute x1, waiting for transfers between devices: 2.52 us -> 0.01 us  [local(): lax.ppermute(sums, line, moves(lambda d, x: (0, x) if d == 1 else (1, ten...]
    ppermute x1, starting transfers between devices: 0.07 us -> 2.29 us  [local(): lax.ppermute(sums, line, moves(lambda d, x: (0, x) if d == 1 else (1, ten...]
    ppermute x1, waiting for transfers between devices: 1.71 us -> 0.01 us  [local(): far1.append(lax.ppermute(after(near1[1], cross, third, other), 'dp', swap))]
    unnamed x18 -> x26, local copies, waits for them, and re-layouts: 3.04 us -> 1.37 us
  transfers between devices with their start and end apart: 20 -> 20, of which waited for: 10 -> 10; matrix products, arithmetic and copies ran while one was open for 3% -> 2% of each run, Pallas kernels for 12% -> 13%
where the time goes in v8:
time: 113 us; the launch traced here: 111 us
  waiting for transfers between devices  39.4 us (35%)
  starting transfers between devices  38.7 us (34%)
  Pallas kernels  25.1 us (22%)
  local copies, waits for them, and re-layouts  3.76 us (3%)
  other arithmetic  2.72 us (2%)
    all_to_all x1, waiting for transfers between devices, local(): lax.all_to_all(partial, 'context', split_axis=0, concat_axis=0, tiled=True)  12.6 us
    ppermute x4, starting transfers between devices, local(): lax.ppermute(piece, line, moves(lambda d, x, s=s: (x // 2, 2 * d + x % 2...  9.91 us
    ppermute x1, waiting for transfers between devices, local(): other = lax.ppermute(chain, 'context', along(lambda i, j: (i ^ 1, j)))  8.05 us
    all_to_all x1, starting transfers between devices, local(): lax.all_to_all(outgoing, 'context', split_axis=0, concat_axis=0, tiled=True)  7.77 us
    pallas_call x1, Pallas kernels, chain_terms(): pl.pallas_call(chain_kernel, in_specs=[vmem, vmem, pl.BlockSpec(memory_sp...  6.54 us
    pallas_call x1, Pallas kernels, outer(): pl.pallas_call(outer_kernel, in_specs=[vmem] * len(sums) + [pl.BlockSpec(...  5.71 us
    pallas_call x1, Pallas kernels, segment_sums(): pl.pallas_call(seg_kernel, in_specs=[vmem, vmem, pl.BlockSpec(memory_spac...  5.34 us
    ppermute x1, waiting for transfers between devices, local(): paired = lax.ppermute(paired, 'tensor', pair)  5.08 us
  transfers between devices with their start and end apart: 20, of which 10 were waited for; matrix products, arithmetic and copies ran while one was open for 2% of the time, Pallas kernels for 13%

profile of v8, /device:TPU:1, one launch (start us, length us, event | category | flops | bytes accessed | tf_op | source)
XLA Modules:
  0.0 110.6 jit_solution(15353925005281907034)
XLA Ops:
  0.6 1.1 %slice_bitcast_fusion = bf16[320,1024]{1,0:T(8,128)(2,1)S(1)} fusion(bf16[1,512,1024]{2,1,0:T(8,128)(2,1)} %param.10), kind=kLoop, calls=%fused_computation | loop fusion | bytes 1310720 | tf_op jit(solution)/shard_map/slice | solution.py:347
  1.8 2.1 %collective-permute-start = (bf16[320,1024]{1,0:T(8,128)(2,1)S(1)}, bf16[320,1024]{1,0:T(8,128)(2,1)S(1)}, u32[]{:S(2)}, u32[]{:S(2)}) collective-permute-start(bf16[320,1024]{1,0:T(8,128)(2,1)S(1)} %slice_bitcast_fusion), channel_id=1, source_target_pairs={{0,1},{1,0},{2,3},{3,2},{4,5},{5,4},{6,7},{7,6},{8,9},{9,8},{10,11... | collective-permute-start | bytes 1966088 | tf_op jit(solution)/shard_map/ppermute | solution.py:347
  3.9 1.0 collective-permute-start.2
  4.8 6.5 %shard_map.86 = (bf16[1024,1024]{1,0:T(8,128)(2,1)}, bf16[128,512]{1,0:T(8,128)(2,1)}, bf16[128,512]{1,0:T(8,128)(2,1)}, bf16[2,128,512]{2,1,0:T(8,128)(2,1)}) custom-call(bf16[1024,1024]{1,0:T(8,128)(2,1)} %value_ref.1, bf16[1024,1024]{1,0:T(8,128)(2,1)} %out_w_ref.1, bf16[4096,1024]{1,0:T(8,128)(2,1)} %global_ref.1), custom_call_target="tpu_custom_call" | custom-call | tf_op jit(solution)/shard_map/pallas_call | solution.py:244
  11.4 1.9 %collective-permute-start.1 = (bf16[2,128,512]{2,1,0:T(8,128)(2,1)}, bf16[2,128,512]{2,1,0:T(8,128)(2,1)S(1)}, u32[]{:S(2)}, u32[]{:S(2)}) collective-permute-start(bf16[2,128,512]{2,1,0:T(8,128)(2,1)} %get-tuple-element.21), channel_id=1, source_target_pairs={{0,3},{1,2},{2,1},{3,0},{4,7},{5,6},{6,5},{7,4},{8,11},{9,10},{10,... | collective-permute-start | bytes 786440 | tf_op jit(solution)/shard_map/ppermute | solution.py:355
  13.3 5.3 %shard_map.87 = bf16[1152,256]{1,0:T(8,128)(2,1)} custom-call(s32[64,128]{1,0:T(8,128)} %bitcast.30, s32[64,128]{1,0:T(8,128)} %bitcast.33, bf16[4096,1024]{1,0:T(8,128)(2,1)} %bitcast.21), custom_call_target="tpu_custom_call" | custom-call | tf_op jit(solution)/shard_map/pallas_call | solution.py:94
  18.7 0.3 convert_reduce_fusion
  18.9 1.9 %collective-permute-done.1 = bf16[2,128,512]{2,1,0:T(8,128)(2,1)S(1)} collective-permute-done((bf16[2,128,512]{2,1,0:T(8,128)(2,1)}, bf16[2,128,512]{2,1,0:T(8,128)(2,1)S(1)}, u32[]{:S(2)}, u32[]{:S(2)}) %collective-permute-start.1) | collective-permute-done | bytes 262176 | tf_op jit(solution)/shard_map/ppermute | solution.py:355
  20.8 7.8 %all-to-all-start = ((bf16[16,72,256]{2,1,0:T(8,128)(2,1)}), bf16[16,72,256]{2,1,0:T(8,128)(2,1)S(1)}, u32[]{:S(2)}, u32[]{:S(2)}) async-start(bf16[16,72,256]{2,1,0:T(8,128)(2,1)} %bitcast.25), calls=%async_computation | async-start | bytes 1179648 | tf_op jit(solution)/shard_map/all_to_all | solution.py:359
  28.6 1.1 %collective-permute-start.3 = (bf16[320,1024]{1,0:T(8,128)(2,1)S(1)}, bf16[320,1024]{1,0:T(8,128)(2,1)S(1)}, u32[]{:S(2)}, u32[]{:S(2)}) collective-permute-start(bf16[320,1024]{1,0:T(8,128)(2,1)S(1)} %collective-permute-done.n1a_ref), channel_id=1, source_target_pairs={{0,64},{64,0},{1,65},{65,1},{2,66},{66,2},{3,67},{67,3},{4,68},{68... | collective-permute-start | bytes 1966088 | tf_op jit(solution)/shard_map/ppermute | solution.py:368
  29.8 0.1 collective-permute-start.4
  29.9 5.1 %collective-permute-done.4 = bf16[128,512]{1,0:T(8,128)(2,1)S(1)} collective-permute-done((bf16[128,512]{1,0:T(8,128)(2,1)S(1)}, bf16[128,512]{1,0:T(8,128)(2,1)S(1)}, u32[]{:S(2)}, u32[]{:S(2)}) %collective-permute-start.4) | collective-permute-done | bytes 131104 | tf_op jit(solution)/shard_map/ppermute | solution.py:363
  35.0 1.0 fusion.2
  35.9 0.0 collective-permute-done.2.f0_ref
  36.0 0.0 copy-start.3
  36.0 3.6 %all-to-all-done = bf16[16,72,256]{2,1,0:T(8,128)(2,1)S(1)} async-done(((bf16[16,72,256]{2,1,0:T(8,128)(2,1)}), bf16[16,72,256]{2,1,0:T(8,128)(2,1)S(1)}, u32[]{:S(2)}, u32[]{:S(2)}) %all-to-all-start) | async-done | bytes 589856 | tf_op jit(solution)/shard_map/all_to_all | solution.py:359
  39.6 1.3 %slice.19 = bf16[192,1024]{1,0:T(8,128)(2,1)S(1)} slice(bf16[512,1024]{1,0:T(8,128)(2,1)} %bitcast.23), slice={[320:512], [0:1024]} | slice | bytes 786432 | tf_op jit(solution)/shard_map/slice | solution.py:371
  40.9 0.1 collective-permute-start.9
  41.0 0.9 shard_map.88.mine_ref
  41.9 2.3 %collective-permute-start.8 = (bf16[256,512]{1,0:T(8,128)(2,1)S(1)}, bf16[256,512]{1,0:T(8,128)(2,1)S(1)}, u32[]{:S(2)}, u32[]{:S(2)}) collective-permute-start(bf16[256,512]{1,0:T(8,128)(2,1)S(1)} %shard_map.88.mine_ref), channel_id=1, source_target_pairs={{0,67},{1,66},{2,65},{3,64},{64,0},{65,1},{66,2},{67,3},{4,71},{5,... | collective-permute-start | bytes 786440 | tf_op jit(solution)/shard_map/ppermute | solution.py:373
  44.1 3.7 %collective-permute-start.7 = (bf16[256,512]{1,0:T(8,128)(2,1)S(1)}, bf16[256,512]{1,0:T(8,128)(2,1)S(1)}, u32[]{:S(2)}, u32[]{:S(2)}) collective-permute-start(bf16[256,512]{1,0:T(8,128)(2,1)S(1)} %shard_map.88.mine_ref), channel_id=1, source_target_pairs={{64,67},{65,66},{66,65},{67,64},{68,71},{69,70},{70,69},{71,68},{7... | collective-permute-start | bytes 786440 | tf_op jit(solution)/shard_map/ppermute | solution.py:374
  47.8 0.4 collective-permute-start.5
  48.2 3.8 %collective-permute-done.5 = bf16[128,512]{1,0:T(8,128)(2,1)S(1)} collective-permute-done((bf16[128,512]{1,0:T(8,128)(2,1)S(1)}, bf16[128,512]{1,0:T(8,128)(2,1)S(1)}, u32[]{:S(2)}, u32[]{:S(2)}) %collective-permute-start.5) | collective-permute-done | bytes 131104 | tf_op jit(solution)/shard_map/ppermute | solution.py:375
  52.0 0.0 collective-permute-done.8.cross_ref
  52.0 0.6 collective-permute-done.7.third_ref
  52.7 0.1 collective-permute-start.10
  52.8 0.6 copy-done.8
  53.4 0.1 collective-permute-start.6
  53.5 8.1 %collective-permute-done.6 = bf16[2,128,512]{2,1,0:T(8,128)(2,1)S(1)} collective-permute-done((bf16[2,128,512]{2,1,0:T(8,128)(2,1)S(1)}, bf16[2,128,512]{2,1,0:T(8,128)(2,1)S(1)}, u32[]{:S(2)}, u32[]{:S(2)}) %collective-permute-start.6) | collective-permute-done | bytes 262176 | tf_op jit(solution)/shard_map/ppermute | solution.py:378
  61.6 0.7 copy-done.9
  62.3 5.7 %shard_map.89 = (bf16[16,256,128]{2,1,0:T(8,128)(2,1)}, bf16[2,256,512]{2,1,0:T(8,128)(2,1)}) custom-call(bf16[256,512]{1,0:T(8,128)(2,1)} %copy-done.2, bf16[256,512]{1,0:T(8,128)(2,1)} %copy-done.8, bf16[256,512]{1,0:T(8,128)(2,1)} %copy-done.7, bf16[512,1024]{1,0:T(8,128)(2,1)} %bitcast.24, bf16[320,1024]{1,0:T(8,128)(2,1)} %copy-done.4, ...), custom_call_target="tpu_custom_call" | custom-call | tf_op jit(solution)/shard_map/pallas_call | solution.py:184
  68.1 0.0 copy-start.1
  68.1 4.5 %all-to-all-start.1 = ((bf16[16,256,128]{2,1,0:T(8,128)(2,1)}), bf16[16,256,128]{2,1,0:T(8,128)(2,1)}, u32[]{:S(2)}, u32[]{:S(2)}) async-start(bf16[16,256,128]{2,1,0:T(8,128)(2,1)} %get-tuple-element.32), calls=%async_computation.1 | async-start | bytes 2097152 | tf_op jit(solution)/shard_map/all_to_all | solution.py:381
  72.6 0.1 pad_maximum_fusion.low_ref
  72.6 2.5 %collective-permute-start.12 = (bf16[2,2,128,512]{3,2,1,0:T(8,128)(2,1)S(1)}, bf16[2,2,128,512]{3,2,1,0:T(8,128)(2,1)}, u32[]{:S(2)}, u32[]{:S(2)}) collective-permute-start(bf16[2,2,128,512]{3,2,1,0:T(8,128)(2,1)S(1)} %pad_maximum_fusion.low_ref), channel_id=1, source_target_pairs={{0,48},{4,52},{8,56},{12,60},{16,32},{20,36},{24,40},{28,44},{32,1... | collective-permute-start | bytes 1572872 | tf_op jit(solution)/shard_map/ppermute | solution.py:383
  75.2 1.1 %collective-permute-start.11 = (bf16[2,256,512]{2,1,0:T(8,128)(2,1)S(1)}, bf16[2,256,512]{2,1,0:T(8,128)(2,1)}, u32[]{:S(2)}, u32[]{:S(2)}) collective-permute-start(bf16[2,256,512]{2,1,0:T(8,128)(2,1)S(1)} %copy-done.1), channel_id=1, source_target_pairs={{0,1},{1,0},{2,3},{3,2},{4,5},{5,4},{6,7},{7,6},{8,9},{9,8},{10,11... | collective-permute-start | bytes 1572872 | tf_op jit(solution)/shard_map/ppermute | solution.py:385
  76.3 12.6 %all-to-all-done.1 = bf16[16,256,128]{2,1,0:T(8,128)(2,1)} async-done(((bf16[16,256,128]{2,1,0:T(8,128)(2,1)}), bf16[16,256,128]{2,1,0:T(8,128)(2,1)}, u32[]{:S(2)}, u32[]{:S(2)}) %all-to-all-start.1) | async-done | bytes 1048608 | tf_op jit(solution)/shard_map/all_to_all | solution.py:381
  88.9 1.4 %reduce_sum.22 = bf16[256,128]{1,0:T(8,128)(2,1)S(1)} reduce(bf16[16,256,128]{2,1,0:T(8,128)(2,1)} %all-to-all-done.1, bf16[]{:T(256)} %constant.25.clone.1), dimensions={0}, to_apply=%region_1.2 | reduce | flops 491520 | bytes 1114114 | tf_op jit(solution)/shard_map/reduce_sum | solution.py:386
  90.3 3.3 %collective-permute-start.16 = (bf16[256,128]{1,0:T(8,128)(2,1)S(1)}, bf16[256,128]{1,0:T(8,128)(2,1)S(1)}, u32[]{:S(2)}, u32[]{:S(2)}) collective-permute-start(bf16[256,128]{1,0:T(8,128)(2,1)S(1)} %reduce_sum.22), channel_id=1, source_target_pairs={{0,3},{1,2},{2,67},{3,66},{64,1},{65,0},{66,65},{67,64},{4,7},{5,6... | collective-permute-start | bytes 196616 | tf_op jit(solution)/shard_map/ppermute | solution.py:389
  93.5 0.8 collective-permute-start.15
  94.4 0.7 collective-permute-done.16.d_ref
  95.1 5.8 %collective-permute-start.13 = (bf16[256,128]{1,0:T(8,128)(2,1)S(1)}, bf16[256,128]{1,0:T(8,128)(2,1)S(1)}, u32[]{:S(2)}, u32[]{:S(2)}) collective-permute-start(bf16[256,128]{1,0:T(8,128)(2,1)S(1)} %reduce_sum.22), channel_id=1, source_target_pairs={{0,0},{1,1},{2,64},{3,65},{64,2},{65,3},{66,66},{67,67},{4,4},{5,5... | collective-permute-start | bytes 196616 | tf_op jit(solution)/shard_map/ppermute | solution.py:389
  100.9 1.9 %collective-permute-done.13.a_ref = bf16[256,128]{1,0:T(8,128)(2,1)S(1)} collective-permute-done((bf16[256,128]{1,0:T(8,128)(2,1)S(1)}, bf16[256,128]{1,0:T(8,128)(2,1)S(1)}, u32[]{:S(2)}, u32[]{:S(2)}) %collective-permute-start.13) | collective-permute-done | bytes 65568 | tf_op jit(solution)/shard_map/ppermute | solution.py:389
  102.8 2.0 %shard_map.90 = bf16[512,1024]{1,0:T(8,128)(2,1)S(1)} custom-call(bf16[2,256,512]{2,1,0:T(8,128)(2,1)S(1)} %copy-done.1, bf16[2,256,512]{2,1,0:T(8,128)(2,1)} %collective-permute-done.11.far_ref, bf16[2,2,128,512]{3,2,1,0:T(8,128)(2,1)S(1)} %pad_maximum_fusion.low_ref, bf16[2,2,128,512]{3,2,1,0:T(8,128)(2,1)} %collective-permute-done.12.high_ref), custom_call_target="tpu_custom_call" | custom-call | tf_op jit(solution)/shard_map/pallas_call | solution.py:283
  104.9 0.1 collective-permute-start.17
  105.0 1.6 %shard_map.92 = f32[128,1024]{1,0:T(8,128)} custom-call(bf16[256,128]{1,0:T(8,128)(2,1)S(1)} %collective-permute-done.13.a_ref, bf16[256,128]{1,0:T(8,128)(2,1)S(1)} %collective-permute-done.14.b_ref, bf16[256,128]{1,0:T(8,128)(2,1)S(1)} %collective-permute-done.15.c_ref, bf16[256,128]{1,0:T(8,128)(2,1)S(1)} %collective-permute-done.16.d_ref, ...), custom_call_target="tpu_custom_call" | custom-call | tf_op jit(solution)/shard_map/pallas_call | solution.py:312
  106.6 1.0 collective-permute-done.17.rest_0_
  107.6 3.0 %shard_map.91 = bf16[512,1024]{1,0:T(8,128)(2,1)} custom-call(bf16[2,256,512]{2,1,0:T(8,128)(2,1)S(1)} %copy-done.1, bf16[2,256,512]{2,1,0:T(8,128)(2,1)} %collective-permute-done.11.far_ref, bf16[2,2,128,512]{3,2,1,0:T(8,128)(2,1)S(1)} %pad_maximum_fusion.low_ref, bf16[2,2,128,512]{3,2,1,0:T(8,128)(2,1)} %collective-permute-done.12.high_ref, ...), custom_call_target="tpu_custom_call" | custom-call | tf_op jit(solution)/shard_map/pallas_call | solution.py:283
  (35 shorter events, 0.1 us)
Async XLA Ops:
  1.8 19.1 %collective-permute-start = (bf16[320,1024]{1,0:T(8,128)(2,1)S(1)}, bf16[320,1024]{1,0:T(8,128)(2,1)S(1)}, u32[]{:S(2)}, u32[]{:S(2)}) collective-permute-start(bf16[320,1024]{1,0:T(8,128)(2,1)S(1)} %slice_bitcast_fusion), channel_id=1, source_target_pairs={{0,1},{1,0},{2,3},{3,2},{4,5},{5,4},{6,7},{7,6},{8,9},{9,8},{10,11... | collective-permute-start | bytes 1966088 | tf_op jit(solution)/shard_map/ppermute | solution.py:347
  3.9 32.1 %collective-permute-start.2 = (bf16[512,1024]{1,0:T(8,128)(2,1)}, bf16[512,1024]{1,0:T(8,128)(2,1)S(1)}, u32[]{:S(2)}, u32[]{:S(2)}) collective-permute-start(bf16[512,1024]{1,0:T(8,128)(2,1)} %bitcast.22), channel_id=1, source_target_pairs={{0,64},{64,0},{1,65},{65,1},{2,66},{66,2},{3,67},{67,3},{4,68},{68... | collective-permute-start | bytes 3145736 | tf_op jit(solution)/shard_map/ppermute | solution.py:346
  11.4 9.4 %collective-permute-start.1 = (bf16[2,128,512]{2,1,0:T(8,128)(2,1)}, bf16[2,128,512]{2,1,0:T(8,128)(2,1)S(1)}, u32[]{:S(2)}, u32[]{:S(2)}) collective-permute-start(bf16[2,128,512]{2,1,0:T(8,128)(2,1)} %get-tuple-element.21), channel_id=1, source_target_pairs={{0,3},{1,2},{2,1},{3,0},{4,7},{5,6},{6,5},{7,4},{8,11},{9,10},{10,... | collective-permute-start | bytes 786440 | tf_op jit(solution)/shard_map/ppermute | solution.py:355
  13.3 5.4 %copy-start.11 = (s32[1,8192]{1,0:T(1,128)S(1)}, s32[1,8192]{1,0:T(1,128)}, u32[]{:S(2)}) copy-start(s32[1,8192]{1,0:T(1,128)} %param.8) | copy-start | bytes 98308
  13.3 16.5 %copy-start.12 = (bf16[128,512]{1,0:T(8,128)(2,1)S(1)}, bf16[128,512]{1,0:T(8,128)(2,1)}, u32[]{:S(2)}) copy-start(bf16[128,512]{1,0:T(8,128)(2,1)} %get-tuple-element.25) | copy-start | bytes 393220
  20.8 32.6 %copy-start.4 = (bf16[320,1024]{1,0:T(8,128)(2,1)}, bf16[320,1024]{1,0:T(8,128)(2,1)S(1)}, u32[]{:S(2)}) copy-start(bf16[320,1024]{1,0:T(8,128)(2,1)S(1)} %collective-permute-done.n1a_ref) | copy-start | bytes 1966084
  20.8 18.7 %all-to-all-start = ((bf16[16,72,256]{2,1,0:T(8,128)(2,1)}), bf16[16,72,256]{2,1,0:T(8,128)(2,1)S(1)}, u32[]{:S(2)}, u32[]{:S(2)}) async-start(bf16[16,72,256]{2,1,0:T(8,128)(2,1)} %bitcast.25), calls=%async_computation | async-start | bytes 1179648 | tf_op jit(solution)/shard_map/all_to_all | solution.py:359
  28.6 11.0 %collective-permute-start.3 = (bf16[320,1024]{1,0:T(8,128)(2,1)S(1)}, bf16[320,1024]{1,0:T(8,128)(2,1)S(1)}, u32[]{:S(2)}, u32[]{:S(2)}) collective-permute-start(bf16[320,1024]{1,0:T(8,128)(2,1)S(1)} %collective-permute-done.n1a_ref), channel_id=1, source_target_pairs={{0,64},{64,0},{1,65},{65,1},{2,66},{66,2},{3,67},{67,3},{4,68},{68... | collective-permute-start | bytes 1966088 | tf_op jit(solution)/shard_map/ppermute | solution.py:368
  29.8 5.2 %collective-permute-start.4 = (bf16[128,512]{1,0:T(8,128)(2,1)S(1)}, bf16[128,512]{1,0:T(8,128)(2,1)S(1)}, u32[]{:S(2)}, u32[]{:S(2)}) collective-permute-start(bf16[128,512]{1,0:T(8,128)(2,1)S(1)} %fusion), channel_id=1, source_target_pairs={{0,1},{1,0},{2,3},{3,2},{4,5},{5,4},{6,7},{7,6},{8,9},{9,8},{10,11... | collective-permute-start | bytes 393224 | tf_op jit(solution)/shard_map/ppermute | solution.py:363
  36.0 26.4 %copy-start.3 = (bf16[512,1024]{1,0:T(8,128)(2,1)}, bf16[512,1024]{1,0:T(8,128)(2,1)S(1)}, u32[]{:S(2)}) copy-start(bf16[512,1024]{1,0:T(8,128)(2,1)S(1)} %collective-permute-done.2.f0_ref) | copy-start | bytes 3145732
  39.6 1.3 %copy-start.5 = (bf16[320,1024]{1,0:T(8,128)(2,1)}, bf16[320,1024]{1,0:T(8,128)(2,1)S(1)}, u32[]{:S(2)}) copy-start(bf16[320,1024]{1,0:T(8,128)(2,1)S(1)} %collective-permute-done.3.f1a_ref) | copy-start | bytes 1966084
  40.9 11.8 %collective-permute-start.9 = (bf16[192,1024]{1,0:T(8,128)(2,1)S(1)}, bf16[192,1024]{1,0:T(8,128)(2,1)S(1)}, u32[]{:S(2)}, u32[]{:S(2)}) collective-permute-start(bf16[192,1024]{1,0:T(8,128)(2,1)S(1)} %slice.19), channel_id=1, source_target_pairs={{0,1},{1,0},{2,3},{3,2},{4,5},{5,4},{6,7},{7,6},{8,9},{9,8},{10,11... | collective-permute-start | bytes 1179656 | tf_op jit(solution)/shard_map/ppermute | solution.py:371
  41.8 20.5 %copy-start.2 = (bf16[256,512]{1,0:T(8,128)(2,1)}, bf16[256,512]{1,0:T(8,128)(2,1)S(1)}, u32[]{:S(2)}) copy-start(bf16[256,512]{1,0:T(8,128)(2,1)S(1)} %shard_map.88.mine_ref) | copy-start | bytes 786436
  41.9 10.2 %collective-permute-start.8 = (bf16[256,512]{1,0:T(8,128)(2,1)S(1)}, bf16[256,512]{1,0:T(8,128)(2,1)S(1)}, u32[]{:S(2)}, u32[]{:S(2)}) collective-permute-start(bf16[256,512]{1,0:T(8,128)(2,1)S(1)} %shard_map.88.mine_ref), channel_id=1, source_target_pairs={{0,67},{1,66},{2,65},{3,64},{64,0},{65,1},{66,2},{67,3},{4,71},{5,... | collective-permute-start | bytes 786440 | tf_op jit(solution)/shard_map/ppermute | solution.py:373
  44.1 8.5 %collective-permute-start.7 = (bf16[256,512]{1,0:T(8,128)(2,1)S(1)}, bf16[256,512]{1,0:T(8,128)(2,1)S(1)}, u32[]{:S(2)}, u32[]{:S(2)}) collective-permute-start(bf16[256,512]{1,0:T(8,128)(2,1)S(1)} %shard_map.88.mine_ref), channel_id=1, source_target_pairs={{64,67},{65,66},{66,65},{67,64},{68,71},{69,70},{70,69},{71,68},{7... | collective-permute-start | bytes 786440 | tf_op jit(solution)/shard_map/ppermute | solution.py:374
  47.8 4.2 %collective-permute-start.5 = (bf16[128,512]{1,0:T(8,128)(2,1)S(1)}, bf16[128,512]{1,0:T(8,128)(2,1)S(1)}, u32[]{:S(2)}, u32[]{:S(2)}) collective-permute-start(bf16[128,512]{1,0:T(8,128)(2,1)S(1)} %fusion.2), channel_id=1, source_target_pairs={{0,4},{4,0},{8,12},{12,8},{16,20},{20,16},{24,28},{28,24},{32,36},... | collective-permute-start | bytes 393224 | tf_op jit(solution)/shard_map/ppermute | solution.py:375
  52.0 10.3 %copy-start.7 = (bf16[256,512]{1,0:T(8,128)(2,1)}, bf16[256,512]{1,0:T(8,128)(2,1)S(1)}, u32[]{:S(2)}) copy-start(bf16[256,512]{1,0:T(8,128)(2,1)S(1)} %collective-permute-done.8.cross_ref) | copy-start | bytes 786436
  52.7 0.7 copy-start.8
  52.7 8.9 %copy-start.6 = (bf16[192,1024]{1,0:T(8,128)(2,1)}, bf16[192,1024]{1,0:T(8,128)(2,1)S(1)}, u32[]{:S(2)}) copy-start(bf16[192,1024]{1,0:T(8,128)(2,1)S(1)} %collective-permute-done.9.n1b_ref) | copy-start | bytes 1179652
  52.7 9.6 %collective-permute-start.10 = (bf16[192,1024]{1,0:T(8,128)(2,1)S(1)}, bf16[192,1024]{1,0:T(8,128)(2,1)}, u32[]{:S(2)}, u32[]{:S(2)}) collective-permute-start(bf16[192,1024]{1,0:T(8,128)(2,1)S(1)} %collective-permute-done.9.n1b_ref), channel_id=1, source_target_pairs={{0,64},{64,0},{1,65},{65,1},{2,66},{66,2},{3,67},{67,3},{4,68},{68... | collective-permute-start | bytes 1179656 | tf_op jit(solution)/shard_map/ppermute | solution.py:376
  53.4 8.1 %collective-permute-start.6 = (bf16[2,128,512]{2,1,0:T(8,128)(2,1)S(1)}, bf16[2,128,512]{2,1,0:T(8,128)(2,1)S(1)}, u32[]{:S(2)}, u32[]{:S(2)}) collective-permute-start(bf16[2,128,512]{2,1,0:T(8,128)(2,1)S(1)} %pad_maximum_fusion.1), channel_id=1, source_target_pairs={{0,16},{4,20},{8,24},{12,28},{16,0},{20,4},{24,8},{28,12},{32,48},... | collective-permute-start | bytes 786440 | tf_op jit(solution)/shard_map/ppermute | solution.py:378
  61.6 0.7 copy-start.9
  68.0 4.5 %copy-start.10 = (bf16[2,128,512]{2,1,0:T(8,128)(2,1)S(1)}, bf16[2,128,512]{2,1,0:T(8,128)(2,1)}, u32[]{:S(2)}) copy-start(bf16[2,128,512]{2,1,0:T(8,128)(2,1)} %copy-done.9) | copy-start | bytes 786436
  68.1 7.1 %copy-start.1 = (bf16[2,256,512]{2,1,0:T(8,128)(2,1)S(1)}, bf16[2,256,512]{2,1,0:T(8,128)(2,1)}, u32[]{:S(2)}) copy-start(bf16[2,256,512]{2,1,0:T(8,128)(2,1)} %get-tuple-element.35.near_ref) | copy-start | bytes 1572868
  68.1 20.8 %all-to-all-start.1 = ((bf16[16,256,128]{2,1,0:T(8,128)(2,1)}), bf16[16,256,128]{2,1,0:T(8,128)(2,1)}, u32[]{:S(2)}, u32[]{:S(2)}) async-start(bf16[16,256,128]{2,1,0:T(8,128)(2,1)} %get-tuple-element.32), calls=%async_computation.1 | async-start | bytes 2097152 | tf_op jit(solution)/shard_map/all_to_all | solution.py:381
  72.6 30.2 %collective-permute-start.12 = (bf16[2,2,128,512]{3,2,1,0:T(8,128)(2,1)S(1)}, bf16[2,2,128,512]{3,2,1,0:T(8,128)(2,1)}, u32[]{:S(2)}, u32[]{:S(2)}) collective-permute-start(bf16[2,2,128,512]{3,2,1,0:T(8,128)(2,1)S(1)} %pad_maximum_fusion.low_ref), channel_id=1, source_target_pairs={{0,48},{4,52},{8,56},{12,60},{16,32},{20,36},{24,40},{28,44},{32,1... | collective-permute-start | bytes 1572872 | tf_op jit(solution)/shard_map/ppermute | solution.py:383
  75.2 29.8 %copy-start = (bf16[1024,1024]{1,0:T(8,128)(2,1)S(1)}, bf16[1024,1024]{1,0:T(8,128)(2,1)}, u32[]{:S(2)}) copy-start(bf16[1024,1024]{1,0:T(8,128)(2,1)} %get-tuple-element.19.w_ref) | copy-start | bytes 6291460
  75.2 27.7 %collective-permute-start.11 = (bf16[2,256,512]{2,1,0:T(8,128)(2,1)S(1)}, bf16[2,256,512]{2,1,0:T(8,128)(2,1)}, u32[]{:S(2)}, u32[]{:S(2)}) collective-permute-start(bf16[2,256,512]{2,1,0:T(8,128)(2,1)S(1)} %copy-done.1), channel_id=1, source_target_pairs={{0,1},{1,0},{2,3},{3,2},{4,5},{5,4},{6,7},{7,6},{8,9},{9,8},{10,11... | collective-permute-start | bytes 1572872 | tf_op jit(solution)/shard_map/ppermute | solution.py:385
  90.3 4.8 %collective-permute-start.16 = (bf16[256,128]{1,0:T(8,128)(2,1)S(1)}, bf16[256,128]{1,0:T(8,128)(2,1)S(1)}, u32[]{:S(2)}, u32[]{:S(2)}) collective-permute-start(bf16[256,128]{1,0:T(8,128)(2,1)S(1)} %reduce_sum.22), channel_id=1, source_target_pairs={{0,3},{1,2},{2,67},{3,66},{64,1},{65,0},{66,65},{67,64},{4,7},{5,6... | collective-permute-start | bytes 196616 | tf_op jit(solution)/shard_map/ppermute | solution.py:389
  93.5 7.4 %collective-permute-start.15 = (bf16[256,128]{1,0:T(8,128)(2,1)S(1)}, bf16[256,128]{1,0:T(8,128)(2,1)S(1)}, u32[]{:S(2)}, u32[]{:S(2)}) collective-permute-start(bf16[256,128]{1,0:T(8,128)(2,1)S(1)} %reduce_sum.22), channel_id=1, source_target_pairs={{0,2},{1,3},{2,66},{3,67},{64,0},{65,1},{66,64},{67,65},{4,6},{5,7... | collective-permute-start | bytes 196616 | tf_op jit(solution)/shard_map/ppermute | solution.py:389
  94.4 6.5 %collective-permute-start.14 = (bf16[256,128]{1,0:T(8,128)(2,1)S(1)}, bf16[256,128]{1,0:T(8,128)(2,1)S(1)}, u32[]{:S(2)}, u32[]{:S(2)}) collective-permute-start(bf16[256,128]{1,0:T(8,128)(2,1)S(1)} %reduce_sum.22), channel_id=1, source_target_pairs={{0,1},{1,0},{2,65},{3,64},{64,3},{65,2},{66,67},{67,66},{4,5},{5,4... | collective-permute-start | bytes 196616 | tf_op jit(solution)/shard_map/ppermute | solution.py:389
  95.1 7.8 %collective-permute-start.13 = (bf16[256,128]{1,0:T(8,128)(2,1)S(1)}, bf16[256,128]{1,0:T(8,128)(2,1)S(1)}, u32[]{:S(2)}, u32[]{:S(2)}) collective-permute-start(bf16[256,128]{1,0:T(8,128)(2,1)S(1)} %reduce_sum.22), channel_id=1, source_target_pairs={{0,0},{1,1},{2,64},{3,65},{64,2},{65,3},{66,66},{67,67},{4,4},{5,5... | collective-permute-start | bytes 196616 | tf_op jit(solution)/shard_map/ppermute | solution.py:389
  104.9 2.7 %collective-permute-start.17 = (bf16[512,1024]{1,0:T(8,128)(2,1)S(1)}, bf16[512,1024]{1,0:T(8,128)(2,1)S(1)}, u32[]{:S(2)}, u32[]{:S(2)}) collective-permute-start(bf16[512,1024]{1,0:T(8,128)(2,1)S(1)} %shard_map.90), channel_id=1, source_target_pairs={{0,64},{64,0},{1,65},{65,1},{2,66},{66,2},{3,67},{67,3},{4,68},{68... | collective-permute-start | bytes 3145736 | tf_op jit(solution)/shard_map/ppermute | solution.py:391

commit v9 on v8

--- a/solution.py
+++ b/solution.py
@@ -362,6 +362,7 @@
     paired = (paired.astype(f32) + away[1].astype(f32)).astype(bf16)
     paired = lax.ppermute(paired, "tensor", pair)
     chain = (own.astype(f32) + away[0].astype(f32) + paired.astype(f32)).astype(bf16)
+    chain = jnp.stack([chain, lax.ppermute(chain, "context", along(lambda i, j: (i, j ^ 1)))])
     edges = jnp.arange(ctx_n, dtype=jnp.int32) * bytes_n
     counts = jnp.sum((patch_starts[0][None, :] <= edges[:, None]).astype(jnp.int32), axis=1)
     first = jnp.minimum((counts - 1) // LANES, starts.shape[0] - WIN)
@@ -372,12 +373,10 @@
     sums = collect(first, incoming, patch_rows)
     cross = lax.ppermute(sums, line, moves(lambda d, x: (0, x) if d == 1 else (1, ten_n - 1 - x)))
     third = lax.ppermute(sums, line, moves(lambda d, x: (1, ten_n - 1 - x) if d == 1 else None))
-    other = lax.ppermute(after(chain, sums), "context", along(lambda i, j: (i, j ^ 1)))
+    other = lax.ppermute(after(chain, sums), "context", along(lambda i, j: (i ^ 1, j)))
     far1.append(lax.ppermute(after(near1[1], cross, third, other), "dp", swap))
-    chain = jnp.stack([chain, other])
-    other = lax.ppermute(chain, "context", along(lambda i, j: (i ^ 1, j)))
     columns = (near0, *near1, far0, *far1)
-    partial, near = outer((after(sums, other), third, cross), columns)
+    partial, near = outer((sums, third, cross), columns)
     pieces = lax.all_to_all(partial, "context", split_axis=0, concat_axis=0, tiled=True)
     chain = jnp.stack([after(chain, partial), after(other, partial)])
     rest = lax.ppermute(chain, "context", along(lambda i, j: (SIDE - 1 - i, j)))

time: 113 us -> 109 us (0.965)
  the two profiles are of different devices: /device:TPU:1 before, /device:TPU:7 now
where the time goes in v9:
time: 109 us
  starting transfers between devices  42.5 us (39%)
  waiting for transfers between devices  36.3 us (33%)
  Pallas kernels  25.2 us (23%)
  local copies, waits for them, and re-layouts  2.05 us (2%)
  other arithmetic  1.81 us (2%)
    all_to_all x1, waiting for transfers between devices, local(): lax.all_to_all(partial, 'context', split_axis=0, concat_axis=0, tiled=True)  14.2 us
    ppermute x1, waiting for transfers between devices, local(): lax.ppermute(chain, 'context', along(lambda i, j: (i, j ^ 1)))  9.75 us
    ppermute x1, starting transfers between devices, local(): back = lax.ppermute(give, 'dp', swap)  8.15 us
    all_to_all x1, starting transfers between devices, local(): lax.all_to_all(outgoing, 'context', split_axis=0, concat_axis=0, tiled=True)  7.77 us
    pallas_call x1, Pallas kernels, chain_terms(): pl.pallas_call(chain_kernel, in_specs=[vmem, vmem, pl.BlockSpec(memory_sp...  6.54 us
    all_to_all x1, starting transfers between devices, local(): lax.all_to_all(partial, 'context', split_axis=0, concat_axis=0, tiled=True)  6.03 us
    pallas_call x1, Pallas kernels, outer(): pl.pallas_call(outer_kernel, in_specs=[vmem] * len(sums) + [pl.BlockSpec(...  5.72 us
    pallas_call x1, Pallas kernels, segment_sums(): pl.pallas_call(seg_kernel, in_specs=[vmem, vmem, pl.BlockSpec(memory_spac...  5.34 us
  transfers between devices with their start and end apart: 20, of which 12 were waited for; matrix products, arithmetic and copies ran while one was open for 2% of the time, Pallas kernels for 13%

profile of v9, /device:TPU:7, one launch (start us, length us, event | category | flops | bytes accessed | tf_op | source)
XLA Modules:
  0.0 108.7 jit_solution(8456707255950869009)
XLA Ops:
  0.6 1.1 %slice_bitcast_fusion = bf16[320,1024]{1,0:T(8,128)(2,1)S(1)} fusion(bf16[1,512,1024]{2,1,0:T(8,128)(2,1)} %param.10), kind=kLoop, calls=%fused_computation | loop fusion | bytes 1310720 | tf_op jit(solution)/shard_map/slice | solution.py:347
  1.8 0.0 copy-start.3
  1.8 0.6 collective-permute-start
  2.4 6.5 %shard_map.86 = (bf16[1024,1024]{1,0:T(8,128)(2,1)}, bf16[128,512]{1,0:T(8,128)(2,1)}, bf16[128,512]{1,0:T(8,128)(2,1)}, bf16[2,128,512]{2,1,0:T(8,128)(2,1)}) custom-call(bf16[1024,1024]{1,0:T(8,128)(2,1)} %value_ref.1, bf16[1024,1024]{1,0:T(8,128)(2,1)} %out_w_ref.1, bf16[4096,1024]{1,0:T(8,128)(2,1)} %global_ref.1), custom_call_target="tpu_custom_call" | custom-call | tf_op jit(solution)/shard_map/pallas_call | solution.py:244
  8.9 0.9 collective-permute-start.1
  9.9 1.2 %collective-permute-start.2 = (bf16[512,1024]{1,0:T(8,128)(2,1)S(1)}, bf16[512,1024]{1,0:T(8,128)(2,1)S(1)}, u32[]{:S(2)}, u32[]{:S(2)}) collective-permute-start(bf16[512,1024]{1,0:T(8,128)(2,1)S(1)} %bitcast.23), channel_id=1, source_target_pairs={{0,64},{64,0},{1,65},{65,1},{2,66},{66,2},{3,67},{67,3},{4,68},{68... | collective-permute-start | bytes 3145736 | tf_op jit(solution)/shard_map/ppermute | solution.py:346
  11.1 5.3 %shard_map.87 = bf16[1152,256]{1,0:T(8,128)(2,1)} custom-call(s32[64,128]{1,0:T(8,128)} %bitcast.30, s32[64,128]{1,0:T(8,128)} %bitcast.33, bf16[4096,1024]{1,0:T(8,128)(2,1)} %bitcast.21), custom_call_target="tpu_custom_call" | custom-call | tf_op jit(solution)/shard_map/pallas_call | solution.py:94
  16.5 0.8 collective-permute-done.1
  17.3 0.3 collective-permute-done.n1a_ref
  17.6 0.6 collective-permute-start.4
  18.2 1.8 %collective-permute-start.3 = (bf16[320,1024]{1,0:T(8,128)(2,1)}, bf16[320,1024]{1,0:T(8,128)(2,1)}, u32[]{:S(2)}, u32[]{:S(2)}) collective-permute-start(bf16[320,1024]{1,0:T(8,128)(2,1)} %collective-permute-done.n1a_ref), channel_id=1, source_target_pairs={{0,64},{64,0},{1,65},{65,1},{2,66},{66,2},{3,67},{67,3},{4,68},{68... | collective-permute-start | bytes 1966088 | tf_op jit(solution)/shard_map/ppermute | solution.py:369
  20.1 0.3 convert_reduce_fusion
  20.3 7.8 %all-to-all-start = ((bf16[16,72,256]{2,1,0:T(8,128)(2,1)}), bf16[16,72,256]{2,1,0:T(8,128)(2,1)S(1)}, u32[]{:S(2)}, u32[]{:S(2)}) async-start(bf16[16,72,256]{2,1,0:T(8,128)(2,1)} %bitcast.25), calls=%async_computation | async-start | bytes 1179648 | tf_op jit(solution)/shard_map/all_to_all | solution.py:359
  28.1 0.1 fusion.2
  28.2 1.4 %collective-permute-start.5 = (bf16[128,512]{1,0:T(8,128)(2,1)S(1)}, bf16[128,512]{1,0:T(8,128)(2,1)S(1)}, u32[]{:S(2)}, u32[]{:S(2)}) collective-permute-start(bf16[128,512]{1,0:T(8,128)(2,1)S(1)} %fusion.2), channel_id=1, source_target_pairs={{0,4},{4,0},{8,12},{12,8},{16,20},{20,16},{24,28},{28,24},{32,36},... | collective-permute-start | bytes 393224 | tf_op jit(solution)/shard_map/ppermute | solution.py:365
  29.6 9.7 %collective-permute-done.5 = bf16[128,512]{1,0:T(8,128)(2,1)S(1)} collective-permute-done((bf16[128,512]{1,0:T(8,128)(2,1)S(1)}, bf16[128,512]{1,0:T(8,128)(2,1)S(1)}, u32[]{:S(2)}, u32[]{:S(2)}) %collective-permute-start.5) | collective-permute-done | bytes 131104 | tf_op jit(solution)/shard_map/ppermute | solution.py:365
  39.4 0.0 collective-permute-done.2.f0_ref
  39.4 0.0 copy-start.4
  39.4 0.5 all-to-all-done
  39.9 1.1 collective-permute-start.8
  41.0 0.9 shard_map.88.mine_ref
  41.9 0.8 collective-permute-start.9
  42.7 1.7 %collective-permute-start.7 = (bf16[256,512]{1,0:T(8,128)(2,1)S(1)}, bf16[256,512]{1,0:T(8,128)(2,1)S(1)}, u32[]{:S(2)}, u32[]{:S(2)}) collective-permute-start(bf16[256,512]{1,0:T(8,128)(2,1)S(1)} %shard_map.88.mine_ref), channel_id=1, source_target_pairs={{0,67},{1,66},{2,65},{3,64},{64,0},{65,1},{66,2},{67,3},{4,71},{5,... | collective-permute-start | bytes 786440 | tf_op jit(solution)/shard_map/ppermute | solution.py:374
  44.4 2.8 %collective-permute-start.6 = (bf16[256,512]{1,0:T(8,128)(2,1)S(1)}, bf16[256,512]{1,0:T(8,128)(2,1)S(1)}, u32[]{:S(2)}, u32[]{:S(2)}) collective-permute-start(bf16[256,512]{1,0:T(8,128)(2,1)S(1)} %shard_map.88.mine_ref), channel_id=1, source_target_pairs={{64,67},{65,66},{66,65},{67,64},{68,71},{69,70},{70,69},{71,68},{7... | collective-permute-start | bytes 786440 | tf_op jit(solution)/shard_map/ppermute | solution.py:375
  47.2 0.3 collective-permute-done.9
  47.5 2.2 %collective-permute-done.7.cross_ref = bf16[256,512]{1,0:T(8,128)(2,1)S(1)} collective-permute-done((bf16[256,512]{1,0:T(8,128)(2,1)S(1)}, bf16[256,512]{1,0:T(8,128)(2,1)S(1)}, u32[]{:S(2)}, u32[]{:S(2)}) %collective-permute-start.7) | collective-permute-done | bytes 262176 | tf_op jit(solution)/shard_map/ppermute | solution.py:374
  49.7 3.0 %collective-permute-done.6.third_ref = bf16[256,512]{1,0:T(8,128)(2,1)S(1)} collective-permute-done((bf16[256,512]{1,0:T(8,128)(2,1)S(1)}, bf16[256,512]{1,0:T(8,128)(2,1)S(1)}, u32[]{:S(2)}, u32[]{:S(2)}) %collective-permute-start.6) | collective-permute-done | bytes 262176 | tf_op jit(solution)/shard_map/ppermute | solution.py:375
  52.8 0.8 copy-done.5
  53.5 0.0 collective-permute-start.10
  53.5 0.1 copy-done.7
  53.6 1.8 %collective-permute-done.10.f1b_ref = bf16[192,1024]{1,0:T(8,128)(2,1)} collective-permute-done((bf16[192,1024]{1,0:T(8,128)(2,1)S(1)}, bf16[192,1024]{1,0:T(8,128)(2,1)}, u32[]{:S(2)}, u32[]{:S(2)}) %collective-permute-start.10) | collective-permute-done | bytes 393248 | tf_op jit(solution)/shard_map/ppermute | solution.py:377
  55.4 5.7 %shard_map.89 = (bf16[16,256,128]{2,1,0:T(8,128)(2,1)}, bf16[2,256,512]{2,1,0:T(8,128)(2,1)}) custom-call(bf16[256,512]{1,0:T(8,128)(2,1)} %copy-done.2, bf16[256,512]{1,0:T(8,128)(2,1)} %copy-done.7, bf16[256,512]{1,0:T(8,128)(2,1)} %copy-done.6, bf16[512,1024]{1,0:T(8,128)(2,1)} %bitcast.22, bf16[320,1024]{1,0:T(8,128)(2,1)} %collective-permute-done.n1a_ref, ...), custom_call_target="tpu_custom_call" | custom-call | tf_op jit(solution)/shard_map/pallas_call | solution.py:184
  61.1 0.0 copy-start.1
  61.1 6.0 %all-to-all-start.1 = ((bf16[16,256,128]{2,1,0:T(8,128)(2,1)}), bf16[16,256,128]{2,1,0:T(8,128)(2,1)}, u32[]{:S(2)}, u32[]{:S(2)}) async-start(bf16[16,256,128]{2,1,0:T(8,128)(2,1)} %get-tuple-element.30), calls=%async_computation.1 | async-start | bytes 2097152 | tf_op jit(solution)/shard_map/all_to_all | solution.py:380
  67.2 0.1 pad_maximum_fusion.low_ref
  67.2 2.6 %collective-permute-start.12 = (bf16[2,2,128,512]{3,2,1,0:T(8,128)(2,1)S(1)}, bf16[2,2,128,512]{3,2,1,0:T(8,128)(2,1)}, u32[]{:S(2)}, u32[]{:S(2)}) collective-permute-start(bf16[2,2,128,512]{3,2,1,0:T(8,128)(2,1)S(1)} %pad_maximum_fusion.low_ref), channel_id=1, source_target_pairs={{0,48},{4,52},{8,56},{12,60},{16,32},{20,36},{24,40},{28,44},{32,1... | collective-permute-start | bytes 1572872 | tf_op jit(solution)/shard_map/ppermute | solution.py:382
  69.9 14.2 %all-to-all-done.1 = bf16[16,256,128]{2,1,0:T(8,128)(2,1)} async-done(((bf16[16,256,128]{2,1,0:T(8,128)(2,1)}), bf16[16,256,128]{2,1,0:T(8,128)(2,1)}, u32[]{:S(2)}, u32[]{:S(2)}) %all-to-all-start.1) | async-done | bytes 1048608 | tf_op jit(solution)/shard_map/all_to_all | solution.py:380
  84.0 1.4 %reduce_sum.22 = bf16[256,128]{1,0:T(8,128)(2,1)S(1)} reduce(bf16[16,256,128]{2,1,0:T(8,128)(2,1)} %all-to-all-done.1, bf16[]{:T(256)} %constant.25.clone.1), dimensions={0}, to_apply=%region_1.2 | reduce | flops 491520 | bytes 1114114 | tf_op jit(solution)/shard_map/reduce_sum | solution.py:385
  85.4 1.2 %collective-permute-start.16 = (bf16[256,128]{1,0:T(8,128)(2,1)S(1)}, bf16[256,128]{1,0:T(8,128)(2,1)S(1)}, u32[]{:S(2)}, u32[]{:S(2)}) collective-permute-start(bf16[256,128]{1,0:T(8,128)(2,1)S(1)} %reduce_sum.22), channel_id=1, source_target_pairs={{0,3},{1,2},{2,67},{3,66},{64,1},{65,0},{66,65},{67,64},{4,7},{5,6... | collective-permute-start | bytes 196616 | tf_op jit(solution)/shard_map/ppermute | solution.py:388
  86.6 3.0 %collective-permute-start.15 = (bf16[256,128]{1,0:T(8,128)(2,1)S(1)}, bf16[256,128]{1,0:T(8,128)(2,1)S(1)}, u32[]{:S(2)}, u32[]{:S(2)}) collective-permute-start(bf16[256,128]{1,0:T(8,128)(2,1)S(1)} %reduce_sum.22), channel_id=1, source_target_pairs={{0,2},{1,3},{2,66},{3,67},{64,0},{65,1},{66,64},{67,65},{4,6},{5,7... | collective-permute-start | bytes 196616 | tf_op jit(solution)/shard_map/ppermute | solution.py:388
  89.6 0.7 collective-permute-start.13
  90.3 0.7 collective-permute-done.15.c_ref
  91.0 2.2 %collective-permute-done.14.b_ref = bf16[256,128]{1,0:T(8,128)(2,1)S(1)} collective-permute-done((bf16[256,128]{1,0:T(8,128)(2,1)S(1)}, bf16[256,128]{1,0:T(8,128)(2,1)S(1)}, u32[]{:S(2)}, u32[]{:S(2)}) %collective-permute-start.14) | collective-permute-done | bytes 65568 | tf_op jit(solution)/shard_map/ppermute | solution.py:388
  93.2 2.0 %shard_map.90 = bf16[512,1024]{1,0:T(8,128)(2,1)S(1)} custom-call(bf16[2,256,512]{2,1,0:T(8,128)(2,1)S(1)} %copy-done.1, bf16[2,256,512]{2,1,0:T(8,128)(2,1)} %collective-permute-done.11.far_ref, bf16[2,2,128,512]{3,2,1,0:T(8,128)(2,1)S(1)} %pad_maximum_fusion.low_ref, bf16[2,2,128,512]{3,2,1,0:T(8,128)(2,1)} %collective-permute-done.12.high_ref), custom_call_target="tpu_custom_call" | custom-call | tf_op jit(solution)/shard_map/pallas_call | solution.py:283
  95.2 8.2 %collective-permute-start.17 = (bf16[512,1024]{1,0:T(8,128)(2,1)S(1)}, bf16[512,1024]{1,0:T(8,128)(2,1)S(1)}, u32[]{:S(2)}, u32[]{:S(2)}) collective-permute-start(bf16[512,1024]{1,0:T(8,128)(2,1)S(1)} %shard_map.90), channel_id=1, source_target_pairs={{0,64},{64,0},{1,65},{65,1},{2,66},{66,2},{3,67},{67,3},{4,68},{68... | collective-permute-start | bytes 3145736 | tf_op jit(solution)/shard_map/ppermute | solution.py:390
  103.4 1.6 %shard_map.92 = f32[128,1024]{1,0:T(8,128)} custom-call(bf16[256,128]{1,0:T(8,128)(2,1)S(1)} %collective-permute-done.13.a_ref, bf16[256,128]{1,0:T(8,128)(2,1)S(1)} %collective-permute-done.14.b_ref, bf16[256,128]{1,0:T(8,128)(2,1)S(1)} %collective-permute-done.15.c_ref, bf16[256,128]{1,0:T(8,128)(2,1)S(1)} %collective-permute-done.16.d_ref, ...), custom_call_target="tpu_custom_call" | custom-call | tf_op jit(solution)/shard_map/pallas_call | solution.py:312
  105.0 0.7 collective-permute-done.17.rest_0_
  105.7 3.0 %shard_map.91 = bf16[512,1024]{1,0:T(8,128)(2,1)} custom-call(bf16[2,256,512]{2,1,0:T(8,128)(2,1)S(1)} %copy-done.1, bf16[2,256,512]{2,1,0:T(8,128)(2,1)} %collective-permute-done.11.far_ref, bf16[2,2,128,512]{3,2,1,0:T(8,128)(2,1)S(1)} %pad_maximum_fusion.low_ref, bf16[2,2,128,512]{3,2,1,0:T(8,128)(2,1)} %collective-permute-done.12.high_ref, ...), custom_call_target="tpu_custom_call" | custom-call | tf_op jit(solution)/shard_map/pallas_call | solution.py:283
  (35 shorter events, 0.2 us)
Async XLA Ops:
  1.8 8.1 %copy-start.3 = (bf16[1,512,1024]{2,1,0:T(8,128)(2,1)S(1)}, bf16[1,512,1024]{2,1,0:T(8,128)(2,1)}, u32[]{:S(2)}) copy-start(bf16[1,512,1024]{2,1,0:T(8,128)(2,1)} %param.10) | copy-start | bytes 3145732
  1.8 15.8 %collective-permute-start = (bf16[320,1024]{1,0:T(8,128)(2,1)S(1)}, bf16[320,1024]{1,0:T(8,128)(2,1)}, u32[]{:S(2)}, u32[]{:S(2)}) collective-permute-start(bf16[320,1024]{1,0:T(8,128)(2,1)S(1)} %slice_bitcast_fusion), channel_id=1, source_target_pairs={{0,1},{1,0},{2,3},{3,2},{4,5},{5,4},{6,7},{7,6},{8,9},{9,8},{10,11... | collective-permute-start | bytes 1966088 | tf_op jit(solution)/shard_map/ppermute | solution.py:347
  8.9 8.4 %collective-permute-start.1 = (bf16[2,128,512]{2,1,0:T(8,128)(2,1)}, bf16[2,128,512]{2,1,0:T(8,128)(2,1)S(1)}, u32[]{:S(2)}, u32[]{:S(2)}) collective-permute-start(bf16[2,128,512]{2,1,0:T(8,128)(2,1)} %get-tuple-element.20), channel_id=1, source_target_pairs={{0,3},{1,2},{2,1},{3,0},{4,7},{5,6},{6,5},{7,4},{8,11},{9,10},{10,... | collective-permute-start | bytes 786440 | tf_op jit(solution)/shard_map/ppermute | solution.py:355
  9.9 29.5 %collective-permute-start.2 = (bf16[512,1024]{1,0:T(8,128)(2,1)S(1)}, bf16[512,1024]{1,0:T(8,128)(2,1)S(1)}, u32[]{:S(2)}, u32[]{:S(2)}) collective-permute-start(bf16[512,1024]{1,0:T(8,128)(2,1)S(1)} %bitcast.23), channel_id=1, source_target_pairs={{0,64},{64,0},{1,65},{65,1},{2,66},{66,2},{3,67},{67,3},{4,68},{68... | collective-permute-start | bytes 3145736 | tf_op jit(solution)/shard_map/ppermute | solution.py:346
  11.1 6.4 %copy-start.11 = (bf16[128,512]{1,0:T(8,128)(2,1)S(1)}, bf16[128,512]{1,0:T(8,128)(2,1)}, u32[]{:S(2)}) copy-start(bf16[128,512]{1,0:T(8,128)(2,1)} %get-tuple-element.24) | copy-start | bytes 393220
  11.1 8.9 %copy-start.10 = (s32[1,8192]{1,0:T(1,128)S(1)}, s32[1,8192]{1,0:T(1,128)}, u32[]{:S(2)}) copy-start(s32[1,8192]{1,0:T(1,128)} %param.8) | copy-start | bytes 98308
  11.1 17.0 %copy-start.12 = (bf16[128,512]{1,0:T(8,128)(2,1)S(1)}, bf16[128,512]{1,0:T(8,128)(2,1)}, u32[]{:S(2)}) copy-start(bf16[128,512]{1,0:T(8,128)(2,1)} %get-tuple-element.22) | copy-start | bytes 393220
  17.6 10.5 %collective-permute-start.4 = (bf16[128,512]{1,0:T(8,128)(2,1)S(1)}, bf16[128,512]{1,0:T(8,128)(2,1)S(1)}, u32[]{:S(2)}, u32[]{:S(2)}) collective-permute-start(bf16[128,512]{1,0:T(8,128)(2,1)S(1)} %fusion), channel_id=1, source_target_pairs={{0,1},{1,0},{2,3},{3,2},{4,5},{5,4},{6,7},{7,6},{8,9},{9,8},{10,11... | collective-permute-start | bytes 393224 | tf_op jit(solution)/shard_map/ppermute | solution.py:363
  18.2 21.7 %collective-permute-start.3 = (bf16[320,1024]{1,0:T(8,128)(2,1)}, bf16[320,1024]{1,0:T(8,128)(2,1)}, u32[]{:S(2)}, u32[]{:S(2)}) collective-permute-start(bf16[320,1024]{1,0:T(8,128)(2,1)} %collective-permute-done.n1a_ref), channel_id=1, source_target_pairs={{0,64},{64,0},{1,65},{65,1},{2,66},{66,2},{3,67},{67,3},{4,68},{68... | collective-permute-start | bytes 1966088 | tf_op jit(solution)/shard_map/ppermute | solution.py:369
  20.3 19.6 %all-to-all-start = ((bf16[16,72,256]{2,1,0:T(8,128)(2,1)}), bf16[16,72,256]{2,1,0:T(8,128)(2,1)S(1)}, u32[]{:S(2)}, u32[]{:S(2)}) async-start(bf16[16,72,256]{2,1,0:T(8,128)(2,1)} %bitcast.25), calls=%async_computation | async-start | bytes 1179648 | tf_op jit(solution)/shard_map/all_to_all | solution.py:359
  28.2 11.2 %collective-permute-start.5 = (bf16[128,512]{1,0:T(8,128)(2,1)S(1)}, bf16[128,512]{1,0:T(8,128)(2,1)S(1)}, u32[]{:S(2)}, u32[]{:S(2)}) collective-permute-start(bf16[128,512]{1,0:T(8,128)(2,1)S(1)} %fusion.2), channel_id=1, source_target_pairs={{0,4},{4,0},{8,12},{12,8},{16,20},{20,16},{24,28},{28,24},{32,36},... | collective-permute-start | bytes 393224 | tf_op jit(solution)/shard_map/ppermute | solution.py:365
  39.4 15.9 %copy-start.4 = (bf16[512,1024]{1,0:T(8,128)(2,1)}, bf16[512,1024]{1,0:T(8,128)(2,1)S(1)}, u32[]{:S(2)}) copy-start(bf16[512,1024]{1,0:T(8,128)(2,1)S(1)} %collective-permute-done.2.f0_ref) | copy-start | bytes 3145732
  39.9 12.8 %collective-permute-start.8 = (bf16[192,1024]{1,0:T(8,128)(2,1)S(1)}, bf16[192,1024]{1,0:T(8,128)(2,1)S(1)}, u32[]{:S(2)}, u32[]{:S(2)}) collective-permute-start(bf16[192,1024]{1,0:T(8,128)(2,1)S(1)} %slice.19), channel_id=1, source_target_pairs={{0,1},{1,0},{2,3},{3,2},{4,5},{5,4},{6,7},{7,6},{8,9},{9,8},{10,11... | collective-permute-start | bytes 1179656 | tf_op jit(solution)/shard_map/ppermute | solution.py:372
  41.9 13.5 %copy-start.2 = (bf16[256,512]{1,0:T(8,128)(2,1)}, bf16[256,512]{1,0:T(8,128)(2,1)S(1)}, u32[]{:S(2)}) copy-start(bf16[256,512]{1,0:T(8,128)(2,1)S(1)} %shard_map.88.mine_ref) | copy-start | bytes 786436
  41.9 5.6 %collective-permute-start.9 = (bf16[2,128,512]{2,1,0:T(8,128)(2,1)S(1)}, bf16[2,128,512]{2,1,0:T(8,128)(2,1)S(1)}, u32[]{:S(2)}, u32[]{:S(2)}) collective-permute-start(bf16[2,128,512]{2,1,0:T(8,128)(2,1)S(1)} %pad_maximum_fusion.1), channel_id=1, source_target_pairs={{0,16},{4,20},{8,24},{12,28},{16,0},{20,4},{24,8},{28,12},{32,48},... | collective-permute-start | bytes 786440 | tf_op jit(solution)/shard_map/ppermute | solution.py:376
  42.7 7.0 %collective-permute-start.7 = (bf16[256,512]{1,0:T(8,128)(2,1)S(1)}, bf16[256,512]{1,0:T(8,128)(2,1)S(1)}, u32[]{:S(2)}, u32[]{:S(2)}) collective-permute-start(bf16[256,512]{1,0:T(8,128)(2,1)S(1)} %shard_map.88.mine_ref), channel_id=1, source_target_pairs={{0,67},{1,66},{2,65},{3,64},{64,0},{65,1},{66,2},{67,3},{4,71},{5,... | collective-permute-start | bytes 786440 | tf_op jit(solution)/shard_map/ppermute | solution.py:374
  44.4 8.3 %collective-permute-start.6 = (bf16[256,512]{1,0:T(8,128)(2,1)S(1)}, bf16[256,512]{1,0:T(8,128)(2,1)S(1)}, u32[]{:S(2)}, u32[]{:S(2)}) collective-permute-start(bf16[256,512]{1,0:T(8,128)(2,1)S(1)} %shard_map.88.mine_ref), channel_id=1, source_target_pairs={{64,67},{65,66},{66,65},{67,64},{68,71},{69,70},{70,69},{71,68},{7... | collective-permute-start | bytes 786440 | tf_op jit(solution)/shard_map/ppermute | solution.py:375
  47.5 6.0 %copy-start.8 = (bf16[2,128,512]{2,1,0:T(8,128)(2,1)}, bf16[2,128,512]{2,1,0:T(8,128)(2,1)S(1)}, u32[]{:S(2)}) copy-start(bf16[2,128,512]{2,1,0:T(8,128)(2,1)S(1)} %collective-permute-done.9) | copy-start | bytes 786436
  49.7 5.7 %copy-start.6 = (bf16[256,512]{1,0:T(8,128)(2,1)}, bf16[256,512]{1,0:T(8,128)(2,1)S(1)}, u32[]{:S(2)}) copy-start(bf16[256,512]{1,0:T(8,128)(2,1)S(1)} %collective-permute-done.7.cross_ref) | copy-start | bytes 786436
  52.7 0.9 copy-start.7
  52.7 0.8 copy-start.5
  53.5 1.9 %collective-permute-start.10 = (bf16[192,1024]{1,0:T(8,128)(2,1)S(1)}, bf16[192,1024]{1,0:T(8,128)(2,1)}, u32[]{:S(2)}, u32[]{:S(2)}) collective-permute-start(bf16[192,1024]{1,0:T(8,128)(2,1)S(1)} %collective-permute-done.8.n1b_ref), channel_id=1, source_target_pairs={{0,64},{64,0},{1,65},{65,1},{2,66},{66,2},{3,67},{67,3},{4,68},{68... | collective-permute-start | bytes 1179656 | tf_op jit(solution)/shard_map/ppermute | solution.py:377
  61.1 6.1 %copy-start.9 = (bf16[2,128,512]{2,1,0:T(8,128)(2,1)S(1)}, bf16[2,128,512]{2,1,0:T(8,128)(2,1)}, u32[]{:S(2)}) copy-start(bf16[2,128,512]{2,1,0:T(8,128)(2,1)} %copy-done.8) | copy-start | bytes 786436
  61.1 8.7 %copy-start.1 = (bf16[2,256,512]{2,1,0:T(8,128)(2,1)S(1)}, bf16[2,256,512]{2,1,0:T(8,128)(2,1)}, u32[]{:S(2)}) copy-start(bf16[2,256,512]{2,1,0:T(8,128)(2,1)} %get-tuple-element.33.near_ref) | copy-start | bytes 1572868
  61.1 22.9 %all-to-all-start.1 = ((bf16[16,256,128]{2,1,0:T(8,128)(2,1)}), bf16[16,256,128]{2,1,0:T(8,128)(2,1)}, u32[]{:S(2)}, u32[]{:S(2)}) async-start(bf16[16,256,128]{2,1,0:T(8,128)(2,1)} %get-tuple-element.30), calls=%async_computation.1 | async-start | bytes 2097152 | tf_op jit(solution)/shard_map/all_to_all | solution.py:380
  67.2 25.9 %collective-permute-start.12 = (bf16[2,2,128,512]{3,2,1,0:T(8,128)(2,1)S(1)}, bf16[2,2,128,512]{3,2,1,0:T(8,128)(2,1)}, u32[]{:S(2)}, u32[]{:S(2)}) collective-permute-start(bf16[2,2,128,512]{3,2,1,0:T(8,128)(2,1)S(1)} %pad_maximum_fusion.low_ref), channel_id=1, source_target_pairs={{0,48},{4,52},{8,56},{12,60},{16,32},{20,36},{24,40},{28,44},{32,1... | collective-permute-start | bytes 1572872 | tf_op jit(solution)/shard_map/ppermute | solution.py:382
  69.9 33.5 %copy-start = (bf16[1024,1024]{1,0:T(8,128)(2,1)S(1)}, bf16[1024,1024]{1,0:T(8,128)(2,1)}, u32[]{:S(2)}) copy-start(bf16[1024,1024]{1,0:T(8,128)(2,1)} %get-tuple-element.18.w_ref) | copy-start | bytes 6291460
  69.9 23.3 %collective-permute-start.11 = (bf16[2,256,512]{2,1,0:T(8,128)(2,1)S(1)}, bf16[2,256,512]{2,1,0:T(8,128)(2,1)}, u32[]{:S(2)}, u32[]{:S(2)}) collective-permute-start(bf16[2,256,512]{2,1,0:T(8,128)(2,1)S(1)} %copy-done.1), channel_id=1, source_target_pairs={{0,1},{1,0},{2,3},{3,2},{4,5},{5,4},{6,7},{7,6},{8,9},{9,8},{10,11... | collective-permute-start | bytes 1572872 | tf_op jit(solution)/shard_map/ppermute | solution.py:384
  85.4 4.2 %collective-permute-start.16 = (bf16[256,128]{1,0:T(8,128)(2,1)S(1)}, bf16[256,128]{1,0:T(8,128)(2,1)S(1)}, u32[]{:S(2)}, u32[]{:S(2)}) collective-permute-start(bf16[256,128]{1,0:T(8,128)(2,1)S(1)} %reduce_sum.22), channel_id=1, source_target_pairs={{0,3},{1,2},{2,67},{3,66},{64,1},{65,0},{66,65},{67,64},{4,7},{5,6... | collective-permute-start | bytes 196616 | tf_op jit(solution)/shard_map/ppermute | solution.py:388
  86.6 4.4 %collective-permute-start.15 = (bf16[256,128]{1,0:T(8,128)(2,1)S(1)}, bf16[256,128]{1,0:T(8,128)(2,1)S(1)}, u32[]{:S(2)}, u32[]{:S(2)}) collective-permute-start(bf16[256,128]{1,0:T(8,128)(2,1)S(1)} %reduce_sum.22), channel_id=1, source_target_pairs={{0,2},{1,3},{2,66},{3,67},{64,0},{65,1},{66,64},{67,65},{4,6},{5,7... | collective-permute-start | bytes 196616 | tf_op jit(solution)/shard_map/ppermute | solution.py:388
  89.6 3.5 %collective-permute-start.14 = (bf16[256,128]{1,0:T(8,128)(2,1)S(1)}, bf16[256,128]{1,0:T(8,128)(2,1)S(1)}, u32[]{:S(2)}, u32[]{:S(2)}) collective-permute-start(bf16[256,128]{1,0:T(8,128)(2,1)S(1)} %reduce_sum.22), channel_id=1, source_target_pairs={{0,1},{1,0},{2,65},{3,64},{64,3},{65,2},{66,67},{67,66},{4,5},{5,4... | collective-permute-start | bytes 196616 | tf_op jit(solution)/shard_map/ppermute | solution.py:388
  89.6 3.5 %collective-permute-start.13 = (bf16[256,128]{1,0:T(8,128)(2,1)S(1)}, bf16[256,128]{1,0:T(8,128)(2,1)S(1)}, u32[]{:S(2)}, u32[]{:S(2)}) collective-permute-start(bf16[256,128]{1,0:T(8,128)(2,1)S(1)} %reduce_sum.22), channel_id=1, source_target_pairs={{0,0},{1,1},{2,64},{3,65},{64,2},{65,3},{66,66},{67,67},{4,4},{5,5... | collective-permute-start | bytes 196616 | tf_op jit(solution)/shard_map/ppermute | solution.py:388
  95.2 10.4 %collective-permute-start.17 = (bf16[512,1024]{1,0:T(8,128)(2,1)S(1)}, bf16[512,1024]{1,0:T(8,128)(2,1)S(1)}, u32[]{:S(2)}, u32[]{:S(2)}) collective-permute-start(bf16[512,1024]{1,0:T(8,128)(2,1)S(1)} %shard_map.90), channel_id=1, source_target_pairs={{0,64},{64,0},{1,65},{65,1},{2,66},{66,2},{3,67},{67,3},{4,68},{68... | collective-permute-start | bytes 3145736 | tf_op jit(solution)/shard_map/ppermute | solution.py:390

commit v10 on v7

--- a/solution.py
+++ b/solution.py
@@ -345,6 +345,7 @@
     paired = (paired.astype(f32) + away[1].astype(f32)).astype(bf16)
     paired = lax.ppermute(paired, "tensor", pair)
     chain = (own.astype(f32) + away[0].astype(f32) + paired.astype(f32)).astype(bf16)
+    chain = jnp.stack([chain, lax.ppermute(chain, "context", along(lambda i, j: (i, j ^ 1)))])
     edges = jnp.arange(ctx_n, dtype=jnp.int32) * bytes_n
     counts = jnp.sum((patch_starts[0][None, :] <= edges[:, None]).astype(jnp.int32), axis=1)
     first = jnp.minimum((counts - 1) // LANES, starts.shape[0] - WIN)
@@ -355,10 +356,8 @@
     sums = collect(first, incoming, patch_rows)
     cross = lax.ppermute(sums, line, moves(lambda d, x: (0, x) if d == 1 else (1, ten_n - 1 - x)))
     third = lax.ppermute(sums, line, moves(lambda d, x: (1, ten_n - 1 - x) if d == 1 else None))
-    other = lax.ppermute(after(chain, sums), "context", along(lambda i, j: (i, j ^ 1)))
+    other = lax.ppermute(after(chain, sums), "context", along(lambda i, j: (i ^ 1, j)))
     far1.append(lax.ppermute(after(near1[1], cross, third, other), "dp", swap))
-    chain = jnp.stack([chain, other])
-    other = lax.ppermute(chain, "context", along(lambda i, j: (i ^ 1, j)))
     columns = (near0, *near1, far0, *far1)
     partial, near = outer((sums, third, cross), columns)
     pieces = lax.all_to_all(partial, "context", split_axis=0, concat_axis=0, tiled=True)
@@ -370,7 +369,7 @@
     parts = []
     for s in range(ten_n):
         parts.append(lax.ppermute(piece, line, moves(lambda d, x, s=s: (x // 2, (2 * d + x % 2) ^ s))))
-    give = context_rows(1, after(near, parts[0]), far, chain, rest)
+    give = context_rows(1, after(near, *parts), far, chain, rest)
     back = lax.ppermute(give, "dp", swap)
     context_grad = context_rows(0, near, far, chain, rest, back)
     weight_grad = last(parts, both_t)

time: 114 us -> 109 us (0.956)
  the two profiles are of different devices: /device:TPU:1 before, /device:TPU:7 now
where the time goes in v10:
time: 109 us; the launch traced here: 108 us
  starting transfers between devices  43.1 us (40%)
  waiting for transfers between devices  35.1 us (32%)
  Pallas kernels  22.2 us (20%)
  other arithmetic  3.55 us (3%)
  local copies, waits for them, and re-layouts  3.51 us (3%)
    all_to_all x1, waiting for transfers between devices, local(): lax.all_to_all(partial, 'context', split_axis=0, concat_axis=0, tiled=True)  14.2 us
    ppermute x1, waiting for transfers between devices, local(): lax.ppermute(chain, 'context', along(lambda i, j: (i, j ^ 1)))  8.73 us
    ppermute x1, starting transfers between devices, local(): back = lax.ppermute(give, 'dp', swap)  8.16 us
    all_to_all x1, starting transfers between devices, local(): lax.all_to_all(outgoing, 'context', split_axis=0, concat_axis=0, tiled=True)  7.78 us
    pallas_call x1, Pallas kernels, chain_terms(): pl.pallas_call(chain_kernel, in_specs=[vmem, vmem, pl.BlockSpec(memory_sp...  6.54 us
    all_to_all x1, starting transfers between devices, local(): lax.all_to_all(partial, 'context', split_axis=0, concat_axis=0, tiled=True)  6.08 us
    pallas_call x2, Pallas kernels, context_rows(): pl.pallas_call(functools.partial(rows_kernel, which), in_specs=[vmem] * (...  5.06 us
    pallas_call x1, Pallas kernels, segment_sums(): pl.pallas_call(seg_kernel, in_specs=[vmem, vmem, pl.BlockSpec(memory_spac...  4.95 us
  transfers between devices with their start and end apart: 20, of which 11 were waited for; matrix products, arithmetic and copies ran while one was open for 3% of the time, Pallas kernels for 13%

profile of v10, /device:TPU:7, one launch (start us, length us, event | category | flops | bytes accessed | tf_op | source)
XLA Modules:
  0.0 108.2 jit_solution(12186920496983936305)
XLA Ops:
  0.6 1.1 %slice_bitcast_fusion = bf16[320,1024]{1,0:T(8,128)(2,1)S(1)} fusion(bf16[1,512,1024]{2,1,0:T(8,128)(2,1)} %param.10), kind=kLoop, calls=%fused_computation | loop fusion | bytes 1310720 | tf_op jit(solution)/shard_map/slice | solution.py:330
  1.8 0.0 copy-start
  1.8 0.6 collective-permute-start
  2.4 6.5 %shard_map.86 = (bf16[1024,1024]{1,0:T(8,128)(2,1)}, bf16[128,512]{1,0:T(8,128)(2,1)}, bf16[128,512]{1,0:T(8,128)(2,1)}, bf16[2,128,512]{2,1,0:T(8,128)(2,1)}) custom-call(bf16[1024,1024]{1,0:T(8,128)(2,1)} %value_ref.1, bf16[1024,1024]{1,0:T(8,128)(2,1)} %out_w_ref.1, bf16[4096,1024]{1,0:T(8,128)(2,1)} %global_ref.1), custom_call_target="tpu_custom_call" | custom-call | tf_op jit(solution)/shard_map/pallas_call | solution.py:227
  8.9 0.9 collective-permute-start.1
  9.9 1.2 %collective-permute-start.2 = (bf16[512,1024]{1,0:T(8,128)(2,1)S(1)}, bf16[512,1024]{1,0:T(8,128)(2,1)S(1)}, u32[]{:S(2)}, u32[]{:S(2)}) collective-permute-start(bf16[512,1024]{1,0:T(8,128)(2,1)S(1)} %bitcast.20), channel_id=1, source_target_pairs={{0,64},{64,0},{1,65},{65,1},{2,66},{66,2},{3,67},{67,3},{4,68},{68... | collective-permute-start | bytes 3145736 | tf_op jit(solution)/shard_map/ppermute | solution.py:329
  11.1 4.9 %shard_map.87 = bf16[1152,256]{1,0:T(8,128)(2,1)} custom-call(s32[64,128]{1,0:T(8,128)} %bitcast.30, s32[64,128]{1,0:T(8,128)} %bitcast.33, bf16[4096,1024]{1,0:T(8,128)(2,1)} %bitcast.24), custom_call_target="tpu_custom_call" | custom-call | tf_op jit(solution)/shard_map/pallas_call | solution.py:94
  16.1 1.2 %collective-permute-done.1 = bf16[2,128,512]{2,1,0:T(8,128)(2,1)S(1)} collective-permute-done((bf16[2,128,512]{2,1,0:T(8,128)(2,1)}, bf16[2,128,512]{2,1,0:T(8,128)(2,1)S(1)}, u32[]{:S(2)}, u32[]{:S(2)}) %collective-permute-start.1) | collective-permute-done | bytes 262176 | tf_op jit(solution)/shard_map/ppermute | solution.py:338
  17.3 0.2 collective-permute-done.n1a_ref
  17.5 0.6 collective-permute-start.4
  18.1 1.8 %collective-permute-start.3 = (bf16[320,1024]{1,0:T(8,128)(2,1)S(1)}, bf16[320,1024]{1,0:T(8,128)(2,1)}, u32[]{:S(2)}, u32[]{:S(2)}) collective-permute-start(bf16[320,1024]{1,0:T(8,128)(2,1)S(1)} %collective-permute-done.n1a_ref), channel_id=1, source_target_pairs={{0,64},{64,0},{1,65},{65,1},{2,66},{66,2},{3,67},{67,3},{4,68},{68... | collective-permute-start | bytes 1966088 | tf_op jit(solution)/shard_map/ppermute | solution.py:352
  20.0 0.3 convert_reduce_fusion
  20.2 7.8 %all-to-all-start = ((bf16[16,72,256]{2,1,0:T(8,128)(2,1)}), bf16[16,72,256]{2,1,0:T(8,128)(2,1)S(1)}, u32[]{:S(2)}, u32[]{:S(2)}) async-start(bf16[16,72,256]{2,1,0:T(8,128)(2,1)} %bitcast.25), calls=%async_computation | async-start | bytes 1179648 | tf_op jit(solution)/shard_map/all_to_all | solution.py:342
  28.0 0.0 collective-permute-done.4
  28.0 1.1 %fusion.2 = bf16[128,512]{1,0:T(8,128)(2,1)S(1)} fusion(bf16[128,512]{1,0:T(8,128)(2,1)} %collective-permute-done.4, bf16[128,512]{1,0:T(8,128)(2,1)} %get-tuple-element.22, bf16[2,128,512]{2,1,0:T(8,128)(2,1)} %copy-done.7), kind=kLoop, calls=%fused_computation.8 | loop fusion | flops 393216 | bytes 524288 | tf_op jit(solution)/shard_map/convert_element_type | solution.py:347
  29.1 1.4 %collective-permute-start.5 = (bf16[128,512]{1,0:T(8,128)(2,1)S(1)}, bf16[128,512]{1,0:T(8,128)(2,1)S(1)}, u32[]{:S(2)}, u32[]{:S(2)}) collective-permute-start(bf16[128,512]{1,0:T(8,128)(2,1)S(1)} %fusion.2), channel_id=1, source_target_pairs={{0,4},{4,0},{8,12},{12,8},{16,20},{20,16},{24,28},{28,24},{32,36},... | collective-permute-start | bytes 393224 | tf_op jit(solution)/shard_map/ppermute | solution.py:348
  30.6 8.7 %collective-permute-done.5 = bf16[128,512]{1,0:T(8,128)(2,1)S(1)} collective-permute-done((bf16[128,512]{1,0:T(8,128)(2,1)S(1)}, bf16[128,512]{1,0:T(8,128)(2,1)S(1)}, u32[]{:S(2)}, u32[]{:S(2)}) %collective-permute-start.5) | collective-permute-done | bytes 131104 | tf_op jit(solution)/shard_map/ppermute | solution.py:348
  39.3 0.7 pad_maximum_fusion.1
  40.0 0.0 all-to-all-done
  40.0 0.0 collective-permute-done.3.f1a_ref
  40.1 1.2 %collective-permute-start.8 = (bf16[192,1024]{1,0:T(8,128)(2,1)S(1)}, bf16[192,1024]{1,0:T(8,128)(2,1)S(1)}, u32[]{:S(2)}, u32[]{:S(2)}) collective-permute-start(bf16[192,1024]{1,0:T(8,128)(2,1)S(1)} %slice.19), channel_id=1, source_target_pairs={{0,1},{1,0},{2,3},{3,2},{4,5},{5,4},{6,7},{7,6},{8,9},{9,8},{10,11... | collective-permute-start | bytes 1179656 | tf_op jit(solution)/shard_map/ppermute | solution.py:355
  41.3 0.9 shard_map.88.mine_ref
  42.1 1.3 %collective-permute-start.9 = (bf16[2,128,512]{2,1,0:T(8,128)(2,1)}, bf16[2,128,512]{2,1,0:T(8,128)(2,1)S(1)}, u32[]{:S(2)}, u32[]{:S(2)}) collective-permute-start(bf16[2,128,512]{2,1,0:T(8,128)(2,1)} %pad_maximum_fusion.1), channel_id=1, source_target_pairs={{0,16},{4,20},{8,24},{12,28},{16,0},{20,4},{24,8},{28,12},{32,48},... | collective-permute-start | bytes 786440 | tf_op jit(solution)/shard_map/ppermute | solution.py:359
  43.4 1.7 %collective-permute-start.7 = (bf16[256,512]{1,0:T(8,128)(2,1)S(1)}, bf16[256,512]{1,0:T(8,128)(2,1)S(1)}, u32[]{:S(2)}, u32[]{:S(2)}) collective-permute-start(bf16[256,512]{1,0:T(8,128)(2,1)S(1)} %shard_map.88.mine_ref), channel_id=1, source_target_pairs={{0,67},{1,66},{2,65},{3,64},{64,0},{65,1},{66,2},{67,3},{4,71},{5,... | collective-permute-start | bytes 786440 | tf_op jit(solution)/shard_map/ppermute | solution.py:357
  45.1 2.8 %collective-permute-start.6 = (bf16[256,512]{1,0:T(8,128)(2,1)S(1)}, bf16[256,512]{1,0:T(8,128)(2,1)S(1)}, u32[]{:S(2)}, u32[]{:S(2)}) collective-permute-start(bf16[256,512]{1,0:T(8,128)(2,1)S(1)} %shard_map.88.mine_ref), channel_id=1, source_target_pairs={{64,67},{65,66},{66,65},{67,64},{68,71},{69,70},{70,69},{71,68},{7... | collective-permute-start | bytes 786440 | tf_op jit(solution)/shard_map/ppermute | solution.py:358
  47.8 0.2 collective-permute-done.9
  48.1 2.3 %collective-permute-done.7.cross_ref = bf16[256,512]{1,0:T(8,128)(2,1)S(1)} collective-permute-done((bf16[256,512]{1,0:T(8,128)(2,1)S(1)}, bf16[256,512]{1,0:T(8,128)(2,1)S(1)}, u32[]{:S(2)}, u32[]{:S(2)}) %collective-permute-start.7) | collective-permute-done | bytes 262176 | tf_op jit(solution)/shard_map/ppermute | solution.py:357
  50.4 3.0 %collective-permute-done.6.third_ref = bf16[256,512]{1,0:T(8,128)(2,1)S(1)} collective-permute-done((bf16[256,512]{1,0:T(8,128)(2,1)S(1)}, bf16[256,512]{1,0:T(8,128)(2,1)S(1)}, u32[]{:S(2)}, u32[]{:S(2)}) %collective-permute-start.6) | collective-permute-done | bytes 262176 | tf_op jit(solution)/shard_map/ppermute | solution.py:358
  53.4 1.7 %collective-permute-done.10.f1b_ref = bf16[192,1024]{1,0:T(8,128)(2,1)S(1)} collective-permute-done((bf16[192,1024]{1,0:T(8,128)(2,1)S(1)}, bf16[192,1024]{1,0:T(8,128)(2,1)S(1)}, u32[]{:S(2)}, u32[]{:S(2)}) %collective-permute-start.10) | collective-permute-done | bytes 393248 | tf_op jit(solution)/shard_map/ppermute | solution.py:360
  55.1 1.2 %copy-done.3 = bf16[512,1024]{1,0:T(8,128)(2,1)S(1)} copy-done((bf16[512,1024]{1,0:T(8,128)(2,1)S(1)}, bf16[512,1024]{1,0:T(8,128)(2,1)}, u32[]{:S(2)}) %copy-start.3) | copy-done | bytes 1048600
  56.3 1.1 %copy-done.5 = bf16[320,1024]{1,0:T(8,128)(2,1)S(1)} copy-done((bf16[320,1024]{1,0:T(8,128)(2,1)S(1)}, bf16[320,1024]{1,0:T(8,128)(2,1)}, u32[]{:S(2)}) %copy-start.5) | copy-done | bytes 655384
  57.4 3.1 %shard_map.89 = (bf16[16,256,128]{2,1,0:T(8,128)(2,1)}, bf16[2,256,512]{2,1,0:T(8,128)(2,1)S(1)}) custom-call(bf16[256,512]{1,0:T(8,128)(2,1)S(1)} %shard_map.88.mine_ref, bf16[256,512]{1,0:T(8,128)(2,1)S(1)} %collective-permute-done.6.third_ref, bf16[256,512]{1,0:T(8,128)(2,1)S(1)} %collective-permute-done.7.cross_ref, bf16[512,1024]{1,0:T(8,128)(2,1)S(1)} %bitcast.22, ...), custom_call_target="tpu_custom_call" | custom-call | tf_op jit(solution)/shard_map/pallas_call | solution.py:172
  60.6 0.0 copy-start.6
  60.6 6.1 %all-to-all-start.1 = ((bf16[16,256,128]{2,1,0:T(8,128)(2,1)}), bf16[16,256,128]{2,1,0:T(8,128)(2,1)}, u32[]{:S(2)}, u32[]{:S(2)}) async-start(bf16[16,256,128]{2,1,0:T(8,128)(2,1)} %get-tuple-element.30), calls=%async_computation.1 | async-start | bytes 2097152 | tf_op jit(solution)/shard_map/all_to_all | solution.py:363
  66.7 0.1 pad_maximum_fusion.low_ref
  66.7 2.6 %collective-permute-start.12 = (bf16[2,2,128,512]{3,2,1,0:T(8,128)(2,1)S(1)}, bf16[2,2,128,512]{3,2,1,0:T(8,128)(2,1)}, u32[]{:S(2)}, u32[]{:S(2)}) collective-permute-start(bf16[2,2,128,512]{3,2,1,0:T(8,128)(2,1)S(1)} %pad_maximum_fusion.low_ref), channel_id=1, source_target_pairs={{0,48},{4,52},{8,56},{12,60},{16,32},{20,36},{24,40},{28,44},{32,1... | collective-permute-start | bytes 1572872 | tf_op jit(solution)/shard_map/ppermute | solution.py:365
  69.3 14.2 %all-to-all-done.1 = bf16[16,256,128]{2,1,0:T(8,128)(2,1)} async-done(((bf16[16,256,128]{2,1,0:T(8,128)(2,1)}), bf16[16,256,128]{2,1,0:T(8,128)(2,1)}, u32[]{:S(2)}, u32[]{:S(2)}) %all-to-all-start.1) | async-done | bytes 1048608 | tf_op jit(solution)/shard_map/all_to_all | solution.py:363
  83.5 1.4 %reduce_sum.22 = bf16[256,128]{1,0:T(8,128)(2,1)S(1)} reduce(bf16[16,256,128]{2,1,0:T(8,128)(2,1)} %all-to-all-done.1, bf16[]{:T(256)} %constant.25.clone.1), dimensions={0}, to_apply=%region_1.2 | reduce | flops 491520 | bytes 1114114 | tf_op jit(solution)/shard_map/reduce_sum | solution.py:368
  84.9 1.2 %collective-permute-start.16 = (bf16[256,128]{1,0:T(8,128)(2,1)S(1)}, bf16[256,128]{1,0:T(8,128)(2,1)S(1)}, u32[]{:S(2)}, u32[]{:S(2)}) collective-permute-start(bf16[256,128]{1,0:T(8,128)(2,1)S(1)} %reduce_sum.22), channel_id=1, source_target_pairs={{0,3},{1,2},{2,67},{3,66},{64,1},{65,0},{66,65},{67,64},{4,7},{5,6... | collective-permute-start | bytes 196616 | tf_op jit(solution)/shard_map/ppermute | solution.py:371
  86.1 3.0 %collective-permute-start.15 = (bf16[256,128]{1,0:T(8,128)(2,1)S(1)}, bf16[256,128]{1,0:T(8,128)(2,1)S(1)}, u32[]{:S(2)}, u32[]{:S(2)}) collective-permute-start(bf16[256,128]{1,0:T(8,128)(2,1)S(1)} %reduce_sum.22), channel_id=1, source_target_pairs={{0,2},{1,3},{2,66},{3,67},{64,0},{65,1},{66,64},{67,65},{4,6},{5,7... | collective-permute-start | bytes 196616 | tf_op jit(solution)/shard_map/ppermute | solution.py:371
  89.1 0.7 collective-permute-start.13
  89.8 0.7 collective-permute-done.15.c_ref
  90.5 2.2 %collective-permute-done.14.b_ref = bf16[256,128]{1,0:T(8,128)(2,1)S(1)} collective-permute-done((bf16[256,128]{1,0:T(8,128)(2,1)S(1)}, bf16[256,128]{1,0:T(8,128)(2,1)S(1)}, u32[]{:S(2)}, u32[]{:S(2)}) %collective-permute-start.14) | collective-permute-done | bytes 65568 | tf_op jit(solution)/shard_map/ppermute | solution.py:371
  92.7 2.0 %shard_map.90 = bf16[512,1024]{1,0:T(8,128)(2,1)S(1)} custom-call(bf16[2,256,512]{2,1,0:T(8,128)(2,1)S(1)} %get-tuple-element.33.near_ref, bf16[2,256,512]{2,1,0:T(8,128)(2,1)} %collective-permute-done.11.far_ref, bf16[2,2,128,512]{3,2,1,0:T(8,128)(2,1)S(1)} %pad_maximum_fusion.low_ref, bf16[2,2,128,512]{3,2,1,0:T(8,128)(2,1)} %collective-permute-done.12.high_ref), custom_call_target="tpu_custom_call" | custom-call | tf_op jit(solution)/shard_map/pallas_call | solution.py:266
  94.7 8.2 %collective-permute-start.17 = (bf16[512,1024]{1,0:T(8,128)(2,1)S(1)}, bf16[512,1024]{1,0:T(8,128)(2,1)S(1)}, u32[]{:S(2)}, u32[]{:S(2)}) collective-permute-start(bf16[512,1024]{1,0:T(8,128)(2,1)S(1)} %shard_map.90), channel_id=1, source_target_pairs={{0,64},{64,0},{1,65},{65,1},{2,66},{66,2},{3,67},{67,3},{4,68},{68... | collective-permute-start | bytes 3145736 | tf_op jit(solution)/shard_map/ppermute | solution.py:373
  102.9 1.6 %shard_map.92 = f32[128,1024]{1,0:T(8,128)} custom-call(bf16[256,128]{1,0:T(8,128)(2,1)S(1)} %collective-permute-done.13.a_ref, bf16[256,128]{1,0:T(8,128)(2,1)S(1)} %collective-permute-done.14.b_ref, bf16[256,128]{1,0:T(8,128)(2,1)S(1)} %collective-permute-done.15.c_ref, bf16[256,128]{1,0:T(8,128)(2,1)S(1)} %collective-permute-done.16.d_ref, ...), custom_call_target="tpu_custom_call" | custom-call | tf_op jit(solution)/shard_map/pallas_call | solution.py:295
  104.5 0.7 collective-permute-done.17.rest_0_
  105.1 3.0 %shard_map.91 = bf16[512,1024]{1,0:T(8,128)(2,1)} custom-call(bf16[2,256,512]{2,1,0:T(8,128)(2,1)S(1)} %get-tuple-element.33.near_ref, bf16[2,256,512]{2,1,0:T(8,128)(2,1)} %collective-permute-done.11.far_ref, bf16[2,2,128,512]{3,2,1,0:T(8,128)(2,1)S(1)} %pad_maximum_fusion.low_ref, bf16[2,2,128,512]{3,2,1,0:T(8,128)(2,1)} %collective-permute-done.12.high_ref, ...), custom_call_target="tpu_custom_call" | custom-call | tf_op jit(solution)/shard_map/pallas_call | solution.py:266
  (29 shorter events, 0.1 us)
Async XLA Ops:
  1.8 8.1 %copy-start = (bf16[1,512,1024]{2,1,0:T(8,128)(2,1)S(1)}, bf16[1,512,1024]{2,1,0:T(8,128)(2,1)}, u32[]{:S(2)}) copy-start(bf16[1,512,1024]{2,1,0:T(8,128)(2,1)} %param.10) | copy-start | bytes 3145732
  1.8 15.7 %collective-permute-start = (bf16[320,1024]{1,0:T(8,128)(2,1)S(1)}, bf16[320,1024]{1,0:T(8,128)(2,1)S(1)}, u32[]{:S(2)}, u32[]{:S(2)}) collective-permute-start(bf16[320,1024]{1,0:T(8,128)(2,1)S(1)} %slice_bitcast_fusion), channel_id=1, source_target_pairs={{0,1},{1,0},{2,3},{3,2},{4,5},{5,4},{6,7},{7,6},{8,9},{9,8},{10,11... | collective-permute-start | bytes 1966088 | tf_op jit(solution)/shard_map/ppermute | solution.py:330
  8.9 8.4 %collective-permute-start.1 = (bf16[2,128,512]{2,1,0:T(8,128)(2,1)}, bf16[2,128,512]{2,1,0:T(8,128)(2,1)S(1)}, u32[]{:S(2)}, u32[]{:S(2)}) collective-permute-start(bf16[2,128,512]{2,1,0:T(8,128)(2,1)} %get-tuple-element.20), channel_id=1, source_target_pairs={{0,3},{1,2},{2,1},{3,0},{4,7},{5,6},{6,5},{7,4},{8,11},{9,10},{10,... | collective-permute-start | bytes 786440 | tf_op jit(solution)/shard_map/ppermute | solution.py:338
  9.9 30.1 %collective-permute-start.2 = (bf16[512,1024]{1,0:T(8,128)(2,1)S(1)}, bf16[512,1024]{1,0:T(8,128)(2,1)S(1)}, u32[]{:S(2)}, u32[]{:S(2)}) collective-permute-start(bf16[512,1024]{1,0:T(8,128)(2,1)S(1)} %bitcast.20), channel_id=1, source_target_pairs={{0,64},{64,0},{1,65},{65,1},{2,66},{66,2},{3,67},{67,3},{4,68},{68... | collective-permute-start | bytes 3145736 | tf_op jit(solution)/shard_map/ppermute | solution.py:329
  11.1 6.3 %copy-start.9 = (bf16[128,512]{1,0:T(8,128)(2,1)S(1)}, bf16[128,512]{1,0:T(8,128)(2,1)}, u32[]{:S(2)}) copy-start(bf16[128,512]{1,0:T(8,128)(2,1)} %get-tuple-element.24) | copy-start | bytes 393220
  11.1 8.8 %copy-start.8 = (s32[1,8192]{1,0:T(1,128)S(1)}, s32[1,8192]{1,0:T(1,128)}, u32[]{:S(2)}) copy-start(s32[1,8192]{1,0:T(1,128)} %param.8) | copy-start | bytes 98308
  17.3 2.9 %copy-start.7 = (bf16[2,128,512]{2,1,0:T(8,128)(2,1)}, bf16[2,128,512]{2,1,0:T(8,128)(2,1)S(1)}, u32[]{:S(2)}) copy-start(bf16[2,128,512]{2,1,0:T(8,128)(2,1)S(1)} %collective-permute-done.1) | copy-start | bytes 786436
  17.5 24.7 %copy-start.4 = (bf16[320,1024]{1,0:T(8,128)(2,1)}, bf16[320,1024]{1,0:T(8,128)(2,1)S(1)}, u32[]{:S(2)}) copy-start(bf16[320,1024]{1,0:T(8,128)(2,1)S(1)} %collective-permute-done.n1a_ref) | copy-start | bytes 1966084
  17.5 10.5 %collective-permute-start.4 = (bf16[128,512]{1,0:T(8,128)(2,1)S(1)}, bf16[128,512]{1,0:T(8,128)(2,1)}, u32[]{:S(2)}, u32[]{:S(2)}) collective-permute-start(bf16[128,512]{1,0:T(8,128)(2,1)S(1)} %fusion), channel_id=1, source_target_pairs={{0,1},{1,0},{2,3},{3,2},{4,5},{5,4},{6,7},{7,6},{8,9},{9,8},{10,11... | collective-permute-start | bytes 393224 | tf_op jit(solution)/shard_map/ppermute | solution.py:346
  18.1 21.9 %collective-permute-start.3 = (bf16[320,1024]{1,0:T(8,128)(2,1)S(1)}, bf16[320,1024]{1,0:T(8,128)(2,1)}, u32[]{:S(2)}, u32[]{:S(2)}) collective-permute-start(bf16[320,1024]{1,0:T(8,128)(2,1)S(1)} %collective-permute-done.n1a_ref), channel_id=1, source_target_pairs={{0,64},{64,0},{1,65},{65,1},{2,66},{66,2},{3,67},{67,3},{4,68},{68... | collective-permute-start | bytes 1966088 | tf_op jit(solution)/shard_map/ppermute | solution.py:352
  20.2 19.8 %all-to-all-start = ((bf16[16,72,256]{2,1,0:T(8,128)(2,1)}), bf16[16,72,256]{2,1,0:T(8,128)(2,1)S(1)}, u32[]{:S(2)}, u32[]{:S(2)}) async-start(bf16[16,72,256]{2,1,0:T(8,128)(2,1)} %bitcast.25), calls=%async_computation | async-start | bytes 1179648 | tf_op jit(solution)/shard_map/all_to_all | solution.py:342
  29.1 10.2 %collective-permute-start.5 = (bf16[128,512]{1,0:T(8,128)(2,1)S(1)}, bf16[128,512]{1,0:T(8,128)(2,1)S(1)}, u32[]{:S(2)}, u32[]{:S(2)}) collective-permute-start(bf16[128,512]{1,0:T(8,128)(2,1)S(1)} %fusion.2), channel_id=1, source_target_pairs={{0,4},{4,0},{8,12},{12,8},{16,20},{20,16},{24,28},{28,24},{32,36},... | collective-permute-start | bytes 393224 | tf_op jit(solution)/shard_map/ppermute | solution.py:348
  40.0 13.4 %copy-start.2 = (bf16[512,1024]{1,0:T(8,128)(2,1)}, bf16[512,1024]{1,0:T(8,128)(2,1)S(1)}, u32[]{:S(2)}) copy-start(bf16[512,1024]{1,0:T(8,128)(2,1)S(1)} %collective-permute-done.2.f0_ref) | copy-start | bytes 3145732
  40.1 13.3 %collective-permute-start.8 = (bf16[192,1024]{1,0:T(8,128)(2,1)S(1)}, bf16[192,1024]{1,0:T(8,128)(2,1)S(1)}, u32[]{:S(2)}, u32[]{:S(2)}) collective-permute-start(bf16[192,1024]{1,0:T(8,128)(2,1)S(1)} %slice.19), channel_id=1, source_target_pairs={{0,1},{1,0},{2,3},{3,2},{4,5},{5,4},{6,7},{7,6},{8,9},{9,8},{10,11... | collective-permute-start | bytes 1179656 | tf_op jit(solution)/shard_map/ppermute | solution.py:355
  42.1 5.9 %collective-permute-start.9 = (bf16[2,128,512]{2,1,0:T(8,128)(2,1)}, bf16[2,128,512]{2,1,0:T(8,128)(2,1)S(1)}, u32[]{:S(2)}, u32[]{:S(2)}) collective-permute-start(bf16[2,128,512]{2,1,0:T(8,128)(2,1)} %pad_maximum_fusion.1), channel_id=1, source_target_pairs={{0,16},{4,20},{8,24},{12,28},{16,0},{20,4},{24,8},{28,12},{32,48},... | collective-permute-start | bytes 786440 | tf_op jit(solution)/shard_map/ppermute | solution.py:359
  43.4 7.0 %collective-permute-start.7 = (bf16[256,512]{1,0:T(8,128)(2,1)S(1)}, bf16[256,512]{1,0:T(8,128)(2,1)S(1)}, u32[]{:S(2)}, u32[]{:S(2)}) collective-permute-start(bf16[256,512]{1,0:T(8,128)(2,1)S(1)} %shard_map.88.mine_ref), channel_id=1, source_target_pairs={{0,67},{1,66},{2,65},{3,64},{64,0},{65,1},{66,2},{67,3},{4,71},{5,... | collective-permute-start | bytes 786440 | tf_op jit(solution)/shard_map/ppermute | solution.py:357
  45.1 8.3 %collective-permute-start.6 = (bf16[256,512]{1,0:T(8,128)(2,1)S(1)}, bf16[256,512]{1,0:T(8,128)(2,1)S(1)}, u32[]{:S(2)}, u32[]{:S(2)}) collective-permute-start(bf16[256,512]{1,0:T(8,128)(2,1)S(1)} %shard_map.88.mine_ref), channel_id=1, source_target_pairs={{64,67},{65,66},{66,65},{67,64},{68,71},{69,70},{70,69},{71,68},{7... | collective-permute-start | bytes 786440 | tf_op jit(solution)/shard_map/ppermute | solution.py:358
  53.4 1.7 %collective-permute-start.10 = (bf16[192,1024]{1,0:T(8,128)(2,1)S(1)}, bf16[192,1024]{1,0:T(8,128)(2,1)S(1)}, u32[]{:S(2)}, u32[]{:S(2)}) collective-permute-start(bf16[192,1024]{1,0:T(8,128)(2,1)S(1)} %collective-permute-done.8.n1b_ref), channel_id=1, source_target_pairs={{0,64},{64,0},{1,65},{65,1},{2,66},{66,2},{3,67},{67,3},{4,68},{68... | collective-permute-start | bytes 1179656 | tf_op jit(solution)/shard_map/ppermute | solution.py:360
  55.1 1.2 %copy-start.3 = (bf16[512,1024]{1,0:T(8,128)(2,1)S(1)}, bf16[512,1024]{1,0:T(8,128)(2,1)}, u32[]{:S(2)}) copy-start(bf16[512,1024]{1,0:T(8,128)(2,1)} %copy-done.2) | copy-start | bytes 3145732
  56.3 1.1 %copy-start.5 = (bf16[320,1024]{1,0:T(8,128)(2,1)S(1)}, bf16[320,1024]{1,0:T(8,128)(2,1)}, u32[]{:S(2)}) copy-start(bf16[320,1024]{1,0:T(8,128)(2,1)} %copy-done.4) | copy-start | bytes 1966084
  60.6 6.1 %copy-start.6 = (bf16[2,128,512]{2,1,0:T(8,128)(2,1)S(1)}, bf16[2,128,512]{2,1,0:T(8,128)(2,1)}, u32[]{:S(2)}) copy-start(bf16[2,128,512]{2,1,0:T(8,128)(2,1)} %pad_maximum_fusion.1) | copy-start | bytes 786436
  60.6 23.0 %all-to-all-start.1 = ((bf16[16,256,128]{2,1,0:T(8,128)(2,1)}), bf16[16,256,128]{2,1,0:T(8,128)(2,1)}, u32[]{:S(2)}, u32[]{:S(2)}) async-start(bf16[16,256,128]{2,1,0:T(8,128)(2,1)} %get-tuple-element.30), calls=%async_computation.1 | async-start | bytes 2097152 | tf_op jit(solution)/shard_map/all_to_all | solution.py:363
  66.7 25.9 %collective-permute-start.12 = (bf16[2,2,128,512]{3,2,1,0:T(8,128)(2,1)S(1)}, bf16[2,2,128,512]{3,2,1,0:T(8,128)(2,1)}, u32[]{:S(2)}, u32[]{:S(2)}) collective-permute-start(bf16[2,2,128,512]{3,2,1,0:T(8,128)(2,1)S(1)} %pad_maximum_fusion.low_ref), channel_id=1, source_target_pairs={{0,48},{4,52},{8,56},{12,60},{16,32},{20,36},{24,40},{28,44},{32,1... | collective-permute-start | bytes 1572872 | tf_op jit(solution)/shard_map/ppermute | solution.py:365
  69.3 33.5 %copy-start.1 = (bf16[1024,1024]{1,0:T(8,128)(2,1)S(1)}, bf16[1024,1024]{1,0:T(8,128)(2,1)}, u32[]{:S(2)}) copy-start(bf16[1024,1024]{1,0:T(8,128)(2,1)} %get-tuple-element.18.w_ref) | copy-start | bytes 6291460
  69.3 23.3 %collective-permute-start.11 = (bf16[2,256,512]{2,1,0:T(8,128)(2,1)S(1)}, bf16[2,256,512]{2,1,0:T(8,128)(2,1)}, u32[]{:S(2)}, u32[]{:S(2)}) collective-permute-start(bf16[2,256,512]{2,1,0:T(8,128)(2,1)S(1)} %get-tuple-element.33.near_ref), channel_id=1, source_target_pairs={{0,1},{1,0},{2,3},{3,2},{4,5},{5,4},{6,7},{7,6},{8,9},{9,8},{10,11... | collective-permute-start | bytes 1572872 | tf_op jit(solution)/shard_map/ppermute | solution.py:367
  84.9 4.2 %collective-permute-start.16 = (bf16[256,128]{1,0:T(8,128)(2,1)S(1)}, bf16[256,128]{1,0:T(8,128)(2,1)S(1)}, u32[]{:S(2)}, u32[]{:S(2)}) collective-permute-start(bf16[256,128]{1,0:T(8,128)(2,1)S(1)} %reduce_sum.22), channel_id=1, source_target_pairs={{0,3},{1,2},{2,67},{3,66},{64,1},{65,0},{66,65},{67,64},{4,7},{5,6... | collective-permute-start | bytes 196616 | tf_op jit(solution)/shard_map/ppermute | solution.py:371
  86.1 4.4 %collective-permute-start.15 = (bf16[256,128]{1,0:T(8,128)(2,1)S(1)}, bf16[256,128]{1,0:T(8,128)(2,1)S(1)}, u32[]{:S(2)}, u32[]{:S(2)}) collective-permute-start(bf16[256,128]{1,0:T(8,128)(2,1)S(1)} %reduce_sum.22), channel_id=1, source_target_pairs={{0,2},{1,3},{2,66},{3,67},{64,0},{65,1},{66,64},{67,65},{4,6},{5,7... | collective-permute-start | bytes 196616 | tf_op jit(solution)/shard_map/ppermute | solution.py:371
  89.1 3.5 %collective-permute-start.14 = (bf16[256,128]{1,0:T(8,128)(2,1)S(1)}, bf16[256,128]{1,0:T(8,128)(2,1)S(1)}, u32[]{:S(2)}, u32[]{:S(2)}) collective-permute-start(bf16[256,128]{1,0:T(8,128)(2,1)S(1)} %reduce_sum.22), channel_id=1, source_target_pairs={{0,1},{1,0},{2,65},{3,64},{64,3},{65,2},{66,67},{67,66},{4,5},{5,4... | collective-permute-start | bytes 196616 | tf_op jit(solution)/shard_map/ppermute | solution.py:371
  89.1 3.5 %collective-permute-start.13 = (bf16[256,128]{1,0:T(8,128)(2,1)S(1)}, bf16[256,128]{1,0:T(8,128)(2,1)S(1)}, u32[]{:S(2)}, u32[]{:S(2)}) collective-permute-start(bf16[256,128]{1,0:T(8,128)(2,1)S(1)} %reduce_sum.22), channel_id=1, source_target_pairs={{0,0},{1,1},{2,64},{3,65},{64,2},{65,3},{66,66},{67,67},{4,4},{5,5... | collective-permute-start | bytes 196616 | tf_op jit(solution)/shard_map/ppermute | solution.py:371
  94.7 10.4 %collective-permute-start.17 = (bf16[512,1024]{1,0:T(8,128)(2,1)S(1)}, bf16[512,1024]{1,0:T(8,128)(2,1)S(1)}, u32[]{:S(2)}, u32[]{:S(2)}) collective-permute-start(bf16[512,1024]{1,0:T(8,128)(2,1)S(1)} %shard_map.90), channel_id=1, source_target_pairs={{0,64},{64,0},{1,65},{65,1},{2,66},{66,2},{3,67},{67,3},{4,68},{68... | collective-permute-start | bytes 3145736 | tf_op jit(solution)/shard_map/ppermute | solution.py:373

commit v11 on v10

--- a/solution.py
+++ b/solution.py
@@ -326,7 +326,6 @@
     swap = [(i, dp_n - 1 - i) for i in range(dp_n)]
     pair = [(x, x ^ 1) for x in range(ten_n)]
     near0 = attn_context[0]
-    far0 = lax.ppermute(near0, "dp", swap)
     near1 = [lax.ppermute(near0[:CUT], "tensor", pair)]
 
     def along(target):
@@ -349,14 +348,15 @@
     edges = jnp.arange(ctx_n, dtype=jnp.int32) * bytes_n
     counts = jnp.sum((patch_starts[0][None, :] <= edges[:, None]).astype(jnp.int32), axis=1)
     first = jnp.minimum((counts - 1) // LANES, starts.shape[0] - WIN)
-    far1 = [lax.ppermute(near1[0], "dp", swap)]
-    incoming = after(incoming, first, far0, far1[0], chain)
+    incoming = after(incoming, first, chain)
 
     near1.append(lax.ppermute(after(near0, incoming)[CUT:], "tensor", pair))
     sums = collect(first, incoming, patch_rows)
     cross = lax.ppermute(sums, line, moves(lambda d, x: (0, x) if d == 1 else (1, ten_n - 1 - x)))
     third = lax.ppermute(sums, line, moves(lambda d, x: (1, ten_n - 1 - x) if d == 1 else None))
     other = lax.ppermute(after(chain, sums), "context", along(lambda i, j: (i ^ 1, j)))
+    far0 = lax.ppermute(after(near0, sums), "dp", swap)
+    far1 = [lax.ppermute(after(near1[0], sums), "dp", swap)]
     far1.append(lax.ppermute(after(near1[1], cross, third, other), "dp", swap))
     columns = (near0, *near1, far0, *far1)
     partial, near = outer((sums, third, cross), columns)

time: 109 us -> 108 us (level)
  the two profiles are of different devices: /device:TPU:7 before, /device:TPU:1 now
where the time goes in v11:
time: 108 us; the launch traced here: 106 us
  starting transfers between devices  44.6 us (41%)
  waiting for transfers between devices  32.3 us (30%)
  Pallas kernels  24.4 us (23%)
  local copies, waits for them, and re-layouts  2.15 us (2%)
  other arithmetic  1.81 us (2%)
    all_to_all x1, waiting for transfers between devices, local(): lax.all_to_all(partial, 'context', split_axis=0, concat_axis=0, tiled=True)  12.9 us
    ppermute x4, starting transfers between devices, local(): lax.ppermute(piece, line, moves(lambda d, x, s=s: (x // 2, 2 * d + x % 2...  10.8 us
    ppermute x1, waiting for transfers between devices, local(): lax.ppermute(chain, 'context', along(lambda i, j: (i, j ^ 1)))  7.86 us
    all_to_all x1, starting transfers between devices, local(): lax.all_to_all(outgoing, 'context', split_axis=0, concat_axis=0, tiled=True)  7.77 us
    pallas_call x1, Pallas kernels, chain_terms(): pl.pallas_call(chain_kernel, in_specs=[vmem, vmem, pl.BlockSpec(memory_sp...  6.54 us
    pallas_call x1, Pallas kernels, segment_sums(): pl.pallas_call(seg_kernel, in_specs=[vmem, vmem, pl.BlockSpec(memory_spac...  5.32 us
    all_to_all x1, starting transfers between devices, local(): lax.all_to_all(partial, 'context', split_axis=0, concat_axis=0, tiled=True)  5.07 us
    pallas_call x2, Pallas kernels, context_rows(): pl.pallas_call(functools.partial(rows_kernel, which), in_specs=[vmem] * (...  5.05 us
  transfers between devices with their start and end apart: 20, of which 12 were waited for; matrix products, arithmetic and copies ran while one was open for 2% of the time, Pallas kernels for 13%

profile of v11, /device:TPU:1, one launch (start us, length us, event | category | flops | bytes accessed | tf_op | source)
XLA Modules:
  0.0 106.1 jit_solution(14962833988164468793)
XLA Ops:
  0.6 1.1 %slice_bitcast_fusion = bf16[320,1024]{1,0:T(8,128)(2,1)S(1)} fusion(bf16[1,512,1024]{2,1,0:T(8,128)(2,1)} %param.10), kind=kLoop, calls=%fused_computation | loop fusion | bytes 1310720 | tf_op jit(solution)/shard_map/slice | solution.py:329
  1.8 2.1 %collective-permute-start = (bf16[320,1024]{1,0:T(8,128)(2,1)S(1)}, bf16[320,1024]{1,0:T(8,128)(2,1)S(1)}, u32[]{:S(2)}, u32[]{:S(2)}) collective-permute-start(bf16[320,1024]{1,0:T(8,128)(2,1)S(1)} %slice_bitcast_fusion), channel_id=1, source_target_pairs={{0,1},{1,0},{2,3},{3,2},{4,5},{5,4},{6,7},{7,6},{8,9},{9,8},{10,11... | collective-permute-start | bytes 1966088 | tf_op jit(solution)/shard_map/ppermute | solution.py:329
  3.9 6.5 %shard_map.86 = (bf16[1024,1024]{1,0:T(8,128)(2,1)}, bf16[128,512]{1,0:T(8,128)(2,1)}, bf16[128,512]{1,0:T(8,128)(2,1)}, bf16[2,128,512]{2,1,0:T(8,128)(2,1)}) custom-call(bf16[1024,1024]{1,0:T(8,128)(2,1)} %value_ref.1, bf16[1024,1024]{1,0:T(8,128)(2,1)} %out_w_ref.1, bf16[4096,1024]{1,0:T(8,128)(2,1)} %global_ref.1), custom_call_target="tpu_custom_call" | custom-call | tf_op jit(solution)/shard_map/pallas_call | solution.py:227
  10.4 1.9 %collective-permute-start.1 = (bf16[2,128,512]{2,1,0:T(8,128)(2,1)}, bf16[2,128,512]{2,1,0:T(8,128)(2,1)S(1)}, u32[]{:S(2)}, u32[]{:S(2)}) collective-permute-start(bf16[2,128,512]{2,1,0:T(8,128)(2,1)} %get-tuple-element.22), channel_id=1, source_target_pairs={{0,3},{1,2},{2,1},{3,0},{4,7},{5,6},{6,5},{7,4},{8,11},{9,10},{10,... | collective-permute-start | bytes 786440 | tf_op jit(solution)/shard_map/ppermute | solution.py:337
  12.3 5.3 %shard_map.87 = bf16[1152,256]{1,0:T(8,128)(2,1)} custom-call(s32[64,128]{1,0:T(8,128)} %bitcast.30, s32[64,128]{1,0:T(8,128)} %bitcast.33, bf16[4096,1024]{1,0:T(8,128)(2,1)} %bitcast.24), custom_call_target="tpu_custom_call" | custom-call | tf_op jit(solution)/shard_map/pallas_call | solution.py:94
  17.7 0.0 copy-start
  17.7 1.1 %collective-permute-done.1 = bf16[2,128,512]{2,1,0:T(8,128)(2,1)S(1)} collective-permute-done((bf16[2,128,512]{2,1,0:T(8,128)(2,1)}, bf16[2,128,512]{2,1,0:T(8,128)(2,1)S(1)}, u32[]{:S(2)}, u32[]{:S(2)}) %collective-permute-start.1) | collective-permute-done | bytes 262176 | tf_op jit(solution)/shard_map/ppermute | solution.py:337
  18.8 0.8 collective-permute-start.2
  19.6 0.3 convert_reduce_fusion
  19.9 7.8 %all-to-all-start = ((bf16[16,72,256]{2,1,0:T(8,128)(2,1)}), bf16[16,72,256]{2,1,0:T(8,128)(2,1)S(1)}, u32[]{:S(2)}, u32[]{:S(2)}) async-start(bf16[16,72,256]{2,1,0:T(8,128)(2,1)} %bitcast.25), calls=%async_computation | async-start | bytes 1179648 | tf_op jit(solution)/shard_map/all_to_all | solution.py:341
  27.7 0.0 collective-permute-done.2
  27.7 0.1 fusion.2
  27.7 1.4 %collective-permute-start.3 = (bf16[128,512]{1,0:T(8,128)(2,1)S(1)}, bf16[128,512]{1,0:T(8,128)(2,1)S(1)}, u32[]{:S(2)}, u32[]{:S(2)}) collective-permute-start(bf16[128,512]{1,0:T(8,128)(2,1)S(1)} %fusion.2), channel_id=1, source_target_pairs={{0,4},{4,0},{8,12},{12,8},{16,20},{20,16},{24,28},{28,24},{32,36},... | collective-permute-start | bytes 393224 | tf_op jit(solution)/shard_map/ppermute | solution.py:347
  29.2 7.9 %collective-permute-done.3 = bf16[128,512]{1,0:T(8,128)(2,1)S(1)} collective-permute-done((bf16[128,512]{1,0:T(8,128)(2,1)S(1)}, bf16[128,512]{1,0:T(8,128)(2,1)S(1)}, u32[]{:S(2)}, u32[]{:S(2)}) %collective-permute-start.3) | collective-permute-done | bytes 131104 | tf_op jit(solution)/shard_map/ppermute | solution.py:347
  37.1 0.8 all-to-all-done
  37.9 0.9 shard_map.88.mine_ref
  38.8 4.4 %collective-permute-start.7 = (bf16[512,1024]{1,0:T(8,128)(2,1)S(1)}, bf16[512,1024]{1,0:T(8,128)(2,1)S(1)}, u32[]{:S(2)}, u32[]{:S(2)}) collective-permute-start(bf16[512,1024]{1,0:T(8,128)(2,1)S(1)} %bitcast.20), channel_id=1, source_target_pairs={{0,64},{64,0},{1,65},{65,1},{2,66},{66,2},{3,67},{67,3},{4,68},{68... | collective-permute-start | bytes 3145736 | tf_op jit(solution)/shard_map/ppermute | solution.py:358
  43.3 0.9 collective-permute-start.6
  44.1 0.4 collective-permute-start.5
  44.5 3.9 %collective-permute-start.4 = (bf16[256,512]{1,0:T(8,128)(2,1)S(1)}, bf16[256,512]{1,0:T(8,128)(2,1)S(1)}, u32[]{:S(2)}, u32[]{:S(2)}) collective-permute-start(bf16[256,512]{1,0:T(8,128)(2,1)S(1)} %shard_map.88.mine_ref), channel_id=1, source_target_pairs={{64,67},{65,66},{66,65},{67,64},{68,71},{69,70},{70,69},{71,68},{7... | collective-permute-start | bytes 786440 | tf_op jit(solution)/shard_map/ppermute | solution.py:356
  48.4 2.7 %collective-permute-done.9 = bf16[2,128,512]{2,1,0:T(8,128)(2,1)S(1)} collective-permute-done((bf16[2,128,512]{2,1,0:T(8,128)(2,1)S(1)}, bf16[2,128,512]{2,1,0:T(8,128)(2,1)S(1)}, u32[]{:S(2)}, u32[]{:S(2)}) %collective-permute-start.9) | collective-permute-done | bytes 262176 | tf_op jit(solution)/shard_map/ppermute | solution.py:357
  51.1 0.9 collective-permute-start.8
  52.0 0.3 collective-permute-done.5.cross_ref
  52.2 1.7 %collective-permute-done.4.third_ref = bf16[256,512]{1,0:T(8,128)(2,1)S(1)} collective-permute-done((bf16[256,512]{1,0:T(8,128)(2,1)S(1)}, bf16[256,512]{1,0:T(8,128)(2,1)S(1)}, u32[]{:S(2)}, u32[]{:S(2)}) %collective-permute-start.4) | collective-permute-done | bytes 262176 | tf_op jit(solution)/shard_map/ppermute | solution.py:356
  54.0 0.1 collective-permute-done.6.n1b_ref
  54.0 0.9 collective-permute-start.10
  54.9 1.3 %collective-permute-done.10.f1b_ref = bf16[192,1024]{1,0:T(8,128)(2,1)S(1)} collective-permute-done((bf16[192,1024]{1,0:T(8,128)(2,1)S(1)}, bf16[192,1024]{1,0:T(8,128)(2,1)S(1)}, u32[]{:S(2)}, u32[]{:S(2)}) %collective-permute-start.10) | collective-permute-done | bytes 393248 | tf_op jit(solution)/shard_map/ppermute | solution.py:360
  56.2 5.0 %shard_map.89 = (bf16[16,256,128]{2,1,0:T(8,128)(2,1)S(1)}, bf16[2,256,512]{2,1,0:T(8,128)(2,1)S(1)}) custom-call(bf16[256,512]{1,0:T(8,128)(2,1)S(1)} %shard_map.88.mine_ref, bf16[256,512]{1,0:T(8,128)(2,1)S(1)} %collective-permute-done.4.third_ref, bf16[256,512]{1,0:T(8,128)(2,1)S(1)} %collective-permute-done.5.cross_ref, bf16[512,1024]{1,0:T(8,128)(2,1)S(1)} %bitcast.22, ...), custom_call_target="tpu_custom_call" | custom-call | tf_op jit(solution)/shard_map/pallas_call | solution.py:172
  61.3 0.0 copy-start.2
  61.3 1.0 copy-done.2
  62.3 5.1 %all-to-all-start.1 = ((bf16[16,256,128]{2,1,0:T(8,128)(2,1)}), bf16[16,256,128]{2,1,0:T(8,128)(2,1)}, u32[]{:S(2)}, u32[]{:S(2)}) async-start(bf16[16,256,128]{2,1,0:T(8,128)(2,1)} %copy-done.2), calls=%async_computation.1 | async-start | bytes 2097152 | tf_op jit(solution)/shard_map/all_to_all | solution.py:363
  67.3 0.1 pad_maximum_fusion.low_ref
  67.4 2.6 %collective-permute-start.12 = (bf16[2,2,128,512]{3,2,1,0:T(8,128)(2,1)S(1)}, bf16[2,2,128,512]{3,2,1,0:T(8,128)(2,1)}, u32[]{:S(2)}, u32[]{:S(2)}) collective-permute-start(bf16[2,2,128,512]{3,2,1,0:T(8,128)(2,1)S(1)} %pad_maximum_fusion.low_ref), channel_id=1, source_target_pairs={{0,48},{4,52},{8,56},{12,60},{16,32},{20,36},{24,40},{28,44},{32,1... | collective-permute-start | bytes 1572872 | tf_op jit(solution)/shard_map/ppermute | solution.py:365
  70.0 0.8 collective-permute-start.11
  70.8 12.9 %all-to-all-done.1 = bf16[16,256,128]{2,1,0:T(8,128)(2,1)} async-done(((bf16[16,256,128]{2,1,0:T(8,128)(2,1)}), bf16[16,256,128]{2,1,0:T(8,128)(2,1)}, u32[]{:S(2)}, u32[]{:S(2)}) %all-to-all-start.1) | async-done | bytes 1048608 | tf_op jit(solution)/shard_map/all_to_all | solution.py:363
  83.7 1.4 %reduce_sum.22 = bf16[256,128]{1,0:T(8,128)(2,1)S(1)} reduce(bf16[16,256,128]{2,1,0:T(8,128)(2,1)} %all-to-all-done.1, bf16[]{:T(256)} %constant.25.clone.1), dimensions={0}, to_apply=%region_1.2 | reduce | flops 491520 | bytes 1114114 | tf_op jit(solution)/shard_map/reduce_sum | solution.py:368
  85.1 2.9 %collective-permute-start.16 = (bf16[256,128]{1,0:T(8,128)(2,1)S(1)}, bf16[256,128]{1,0:T(8,128)(2,1)S(1)}, u32[]{:S(2)}, u32[]{:S(2)}) collective-permute-start(bf16[256,128]{1,0:T(8,128)(2,1)S(1)} %reduce_sum.22), channel_id=1, source_target_pairs={{0,3},{1,2},{2,67},{3,66},{64,1},{65,0},{66,65},{67,64},{4,7},{5,6... | collective-permute-start | bytes 196616 | tf_op jit(solution)/shard_map/ppermute | solution.py:371
  88.0 1.4 %collective-permute-start.15 = (bf16[256,128]{1,0:T(8,128)(2,1)S(1)}, bf16[256,128]{1,0:T(8,128)(2,1)S(1)}, u32[]{:S(2)}, u32[]{:S(2)}) collective-permute-start(bf16[256,128]{1,0:T(8,128)(2,1)S(1)} %reduce_sum.22), channel_id=1, source_target_pairs={{0,2},{1,3},{2,66},{3,67},{64,0},{65,1},{66,64},{67,65},{4,6},{5,7... | collective-permute-start | bytes 196616 | tf_op jit(solution)/shard_map/ppermute | solution.py:371
  89.4 0.0 collective-permute-start.14
  89.4 0.5 collective-permute-done.16.d_ref
  89.9 6.5 %collective-permute-start.13 = (bf16[256,128]{1,0:T(8,128)(2,1)S(1)}, bf16[256,128]{1,0:T(8,128)(2,1)S(1)}, u32[]{:S(2)}, u32[]{:S(2)}) collective-permute-start(bf16[256,128]{1,0:T(8,128)(2,1)S(1)} %reduce_sum.22), channel_id=1, source_target_pairs={{0,0},{1,1},{2,64},{3,65},{64,2},{65,3},{66,66},{67,67},{4,4},{5,5... | collective-permute-start | bytes 196616 | tf_op jit(solution)/shard_map/ppermute | solution.py:371
  96.4 0.0 collective-permute-done.14.b_ref
  96.4 1.9 %collective-permute-done.13.a_ref = bf16[256,128]{1,0:T(8,128)(2,1)S(1)} collective-permute-done((bf16[256,128]{1,0:T(8,128)(2,1)S(1)}, bf16[256,128]{1,0:T(8,128)(2,1)S(1)}, u32[]{:S(2)}, u32[]{:S(2)}) %collective-permute-start.13) | collective-permute-done | bytes 65568 | tf_op jit(solution)/shard_map/ppermute | solution.py:371
  98.3 2.0 %shard_map.90 = bf16[512,1024]{1,0:T(8,128)(2,1)S(1)} custom-call(bf16[2,256,512]{2,1,0:T(8,128)(2,1)S(1)} %get-tuple-element.37.near_ref, bf16[2,256,512]{2,1,0:T(8,128)(2,1)} %collective-permute-done.11.far_ref, bf16[2,2,128,512]{3,2,1,0:T(8,128)(2,1)S(1)} %pad_maximum_fusion.low_ref, bf16[2,2,128,512]{3,2,1,0:T(8,128)(2,1)} %collective-permute-done.12.high_ref), custom_call_target="tpu_custom_call" | custom-call | tf_op jit(solution)/shard_map/pallas_call | solution.py:266
  100.4 0.1 collective-permute-start.17
  100.5 1.6 %shard_map.92 = f32[128,1024]{1,0:T(8,128)} custom-call(bf16[256,128]{1,0:T(8,128)(2,1)S(1)} %collective-permute-done.13.a_ref, bf16[256,128]{1,0:T(8,128)(2,1)S(1)} %collective-permute-done.14.b_ref, bf16[256,128]{1,0:T(8,128)(2,1)S(1)} %collective-permute-done.15.c_ref, bf16[256,128]{1,0:T(8,128)(2,1)S(1)} %collective-permute-done.16.d_ref, ...), custom_call_target="tpu_custom_call" | custom-call | tf_op jit(solution)/shard_map/pallas_call | solution.py:295
  102.1 1.0 collective-permute-done.17.rest_0_
  103.1 3.0 %shard_map.91 = bf16[512,1024]{1,0:T(8,128)(2,1)} custom-call(bf16[2,256,512]{2,1,0:T(8,128)(2,1)S(1)} %get-tuple-element.37.near_ref, bf16[2,256,512]{2,1,0:T(8,128)(2,1)} %collective-permute-done.11.far_ref, bf16[2,2,128,512]{3,2,1,0:T(8,128)(2,1)S(1)} %pad_maximum_fusion.low_ref, bf16[2,2,128,512]{3,2,1,0:T(8,128)(2,1)} %collective-permute-done.12.high_ref, ...), custom_call_target="tpu_custom_call" | custom-call | tf_op jit(solution)/shard_map/pallas_call | solution.py:266
  (25 shorter events, 0.1 us)
Async XLA Ops:
  1.8 17.0 %collective-permute-start = (bf16[320,1024]{1,0:T(8,128)(2,1)S(1)}, bf16[320,1024]{1,0:T(8,128)(2,1)S(1)}, u32[]{:S(2)}, u32[]{:S(2)}) collective-permute-start(bf16[320,1024]{1,0:T(8,128)(2,1)S(1)} %slice_bitcast_fusion), channel_id=1, source_target_pairs={{0,1},{1,0},{2,3},{3,2},{4,5},{5,4},{6,7},{7,6},{8,9},{9,8},{10,11... | collective-permute-start | bytes 1966088 | tf_op jit(solution)/shard_map/ppermute | solution.py:329
  10.4 8.4 %collective-permute-start.1 = (bf16[2,128,512]{2,1,0:T(8,128)(2,1)}, bf16[2,128,512]{2,1,0:T(8,128)(2,1)S(1)}, u32[]{:S(2)}, u32[]{:S(2)}) collective-permute-start(bf16[2,128,512]{2,1,0:T(8,128)(2,1)} %get-tuple-element.22), channel_id=1, source_target_pairs={{0,3},{1,2},{2,1},{3,0},{4,7},{5,6},{6,5},{7,4},{8,11},{9,10},{10,... | collective-permute-start | bytes 786440 | tf_op jit(solution)/shard_map/ppermute | solution.py:337
  12.3 6.5 %copy-start.6 = (bf16[128,512]{1,0:T(8,128)(2,1)S(1)}, bf16[128,512]{1,0:T(8,128)(2,1)}, u32[]{:S(2)}) copy-start(bf16[128,512]{1,0:T(8,128)(2,1)} %get-tuple-element.26) | copy-start | bytes 393220
  12.3 7.3 %copy-start.5 = (s32[1,8192]{1,0:T(1,128)S(1)}, s32[1,8192]{1,0:T(1,128)}, u32[]{:S(2)}) copy-start(s32[1,8192]{1,0:T(1,128)} %param.8) | copy-start | bytes 98308
  12.3 15.3 %copy-start.7 = (bf16[128,512]{1,0:T(8,128)(2,1)S(1)}, bf16[128,512]{1,0:T(8,128)(2,1)}, u32[]{:S(2)}) copy-start(bf16[128,512]{1,0:T(8,128)(2,1)} %get-tuple-element.24) | copy-start | bytes 393220
  17.7 21.1 %copy-start = (bf16[1,512,1024]{2,1,0:T(8,128)(2,1)S(1)}, bf16[1,512,1024]{2,1,0:T(8,128)(2,1)}, u32[]{:S(2)}) copy-start(bf16[1,512,1024]{2,1,0:T(8,128)(2,1)} %param.10) | copy-start | bytes 3145732
  18.8 8.8 %collective-permute-start.2 = (bf16[128,512]{1,0:T(8,128)(2,1)S(1)}, bf16[128,512]{1,0:T(8,128)(2,1)S(1)}, u32[]{:S(2)}, u32[]{:S(2)}) collective-permute-start(bf16[128,512]{1,0:T(8,128)(2,1)S(1)} %fusion), channel_id=1, source_target_pairs={{0,1},{1,0},{2,3},{3,2},{4,5},{5,4},{6,7},{7,6},{8,9},{9,8},{10,11... | collective-permute-start | bytes 393224 | tf_op jit(solution)/shard_map/ppermute | solution.py:345
  19.9 18.1 %all-to-all-start = ((bf16[16,72,256]{2,1,0:T(8,128)(2,1)}), bf16[16,72,256]{2,1,0:T(8,128)(2,1)S(1)}, u32[]{:S(2)}, u32[]{:S(2)}) async-start(bf16[16,72,256]{2,1,0:T(8,128)(2,1)} %bitcast.25), calls=%async_computation | async-start | bytes 1179648 | tf_op jit(solution)/shard_map/all_to_all | solution.py:341
  27.7 9.3 %collective-permute-start.3 = (bf16[128,512]{1,0:T(8,128)(2,1)S(1)}, bf16[128,512]{1,0:T(8,128)(2,1)S(1)}, u32[]{:S(2)}, u32[]{:S(2)}) collective-permute-start(bf16[128,512]{1,0:T(8,128)(2,1)S(1)} %fusion.2), channel_id=1, source_target_pairs={{0,4},{4,0},{8,12},{12,8},{16,20},{20,16},{24,28},{28,24},{32,36},... | collective-permute-start | bytes 393224 | tf_op jit(solution)/shard_map/ppermute | solution.py:347
  38.8 17.4 %collective-permute-start.7 = (bf16[512,1024]{1,0:T(8,128)(2,1)S(1)}, bf16[512,1024]{1,0:T(8,128)(2,1)S(1)}, u32[]{:S(2)}, u32[]{:S(2)}) collective-permute-start(bf16[512,1024]{1,0:T(8,128)(2,1)S(1)} %bitcast.20), channel_id=1, source_target_pairs={{0,64},{64,0},{1,65},{65,1},{2,66},{66,2},{3,67},{67,3},{4,68},{68... | collective-permute-start | bytes 3145736 | tf_op jit(solution)/shard_map/ppermute | solution.py:358
  43.2 7.9 %collective-permute-start.9 = (bf16[2,128,512]{2,1,0:T(8,128)(2,1)S(1)}, bf16[2,128,512]{2,1,0:T(8,128)(2,1)S(1)}, u32[]{:S(2)}, u32[]{:S(2)}) collective-permute-start(bf16[2,128,512]{2,1,0:T(8,128)(2,1)S(1)} %pad_maximum_fusion.1), channel_id=1, source_target_pairs={{0,16},{4,20},{8,24},{12,28},{16,0},{20,4},{24,8},{28,12},{32,48},... | collective-permute-start | bytes 786440 | tf_op jit(solution)/shard_map/ppermute | solution.py:357
  43.3 10.8 %collective-permute-start.6 = (bf16[192,1024]{1,0:T(8,128)(2,1)S(1)}, bf16[192,1024]{1,0:T(8,128)(2,1)S(1)}, u32[]{:S(2)}, u32[]{:S(2)}) collective-permute-start(bf16[192,1024]{1,0:T(8,128)(2,1)S(1)} %slice.19), channel_id=1, source_target_pairs={{0,1},{1,0},{2,3},{3,2},{4,5},{5,4},{6,7},{7,6},{8,9},{9,8},{10,11... | collective-permute-start | bytes 1179656 | tf_op jit(solution)/shard_map/ppermute | solution.py:353
  44.1 8.1 %collective-permute-start.5 = (bf16[256,512]{1,0:T(8,128)(2,1)S(1)}, bf16[256,512]{1,0:T(8,128)(2,1)S(1)}, u32[]{:S(2)}, u32[]{:S(2)}) collective-permute-start(bf16[256,512]{1,0:T(8,128)(2,1)S(1)} %shard_map.88.mine_ref), channel_id=1, source_target_pairs={{0,67},{1,66},{2,65},{3,64},{64,0},{65,1},{66,2},{67,3},{4,71},{5,... | collective-permute-start | bytes 786440 | tf_op jit(solution)/shard_map/ppermute | solution.py:355
  44.5 9.5 %collective-permute-start.4 = (bf16[256,512]{1,0:T(8,128)(2,1)S(1)}, bf16[256,512]{1,0:T(8,128)(2,1)S(1)}, u32[]{:S(2)}, u32[]{:S(2)}) collective-permute-start(bf16[256,512]{1,0:T(8,128)(2,1)S(1)} %shard_map.88.mine_ref), channel_id=1, source_target_pairs={{64,67},{65,66},{66,65},{67,64},{68,71},{69,70},{70,69},{71,68},{7... | collective-permute-start | bytes 786440 | tf_op jit(solution)/shard_map/ppermute | solution.py:356
  51.1 10.2 %copy-start.3 = (bf16[2,128,512]{2,1,0:T(8,128)(2,1)}, bf16[2,128,512]{2,1,0:T(8,128)(2,1)S(1)}, u32[]{:S(2)}) copy-start(bf16[2,128,512]{2,1,0:T(8,128)(2,1)S(1)} %collective-permute-done.9) | copy-start | bytes 786436
  51.1 3.8 %collective-permute-start.8 = (bf16[320,1024]{1,0:T(8,128)(2,1)S(1)}, bf16[320,1024]{1,0:T(8,128)(2,1)S(1)}, u32[]{:S(2)}, u32[]{:S(2)}) collective-permute-start(bf16[320,1024]{1,0:T(8,128)(2,1)S(1)} %collective-permute-done.n1a_ref), channel_id=1, source_target_pairs={{0,64},{64,0},{1,65},{65,1},{2,66},{66,2},{3,67},{67,3},{4,68},{68... | collective-permute-start | bytes 1966088 | tf_op jit(solution)/shard_map/ppermute | solution.py:359
  54.0 2.2 %collective-permute-start.10 = (bf16[192,1024]{1,0:T(8,128)(2,1)S(1)}, bf16[192,1024]{1,0:T(8,128)(2,1)S(1)}, u32[]{:S(2)}, u32[]{:S(2)}) collective-permute-start(bf16[192,1024]{1,0:T(8,128)(2,1)S(1)} %collective-permute-done.6.n1b_ref), channel_id=1, source_target_pairs={{0,64},{64,0},{1,65},{65,1},{2,66},{66,2},{3,67},{67,3},{4,68},{68... | collective-permute-start | bytes 1179656 | tf_op jit(solution)/shard_map/ppermute | solution.py:360
  61.3 1.0 copy-start.2
  62.3 5.1 %copy-start.4 = (bf16[2,128,512]{2,1,0:T(8,128)(2,1)S(1)}, bf16[2,128,512]{2,1,0:T(8,128)(2,1)}, u32[]{:S(2)}) copy-start(bf16[2,128,512]{2,1,0:T(8,128)(2,1)} %copy-done.3) | copy-start | bytes 786436
  62.3 21.5 %all-to-all-start.1 = ((bf16[16,256,128]{2,1,0:T(8,128)(2,1)}), bf16[16,256,128]{2,1,0:T(8,128)(2,1)}, u32[]{:S(2)}, u32[]{:S(2)}) async-start(bf16[16,256,128]{2,1,0:T(8,128)(2,1)} %copy-done.2), calls=%async_computation.1 | async-start | bytes 2097152 | tf_op jit(solution)/shard_map/all_to_all | solution.py:363
  67.4 30.9 %collective-permute-start.12 = (bf16[2,2,128,512]{3,2,1,0:T(8,128)(2,1)S(1)}, bf16[2,2,128,512]{3,2,1,0:T(8,128)(2,1)}, u32[]{:S(2)}, u32[]{:S(2)}) collective-permute-start(bf16[2,2,128,512]{3,2,1,0:T(8,128)(2,1)S(1)} %pad_maximum_fusion.low_ref), channel_id=1, source_target_pairs={{0,48},{4,52},{8,56},{12,60},{16,32},{20,36},{24,40},{28,44},{32,1... | collective-permute-start | bytes 1572872 | tf_op jit(solution)/shard_map/ppermute | solution.py:365
  70.0 30.5 %copy-start.1 = (bf16[1024,1024]{1,0:T(8,128)(2,1)S(1)}, bf16[1024,1024]{1,0:T(8,128)(2,1)}, u32[]{:S(2)}) copy-start(bf16[1024,1024]{1,0:T(8,128)(2,1)} %get-tuple-element.20.w_ref) | copy-start | bytes 6291460
  70.0 28.3 %collective-permute-start.11 = (bf16[2,256,512]{2,1,0:T(8,128)(2,1)S(1)}, bf16[2,256,512]{2,1,0:T(8,128)(2,1)}, u32[]{:S(2)}, u32[]{:S(2)}) collective-permute-start(bf16[2,256,512]{2,1,0:T(8,128)(2,1)S(1)} %get-tuple-element.37.near_ref), channel_id=1, source_target_pairs={{0,1},{1,0},{2,3},{3,2},{4,5},{5,4},{6,7},{7,6},{8,9},{9,8},{10,11... | collective-permute-start | bytes 1572872 | tf_op jit(solution)/shard_map/ppermute | solution.py:367
  85.1 4.8 %collective-permute-start.16 = (bf16[256,128]{1,0:T(8,128)(2,1)S(1)}, bf16[256,128]{1,0:T(8,128)(2,1)S(1)}, u32[]{:S(2)}, u32[]{:S(2)}) collective-permute-start(bf16[256,128]{1,0:T(8,128)(2,1)S(1)} %reduce_sum.22), channel_id=1, source_target_pairs={{0,3},{1,2},{2,67},{3,66},{64,1},{65,0},{66,65},{67,64},{4,7},{5,6... | collective-permute-start | bytes 196616 | tf_op jit(solution)/shard_map/ppermute | solution.py:371
  88.0 8.4 %collective-permute-start.15 = (bf16[256,128]{1,0:T(8,128)(2,1)S(1)}, bf16[256,128]{1,0:T(8,128)(2,1)S(1)}, u32[]{:S(2)}, u32[]{:S(2)}) collective-permute-start(bf16[256,128]{1,0:T(8,128)(2,1)S(1)} %reduce_sum.22), channel_id=1, source_target_pairs={{0,2},{1,3},{2,66},{3,67},{64,0},{65,1},{66,64},{67,65},{4,6},{5,7... | collective-permute-start | bytes 196616 | tf_op jit(solution)/shard_map/ppermute | solution.py:371
  89.4 6.9 %collective-permute-start.14 = (bf16[256,128]{1,0:T(8,128)(2,1)S(1)}, bf16[256,128]{1,0:T(8,128)(2,1)S(1)}, u32[]{:S(2)}, u32[]{:S(2)}) collective-permute-start(bf16[256,128]{1,0:T(8,128)(2,1)S(1)} %reduce_sum.22), channel_id=1, source_target_pairs={{0,1},{1,0},{2,65},{3,64},{64,3},{65,2},{66,67},{67,66},{4,5},{5,4... | collective-permute-start | bytes 196616 | tf_op jit(solution)/shard_map/ppermute | solution.py:371
  89.9 8.4 %collective-permute-start.13 = (bf16[256,128]{1,0:T(8,128)(2,1)S(1)}, bf16[256,128]{1,0:T(8,128)(2,1)S(1)}, u32[]{:S(2)}, u32[]{:S(2)}) collective-permute-start(bf16[256,128]{1,0:T(8,128)(2,1)S(1)} %reduce_sum.22), channel_id=1, source_target_pairs={{0,0},{1,1},{2,64},{3,65},{64,2},{65,3},{66,66},{67,67},{4,4},{5,5... | collective-permute-start | bytes 196616 | tf_op jit(solution)/shard_map/ppermute | solution.py:371
  100.4 2.7 %collective-permute-start.17 = (bf16[512,1024]{1,0:T(8,128)(2,1)S(1)}, bf16[512,1024]{1,0:T(8,128)(2,1)S(1)}, u32[]{:S(2)}, u32[]{:S(2)}) collective-permute-start(bf16[512,1024]{1,0:T(8,128)(2,1)S(1)} %shard_map.90), channel_id=1, source_target_pairs={{0,64},{64,0},{1,65},{65,1},{2,66},{66,2},{3,67},{67,3},{4,68},{68... | collective-permute-start | bytes 3145736 | tf_op jit(solution)/shard_map/ppermute | solution.py:373

commit v12 on v11

--- a/solution.py
+++ b/solution.py
@@ -13,7 +13,7 @@
 WIN = 9
 SLOT = WIN * SUB
 SIDE = 4
-CUT = 320
+CUT = 352
 VMEM = 24 * 1024 * 1024
 WIDE = 56 * 1024 * 1024
 

time: 108 us -> 114 us (1.056)
  waiting for transfers between devices: 32.3 us -> 44.8 us
  starting transfers between devices: 44.6 us -> 38.4 us
    ppermute x1, waiting for transfers between devices: 2.72 us -> 6.71 us  [local(): lax.ppermute(after(chain, sums), 'context', along(lambda i, j: (i ^ 1, j)))]
    ppermute x4, starting transfers between devices: 10.8 us -> 7.25 us  [local(): lax.ppermute(piece, line, moves(lambda d, x, s=s: (x // 2, 2 * d + x % 2...]
    ppermute x1, waiting for transfers between devices: 1.74 us -> 4.58 us  [local(): lax.ppermute(sums, line, moves(lambda d, x: (1, ten_n - 1 - x) if d == 1...]
    all_to_all x1, waiting for transfers between devices: 12.9 us -> 15.8 us  [local(): lax.all_to_all(partial, 'context', split_axis=0, concat_axis=0, tiled=True)]
    ppermute x4, waiting for transfers between devices: 2.38 us -> 4.6 us  [local(): lax.ppermute(piece, line, moves(lambda d, x, s=s: (x // 2, 2 * d + x % 2...]
  transfers between devices with their start and end apart: 20 -> 20, of which waited for: 12 -> 11; matrix products, arithmetic and copies ran while one was open for 2% -> 2% of each run, Pallas kernels for 13% -> 12%
where the time goes in v12:
time: 114 us; the launch traced here: 112 us
  waiting for transfers between devices  44.8 us (39%)
  starting transfers between devices  38.4 us (34%)
  Pallas kernels  24.2 us (21%)
  local copies, waits for them, and re-layouts  2.17 us (2%)
  other arithmetic  1.81 us (2%)
    all_to_all x1, waiting for transfers between devices, local(): lax.all_to_all(partial, 'context', split_axis=0, concat_axis=0, tiled=True)  15.8 us
    ppermute x1, waiting for transfers between devices, local(): lax.ppermute(chain, 'context', along(lambda i, j: (i, j ^ 1)))  7.86 us
    all_to_all x1, starting transfers between devices, local(): lax.all_to_all(outgoing, 'context', split_axis=0, concat_axis=0, tiled=True)  7.77 us
    ppermute x4, starting transfers between devices, local(): lax.ppermute(piece, line, moves(lambda d, x, s=s: (x // 2, 2 * d + x % 2...  7.25 us
    ppermute x1, waiting for transfers between devices, local(): lax.ppermute(after(chain, sums), 'context', along(lambda i, j: (i ^ 1, j)))  6.71 us
    pallas_call x1, Pallas kernels, chain_terms(): pl.pallas_call(chain_kernel, in_specs=[vmem, vmem, pl.BlockSpec(memory_sp...  6.54 us
    pallas_call x1, Pallas kernels, segment_sums(): pl.pallas_call(seg_kernel, in_specs=[vmem, vmem, pl.BlockSpec(memory_spac...  5.13 us
    pallas_call x2, Pallas kernels, context_rows(): pl.pallas_call(functools.partial(rows_kernel, which), in_specs=[vmem] * (...  5.04 us
  transfers between devices with their start and end apart: 20, of which 11 were waited for; matrix products, arithmetic and copies ran while one was open for 2% of the time, Pallas kernels for 12%

profile of v12, /device:TPU:1, one launch (start us, length us, event | category | flops | bytes accessed | tf_op | source)
XLA Modules:
  0.0 112.3 jit_solution(6533753610365727837)
XLA Ops:
  0.6 1.2 %slice_bitcast_fusion = bf16[352,1024]{1,0:T(8,128)(2,1)S(1)} fusion(bf16[1,512,1024]{2,1,0:T(8,128)(2,1)} %param.10), kind=kLoop, calls=%fused_computation | loop fusion | bytes 1441792 | tf_op jit(solution)/shard_map/slice | solution.py:329
  1.8 2.1 %collective-permute-start = (bf16[352,1024]{1,0:T(8,128)(2,1)S(1)}, bf16[352,1024]{1,0:T(8,128)(2,1)S(1)}, u32[]{:S(2)}, u32[]{:S(2)}) collective-permute-start(bf16[352,1024]{1,0:T(8,128)(2,1)S(1)} %slice_bitcast_fusion), channel_id=1, source_target_pairs={{0,1},{1,0},{2,3},{3,2},{4,5},{5,4},{6,7},{7,6},{8,9},{9,8},{10,11... | collective-permute-start | bytes 2162696 | tf_op jit(solution)/shard_map/ppermute | solution.py:329
  3.9 6.5 %shard_map.86 = (bf16[1024,1024]{1,0:T(8,128)(2,1)}, bf16[128,512]{1,0:T(8,128)(2,1)}, bf16[128,512]{1,0:T(8,128)(2,1)}, bf16[2,128,512]{2,1,0:T(8,128)(2,1)}) custom-call(bf16[1024,1024]{1,0:T(8,128)(2,1)} %value_ref.1, bf16[1024,1024]{1,0:T(8,128)(2,1)} %out_w_ref.1, bf16[4096,1024]{1,0:T(8,128)(2,1)} %global_ref.1), custom_call_target="tpu_custom_call" | custom-call | tf_op jit(solution)/shard_map/pallas_call | solution.py:227
  10.5 1.9 %collective-permute-start.1 = (bf16[2,128,512]{2,1,0:T(8,128)(2,1)}, bf16[2,128,512]{2,1,0:T(8,128)(2,1)S(1)}, u32[]{:S(2)}, u32[]{:S(2)}) collective-permute-start(bf16[2,128,512]{2,1,0:T(8,128)(2,1)} %get-tuple-element.22), channel_id=1, source_target_pairs={{0,3},{1,2},{2,1},{3,0},{4,7},{5,6},{6,5},{7,4},{8,11},{9,10},{10,... | collective-permute-start | bytes 786440 | tf_op jit(solution)/shard_map/ppermute | solution.py:337
  12.4 5.1 %shard_map.87 = bf16[1152,256]{1,0:T(8,128)(2,1)} custom-call(s32[64,128]{1,0:T(8,128)} %bitcast.30, s32[64,128]{1,0:T(8,128)} %bitcast.33, bf16[4096,1024]{1,0:T(8,128)(2,1)} %bitcast.24), custom_call_target="tpu_custom_call" | custom-call | tf_op jit(solution)/shard_map/pallas_call | solution.py:94
  17.5 0.0 copy-start
  17.5 1.3 %collective-permute-done.1 = bf16[2,128,512]{2,1,0:T(8,128)(2,1)S(1)} collective-permute-done((bf16[2,128,512]{2,1,0:T(8,128)(2,1)}, bf16[2,128,512]{2,1,0:T(8,128)(2,1)S(1)}, u32[]{:S(2)}, u32[]{:S(2)}) %collective-permute-start.1) | collective-permute-done | bytes 262176 | tf_op jit(solution)/shard_map/ppermute | solution.py:337
  18.8 0.4 collective-permute-done.n1a_ref
  19.3 1.7 %collective-permute-start.2 = (bf16[128,512]{1,0:T(8,128)(2,1)S(1)}, bf16[128,512]{1,0:T(8,128)(2,1)S(1)}, u32[]{:S(2)}, u32[]{:S(2)}) collective-permute-start(bf16[128,512]{1,0:T(8,128)(2,1)S(1)} %fusion), channel_id=1, source_target_pairs={{0,1},{1,0},{2,3},{3,2},{4,5},{5,4},{6,7},{7,6},{8,9},{9,8},{10,11... | collective-permute-start | bytes 393224 | tf_op jit(solution)/shard_map/ppermute | solution.py:345
  21.0 0.3 convert_reduce_fusion
  21.3 7.8 %all-to-all-start = ((bf16[16,72,256]{2,1,0:T(8,128)(2,1)}), bf16[16,72,256]{2,1,0:T(8,128)(2,1)S(1)}, u32[]{:S(2)}, u32[]{:S(2)}) async-start(bf16[16,72,256]{2,1,0:T(8,128)(2,1)} %bitcast.25), calls=%async_computation | async-start | bytes 1179648 | tf_op jit(solution)/shard_map/all_to_all | solution.py:341
  29.1 0.1 fusion.2
  29.2 1.4 %collective-permute-start.3 = (bf16[128,512]{1,0:T(8,128)(2,1)S(1)}, bf16[128,512]{1,0:T(8,128)(2,1)S(1)}, u32[]{:S(2)}, u32[]{:S(2)}) collective-permute-start(bf16[128,512]{1,0:T(8,128)(2,1)S(1)} %fusion.2), channel_id=1, source_target_pairs={{0,4},{4,0},{8,12},{12,8},{16,20},{20,16},{24,28},{28,24},{32,36},... | collective-permute-start | bytes 393224 | tf_op jit(solution)/shard_map/ppermute | solution.py:347
  30.6 7.9 %collective-permute-done.3 = bf16[128,512]{1,0:T(8,128)(2,1)S(1)} collective-permute-done((bf16[128,512]{1,0:T(8,128)(2,1)S(1)}, bf16[128,512]{1,0:T(8,128)(2,1)S(1)}, u32[]{:S(2)}, u32[]{:S(2)}) %collective-permute-start.3) | collective-permute-done | bytes 131104 | tf_op jit(solution)/shard_map/ppermute | solution.py:347
  38.5 0.8 all-to-all-done
  39.4 0.9 shard_map.88.mine_ref
  40.2 4.4 %collective-permute-start.7 = (bf16[512,1024]{1,0:T(8,128)(2,1)S(1)}, bf16[512,1024]{1,0:T(8,128)(2,1)S(1)}, u32[]{:S(2)}, u32[]{:S(2)}) collective-permute-start(bf16[512,1024]{1,0:T(8,128)(2,1)S(1)} %bitcast.20), channel_id=1, source_target_pairs={{0,64},{64,0},{1,65},{65,1},{2,66},{66,2},{3,67},{67,3},{4,68},{68... | collective-permute-start | bytes 3145736 | tf_op jit(solution)/shard_map/ppermute | solution.py:358
  44.7 0.2 collective-permute-start.8
  44.9 0.3 collective-permute-start.6
  45.2 0.6 collective-permute-start.5
  45.8 6.7 %collective-permute-done.9 = bf16[2,128,512]{2,1,0:T(8,128)(2,1)S(1)} collective-permute-done((bf16[2,128,512]{2,1,0:T(8,128)(2,1)S(1)}, bf16[2,128,512]{2,1,0:T(8,128)(2,1)S(1)}, u32[]{:S(2)}, u32[]{:S(2)}) %collective-permute-start.9) | collective-permute-done | bytes 262176 | tf_op jit(solution)/shard_map/ppermute | solution.py:357
  52.5 3.7 %collective-permute-start.4 = (bf16[256,512]{1,0:T(8,128)(2,1)S(1)}, bf16[256,512]{1,0:T(8,128)(2,1)S(1)}, u32[]{:S(2)}, u32[]{:S(2)}) collective-permute-start(bf16[256,512]{1,0:T(8,128)(2,1)S(1)} %shard_map.88.mine_ref), channel_id=1, source_target_pairs={{64,67},{65,66},{66,65},{67,64},{68,71},{69,70},{70,69},{71,68},{7... | collective-permute-start | bytes 786440 | tf_op jit(solution)/shard_map/ppermute | solution.py:356
  56.2 0.0 collective-permute-done.5.cross_ref
  56.2 4.6 %collective-permute-done.4.third_ref = bf16[256,512]{1,0:T(8,128)(2,1)S(1)} collective-permute-done((bf16[256,512]{1,0:T(8,128)(2,1)S(1)}, bf16[256,512]{1,0:T(8,128)(2,1)S(1)}, u32[]{:S(2)}, u32[]{:S(2)}) %collective-permute-start.4) | collective-permute-done | bytes 262176 | tf_op jit(solution)/shard_map/ppermute | solution.py:356
  60.8 0.0 collective-permute-done.6.n1b_ref
  60.8 0.0 collective-permute-start.10
  60.8 1.6 %collective-permute-done.10.f1b_ref = bf16[160,1024]{1,0:T(8,128)(2,1)S(1)} collective-permute-done((bf16[160,1024]{1,0:T(8,128)(2,1)S(1)}, bf16[160,1024]{1,0:T(8,128)(2,1)S(1)}, u32[]{:S(2)}, u32[]{:S(2)}) %collective-permute-start.10) | collective-permute-done | bytes 327712 | tf_op jit(solution)/shard_map/ppermute | solution.py:360
  62.5 5.0 %shard_map.89 = (bf16[16,256,128]{2,1,0:T(8,128)(2,1)S(1)}, bf16[2,256,512]{2,1,0:T(8,128)(2,1)S(1)}) custom-call(bf16[256,512]{1,0:T(8,128)(2,1)S(1)} %shard_map.88.mine_ref, bf16[256,512]{1,0:T(8,128)(2,1)S(1)} %collective-permute-done.4.third_ref, bf16[256,512]{1,0:T(8,128)(2,1)S(1)} %collective-permute-done.5.cross_ref, bf16[512,1024]{1,0:T(8,128)(2,1)S(1)} %bitcast.22, ...), custom_call_target="tpu_custom_call" | custom-call | tf_op jit(solution)/shard_map/pallas_call | solution.py:172
  67.5 0.0 copy-start.2
  67.5 1.0 copy-done.2
  68.5 4.3 %all-to-all-start.1 = ((bf16[16,256,128]{2,1,0:T(8,128)(2,1)}), bf16[16,256,128]{2,1,0:T(8,128)(2,1)}, u32[]{:S(2)}, u32[]{:S(2)}) async-start(bf16[16,256,128]{2,1,0:T(8,128)(2,1)} %copy-done.2), calls=%async_computation.1 | async-start | bytes 2097152 | tf_op jit(solution)/shard_map/all_to_all | solution.py:363
  72.8 0.1 pad_maximum_fusion.low_ref
  72.9 2.5 %collective-permute-start.12 = (bf16[2,2,128,512]{3,2,1,0:T(8,128)(2,1)S(1)}, bf16[2,2,128,512]{3,2,1,0:T(8,128)(2,1)}, u32[]{:S(2)}, u32[]{:S(2)}) collective-permute-start(bf16[2,2,128,512]{3,2,1,0:T(8,128)(2,1)S(1)} %pad_maximum_fusion.low_ref), channel_id=1, source_target_pairs={{0,48},{4,52},{8,56},{12,60},{16,32},{20,36},{24,40},{28,44},{32,1... | collective-permute-start | bytes 1572872 | tf_op jit(solution)/shard_map/ppermute | solution.py:365
  75.4 15.8 %all-to-all-done.1 = bf16[16,256,128]{2,1,0:T(8,128)(2,1)} async-done(((bf16[16,256,128]{2,1,0:T(8,128)(2,1)}), bf16[16,256,128]{2,1,0:T(8,128)(2,1)}, u32[]{:S(2)}, u32[]{:S(2)}) %all-to-all-start.1) | async-done | bytes 1048608 | tf_op jit(solution)/shard_map/all_to_all | solution.py:363
  91.2 1.4 %reduce_sum.22 = bf16[256,128]{1,0:T(8,128)(2,1)S(1)} reduce(bf16[16,256,128]{2,1,0:T(8,128)(2,1)} %all-to-all-done.1, bf16[]{:T(256)} %constant.25.clone.1), dimensions={0}, to_apply=%region_1.2 | reduce | flops 491520 | bytes 1114114 | tf_op jit(solution)/shard_map/reduce_sum | solution.py:368
  92.6 0.5 collective-permute-start.16
  93.1 2.8 %collective-permute-start.15 = (bf16[256,128]{1,0:T(8,128)(2,1)S(1)}, bf16[256,128]{1,0:T(8,128)(2,1)S(1)}, u32[]{:S(2)}, u32[]{:S(2)}) collective-permute-start(bf16[256,128]{1,0:T(8,128)(2,1)S(1)} %reduce_sum.22), channel_id=1, source_target_pairs={{0,2},{1,3},{2,66},{3,67},{64,0},{65,1},{66,64},{67,65},{4,6},{5,7... | collective-permute-start | bytes 196616 | tf_op jit(solution)/shard_map/ppermute | solution.py:371
  95.9 0.0 collective-permute-start.14
  95.9 1.5 %collective-permute-done.16.d_ref = bf16[256,128]{1,0:T(8,128)(2,1)S(1)} collective-permute-done((bf16[256,128]{1,0:T(8,128)(2,1)S(1)}, bf16[256,128]{1,0:T(8,128)(2,1)S(1)}, u32[]{:S(2)}, u32[]{:S(2)}) %collective-permute-start.16) | collective-permute-done | bytes 65568 | tf_op jit(solution)/shard_map/ppermute | solution.py:371
  97.4 4.0 %collective-permute-start.13 = (bf16[256,128]{1,0:T(8,128)(2,1)S(1)}, bf16[256,128]{1,0:T(8,128)(2,1)S(1)}, u32[]{:S(2)}, u32[]{:S(2)}) collective-permute-start(bf16[256,128]{1,0:T(8,128)(2,1)S(1)} %reduce_sum.22), channel_id=1, source_target_pairs={{0,0},{1,1},{2,64},{3,65},{64,2},{65,3},{66,66},{67,67},{4,4},{5,5... | collective-permute-start | bytes 196616 | tf_op jit(solution)/shard_map/ppermute | solution.py:371
  101.4 0.0 collective-permute-done.14.b_ref
  101.4 3.1 %collective-permute-done.13.a_ref = bf16[256,128]{1,0:T(8,128)(2,1)S(1)} collective-permute-done((bf16[256,128]{1,0:T(8,128)(2,1)S(1)}, bf16[256,128]{1,0:T(8,128)(2,1)S(1)}, u32[]{:S(2)}, u32[]{:S(2)}) %collective-permute-start.13) | collective-permute-done | bytes 65568 | tf_op jit(solution)/shard_map/ppermute | solution.py:371
  104.5 0.0 collective-permute-done.12.high_ref
  104.5 2.0 %shard_map.90 = bf16[512,1024]{1,0:T(8,128)(2,1)S(1)} custom-call(bf16[2,256,512]{2,1,0:T(8,128)(2,1)S(1)} %get-tuple-element.37.near_ref, bf16[2,256,512]{2,1,0:T(8,128)(2,1)} %collective-permute-done.11.far_ref, bf16[2,2,128,512]{3,2,1,0:T(8,128)(2,1)S(1)} %pad_maximum_fusion.low_ref, bf16[2,2,128,512]{3,2,1,0:T(8,128)(2,1)} %collective-permute-done.12.high_ref), custom_call_target="tpu_custom_call" | custom-call | tf_op jit(solution)/shard_map/pallas_call | solution.py:266
  106.5 0.1 collective-permute-start.17
  106.6 1.6 %shard_map.92 = f32[128,1024]{1,0:T(8,128)} custom-call(bf16[256,128]{1,0:T(8,128)(2,1)S(1)} %collective-permute-done.13.a_ref, bf16[256,128]{1,0:T(8,128)(2,1)S(1)} %collective-permute-done.14.b_ref, bf16[256,128]{1,0:T(8,128)(2,1)S(1)} %collective-permute-done.15.c_ref, bf16[256,128]{1,0:T(8,128)(2,1)S(1)} %collective-permute-done.16.d_ref, ...), custom_call_target="tpu_custom_call" | custom-call | tf_op jit(solution)/shard_map/pallas_call | solution.py:295
  108.2 1.0 collective-permute-done.17.rest_0_
  109.2 3.0 %shard_map.91 = bf16[512,1024]{1,0:T(8,128)(2,1)} custom-call(bf16[2,256,512]{2,1,0:T(8,128)(2,1)S(1)} %get-tuple-element.37.near_ref, bf16[2,256,512]{2,1,0:T(8,128)(2,1)} %collective-permute-done.11.far_ref, bf16[2,2,128,512]{3,2,1,0:T(8,128)(2,1)S(1)} %pad_maximum_fusion.low_ref, bf16[2,2,128,512]{3,2,1,0:T(8,128)(2,1)} %collective-permute-done.12.high_ref, ...), custom_call_target="tpu_custom_call" | custom-call | tf_op jit(solution)/shard_map/pallas_call | solution.py:266
  (21 shorter events, 0.1 us)
Async XLA Ops:
  1.8 17.5 %collective-permute-start = (bf16[352,1024]{1,0:T(8,128)(2,1)S(1)}, bf16[352,1024]{1,0:T(8,128)(2,1)S(1)}, u32[]{:S(2)}, u32[]{:S(2)}) collective-permute-start(bf16[352,1024]{1,0:T(8,128)(2,1)S(1)} %slice_bitcast_fusion), channel_id=1, source_target_pairs={{0,1},{1,0},{2,3},{3,2},{4,5},{5,4},{6,7},{7,6},{8,9},{9,8},{10,11... | collective-permute-start | bytes 2162696 | tf_op jit(solution)/shard_map/ppermute | solution.py:329
  10.5 8.4 %collective-permute-start.1 = (bf16[2,128,512]{2,1,0:T(8,128)(2,1)}, bf16[2,128,512]{2,1,0:T(8,128)(2,1)S(1)}, u32[]{:S(2)}, u32[]{:S(2)}) collective-permute-start(bf16[2,128,512]{2,1,0:T(8,128)(2,1)} %get-tuple-element.22), channel_id=1, source_target_pairs={{0,3},{1,2},{2,1},{3,0},{4,7},{5,6},{6,5},{7,4},{8,11},{9,10},{10,... | collective-permute-start | bytes 786440 | tf_op jit(solution)/shard_map/ppermute | solution.py:337
  12.4 6.9 %copy-start.4 = (bf16[128,512]{1,0:T(8,128)(2,1)S(1)}, bf16[128,512]{1,0:T(8,128)(2,1)}, u32[]{:S(2)}) copy-start(bf16[128,512]{1,0:T(8,128)(2,1)} %get-tuple-element.26) | copy-start | bytes 393220
  12.4 8.7 %copy-start.3 = (s32[1,8192]{1,0:T(1,128)S(1)}, s32[1,8192]{1,0:T(1,128)}, u32[]{:S(2)}) copy-start(s32[1,8192]{1,0:T(1,128)} %param.8) | copy-start | bytes 98308
  12.4 16.7 %copy-start.5 = (bf16[128,512]{1,0:T(8,128)(2,1)S(1)}, bf16[128,512]{1,0:T(8,128)(2,1)}, u32[]{:S(2)}) copy-start(bf16[128,512]{1,0:T(8,128)(2,1)} %get-tuple-element.24) | copy-start | bytes 393220
  17.5 22.7 %copy-start = (bf16[1,512,1024]{2,1,0:T(8,128)(2,1)S(1)}, bf16[1,512,1024]{2,1,0:T(8,128)(2,1)}, u32[]{:S(2)}) copy-start(bf16[1,512,1024]{2,1,0:T(8,128)(2,1)} %param.10) | copy-start | bytes 3145732
  19.3 9.8 %collective-permute-start.2 = (bf16[128,512]{1,0:T(8,128)(2,1)S(1)}, bf16[128,512]{1,0:T(8,128)(2,1)S(1)}, u32[]{:S(2)}, u32[]{:S(2)}) collective-permute-start(bf16[128,512]{1,0:T(8,128)(2,1)S(1)} %fusion), channel_id=1, source_target_pairs={{0,1},{1,0},{2,3},{3,2},{4,5},{5,4},{6,7},{7,6},{8,9},{9,8},{10,11... | collective-permute-start | bytes 393224 | tf_op jit(solution)/shard_map/ppermute | solution.py:345
  21.3 18.1 %all-to-all-start = ((bf16[16,72,256]{2,1,0:T(8,128)(2,1)}), bf16[16,72,256]{2,1,0:T(8,128)(2,1)S(1)}, u32[]{:S(2)}, u32[]{:S(2)}) async-start(bf16[16,72,256]{2,1,0:T(8,128)(2,1)} %bitcast.25), calls=%async_computation | async-start | bytes 1179648 | tf_op jit(solution)/shard_map/all_to_all | solution.py:341
  29.2 9.3 %collective-permute-start.3 = (bf16[128,512]{1,0:T(8,128)(2,1)S(1)}, bf16[128,512]{1,0:T(8,128)(2,1)S(1)}, u32[]{:S(2)}, u32[]{:S(2)}) collective-permute-start(bf16[128,512]{1,0:T(8,128)(2,1)S(1)} %fusion.2), channel_id=1, source_target_pairs={{0,4},{4,0},{8,12},{12,8},{16,20},{20,16},{24,28},{28,24},{32,36},... | collective-permute-start | bytes 393224 | tf_op jit(solution)/shard_map/ppermute | solution.py:347
  40.2 22.2 %collective-permute-start.7 = (bf16[512,1024]{1,0:T(8,128)(2,1)S(1)}, bf16[512,1024]{1,0:T(8,128)(2,1)S(1)}, u32[]{:S(2)}, u32[]{:S(2)}) collective-permute-start(bf16[512,1024]{1,0:T(8,128)(2,1)S(1)} %bitcast.20), channel_id=1, source_target_pairs={{0,64},{64,0},{1,65},{65,1},{2,66},{66,2},{3,67},{67,3},{4,68},{68... | collective-permute-start | bytes 3145736 | tf_op jit(solution)/shard_map/ppermute | solution.py:358
  44.7 7.9 %collective-permute-start.9 = (bf16[2,128,512]{2,1,0:T(8,128)(2,1)S(1)}, bf16[2,128,512]{2,1,0:T(8,128)(2,1)S(1)}, u32[]{:S(2)}, u32[]{:S(2)}) collective-permute-start(bf16[2,128,512]{2,1,0:T(8,128)(2,1)S(1)} %pad_maximum_fusion.1), channel_id=1, source_target_pairs={{0,16},{4,20},{8,24},{12,28},{16,0},{20,4},{24,8},{28,12},{32,48},... | collective-permute-start | bytes 786440 | tf_op jit(solution)/shard_map/ppermute | solution.py:357
  44.7 17.8 %collective-permute-start.8 = (bf16[352,1024]{1,0:T(8,128)(2,1)S(1)}, bf16[352,1024]{1,0:T(8,128)(2,1)S(1)}, u32[]{:S(2)}, u32[]{:S(2)}) collective-permute-start(bf16[352,1024]{1,0:T(8,128)(2,1)S(1)} %collective-permute-done.n1a_ref), channel_id=1, source_target_pairs={{0,64},{64,0},{1,65},{65,1},{2,66},{66,2},{3,67},{67,3},{4,68},{68... | collective-permute-start | bytes 2162696 | tf_op jit(solution)/shard_map/ppermute | solution.py:359
  44.9 16.0 %collective-permute-start.6 = (bf16[160,1024]{1,0:T(8,128)(2,1)S(1)}, bf16[160,1024]{1,0:T(8,128)(2,1)S(1)}, u32[]{:S(2)}, u32[]{:S(2)}) collective-permute-start(bf16[160,1024]{1,0:T(8,128)(2,1)S(1)} %slice.19), channel_id=1, source_target_pairs={{0,1},{1,0},{2,3},{3,2},{4,5},{5,4},{6,7},{7,6},{8,9},{9,8},{10,11... | collective-permute-start | bytes 983048 | tf_op jit(solution)/shard_map/ppermute | solution.py:353
  45.2 11.0 %collective-permute-start.5 = (bf16[256,512]{1,0:T(8,128)(2,1)S(1)}, bf16[256,512]{1,0:T(8,128)(2,1)S(1)}, u32[]{:S(2)}, u32[]{:S(2)}) collective-permute-start(bf16[256,512]{1,0:T(8,128)(2,1)S(1)} %shard_map.88.mine_ref), channel_id=1, source_target_pairs={{0,67},{1,66},{2,65},{3,64},{64,0},{65,1},{66,2},{67,3},{4,71},{5,... | collective-permute-start | bytes 786440 | tf_op jit(solution)/shard_map/ppermute | solution.py:355
  52.5 8.3 %collective-permute-start.4 = (bf16[256,512]{1,0:T(8,128)(2,1)S(1)}, bf16[256,512]{1,0:T(8,128)(2,1)S(1)}, u32[]{:S(2)}, u32[]{:S(2)}) collective-permute-start(bf16[256,512]{1,0:T(8,128)(2,1)S(1)} %shard_map.88.mine_ref), channel_id=1, source_target_pairs={{64,67},{65,66},{66,65},{67,64},{68,71},{69,70},{70,69},{71,68},{7... | collective-permute-start | bytes 786440 | tf_op jit(solution)/shard_map/ppermute | solution.py:356
  60.8 1.6 %collective-permute-start.10 = (bf16[160,1024]{1,0:T(8,128)(2,1)S(1)}, bf16[160,1024]{1,0:T(8,128)(2,1)S(1)}, u32[]{:S(2)}, u32[]{:S(2)}) collective-permute-start(bf16[160,1024]{1,0:T(8,128)(2,1)S(1)} %collective-permute-done.6.n1b_ref), channel_id=1, source_target_pairs={{0,64},{64,0},{1,65},{65,1},{2,66},{66,2},{3,67},{67,3},{4,68},{68... | collective-permute-start | bytes 983048 | tf_op jit(solution)/shard_map/ppermute | solution.py:360
  67.5 1.0 copy-start.2
  68.5 22.7 %all-to-all-start.1 = ((bf16[16,256,128]{2,1,0:T(8,128)(2,1)}), bf16[16,256,128]{2,1,0:T(8,128)(2,1)}, u32[]{:S(2)}, u32[]{:S(2)}) async-start(bf16[16,256,128]{2,1,0:T(8,128)(2,1)} %copy-done.2), calls=%async_computation.1 | async-start | bytes 2097152 | tf_op jit(solution)/shard_map/all_to_all | solution.py:363
  72.9 31.6 %collective-permute-start.12 = (bf16[2,2,128,512]{3,2,1,0:T(8,128)(2,1)S(1)}, bf16[2,2,128,512]{3,2,1,0:T(8,128)(2,1)}, u32[]{:S(2)}, u32[]{:S(2)}) collective-permute-start(bf16[2,2,128,512]{3,2,1,0:T(8,128)(2,1)S(1)} %pad_maximum_fusion.low_ref), channel_id=1, source_target_pairs={{0,48},{4,52},{8,56},{12,60},{16,32},{20,36},{24,40},{28,44},{32,1... | collective-permute-start | bytes 1572872 | tf_op jit(solution)/shard_map/ppermute | solution.py:365
  75.4 31.2 %copy-start.1 = (bf16[1024,1024]{1,0:T(8,128)(2,1)S(1)}, bf16[1024,1024]{1,0:T(8,128)(2,1)}, u32[]{:S(2)}) copy-start(bf16[1024,1024]{1,0:T(8,128)(2,1)} %get-tuple-element.20.w_ref) | copy-start | bytes 6291460
  75.4 29.0 %collective-permute-start.11 = (bf16[2,256,512]{2,1,0:T(8,128)(2,1)S(1)}, bf16[2,256,512]{2,1,0:T(8,128)(2,1)}, u32[]{:S(2)}, u32[]{:S(2)}) collective-permute-start(bf16[2,256,512]{2,1,0:T(8,128)(2,1)S(1)} %get-tuple-element.37.near_ref), channel_id=1, source_target_pairs={{0,1},{1,0},{2,3},{3,2},{4,5},{5,4},{6,7},{7,6},{8,9},{9,8},{10,11... | collective-permute-start | bytes 1572872 | tf_op jit(solution)/shard_map/ppermute | solution.py:367
  92.6 4.8 %collective-permute-start.16 = (bf16[256,128]{1,0:T(8,128)(2,1)S(1)}, bf16[256,128]{1,0:T(8,128)(2,1)S(1)}, u32[]{:S(2)}, u32[]{:S(2)}) collective-permute-start(bf16[256,128]{1,0:T(8,128)(2,1)S(1)} %reduce_sum.22), channel_id=1, source_target_pairs={{0,3},{1,2},{2,67},{3,66},{64,1},{65,0},{66,65},{67,64},{4,7},{5,6... | collective-permute-start | bytes 196616 | tf_op jit(solution)/shard_map/ppermute | solution.py:371
  93.1 8.2 %collective-permute-start.15 = (bf16[256,128]{1,0:T(8,128)(2,1)S(1)}, bf16[256,128]{1,0:T(8,128)(2,1)S(1)}, u32[]{:S(2)}, u32[]{:S(2)}) collective-permute-start(bf16[256,128]{1,0:T(8,128)(2,1)S(1)} %reduce_sum.22), channel_id=1, source_target_pairs={{0,2},{1,3},{2,66},{3,67},{64,0},{65,1},{66,64},{67,65},{4,6},{5,7... | collective-permute-start | bytes 196616 | tf_op jit(solution)/shard_map/ppermute | solution.py:371
  95.9 5.5 %collective-permute-start.14 = (bf16[256,128]{1,0:T(8,128)(2,1)S(1)}, bf16[256,128]{1,0:T(8,128)(2,1)S(1)}, u32[]{:S(2)}, u32[]{:S(2)}) collective-permute-start(bf16[256,128]{1,0:T(8,128)(2,1)S(1)} %reduce_sum.22), channel_id=1, source_target_pairs={{0,1},{1,0},{2,65},{3,64},{64,3},{65,2},{66,67},{67,66},{4,5},{5,4... | collective-permute-start | bytes 196616 | tf_op jit(solution)/shard_map/ppermute | solution.py:371
  97.4 7.1 %collective-permute-start.13 = (bf16[256,128]{1,0:T(8,128)(2,1)S(1)}, bf16[256,128]{1,0:T(8,128)(2,1)S(1)}, u32[]{:S(2)}, u32[]{:S(2)}) collective-permute-start(bf16[256,128]{1,0:T(8,128)(2,1)S(1)} %reduce_sum.22), channel_id=1, source_target_pairs={{0,0},{1,1},{2,64},{3,65},{64,2},{65,3},{66,66},{67,67},{4,4},{5,5... | collective-permute-start | bytes 196616 | tf_op jit(solution)/shard_map/ppermute | solution.py:371
  106.5 2.7 %collective-permute-start.17 = (bf16[512,1024]{1,0:T(8,128)(2,1)S(1)}, bf16[512,1024]{1,0:T(8,128)(2,1)S(1)}, u32[]{:S(2)}, u32[]{:S(2)}) collective-permute-start(bf16[512,1024]{1,0:T(8,128)(2,1)S(1)} %shard_map.90), channel_id=1, source_target_pairs={{0,64},{64,0},{1,65},{65,1},{2,66},{66,2},{3,67},{67,3},{4,68},{68... | collective-permute-start | bytes 3145736 | tf_op jit(solution)/shard_map/ppermute | solution.py:373
